TPU v7x, 512 devices: a whole 4x4x16 slice. The times are simulated.
512 devices in a mesh: dp: 32 (over z, core), section: 4 (over y), shard: 4 (over x).
Axes of the slice: x: 4, y: 4, z: 16, core: 2. Of those that a mesh axis runs over, the one named last changes fastest.
Arguments:
- boards: int32 [512, 361], P(('dp', 'shard')), may hold values from 0 to 2
- neighbours: int32 [512, 10], P(('dp', 'shard')), may hold values from 0 to 1023
- counts: int32 [512], P(('dp', 'shard')), may hold values from 0 to 10
- database: bfloat16 [1024, 1024], P('shard'), may hold values from -6 to 6
- w_first: bfloat16 [1024, 1024], replicated, may hold values from -0.1875 to 0.1875
- w_second: bfloat16 [1024, 256], replicated, may hold values from -0.1875 to 0.1875
- embed: bfloat16 [3, 256], replicated, may hold values from -4 to 4
- conv_weight: bfloat16 [4, 2304, 256], P('section', None, 'shard'), may hold values from -0.125 to 0.125
- cotangent: bfloat16 [512, 361, 256], P(('dp', 'shard')), may hold values from -6 to 6
Outputs:
- w1_grad: bfloat16 [1024, 1024], P(('section', 'shard'))
- w2_grad: bfloat16 [1024, 256], P(('section', 'shard'))
- embed_grad: bfloat16 [3, 256], replicated
- conv_grad: bfloat16 [4, 2304, 256], P('section', None, 'shard')
Inputs may be any that keep to these rules, and one draw needn't show every extreme that they name: Slots from counts[i] on are unused. `neighbours`: rows of database.
All inputs are finite; a program needn't handle non-finite values.
Results may differ from a plain program's by a relative error of at most 0.023.
Values may be sent and summed in bfloat16 or wider, within the bound.
No kernel may reach another device: no remote copies, remote signals or barrier semaphores. Data moves between devices by JAX's collectives and lax.ppermute only.
A program may use at most 128 MiB of HBM per device.

v0:
```python
import jax
import jax.numpy as jnp
from jax import lax
from jax.sharding import PartitionSpec as P

BOARD = 19


NORM_EPS = 1e-05


def shifted(block, axis, distance):
    devices = range(lax.axis_size(axis))
    route = [(i - distance, i) for i in devices if i - distance in devices]
    return lax.ppermute(block, axis, route)


def tap_patches(stream):
    grid = stream.reshape(BOARD, BOARD, -1)
    padded = jnp.pad(grid, ((1, 1), (1, 1), (0, 0)))
    taps = [padded[a : a + BOARD, b : b + BOARD] for a in range(3) for b in range(3)]
    return jnp.concatenate(taps, axis=-1).reshape(BOARD * BOARD, -1)


def fold_taps(spread, channels):
    grid = spread.reshape(BOARD, BOARD, 9, channels)
    folded = jnp.zeros((BOARD + 2, BOARD + 2, channels), jnp.float32)
    for a in range(3):
        for b in range(3):
            folded = folded.at[a : a + BOARD, b : b + BOARD].add(grid[:, :, 3 * a + b])
    return folded[1 : BOARD + 1, 1 : BOARD + 1].reshape(BOARD * BOARD, channels)


def gelu_slope(value):
    normal_cdf = 0.5 * (1.0 + jax.scipy.special.erf(value * 0.7071067811865476))
    density = jnp.exp(-0.5 * value * value) * 0.3989422804014327
    return normal_cdf + value * density


def silu_slope(value):
    sigma = jax.nn.sigmoid(value)
    return sigma * (1.0 + value * (1.0 - sigma))


def body(boards, neighbours, counts, database, w_first, w_second, embed, conv_weight, cotangent):
    micro = boards.shape[0]
    slots = neighbours.shape[1]
    rows_dev, width = database.shape
    channels = embed.shape[1]
    points = boards.shape[1]
    shards = lax.axis_size("shard")
    sections = lax.axis_size("section")
    shard_pos = lax.axis_index("shard")
    section_pos = lax.axis_index("section")
    live = lax.broadcasted_iota(jnp.int32, (micro, slots), 1) < counts[:, None]
    divisor = jnp.maximum(counts, 1).astype(jnp.float32)[:, None]
    piece = lax.all_gather(database, "shard", axis=0, tiled=True)
    positions = lax.broadcasted_iota(jnp.int32, (1, 1, piece.shape[0]), 2)
    hits = (neighbours[:, :, None] == positions) & live[:, :, None]
    weights = jnp.sum(hits.astype(jnp.float32), axis=1).astype(jnp.bfloat16)
    summed = jnp.dot(weights, piece, preferred_element_type=jnp.float32)
    context = (summed / divisor).astype(jnp.bfloat16)
    preact = jnp.dot(context, w_first, preferred_element_type=jnp.float32)
    hidden = jax.nn.gelu(preact, approximate=False).astype(jnp.bfloat16)
    encoded = jnp.dot(hidden, w_second, preferred_element_type=jnp.float32)
    onehot = (boards[:, :, None] == lax.broadcasted_iota(jnp.int32, (1, 1, 3), 2)).astype(
        jnp.bfloat16
    )
    stones = jnp.einsum("mcv,vd->mcd", onehot, embed, preferred_element_type=jnp.float32)
    start_stream = (stones + encoded[:, None, :]).astype(jnp.bfloat16)
    full_weight = lax.all_gather(conv_weight[0], "shard", axis=1, tiled=True)
    ticks = micro + sections - 1

    def forward_block(stream):
        patches = tap_patches(stream)
        zconv = jnp.dot(patches, full_weight, preferred_element_type=jnp.float32)
        rscale = lax.rsqrt(jnp.mean(zconv * zconv, axis=-1, keepdims=True) + NORM_EPS)
        normed = zconv * rscale
        result = (stream.astype(jnp.float32) + jax.nn.silu(normed)).astype(jnp.bfloat16)
        return (result, normed, rscale)

    def forward_empty(stream):
        return (
            jnp.zeros((points, channels), jnp.bfloat16),
            jnp.zeros((points, channels), jnp.float32),
            jnp.zeros((points, 1), jnp.float32),
        )

    def forward_tick(step, carry):
        arriving, inputs, norms, scales = carry
        position = step - section_pos
        active = (position >= 0) & (position < micro)
        buffer_slot = jnp.clip(position, 0, micro - 1)
        feeding = lax.dynamic_index_in_dim(
            start_stream, jnp.minimum(step, micro - 1), 0, keepdims=False
        )
        stream_in = jnp.where(section_pos == 0, feeding, arriving)
        result, normed, rscale = lax.cond(active, forward_block, forward_empty, stream_in)
        inputs = jnp.where(
            active, lax.dynamic_update_index_in_dim(inputs, stream_in, buffer_slot, 0), inputs
        )
        norms = jnp.where(
            active, lax.dynamic_update_index_in_dim(norms, normed, buffer_slot, 0), norms
        )
        scales = jnp.where(
            active, lax.dynamic_update_index_in_dim(scales, rscale, buffer_slot, 0), scales
        )
        arriving = shifted(result, "section", 1)
        return (arriving, inputs, norms, scales)

    forward_init = (
        jnp.zeros((points, channels), jnp.bfloat16),
        jnp.zeros((micro, points, channels), jnp.bfloat16),
        jnp.zeros((micro, points, channels), jnp.float32),
        jnp.zeros((micro, points, 1), jnp.float32),
    )
    _, inputs, norms, scales = lax.fori_loop(0, ticks, forward_tick, forward_init)

    def backward_block(operands):
        grad, stream, normed, rscale = operands
        patches = tap_patches(stream)
        dnorm = grad.astype(jnp.float32) * silu_slope(normed)
        dconv = (
            rscale * (dnorm - normed * jnp.mean(dnorm * normed, axis=-1, keepdims=True))
        ).astype(jnp.bfloat16)
        contrib = lax.dot_general(
            patches, dconv, (((0,), (0,)), ((), ())), preferred_element_type=jnp.float32
        )
        spread = lax.dot_general(
            dconv, full_weight, (((1,), (1,)), ((), ())), preferred_element_type=jnp.float32
        )
        earlier = (grad.astype(jnp.float32) + fold_taps(spread, channels)).astype(jnp.bfloat16)
        return (earlier, contrib)

    def backward_empty(operands):
        return (
            jnp.zeros((points, channels), jnp.bfloat16),
            jnp.zeros((9 * channels, channels), jnp.float32),
        )

    def backward_tick(step, carry):
        arriving, accumulated, firsts = carry
        position = step - (sections - 1 - section_pos)
        active = (position >= 0) & (position < micro)
        buffer_slot = jnp.clip(position, 0, micro - 1)
        feeding = lax.dynamic_index_in_dim(
            cotangent, jnp.minimum(step, micro - 1), 0, keepdims=False
        )
        grad = jnp.where(section_pos == sections - 1, feeding, arriving)
        operands = (
            grad,
            lax.dynamic_index_in_dim(inputs, buffer_slot, 0, keepdims=False),
            lax.dynamic_index_in_dim(norms, buffer_slot, 0, keepdims=False),
            lax.dynamic_index_in_dim(scales, buffer_slot, 0, keepdims=False),
        )
        earlier, contrib = lax.cond(active, backward_block, backward_empty, operands)
        accumulated = accumulated + contrib
        keep_first = active & (section_pos == 0)
        firsts = jnp.where(
            keep_first, lax.dynamic_update_index_in_dim(firsts, earlier, buffer_slot, 0), firsts
        )
        arriving = shifted(earlier, "section", -1)
        return (arriving, accumulated, firsts)

    backward_init = (
        jnp.zeros((points, channels), jnp.bfloat16),
        jnp.zeros((9 * channels, channels), jnp.float32),
        jnp.zeros((micro, points, channels), jnp.bfloat16),
    )
    _, accumulated, firsts = lax.fori_loop(0, ticks, backward_tick, backward_init)
    first_section = (section_pos == 0).astype(jnp.float32)
    enc_sum = jnp.sum(firsts, axis=1, dtype=jnp.float32) * first_section
    stone_sum = (
        jnp.einsum("mcv,mcd->mvd", onehot, firsts, preferred_element_type=jnp.float32).reshape(
            micro, 3 * channels
        )
        * first_section
    )
    enc_sum, stone_sum = lax.psum((enc_sum, stone_sum), "section")
    enc_grad = enc_sum.astype(jnp.bfloat16)
    stone_grad = stone_sum.astype(jnp.bfloat16)
    hidden_grad = lax.dot_general(
        enc_grad, w_second, (((1,), (1,)), ((), ())), preferred_element_type=jnp.float32
    )
    pre_grad = (hidden_grad * gelu_slope(preact)).astype(jnp.bfloat16)
    all_context, all_hidden, all_pre, all_enc, all_stone = (
        lax.all_gather(context, ("dp", "shard"), axis=0, tiled=True),
        lax.all_gather(hidden, ("dp", "shard"), axis=0, tiled=True),
        lax.all_gather(pre_grad, ("dp", "shard"), axis=0, tiled=True),
        lax.all_gather(enc_grad, ("dp", "shard"), axis=0, tiled=True),
        lax.all_gather(stone_grad, ("dp", "shard"), axis=0, tiled=True),
    )
    inverse_states = 1.0 / all_context.shape[0]
    part_index = section_pos * shards + shard_pos
    row_block = width // (sections * shards)
    context_rows = lax.dynamic_slice_in_dim(all_context, part_index * row_block, row_block, 1)
    hidden_rows = lax.dynamic_slice_in_dim(all_hidden, part_index * row_block, row_block, 1)
    w1_grad = (
        lax.dot_general(
            context_rows, all_pre, (((0,), (0,)), ((), ())), preferred_element_type=jnp.float32
        )
        * inverse_states
    ).astype(jnp.bfloat16)
    w2_grad = (
        lax.dot_general(
            hidden_rows, all_enc, (((0,), (0,)), ((), ())), preferred_element_type=jnp.float32
        )
        * inverse_states
    ).astype(jnp.bfloat16)
    embed_grad = (
        (jnp.sum(all_stone, axis=0, dtype=jnp.float32) * inverse_states)
        .reshape(3, channels)
        .astype(jnp.bfloat16)
    )
    local_grad = accumulated * inverse_states
    column_count = channels // shards
    summed_grad = lax.psum(local_grad, ("dp", "shard"))
    own_columns = lax.dynamic_slice_in_dim(summed_grad, shard_pos * column_count, column_count, 1)
    conv_grad = own_columns.astype(jnp.bfloat16)[None]
    return (w1_grad, w2_grad, embed_grad, conv_grad)


def solution(mesh):
    placed = (
        P(("dp", "shard"), None),
        P(("dp", "shard"), None),
        P(("dp", "shard")),
        P("shard", None),
        P(),
        P(),
        P(),
        P("section", None, "shard"),
        P(("dp", "shard"), None, None),
    )
    return jax.shard_map(
        body,
        mesh=mesh,
        in_specs=placed,
        out_specs=(
            P(("section", "shard"), None),
            P(("section", "shard"), None),
            P(),
            P("section", None, "shard"),
        ),
        check_vma=False,
    )
```

profile of v0, /device:TPU:1, one launch (start us, length us, event | category | flops | bytes accessed | tf_op | source)
XLA Modules:
  0.0 1934.2 jit_solution(1790660043152087305)
XLA Ops:
  11.8 34.8 %all-gather.14.cloned.1.call-done = bf16[1,2304,256]{1,2,0:T(8,128)(2,1)} async-done(((bf16[1,2304,64]{1,2,0:T(8,128)(2,1)}), bf16[1,2304,256]{1,2,0:T(8,128)(2,1)}) %all-gather.14.cloned.1.call-update) | async-done | bytes 1179664 | tf_op jit(solution)/shard_map/all_gather | solution.py:71
  48.9 39.9 %all-gather.12.cloned.1.call-done = bf16[1024,1024]{1,0:T(8,128)(2,1)} async-done(((bf16[256,1024]{1,0:T(8,128)(2,1)}), bf16[1024,1024]{1,0:T(8,128)(2,1)}) %all-gather.12.cloned.1.call-update) | async-done | bytes 2097168 | tf_op jit(solution)/shard_map/all_gather | solution.py:57
  95.8 200.9 %while.49 = (s32[]{:T(128)}, bf16[361,256]{1,0:T(8,128)(2,1)}, bf16[4,361,256]{2,1,0:T(8,128)(2,1)}, f32[4,361,256]{2,1,0:T(8,128)}, f32[4,361,1]{1,2,0:T(1,128)...) while((s32[]{:T(128)}, bf16[361,256]{1,0:T(8,128)(2,1)}, ...), condition=%wide.region_5.6_spmd, body=%wide.region_1.5_spmd.sunk | while | flops 427055072 | bytes 15500308 | solution.py:117
  97.5 23.8 %conditional.5 = (bf16[361,256]{1,0:T(8,128)(2,1)}, f32[1,361,256]{2,1,0:T(8,128)S(1)}, f32[1,361,1]{1,2,0:T(1,128)S(1)}) conditional(s32[]{:T(128)} %convert_element_type.153, () %tuple.175, (bf16[361,256]{1,0:T(8,128)(2,1)S(1)}, bf16[2304,256]{1,0:T(8,128)(2,1)}) %tuple.176), branch_computations={%region_2.2_spmd, %region_3.4_spmd} | conditional | flops 426777472 | bytes 12690928 | solution.py:98
  128.4 23.8 %conditional.5 = (bf16[361,256]{1,0:T(8,128)(2,1)}, f32[1,361,256]{2,1,0:T(8,128)S(1)}, f32[1,361,1]{1,2,0:T(1,128)S(1)}) conditional(s32[]{:T(128)} %convert_element_type.153, () %tuple.175, (bf16[361,256]{1,0:T(8,128)(2,1)S(1)}, bf16[2304,256]{1,0:T(8,128)(2,1)}) %tuple.176), branch_computations={%region_2.2_spmd, %region_3.4_spmd} | conditional | flops 426777472 | bytes 12690928 | solution.py:98
  152.3 4.9 collective-permute-start
  161.3 23.8 %conditional.5 = (bf16[361,256]{1,0:T(8,128)(2,1)}, f32[1,361,256]{2,1,0:T(8,128)S(1)}, f32[1,361,1]{1,2,0:T(1,128)S(1)}) conditional(s32[]{:T(128)} %convert_element_type.153, () %tuple.175, (bf16[361,256]{1,0:T(8,128)(2,1)S(1)}, bf16[2304,256]{1,0:T(8,128)(2,1)}) %tuple.176), branch_computations={%region_2.2_spmd, %region_3.4_spmd} | conditional | flops 426777472 | bytes 12690928 | solution.py:98
  185.1 4.9 collective-permute-start
  193.9 23.8 %conditional.5 = (bf16[361,256]{1,0:T(8,128)(2,1)}, f32[1,361,256]{2,1,0:T(8,128)S(1)}, f32[1,361,1]{1,2,0:T(1,128)S(1)}) conditional(s32[]{:T(128)} %convert_element_type.153, () %tuple.175, (bf16[361,256]{1,0:T(8,128)(2,1)S(1)}, bf16[2304,256]{1,0:T(8,128)(2,1)}) %tuple.176), branch_computations={%region_2.2_spmd, %region_3.4_spmd} | conditional | flops 426777472 | bytes 12690928 | solution.py:98
  217.7 4.6 collective-permute-start
  226.9 27.7 %collective-permute-start = (bf16[361,256]{1,0:T(8,128)(2,1)}, bf16[361,256]{1,0:T(8,128)(2,1)}, u32[]{:S(2)}, u32[]{:S(2)}) collective-permute-start(bf16[361,256]{1,0:T(8,128)(2,1)} %get-tuple-element.977), channel_id=1, source_target_pairs={{0,4},{4,8},{8,12},{1,5},{5,9},{9,13},{2,6},{6,10},{10,14},{3,7},{... | collective-permute-start | bytes 554504 | tf_op jit(solution)/shard_map/while/body/eval_jaxpr/ppermute | solution.py:15
  259.3 4.6 collective-permute-start
  268.5 26.0 %collective-permute-start = (bf16[361,256]{1,0:T(8,128)(2,1)}, bf16[361,256]{1,0:T(8,128)(2,1)}, u32[]{:S(2)}, u32[]{:S(2)}) collective-permute-start(bf16[361,256]{1,0:T(8,128)(2,1)} %get-tuple-element.977), channel_id=1, source_target_pairs={{0,4},{4,8},{8,12},{1,5},{5,9},{9,13},{2,6},{6,10},{10,14},{3,7},{... | collective-permute-start | bytes 554504 | tf_op jit(solution)/shard_map/while/body/eval_jaxpr/ppermute | solution.py:15
  297.6 734.0 %while.50 = (s32[]{:T(128)}, bf16[361,256]{1,0:T(8,128)(2,1)S(1)}, f32[2304,256]{1,0:T(8,128)}, bf16[4,361,256]{2,1,0:T(8,128)(2,1)}, s32[]{:T(128)}, /*index=5*...) while((s32[]{:T(128)}, bf16[361,256]{1,0:T(8,128)(2,1)S(1)}, ...), condition=%wide.region_11.12_spmd.clone, body=%wide.region_6.11_spmd.clone.sunk | while | flops 857875968 | bytes 61836660 | solution.py:170
  311.9 4.1 select_add_fusion.2
  317.7 21.1 %collective-permute-done.1 = bf16[361,256]{1,0:T(8,128)(2,1)S(1)} collective-permute-done((bf16[361,256]{1,0:T(8,128)(2,1)}, bf16[361,256]{1,0:T(8,128)(2,1)S(1)}, u32[]{:S(2)}, u32[]{:S(2)}) %collective-permute-start.1) | collective-permute-done | bytes 184864 | tf_op jit(solution)/shard_map/while/body/eval_jaxpr/ppermute | solution.py:15
  343.1 4.1 select_add_fusion.2
  348.8 274.2 %collective-permute-done.1 = bf16[361,256]{1,0:T(8,128)(2,1)S(1)} collective-permute-done((bf16[361,256]{1,0:T(8,128)(2,1)}, bf16[361,256]{1,0:T(8,128)(2,1)S(1)}, u32[]{:S(2)}, u32[]{:S(2)}) %collective-permute-start.1) | collective-permute-done | bytes 184864 | tf_op jit(solution)/shard_map/while/body/eval_jaxpr/ppermute | solution.py:15
  623.0 93.9 %conditional.6 = (bf16[361,256]{1,0:T(8,128)(2,1)}, f32[2304,256]{1,0:T(8,128)}, bf16[1,361,256]{2,1,0:T(8,128)(2,1)S(1)}) conditional(s32[]{:T(128)} %convert_element_type.154, () %tuple.178, (pred[]{:T(512)}, s32[]{:T(128)}, bf16[4,361,256]{2,1,0:T(8,128)(2,1)}, bf16[361,256]{1,0:T(8,128)(2,1)S(1)}, f32[4,361,1]{1,2,0:T(1,128)S(1)}, ...), branch_computations={%region_7.7_spmd, %region_8.10_spmd} | conditional | flops 856603904 | bytes 51978224 | solution.py:156
  624.3 4.0 fusion.14
  628.3 5.1 reshape.469
  633.5 13.8 fusion.46
  649.4 4.6 scatter-add.6
  658.4 4.6 scatter-add.19
  718.9 4.1 select_add_fusion.2
  725.3 93.9 %conditional.6 = (bf16[361,256]{1,0:T(8,128)(2,1)}, f32[2304,256]{1,0:T(8,128)}, bf16[1,361,256]{2,1,0:T(8,128)(2,1)S(1)}) conditional(s32[]{:T(128)} %convert_element_type.154, () %tuple.178, (pred[]{:T(512)}, s32[]{:T(128)}, bf16[4,361,256]{2,1,0:T(8,128)(2,1)}, bf16[361,256]{1,0:T(8,128)(2,1)S(1)}, f32[4,361,1]{1,2,0:T(1,128)S(1)}, ...), branch_computations={%region_7.7_spmd, %region_8.10_spmd} | conditional | flops 856603904 | bytes 51978224 | solution.py:156
  726.6 4.0 fusion.14
  730.7 5.1 reshape.469
  735.8 13.8 fusion.46
  751.7 4.6 scatter-add.6
  760.7 4.6 scatter-add.19
  821.2 4.1 select_add_fusion.2
  827.6 93.9 %conditional.6 = (bf16[361,256]{1,0:T(8,128)(2,1)}, f32[2304,256]{1,0:T(8,128)}, bf16[1,361,256]{2,1,0:T(8,128)(2,1)S(1)}) conditional(s32[]{:T(128)} %convert_element_type.154, () %tuple.178, (pred[]{:T(512)}, s32[]{:T(128)}, bf16[4,361,256]{2,1,0:T(8,128)(2,1)}, bf16[361,256]{1,0:T(8,128)(2,1)S(1)}, f32[4,361,1]{1,2,0:T(1,128)S(1)}, ...), branch_computations={%region_7.7_spmd, %region_8.10_spmd} | conditional | flops 856603904 | bytes 51978224 | solution.py:156
  833.0 5.1 reshape.469
  838.1 13.8 fusion.46
  854.0 4.6 scatter-add.6
  863.1 4.6 scatter-add.19
  923.6 4.1 select_add_fusion.2
  930.0 93.9 %conditional.6 = (bf16[361,256]{1,0:T(8,128)(2,1)}, f32[2304,256]{1,0:T(8,128)}, bf16[1,361,256]{2,1,0:T(8,128)(2,1)S(1)}) conditional(s32[]{:T(128)} %convert_element_type.154, () %tuple.178, (pred[]{:T(512)}, s32[]{:T(128)}, bf16[4,361,256]{2,1,0:T(8,128)(2,1)}, bf16[361,256]{1,0:T(8,128)(2,1)S(1)}, f32[4,361,1]{1,2,0:T(1,128)S(1)}, ...), branch_computations={%region_7.7_spmd, %region_8.10_spmd} | conditional | flops 856603904 | bytes 51978224 | solution.py:156
  935.3 5.1 reshape.469
  940.4 13.8 fusion.46
  956.4 4.6 scatter-add.6
  965.4 4.6 scatter-add.19
  1025.9 4.1 select_add_fusion.2
  1034.2 12.8 all-reduce.3
  1052.7 173.4 %all-gather.5 = bf16[128,4,768]{2,1,0:T(4,128)(2,1)S(1)} all-gather(bf16[1,4,768]{2,1,0:T(4,128)(2,1)S(1)} %bitcast.137), channel_id=1, replica_groups=mesh['dp'=32,'section'=4,'shard'=4] {'dp','shard'}, dimensions={0}, use_global_device_ids=true | all-gather | bytes 792576 | tf_op jit(solution)/shard_map/all_gather | solution.py:191
  1229.7 173.1 %all-gather.4 = bf16[128,4,256]{2,1,0:T(4,128)(2,1)S(1)} all-gather(bf16[1,4,256]{2,1,0:T(4,128)(2,1)S(1)} %bitcast.136), channel_id=1, replica_groups=mesh['dp'=32,'section'=4,'shard'=4] {'dp','shard'}, dimensions={0}, use_global_device_ids=true | all-gather | bytes 264192 | tf_op jit(solution)/shard_map/all_gather | solution.py:190
  1403.4 515.7 %all-reduce.5 = bf16[2304,256]{0,1:T(8,128)(2,1)S(1)} all-reduce(f32[2304,256]{0,1:T(8,128)} %broadcast_multiply_fusion.1), channel_id=1, replica_groups=mesh['dp'=32,'section'=4,'shard'=4] {'dp','shard'}, use_global_device_ids=true, to_apply=%region_16.17 | all-reduce | flops 589824 | bytes 3538944 | tf_op jit(solution)/shard_map/psum | solution.py:217
  (467 shorter events, 466.0 us)
Async XLA Ops:
  7.2 83.6 %copy-start = (bf16[1024,1024]{1,0:T(8,128)(2,1)S(1)}, bf16[1024,1024]{1,0:T(8,128)(2,1)}, u32[]{:S(2)}) copy-start(bf16[1024,1024]{1,0:T(8,128)(2,1)} %param.39) | copy-start | bytes 6291460
  7.2 4.4 copy-start.9
  7.2 39.4 %all-gather.14.cloned.1.call-start = ((), (), s32[]{:S(2)}) async-start(), calls=%async_computation.1 | async-start | bytes 1474560 | tf_op jit(solution)/shard_map/all_gather | solution.py:71
  7.9 80.9 %all-gather.12.cloned.1.call-start = ((), (), s32[]{:S(2)}) async-start(), calls=%async_computation | async-start | bytes 2621440 | tf_op jit(solution)/shard_map/all_gather | solution.py:57
  8.7 1911.2 %all-gather.18.cloned.1.call-start = ((), (), s32[]{:S(2)}) async-start(), calls=%async_computation.3 | async-start | bytes 1056768 | tf_op jit(solution)/shard_map/all_gather | solution.py:189
  48.9 42.3 %copy-start.3 = (bf16[1024,256]{1,0:T(8,128)(2,1)S(1)}, bf16[1024,256]{1,0:T(8,128)(2,1)}, u32[]{:S(2)}) copy-start(bf16[1024,256]{1,0:T(8,128)(2,1)} %param.40) | copy-start | bytes 1572868
  90.8 2.0 copy-start.5
  90.8 0.7 copy-start.6
  90.8 0.7 copy-start.8
  91.2 4.5 copy-start.4
  121.4 5.3 collective-permute-start
  152.3 7.3 collective-permute-start
  185.1 7.0 collective-permute-start
  217.7 6.7 collective-permute-start
  226.9 29.8 %collective-permute-start = (bf16[361,256]{1,0:T(8,128)(2,1)}, bf16[361,256]{1,0:T(8,128)(2,1)}, u32[]{:S(2)}, u32[]{:S(2)}) collective-permute-start(bf16[361,256]{1,0:T(8,128)(2,1)} %get-tuple-element.977), channel_id=1, source_target_pairs={{0,4},{4,8},{8,12},{1,5},{5,9},{9,13},{2,6},{6,10},{10,14},{3,7},{... | collective-permute-start | bytes 554504 | tf_op jit(solution)/shard_map/while/body/eval_jaxpr/ppermute | solution.py:15
  259.3 6.7 collective-permute-start
  268.5 28.2 %collective-permute-start = (bf16[361,256]{1,0:T(8,128)(2,1)}, bf16[361,256]{1,0:T(8,128)(2,1)}, u32[]{:S(2)}, u32[]{:S(2)}) collective-permute-start(bf16[361,256]{1,0:T(8,128)(2,1)} %get-tuple-element.977), channel_id=1, source_target_pairs={{0,4},{4,8},{8,12},{1,5},{5,9},{9,13},{2,6},{6,10},{10,14},{3,7},{... | collective-permute-start | bytes 554504 | tf_op jit(solution)/shard_map/while/body/eval_jaxpr/ppermute | solution.py:15
  300.0 0.7 copy-start.1
  300.6 7.0 collective-permute-start.1
  301.9 3.4 copy-start.2
  309.9 0.7 copy-start.1
  310.6 28.2 %collective-permute-start.1 = (bf16[361,256]{1,0:T(8,128)(2,1)}, bf16[361,256]{1,0:T(8,128)(2,1)S(1)}, u32[]{:S(2)}, u32[]{:S(2)}) collective-permute-start(bf16[361,256]{1,0:T(8,128)(2,1)} %get-tuple-element.993), channel_id=1, source_target_pairs={{4,0},{8,4},{12,8},{5,1},{9,5},{13,9},{6,2},{10,6},{14,10},{7,3},{... | collective-permute-start | bytes 554504 | tf_op jit(solution)/shard_map/while/body/eval_jaxpr/ppermute | solution.py:15
  311.9 4.1 copy-start.2
  341.1 0.7 copy-start.1
  341.8 281.2 %collective-permute-start.1 = (bf16[361,256]{1,0:T(8,128)(2,1)}, bf16[361,256]{1,0:T(8,128)(2,1)S(1)}, u32[]{:S(2)}, u32[]{:S(2)}) collective-permute-start(bf16[361,256]{1,0:T(8,128)(2,1)} %get-tuple-element.993), channel_id=1, source_target_pairs={{4,0},{8,4},{12,8},{5,1},{9,5},{13,9},{6,2},{10,6},{14,10},{7,3},{... | collective-permute-start | bytes 554504 | tf_op jit(solution)/shard_map/while/body/eval_jaxpr/ppermute | solution.py:15
  343.1 4.1 copy-start.2
  647.3 7.3 copy-start.7
  716.9 0.7 copy-start.1
  717.6 7.7 collective-permute-start.1
  718.9 4.1 copy-start.2
  749.6 7.3 copy-start.7
  819.3 0.7 copy-start.1
  819.9 7.7 collective-permute-start.1
  821.2 4.1 copy-start.2
  851.9 7.3 copy-start.7
  921.6 0.7 copy-start.1
  922.2 7.7 collective-permute-start.1
  923.5 4.1 copy-start.2
  954.2 7.3 copy-start.7
  1023.9 0.7 copy-start.1
  1024.6 7.1 collective-permute-start.1
  1025.9 4.1 copy-start.2
  1048.9 872.3 %all-gather.16.cloned.1.call-start = ((), (), s32[]{:S(2)}) async-start(), calls=%async_computation.2 | async-start | bytes 1056768 | tf_op jit(solution)/shard_map/all_gather | solution.py:187
  1049.5 875.9 %all-gather.20.cloned.1.call-start = ((), (), s32[]{:S(2)}) async-start(), calls=%async_computation.4 | async-start | bytes 1056768 | tf_op jit(solution)/shard_map/all_gather | solution.py:188
Sparse Core Ops, SparseCore 0:
  10.1 36.3 all-gather.13
  48.6 40.0 all-gather.11
  1049.1 142.4 all-gather.17
  1195.0 126.4 all-gather.15
  1324.3 126.4 all-gather.19
where the time goes:
time: 1940 us; the launch traced here: 1930 us
  blocking collectives  875 us (45%)
  local copies, waits for them, and re-layouts  398 us (21%)
  waiting for transfers between devices  378 us (19%)
  other arithmetic  132 us (7%)
  starting transfers between devices  83.7 us (4%)
  matrix products  51.9 us (3%)
    psum x1, blocking collectives, body(): summed_grad = lax.psum(local_grad, ('dp', 'shard'))  516 us
    ppermute x14, waiting for transfers between devices, shifted(): return lax.ppermute(block, axis, route)  302 us
    all_gather x1, blocking collectives, body(): lax.all_gather(stone_grad, ('dp', 'shard'), axis=0, tiled=True)  173 us
    all_gather x1, blocking collectives, body(): lax.all_gather(enc_grad, ('dp', 'shard'), axis=0, tiled=True)  173 us
    scatter-add x36, local copies, waits for them, and re-layouts, fold_taps(): folded = folded.at[a:a + BOARD, b:b + BOARD].add(grid[:, :, 3 * a + b])  111 us
    ppermute x14, starting transfers between devices, shifted(): return lax.ppermute(block, axis, route)  83.5 us
    cond x80, local copies, waits for them, and re-layouts  83 us
    slice x4, local copies, waits for them, and re-layouts, fold_taps(): folded = folded.at[a:a + BOARD, b:b + BOARD].add(grid[:, :, 3 * a + b])  55 us
  transfers between devices with their start and end apart: 19, of which 15 were waited for; matrix products, arithmetic and copies ran while one was open for 4% of the time, Pallas kernels for 0%

commit v1 on v0

v1 whole, which is shorter than its diff:
```python
import functools

import jax
import jax.numpy as jnp
from jax import lax
from jax.experimental import pallas as pl
from jax.experimental.pallas import tpu as pltpu
from jax.sharding import PartitionSpec as P

BOARD = 19
PITCH = 20
ROWS = 384
FRONT = 24
NORM_EPS = 1e-05
XOR = (0, 1, 3, 2)
TAP_SHIFTS = [(a - 1) * PITCH + (b - 1) for a in range(3) for b in range(3)]
VMEM_BYTES = 58 * 1024 * 1024
F32 = jnp.float32
BF16 = jnp.bfloat16


def swap(block, axis, bits):
    return lax.ppermute(block, axis, [(i, i ^ bits) for i in range(lax.axis_size(axis))])


def turned(block, axis, distance):
    size = lax.axis_size(axis)
    return lax.ppermute(block, axis, [(i, (i + distance) % size) for i in range(size)])


def nn(left, right):
    return lax.dot_general(left, right, (((1,), (0,)), ((), ())), preferred_element_type=F32)


def nt(left, right):
    return lax.dot_general(left, right, (((1,), (1,)), ((), ())), preferred_element_type=F32)


def tn(left, right):
    return lax.dot_general(left, right, (((0,), (0,)), ((), ())), preferred_element_type=F32)


def vmem_call(kernel, outs, scratch, name, flops, moved):
    spec = pl.BlockSpec(memory_space=pltpu.VMEM)

    def call(scalars, *arrays):
        return pl.pallas_call(
            kernel,
            out_shape=outs,
            in_specs=[pl.BlockSpec(memory_space=pltpu.SMEM)] + [spec] * len(arrays),
            out_specs=tuple(spec for _ in outs),
            scratch_shapes=scratch,
            compiler_params=pltpu.CompilerParams(vmem_limit_bytes=VMEM_BYTES),
            cost_estimate=pl.CostEstimate(flops=flops, bytes_accessed=moved, transcendentals=0),
            name=name,
        )(scalars, *arrays)

    return call


def trunk_kernel(
    where, context, w_first, w_second, embed, code_col, code_row, cotangent,
    a_near, a_far, a_near2, a_far2, b_near, b_far, b_near2, b_far2,
    own_a_hi, own_a_lo, own_b_hi, own_b_lo, oth_a_hi, oth_a_lo, oth_b_hi, oth_b_lo, vectors,
    wt, patches, gt, normed, rscales, buf, grad,
):
    s, h, c = where[0], where[1], where[2]

    def rows_of(jx, core, part):
        return pl.ds(pl.multiple_of((h ^ XOR[jx]) * 64 + core * 32 + part * 16, 16), 16)

    for core, near, far in ((c, a_near, a_far), (1 - c, a_near2, a_far2)):
        for jy in range(4):
            for jx in range(4):
                source = near if jy < 2 else far
                wt[s ^ XOR[jy], rows_of(jx, core, 0), :] = source[(jy % 2) * 4 + jx]
    for core, near, far in ((c, b_near, b_far), (1 - c, b_near2, b_far2)):
        for jx in range(4):
            for jy in range(4):
                source = near if jx < 2 else far
                wt[s ^ XOR[jy], rows_of(jx, core, 1), :] = source[(jx % 2) * 4 + jy]

    point = lax.broadcasted_iota(jnp.int32, (ROWS, 1), 0)
    column = point - ((point * 3277) >> 16) * PITCH
    mask = jnp.where((column < BOARD) & (point < BOARD * PITCH), 1.0, 0.0).astype(F32)

    preact = nn(context[...], w_first[...])
    cdf = 0.5 * (1.0 + lax.erf(preact * 0.7071067811865476))
    hidden = (preact * cdf).astype(BF16)
    encoded = nn(hidden, w_second[...])
    code = code_col[...]
    stone = embed[...].astype(F32)
    stones = jnp.where(code == 0, stone[0:1], jnp.where(code == 1, stone[1:2], stone[2:3]))
    start = (stones + encoded[0:1]).astype(BF16).astype(F32) * mask

    buf[0:FRONT, :] = jnp.zeros((FRONT, buf.shape[1]), F32)
    buf[FRONT + ROWS :, :] = jnp.zeros((FRONT, buf.shape[1]), F32)
    buf[FRONT : FRONT + ROWS, :] = start
    channels = start.shape[1]

    def forward(block, carry):
        for tap, shift in enumerate(TAP_SHIFTS):
            patches[block, :, tap * channels : (tap + 1) * channels] = buf[
                FRONT + shift : FRONT + shift + ROWS, :
            ].astype(BF16)
        zconv = nt(patches[block], wt[block])
        rscale = lax.rsqrt(jnp.mean(zconv * zconv, axis=-1, keepdims=True) + NORM_EPS)
        value = zconv * rscale
        normed[block] = value
        rscales[block] = rscale
        stream = buf[FRONT : FRONT + ROWS, :] + value * jax.nn.sigmoid(value)
        buf[FRONT : FRONT + ROWS, :] = stream.astype(BF16).astype(F32) * mask
        return carry

    lax.fori_loop(0, 4, forward, 0)
    grad[...] = cotangent[...].astype(F32)

    def backward(step, carry):
        block = 3 - step
        value = normed[block]
        upper = grad[...]
        sigma = jax.nn.sigmoid(value)
        dnorm = upper * (sigma * (1.0 + value * (1.0 - sigma)))
        inner = jnp.mean(dnorm * value, axis=-1, keepdims=True)
        dconv = rscales[block] * (dnorm - value * inner)
        gt[block] = nn(dconv.T.astype(BF16), patches[block]).astype(BF16)
        buf[FRONT : FRONT + ROWS, :] = dconv.astype(BF16).astype(F32)
        total = upper
        for tap, shift in enumerate(TAP_SHIFTS):
            total += nn(
                buf[FRONT - shift : FRONT - shift + ROWS, :].astype(BF16),
                wt[block, :, tap * channels : (tap + 1) * channels],
            )
        grad[...] = total.astype(BF16).astype(F32) * mask
        return carry

    lax.fori_loop(0, 4, backward, 0)

    kind = lax.broadcasted_iota(jnp.int32, (16, ROWS), 0)
    codes = code_row[...]
    picked = ((kind < 3) & (codes == kind)) | ((kind == 3) & (codes < 3))
    sums = nn(jnp.where(picked, 1.0, 0.0).astype(BF16), grad[...].astype(BF16))
    rounded = sums.astype(BF16)
    density = jnp.exp(-0.5 * preact * preact) * 0.3989422804014327
    pre_grad = (nt(rounded, w_second[...]) * (cdf + preact * density)).astype(BF16)
    vectors[...] = jnp.zeros(vectors.shape, F32)
    vectors[0:1, 0:1024] = context[...].astype(F32)[0:1]
    vectors[0:1, 1024:2048] = hidden.astype(F32)[0:1]
    vectors[0:1, 2048:3072] = pre_grad.astype(F32)[3:4]
    for place, row in enumerate((3, 0, 1, 2)):
        first = 3072 + place * channels
        vectors[0:1, first : first + channels] = rounded.astype(F32)[row : row + 1]

    for core, pieces in (
        (c, (own_a_lo, own_a_hi, own_b_lo, own_b_hi)),
        (1 - c, (oth_a_lo, oth_a_hi, oth_b_lo, oth_b_hi)),
    ):
        for jy in range(4):
            for jx in range(4):
                block = s ^ XOR[jy]
                pieces[jy // 2][jy % 2, jx] = gt[block, rows_of(jx, core, 0), :]
                pieces[2 + jx // 2][jx % 2, jy] = gt[block, rows_of(jx, core, 1), :]


def pack_kernel(where, a_own, a_come, b_own, b_come, near, far, *rest):
    outs, whole, product = rest[:4], rest[4], rest[5]
    first = where[0] * 256 + where[1] * 64 + where[2] * 32
    low = where[3]
    lanes = pl.multiple_of((first // 128) * 128, 128)
    rows = pl.ds(pl.multiple_of(first - lanes, 32), 32)
    whole[:, :, 896:1024] = jnp.zeros((4, 32, 128), F32)

    def spread(place, block):
        width = block.shape[1]
        done = 0
        while done < width:
            group, inside = divmod(place + done, 896)
            take = min(width - done, 896 - inside)
            whole[group, :, inside : inside + take] = block[:, done : done + take]
            done += take

    conv = jnp.concatenate(
        [a_own[...].astype(F32) + a_come[...], b_own[...].astype(F32) + b_come[...]], axis=0
    )
    spread(0, conv)
    product[:, 0:1024] = tn(near[:, pl.ds(lanes, 128)], near[:, 2048:3072]) + tn(
        far[:, pl.ds(lanes, 128)], far[:, 2048:3072]
    )
    lanes2 = pl.multiple_of(lanes + 1024, 128)
    product[:, 1024:1280] = tn(near[:, pl.ds(lanes2, 128)], near[:, 3072:3328]) + tn(
        far[:, pl.ds(lanes2, 128)], far[:, 3072:3328]
    )
    spread(2304, product[rows, :])
    stones = jnp.sum(
        near[:, 3328:4096].astype(F32) + far[:, 3328:4096].astype(F32), axis=0, keepdims=True
    )
    for piece in range(6):
        row = piece // 4
        whole[piece % 4, row : row + 1, 896:1024] = stones[:, piece * 128 : (piece + 1) * 128]
    for k in range(4):
        outs[k][...] = whole[low ^ k].astype(BF16)


def split_kernel(where, own, one, two, three, *rest):
    outs, total = rest[:4], rest[4]
    high = where[4]
    total[...] = own[...].astype(F32) + one[...] + two[...] + three[...]
    for k in range(4):
        place = high ^ k
        rows = pl.ds(pl.multiple_of((place // 2) * 16, 16), 16)
        lanes = pl.ds(pl.multiple_of((place % 2) * 512, 512), 512)
        outs[k][...] = total[rows, lanes].astype(BF16)


def join_kernel(where, own, one, two, three, out):
    high = where[4]
    for k, piece in enumerate((own, one, two, three)):
        place = high ^ k
        rows = pl.ds(pl.multiple_of((place // 2) * 16, 16), 16)
        lanes = pl.ds(pl.multiple_of((place % 2) * 512, 512), 512)
        out[rows, lanes] = piece[...]


def finish_kernel(where, *rest):
    own, other = rest[0:4], rest[4:8]
    conv, first, second, stones, whole, rows3 = rest[8:]
    c, low = where[2], where[3]
    for core, pieces in ((c, own), (1 - c, other)):
        rows = pl.ds(pl.multiple_of(core * 32, 32), 32)
        for k in range(4):
            whole[low ^ k, rows, :] = pieces[k][...].astype(F32) * (1.0 / 512.0)
    for group in range(4):
        for out, start, width in ((conv, 0, 2304), (first, 2304, 1024), (second, 3328, 256)):
            begin = max(start, group * 896)
            end = min(start + width, (group + 1) * 896)
            if begin < end:
                out[:, begin - start : end - start] = whole[
                    group, :, begin - group * 896 : end - group * 896
                ].astype(BF16)
    for piece in range(6):
        row = piece // 4
        v, half = divmod(piece, 2)
        rows3[v : v + 1, half * 128 : (half + 1) * 128] = whole[
            piece % 4, row : row + 1, 896:1024
        ]
    stones[...] = rows3[0:3, :].astype(BF16)


def body(boards, neighbours, counts, database, w_first, w_second, embed, conv_weight, cotangent):
    h = lax.axis_index("shard")
    s = lax.axis_index("section")
    dp = lax.axis_index("dp")
    c, z = dp % 2, dp // 2
    where = jnp.stack([s, h, c, z % 4, z // 4]).astype(jnp.int32)
    channels = embed.shape[1]
    taps = conv_weight.shape[1]

    mine = lax.dynamic_slice_in_dim(conv_weight[0].T, c * 32, 32, 0).reshape(2, 16, taps)

    def gather(unit, first, second):
        block = unit[None]
        block = jnp.concatenate([block, swap(block, first, 1)])
        block = jnp.concatenate([block, swap(block, first, 3)])
        block = jnp.concatenate([block, swap(block, second, 1)])
        return block, swap(block, second, 3)

    a_near, a_far = gather(mine[0], "shard", "section")
    b_near, b_far = gather(mine[1], "section", "shard")
    weights = (
        a_near, a_far, swap(a_near, "dp", 1), swap(a_far, "dp", 1),
        b_near, b_far, swap(b_near, "dp", 1), swap(b_far, "dp", 1),
    )

    ids = lax.dynamic_slice_in_dim(neighbours, s, 1, 0)
    count = lax.dynamic_slice_in_dim(counts, s, 1, 0)
    asked = jnp.concatenate([ids, count[:, None]], axis=1)
    asked = jnp.concatenate([asked] + [turned(asked, "shard", d) for d in (1, 2, 3)])
    slots = ids.shape[1]
    live = lax.broadcasted_iota(jnp.int32, (4, slots), 1) < asked[:, slots:]
    stored = database.shape[0]
    positions = lax.broadcasted_iota(jnp.int32, (1, 1, stored), 2) + h * stored
    hits = (asked[:, :slots, None] == positions) & live[:, :, None]
    picks = jnp.sum(hits.astype(F32), axis=1).astype(BF16)
    partial = jnp.dot(picks, database, preferred_element_type=F32)
    summed = partial[0:1]
    for d in (1, 2, 3):
        summed = summed + turned(partial[d : d + 1], "shard", -d)
    context = (summed / jnp.maximum(count, 1).astype(F32)[:, None]).astype(BF16)
    context = jnp.broadcast_to(context, (16, context.shape[1]))

    board = lax.dynamic_index_in_dim(boards, s, 0, keepdims=False).reshape(BOARD, BOARD)
    code = jnp.pad(board, ((0, 0), (0, 1)), constant_values=3).reshape(-1)
    code = jnp.pad(code, (0, ROWS - BOARD * PITCH), constant_values=3)
    upper = lax.dynamic_index_in_dim(cotangent, s, 0, keepdims=False)
    upper = jnp.pad(upper.reshape(BOARD, BOARD, channels), ((0, 0), (0, 1), (0, 0)))
    upper = jnp.pad(upper.reshape(-1, channels), ((0, ROWS - BOARD * PITCH), (0, 0)))

    part = jax.ShapeDtypeStruct((2, 4, 16, taps), BF16)
    own_a_hi, own_a_lo, own_b_hi, own_b_lo, oth_a_hi, oth_a_lo, oth_b_hi, oth_b_lo, vectors = vmem_call(
        trunk_kernel,
        (part,) * 8 + (jax.ShapeDtypeStruct((8, 4096), F32),),
        [
            pltpu.VMEM((4, channels, taps), BF16),
            pltpu.VMEM((4, ROWS, taps), BF16),
            pltpu.VMEM((4, channels, taps), BF16),
            pltpu.VMEM((4, ROWS, channels), F32),
            pltpu.VMEM((4, ROWS, 1), F32),
            pltpu.VMEM((2 * FRONT + ROWS, channels), F32),
            pltpu.VMEM((ROWS, channels), F32),
        ],
        "trunk",
        12 * 2 * ROWS * taps * channels,
        16 << 20,
    )(where, context, w_first, w_second, embed, code[:, None], code[None, :], upper, *weights)

    def plus(kept, come):
        return (kept.astype(F32) + come.astype(F32)).astype(BF16)

    a_hi = plus(own_a_hi, swap(oth_a_hi, "dp", 1))
    b_hi = plus(own_b_hi, swap(oth_b_hi, "dp", 1))
    a_lo = plus(own_a_lo, swap(oth_a_lo, "dp", 1))
    b_lo = plus(own_b_lo, swap(oth_b_lo, "dp", 1))

    def scatter(low, high, first, second):
        block = plus(low, swap(high, first, 3))
        block = plus(block[0], swap(block[1], first, 1))
        block = plus(block[0:2], swap(block[2:4], second, 3))
        return block[0], swap(block[1], second, 1)

    a_own, a_come = scatter(a_lo, a_hi, "section", "shard")
    b_own, b_come = scatter(b_lo, b_hi, "shard", "section")

    rows = vectors[0:1].astype(BF16)
    rows = jnp.concatenate([rows, swap(rows, "shard", 1)])
    rows = jnp.concatenate([rows, swap(rows, "shard", 3)])
    rows = jnp.concatenate([rows, swap(rows, "section", 1)])
    rows = jnp.concatenate([rows, swap(rows, "section", 3)])
    group = jax.ShapeDtypeStruct((32, 1024), BF16)
    groups = vmem_call(
        pack_kernel,
        (group,) * 4,
        [pltpu.VMEM((4, 32, 1024), F32), pltpu.VMEM((128, 1280), F32)],
        "pack",
        4 * 32 * 128 * 1280,
        1 << 20,
    )(where, a_own, a_come, b_own, b_come, rows, swap(rows, "dp", 1))

    come = [swap(groups[k], "dp", 2 * k) for k in (1, 2, 3)]
    chunk = jax.ShapeDtypeStruct((16, 512), BF16)
    chunks = vmem_call(
        split_kernel, (chunk,) * 4, [pltpu.VMEM((32, 1024), F32)], "split", 1 << 17, 1 << 19
    )(where, groups[0], *come)
    come = [swap(chunks[k], "dp", 8 * k) for k in (1, 2, 3)]
    total = plus(plus(chunks[0], come[0]).astype(F32), plus(come[1], come[2]).astype(F32))
    come = [swap(total, "dp", 8 * k) for k in (1, 2, 3)]
    (joined,) = vmem_call(join_kernel, (group,), [], "join", 1 << 10, 1 << 18)(where, total, *come)
    own = [joined] + [swap(joined, "dp", 2 * k) for k in (1, 2, 3)]
    other = [swap(piece, "dp", 1) for piece in own]
    conv, w1_grad, w2_grad, embed_grad = vmem_call(
        finish_kernel,
        (
            jax.ShapeDtypeStruct((64, taps), BF16),
            jax.ShapeDtypeStruct((64, 1024), BF16),
            jax.ShapeDtypeStruct((64, channels), BF16),
            jax.ShapeDtypeStruct((3, channels), BF16),
        ),
        [pltpu.VMEM((4, 64, 1024), F32), pltpu.VMEM((8, channels), F32)],
        "finish",
        1 << 18,
        1 << 20,
    )(where, *own, *other)
    return (w1_grad, w2_grad, embed_grad, conv.T[None])


def solution(mesh):
    placed = (
        P(("dp", "shard"), None),
        P(("dp", "shard"), None),
        P(("dp", "shard")),
        P("shard", None),
        P(),
        P(),
        P(),
        P("section", None, "shard"),
        P(("dp", "shard"), None, None),
    )
    return jax.shard_map(
        body,
        mesh=mesh,
        in_specs=placed,
        out_specs=(
            P(("section", "shard"), None),
            P(("section", "shard"), None),
            P(),
            P("section", None, "shard"),
        ),
        check_vma=False,
    )
```

time: 1940 us -> 279 us (0.14)
  blocking collectives: 875 us -> 0 us
  local copies, waits for them, and re-layouts: 398 us -> 13.7 us
  waiting for transfers between devices: 378 us -> 49.8 us
  other arithmetic: 132 us -> 6.02 us
  starting transfers between devices: 83.7 us -> 181 us
  matrix products: 51.9 us -> 0.18 us
  Pallas kernels: 0 us -> 23.8 us
    psum x2 -> x0, blocking collectives: 529 us -> none  [the longest x1 516 us: body(): summed_grad = lax.psum(local_grad, ('dp', 'shard'))]
    all_gather x2 -> x0, blocking collectives: 346 us -> none  [the longest x1 173 us: body(): lax.all_gather(stone_grad, ('dp', 'shard'), axis=0, tiled=True)]
    ppermute x14 -> x51, waiting for transfers between devices: 302 us -> 49.8 us  [the longest x45 45.2 us: swap(): lax.ppermute(block, axis, [(i, i ^ bits) for i in range(lax.axis_size(axi...]
    scatter-add x36 -> x0, local copies, waits for them, and re-layouts: 111 us -> none  [fold_taps(): folded = folded.at[a:a + BOARD, b:b + BOARD].add(grid[:, :, 3 * a + b])]
    ppermute x14 -> x51, starting transfers between devices: 83.5 us -> 181 us  [the longest x45 163 us: swap(): lax.ppermute(block, axis, [(i, i ^ bits) for i in range(lax.axis_size(axi...]
    cond x80 -> x0, local copies, waits for them, and re-layouts: 83 us -> none
    slice x16 -> x7, local copies, waits for them, and re-layouts: 82.1 us -> 1.31 us  [the longest x1 0.98 us: body(): rows = vectors[0:1].astype(BF16)]
    all_gather x5 -> x0, waiting for transfers between devices: 74.7 us -> none  [the longest x1 39.9 us: body(): piece = lax.all_gather(database, 'shard', axis=0, tiled=True)]
  transfers between devices with their start and end apart: 19 -> 51, of which waited for: 15 -> 20; matrix products, arithmetic and copies ran while one was open for 4% -> 5% of each run, Pallas kernels for 0% -> 0%
where the time goes in v1:
time: 279 us; the launch traced here: 277 us
  starting transfers between devices  181 us (65%)
  waiting for transfers between devices  49.8 us (18%)
  Pallas kernels  23.8 us (9%)
  local copies, waits for them, and re-layouts  13.7 us (5%)
  other arithmetic  6.02 us (2%)
    ppermute x45, starting transfers between devices, swap(): lax.ppermute(block, axis, [(i, i ^ bits) for i in range(lax.axis_size(axi...  163 us
    ppermute x45, waiting for transfers between devices, swap(): lax.ppermute(block, axis, [(i, i ^ bits) for i in range(lax.axis_size(axi...  45.2 us
    pallas_call x5, Pallas kernels, call(): pl.pallas_call(kernel, out_shape=outs, in_specs=[pl.BlockSpec(memory_spac...  23.8 us
    ppermute x6, starting transfers between devices, turned(): lax.ppermute(block, axis, [(i, (i + distance) % size) for i in range(size)])  17.7 us
  transfers between devices with their start and end apart: 51, of which 20 were waited for; matrix products, arithmetic and copies ran while one was open for 5% of the time, Pallas kernels for 0%

profile of v1, /device:TPU:1, one launch (start us, length us, event | category | flops | bytes accessed | tf_op | source)
XLA Modules:
  0.0 277.2 jit_solution(15162840708230731736)
XLA Ops:
  1.7 3.9 %collective-permute-start.6 = (bf16[1,16,2304]{2,1,0:T(8,128)(2,1)S(1)}, bf16[1,16,2304]{2,1,0:T(8,128)(2,1)S(1)}, u32[]{:S(2)}, u32[]{:S(2)}) collective-permute-start(bf16[1,16,2304]{2,1,0:T(8,128)(2,1)S(1)} %get-tuple-element.51), channel_id=1, source_target_pairs={{0,1},{1,0},{2,3},{3,2},{4,5},{5,4},{6,7},{7,6},{8,9},{9,8},{10,11... | collective-permute-start | bytes 221192 | tf_op jit(solution)/shard_map/ppermute | solution.py:23
  8.4 3.7 %collective-permute-start.2 = (s32[1,11]{1,0:T(1,128)S(1)}, s32[1,11]{1,0:T(1,128)S(1)}, u32[]{:S(2)}, u32[]{:S(2)}) collective-permute-start(s32[1,11]{1,0:T(1,128)S(1)} %pad_add_fusion.1), channel_id=1, source_target_pairs={{0,3},{1,0},{2,1},{3,2},{4,7},{5,4},{6,5},{7,6},{8,11},{9,8},{10,9... | collective-permute-start | bytes 140 | tf_op jit(solution)/shard_map/ppermute | solution.py:28
  12.1 2.6 collective-permute-start.1
  14.7 2.8 collective-permute-start
  17.5 3.2 %collective-permute-start.12 = (bf16[1,16,2304]{2,1,0:T(8,128)(2,1)S(1)}, bf16[1,16,2304]{2,1,0:T(8,128)(2,1)S(1)}, u32[]{:S(2)}, u32[]{:S(2)}) collective-permute-start(bf16[1,16,2304]{2,1,0:T(8,128)(2,1)S(1)} %get-tuple-element.50), channel_id=1, source_target_pairs={{0,4},{4,0},{8,12},{12,8},{1,5},{5,1},{9,13},{13,9},{2,6},{6,2},{1... | collective-permute-start | bytes 221192 | tf_op jit(solution)/shard_map/ppermute | solution.py:23
  20.7 3.7 %collective-permute-start.7 = (bf16[2,16,2304]{2,1,0:T(8,128)(2,1)S(1)}, bf16[2,16,2304]{2,1,0:T(8,128)(2,1)S(1)}, u32[]{:S(2)}, u32[]{:S(2)}) collective-permute-start(bf16[2,16,2304]{2,1,0:T(8,128)(2,1)S(1)} %pad_maximum_fusion.4), channel_id=1, source_target_pairs={{0,3},{1,2},{2,1},{3,0},{4,7},{5,6},{6,5},{7,4},{8,11},{9,10},{10,... | collective-permute-start | bytes 442376 | tf_op jit(solution)/shard_map/ppermute | solution.py:23
  24.5 3.8 %collective-permute-start.13 = (bf16[2,16,2304]{2,1,0:T(8,128)(2,1)S(1)}, bf16[2,16,2304]{2,1,0:T(8,128)(2,1)S(1)}, u32[]{:S(2)}, u32[]{:S(2)}) collective-permute-start(bf16[2,16,2304]{2,1,0:T(8,128)(2,1)S(1)} %pad_maximum_fusion.5), channel_id=1, source_target_pairs={{0,12},{4,8},{8,4},{12,0},{1,13},{5,9},{9,5},{13,1},{2,14},{6,10},... | collective-permute-start | bytes 442376 | tf_op jit(solution)/shard_map/ppermute | solution.py:23
  28.4 2.3 collective-permute-start.8
  35.9 3.6 %collective-permute-start.9 = (bf16[8,16,2304]{2,1,0:T(8,128)(2,1)S(1)}, bf16[8,16,2304]{2,1,0:T(8,128)(2,1)S(1)}, u32[]{:S(2)}, u32[]{:S(2)}) collective-permute-start(bf16[8,16,2304]{2,1,0:T(8,128)(2,1)S(1)} %pad_maximum_fusion.a_near), channel_id=1, source_target_pairs={{0,12},{4,8},{8,4},{12,0},{1,13},{5,9},{9,5},{13,1},{2,14},{6,10},... | collective-permute-start | bytes 1769480 | tf_op jit(solution)/shard_map/ppermute | solution.py:23
  39.9 3.4 %collective-permute-start.15 = (bf16[8,16,2304]{2,1,0:T(8,128)(2,1)S(1)}, bf16[8,16,2304]{2,1,0:T(8,128)(2,1)}, u32[]{:S(2)}, u32[]{:S(2)}) collective-permute-start(bf16[8,16,2304]{2,1,0:T(8,128)(2,1)S(1)} %pad_maximum_fusion.1.b_near), channel_id=1, source_target_pairs={{0,3},{1,2},{2,1},{3,0},{4,7},{5,6},{6,5},{7,4},{8,11},{9,10},{10,... | collective-permute-start | bytes 1769480 | tf_op jit(solution)/shard_map/ppermute | solution.py:23
  44.5 10.2 %collective-permute-start.10 = (bf16[8,16,2304]{2,1,0:T(8,128)(2,1)S(1)}, bf16[8,16,2304]{2,1,0:T(8,128)(2,1)}, u32[]{:S(2)}, u32[]{:S(2)}) collective-permute-start(bf16[8,16,2304]{2,1,0:T(8,128)(2,1)S(1)} %pad_maximum_fusion.a_near), channel_id=1, source_target_pairs={{0,16},{16,0},{32,48},{48,32},{64,80},{80,64},{96,112},{112,96},{1... | collective-permute-start | bytes 1769480 | tf_op jit(solution)/shard_map/ppermute | solution.py:23
  56.7 2.4 collective-permute-start.11
  59.1 3.2 %collective-permute-start.17 = (bf16[8,16,2304]{2,1,0:T(8,128)(2,1)}, bf16[8,16,2304]{2,1,0:T(8,128)(2,1)}, u32[]{:S(2)}, u32[]{:S(2)}) collective-permute-start(bf16[8,16,2304]{2,1,0:T(8,128)(2,1)} %collective-permute-done.15.b_far), channel_id=1, source_target_pairs={{0,16},{16,0},{32,48},{48,32},{64,80},{80,64},{96,112},{112,96},{1... | collective-permute-start | bytes 1769480 | tf_op jit(solution)/shard_map/ppermute | solution.py:23
  62.6 4.0 %collective-permute-start.3 = (f32[1,1024]{1,0:T(1,128)S(1)}, f32[1,1024]{1,0:T(1,128)S(1)}, u32[]{:S(2)}, u32[]{:S(2)}) collective-permute-start(f32[1,1024]{1,0:T(1,128)S(1)} %get-tuple-element.52), channel_id=1, source_target_pairs={{0,3},{1,0},{2,1},{3,2},{4,7},{5,4},{6,5},{7,6},{8,11},{9,8},{10,9... | collective-permute-start | bytes 12296 | tf_op jit(solution)/shard_map/ppermute | solution.py:28
  69.2 3.9 %collective-permute-done.5 = f32[1,1024]{1,0:T(1,128)S(1)} collective-permute-done((f32[1,1024]{1,0:T(1,128)S(1)}, f32[1,1024]{1,0:T(1,128)S(1)}, u32[]{:S(2)}, u32[]{:S(2)}) %collective-permute-start.5) | collective-permute-done | bytes 4128 | tf_op jit(solution)/shard_map/ppermute | solution.py:28
  73.1 2.8 %collective-permute-start.4 = (f32[1,1024]{1,0:T(1,128)S(1)}, f32[1,1024]{1,0:T(1,128)S(1)}, u32[]{:S(2)}, u32[]{:S(2)}) collective-permute-start(f32[1,1024]{1,0:T(1,128)S(1)} %get-tuple-element.54), channel_id=1, source_target_pairs={{0,2},{1,3},{2,0},{3,1},{4,6},{5,7},{6,4},{7,5},{8,10},{9,11},{10,... | collective-permute-start | bytes 12296 | tf_op jit(solution)/shard_map/ppermute | solution.py:28
  82.3 16.6 %trunk.1 = (bf16[2,4,16,2304]{3,2,1,0:T(8,128)(2,1)}, bf16[2,4,16,2304]{3,2,1,0:T(8,128)(2,1)}, bf16[2,4,16,2304]{3,2,1,0:T(8,128)(2,1)}, bf16[2,4,16,2304]{3,2,...) custom-call(s32[5]{0:T(128)} %stack.23.where, ...), custom_call_target="tpu_custom_call" | custom-call | flops 5435817984 | bytes 16777216 | tf_op jit(solution)/shard_map/trunk/pallas_call | solution.py:47
  99.9 3.0 %collective-permute-start.30 = (bf16[1,4096]{1,0:T(2,128)(2,1)S(1)}, bf16[1,4096]{1,0:T(2,128)(2,1)S(1)}, u32[]{:S(2)}, u32[]{:S(2)}) collective-permute-start(bf16[1,4096]{1,0:T(2,128)(2,1)S(1)} %slice.140), channel_id=1, source_target_pairs={{0,1},{1,0},{2,3},{3,2},{4,5},{5,4},{6,7},{7,6},{8,9},{9,8},{10,11... | collective-permute-start | bytes 24584 | tf_op jit(solution)/shard_map/ppermute | solution.py:23
  104.4 2.8 %collective-permute-start.31 = (bf16[2,4096]{1,0:T(2,128)(2,1)S(1)}, bf16[2,4096]{1,0:T(2,128)(2,1)S(1)}, u32[]{:S(2)}, u32[]{:S(2)}) collective-permute-start(bf16[2,4096]{1,0:T(2,128)(2,1)S(1)} %pad_maximum_fusion.8), channel_id=1, source_target_pairs={{0,3},{1,2},{2,1},{3,0},{4,7},{5,6},{6,5},{7,4},{8,11},{9,10},{10,... | collective-permute-start | bytes 49160 | tf_op jit(solution)/shard_map/ppermute | solution.py:23
  107.2 5.4 %collective-permute-start.19 = (bf16[2,4,16,2304]{3,2,1,0:T(8,128)(2,1)}, bf16[2,4,16,2304]{3,2,1,0:T(8,128)(2,1)S(1)}, u32[]{:S(2)}, u32[]{:S(2)}) collective-permute-start(bf16[2,4,16,2304]{3,2,1,0:T(8,128)(2,1)} %get-tuple-element.28), channel_id=1, source_target_pairs={{0,16},{16,0},{32,48},{48,32},{64,80},{80,64},{96,112},{112,96},{1... | collective-permute-start | bytes 1769480 | tf_op jit(solution)/shard_map/ppermute | solution.py:23
  112.7 2.1 collective-permute-start.32
  114.8 2.5 collective-permute-done.32
  117.4 2.4 collective-permute-start.33
  119.9 5.5 %collective-permute-start.18 = (bf16[2,4,16,2304]{3,2,1,0:T(8,128)(2,1)}, bf16[2,4,16,2304]{3,2,1,0:T(8,128)(2,1)}, u32[]{:S(2)}, u32[]{:S(2)}) collective-permute-start(bf16[2,4,16,2304]{3,2,1,0:T(8,128)(2,1)} %get-tuple-element.26), channel_id=1, source_target_pairs={{0,16},{16,0},{32,48},{48,32},{64,80},{80,64},{96,112},{112,96},{1... | collective-permute-start | bytes 1769480 | tf_op jit(solution)/shard_map/ppermute | solution.py:23
  127.2 2.4 collective-permute-start.25
  133.0 4.2 %collective-permute-start.20 = (bf16[2,4,16,2304]{3,2,1,0:T(8,128)(2,1)S(1)}, bf16[2,4,16,2304]{3,2,1,0:T(8,128)(2,1)S(1)}, u32[]{:S(2)}, u32[]{:S(2)}) collective-permute-start(bf16[2,4,16,2304]{3,2,1,0:T(8,128)(2,1)S(1)} %add_convert_fusion.4), channel_id=1, source_target_pairs={{0,12},{4,8},{8,4},{12,0},{1,13},{5,9},{9,5},{13,1},{2,14},{6,10},... | collective-permute-start | bytes 1769480 | tf_op jit(solution)/shard_map/ppermute | solution.py:23
  137.4 2.5 collective-permute-start.26
  139.9 10.7 %collective-permute-done.20 = bf16[2,4,16,2304]{3,2,1,0:T(8,128)(2,1)S(1)} collective-permute-done((bf16[2,4,16,2304]{3,2,1,0:T(8,128)(2,1)S(1)}, bf16[2,4,16,2304]{3,2,1,0:T(8,128)(2,1)S(1)}, u32[]{:S(2)}, u32[]{:S(2)}) %collective-permute-start.20) | collective-permute-done | bytes 589856 | tf_op jit(solution)/shard_map/ppermute | solution.py:23
  156.7 4.4 %collective-permute-done.21 = bf16[4,16,2304]{2,1,0:T(8,128)(2,1)S(1)} collective-permute-done((bf16[4,16,2304]{2,1,0:T(8,128)(2,1)S(1)}, bf16[4,16,2304]{2,1,0:T(8,128)(2,1)S(1)}, u32[]{:S(2)}, u32[]{:S(2)}) %collective-permute-start.21) | collective-permute-done | bytes 294944 | tf_op jit(solution)/shard_map/ppermute | solution.py:23
  161.2 2.5 collective-permute-start.22
  163.8 4.1 %collective-permute-start.28 = (bf16[2,16,2304]{2,1,0:T(8,128)(2,1)S(1)}, bf16[2,16,2304]{2,1,0:T(8,128)(2,1)S(1)}, u32[]{:S(2)}, u32[]{:S(2)}) collective-permute-start(bf16[2,16,2304]{2,1,0:T(8,128)(2,1)S(1)} %slice.111), channel_id=1, source_target_pairs={{0,12},{4,8},{8,4},{12,0},{1,13},{5,9},{9,5},{13,1},{2,14},{6,10},... | collective-permute-start | bytes 442376 | tf_op jit(solution)/shard_map/ppermute | solution.py:23
  174.2 2.7 collective-permute-done.29.b_come
  177.6 2.2 pack.1
  179.8 2.5 collective-permute-start.35
  182.3 4.9 %collective-permute-start.36 = (bf16[32,1024]{1,0:T(8,128)(2,1)}, bf16[32,1024]{1,0:T(8,128)(2,1)S(1)}, u32[]{:S(2)}, u32[]{:S(2)}) collective-permute-start(bf16[32,1024]{1,0:T(8,128)(2,1)} %get-tuple-element.36), channel_id=1, source_target_pairs={{0,64},{16,80},{32,96},{48,112},{64,0},{80,16},{96,32},{112,48},{1... | collective-permute-start | bytes 196616 | tf_op jit(solution)/shard_map/ppermute | solution.py:23
  189.8 5.1 %collective-permute-done.37.three = bf16[32,1024]{1,0:T(8,128)(2,1)S(1)} collective-permute-done((bf16[32,1024]{1,0:T(8,128)(2,1)}, bf16[32,1024]{1,0:T(8,128)(2,1)S(1)}, u32[]{:S(2)}, u32[]{:S(2)}) %collective-permute-start.37) | collective-permute-done | bytes 65568 | tf_op jit(solution)/shard_map/ppermute | solution.py:23
  197.1 8.3 %collective-permute-start.38 = (bf16[16,512]{1,0:T(8,128)(2,1)}, bf16[16,512]{1,0:T(8,128)(2,1)S(1)}, u32[]{:S(2)}, u32[]{:S(2)}) collective-permute-start(bf16[16,512]{1,0:T(8,128)(2,1)} %get-tuple-element.39), channel_id=1, source_target_pairs={{0,128},{16,144},{32,160},{48,176},{64,192},{80,208},{96,224},{112... | collective-permute-start | bytes 49160 | tf_op jit(solution)/shard_map/ppermute | solution.py:23
  205.4 7.7 %collective-permute-start.39 = (bf16[16,512]{1,0:T(8,128)(2,1)}, bf16[16,512]{1,0:T(8,128)(2,1)S(1)}, u32[]{:S(2)}, u32[]{:S(2)}) collective-permute-start(bf16[16,512]{1,0:T(8,128)(2,1)} %get-tuple-element.40), channel_id=1, source_target_pairs={{0,256},{16,272},{32,288},{48,304},{64,320},{80,336},{96,352},{112... | collective-permute-start | bytes 49160 | tf_op jit(solution)/shard_map/ppermute | solution.py:23
  215.1 3.7 %collective-permute-done.39 = bf16[16,512]{1,0:T(8,128)(2,1)S(1)} collective-permute-done((bf16[16,512]{1,0:T(8,128)(2,1)}, bf16[16,512]{1,0:T(8,128)(2,1)S(1)}, u32[]{:S(2)}, u32[]{:S(2)}) %collective-permute-start.39) | collective-permute-done | bytes 16416 | tf_op jit(solution)/shard_map/ppermute | solution.py:23
  218.9 2.9 %collective-permute-done.40 = bf16[16,512]{1,0:T(8,128)(2,1)S(1)} collective-permute-done((bf16[16,512]{1,0:T(8,128)(2,1)}, bf16[16,512]{1,0:T(8,128)(2,1)S(1)}, u32[]{:S(2)}, u32[]{:S(2)}) %collective-permute-start.40) | collective-permute-done | bytes 16416 | tf_op jit(solution)/shard_map/ppermute | solution.py:23
  222.5 3.0 %collective-permute-start.43 = (bf16[16,512]{1,0:T(8,128)(2,1)S(1)}, bf16[16,512]{1,0:T(8,128)(2,1)S(1)}, u32[]{:S(2)}, u32[]{:S(2)}) collective-permute-start(bf16[16,512]{1,0:T(8,128)(2,1)S(1)} %add_convert_fusion.8.own), channel_id=1, source_target_pairs={{0,384},{16,400},{32,416},{48,432},{64,448},{80,464},{96,480},{112... | collective-permute-start | bytes 49160 | tf_op jit(solution)/shard_map/ppermute | solution.py:23
  225.5 9.5 %collective-permute-start.42 = (bf16[16,512]{1,0:T(8,128)(2,1)S(1)}, bf16[16,512]{1,0:T(8,128)(2,1)S(1)}, u32[]{:S(2)}, u32[]{:S(2)}) collective-permute-start(bf16[16,512]{1,0:T(8,128)(2,1)S(1)} %add_convert_fusion.8.own), channel_id=1, source_target_pairs={{0,256},{16,272},{32,288},{48,304},{64,320},{80,336},{96,352},{112... | collective-permute-start | bytes 49160 | tf_op jit(solution)/shard_map/ppermute | solution.py:23
  235.0 3.7 %collective-permute-start.41 = (bf16[16,512]{1,0:T(8,128)(2,1)S(1)}, bf16[16,512]{1,0:T(8,128)(2,1)S(1)}, u32[]{:S(2)}, u32[]{:S(2)}) collective-permute-start(bf16[16,512]{1,0:T(8,128)(2,1)S(1)} %add_convert_fusion.8.own), channel_id=1, source_target_pairs={{0,128},{16,144},{32,160},{48,176},{64,192},{80,208},{96,224},{112... | collective-permute-start | bytes 49160 | tf_op jit(solution)/shard_map/ppermute | solution.py:23
  238.8 4.6 %collective-permute-done.41.one = bf16[16,512]{1,0:T(8,128)(2,1)S(1)} collective-permute-done((bf16[16,512]{1,0:T(8,128)(2,1)S(1)}, bf16[16,512]{1,0:T(8,128)(2,1)S(1)}, u32[]{:S(2)}, u32[]{:S(2)}) %collective-permute-start.41) | collective-permute-done | bytes 16416 | tf_op jit(solution)/shard_map/ppermute | solution.py:23
  245.5 3.2 %collective-permute-start.46 = (bf16[32,1024]{1,0:T(8,128)(2,1)}, bf16[32,1024]{1,0:T(8,128)(2,1)S(1)}, u32[]{:S(2)}, u32[]{:S(2)}) collective-permute-start(bf16[32,1024]{1,0:T(8,128)(2,1)} %join.1.rest_0_), channel_id=1, source_target_pairs={{0,96},{16,112},{32,64},{48,80},{64,32},{80,48},{96,0},{112,16},{1... | collective-permute-start | bytes 196616 | tf_op jit(solution)/shard_map/ppermute | solution.py:23
  250.6 4.1 %collective-permute-start.44 = (bf16[32,1024]{1,0:T(8,128)(2,1)}, bf16[32,1024]{1,0:T(8,128)(2,1)S(1)}, u32[]{:S(2)}, u32[]{:S(2)}) collective-permute-start(bf16[32,1024]{1,0:T(8,128)(2,1)} %join.1.rest_0_), channel_id=1, source_target_pairs={{0,32},{16,48},{32,0},{48,16},{64,96},{80,112},{96,64},{112,80},{1... | collective-permute-start | bytes 196616 | tf_op jit(solution)/shard_map/ppermute | solution.py:23
  254.8 12.2 %collective-permute-start.47 = (bf16[32,1024]{1,0:T(8,128)(2,1)}, bf16[32,1024]{1,0:T(8,128)(2,1)S(1)}, u32[]{:S(2)}, u32[]{:S(2)}) collective-permute-start(bf16[32,1024]{1,0:T(8,128)(2,1)} %join.1.rest_0_), channel_id=1, source_target_pairs={{0,16},{16,0},{32,48},{48,32},{64,80},{80,64},{96,112},{112,96},{1... | collective-permute-start | bytes 196616 | tf_op jit(solution)/shard_map/ppermute | solution.py:23
  269.0 2.4 collective-permute-start.49
  (165 shorter events, 61.0 us)
Async XLA Ops:
  1.7 19.0 %collective-permute-start.6 = (bf16[1,16,2304]{2,1,0:T(8,128)(2,1)S(1)}, bf16[1,16,2304]{2,1,0:T(8,128)(2,1)S(1)}, u32[]{:S(2)}, u32[]{:S(2)}) collective-permute-start(bf16[1,16,2304]{2,1,0:T(8,128)(2,1)S(1)} %get-tuple-element.51), channel_id=1, source_target_pairs={{0,1},{1,0},{2,3},{3,2},{4,5},{5,4},{6,7},{7,6},{8,9},{9,8},{10,11... | collective-permute-start | bytes 221192 | tf_op jit(solution)/shard_map/ppermute | solution.py:23
  8.4 34.9 %collective-permute-start.2 = (s32[1,11]{1,0:T(1,128)S(1)}, s32[1,11]{1,0:T(1,128)S(1)}, u32[]{:S(2)}, u32[]{:S(2)}) collective-permute-start(s32[1,11]{1,0:T(1,128)S(1)} %pad_add_fusion.1), channel_id=1, source_target_pairs={{0,3},{1,0},{2,1},{3,2},{4,7},{5,4},{6,5},{7,6},{8,11},{9,8},{10,9... | collective-permute-start | bytes 140 | tf_op jit(solution)/shard_map/ppermute | solution.py:28
  12.1 31.2 %collective-permute-start.1 = (s32[1,11]{1,0:T(1,128)S(1)}, s32[1,11]{1,0:T(1,128)S(1)}, u32[]{:S(2)}, u32[]{:S(2)}) collective-permute-start(s32[1,11]{1,0:T(1,128)S(1)} %pad_add_fusion.1), channel_id=1, source_target_pairs={{0,2},{1,3},{2,0},{3,1},{4,6},{5,7},{6,4},{7,5},{8,10},{9,11},{10,... | collective-permute-start | bytes 140 | tf_op jit(solution)/shard_map/ppermute | solution.py:28
  14.7 28.7 %collective-permute-start = (s32[1,11]{1,0:T(1,128)S(1)}, s32[1,11]{1,0:T(1,128)S(1)}, u32[]{:S(2)}, u32[]{:S(2)}) collective-permute-start(s32[1,11]{1,0:T(1,128)S(1)} %pad_add_fusion.1), channel_id=1, source_target_pairs={{0,1},{1,2},{2,3},{3,0},{4,5},{5,6},{6,7},{7,4},{8,9},{9,10},{10,1... | collective-permute-start | bytes 140 | tf_op jit(solution)/shard_map/ppermute | solution.py:28
  17.5 7.0 %collective-permute-start.12 = (bf16[1,16,2304]{2,1,0:T(8,128)(2,1)S(1)}, bf16[1,16,2304]{2,1,0:T(8,128)(2,1)S(1)}, u32[]{:S(2)}, u32[]{:S(2)}) collective-permute-start(bf16[1,16,2304]{2,1,0:T(8,128)(2,1)S(1)} %get-tuple-element.50), channel_id=1, source_target_pairs={{0,4},{4,0},{8,12},{12,8},{1,5},{5,1},{9,13},{13,9},{2,6},{6,2},{1... | collective-permute-start | bytes 221192 | tf_op jit(solution)/shard_map/ppermute | solution.py:23
  20.7 7.6 %collective-permute-start.7 = (bf16[2,16,2304]{2,1,0:T(8,128)(2,1)S(1)}, bf16[2,16,2304]{2,1,0:T(8,128)(2,1)S(1)}, u32[]{:S(2)}, u32[]{:S(2)}) collective-permute-start(bf16[2,16,2304]{2,1,0:T(8,128)(2,1)S(1)} %pad_maximum_fusion.4), channel_id=1, source_target_pairs={{0,3},{1,2},{2,1},{3,0},{4,7},{5,6},{6,5},{7,4},{8,11},{9,10},{10,... | collective-permute-start | bytes 442376 | tf_op jit(solution)/shard_map/ppermute | solution.py:23
  24.5 7.4 %collective-permute-start.13 = (bf16[2,16,2304]{2,1,0:T(8,128)(2,1)S(1)}, bf16[2,16,2304]{2,1,0:T(8,128)(2,1)S(1)}, u32[]{:S(2)}, u32[]{:S(2)}) collective-permute-start(bf16[2,16,2304]{2,1,0:T(8,128)(2,1)S(1)} %pad_maximum_fusion.5), channel_id=1, source_target_pairs={{0,12},{4,8},{8,4},{12,0},{1,13},{5,9},{9,5},{13,1},{2,14},{6,10},... | collective-permute-start | bytes 442376 | tf_op jit(solution)/shard_map/ppermute | solution.py:23
  28.4 7.5 %collective-permute-start.8 = (bf16[4,16,2304]{2,1,0:T(8,128)(2,1)S(1)}, bf16[4,16,2304]{2,1,0:T(8,128)(2,1)S(1)}, u32[]{:S(2)}, u32[]{:S(2)}) collective-permute-start(bf16[4,16,2304]{2,1,0:T(8,128)(2,1)S(1)} %pad_maximum_fusion.2), channel_id=1, source_target_pairs={{0,4},{4,0},{8,12},{12,8},{1,5},{5,1},{9,13},{13,9},{2,6},{6,2},{1... | collective-permute-start | bytes 884744 | tf_op jit(solution)/shard_map/ppermute | solution.py:23
  31.9 7.9 %collective-permute-start.14 = (bf16[4,16,2304]{2,1,0:T(8,128)(2,1)S(1)}, bf16[4,16,2304]{2,1,0:T(8,128)(2,1)S(1)}, u32[]{:S(2)}, u32[]{:S(2)}) collective-permute-start(bf16[4,16,2304]{2,1,0:T(8,128)(2,1)S(1)} %pad_maximum_fusion.3), channel_id=1, source_target_pairs={{0,1},{1,0},{2,3},{3,2},{4,5},{5,4},{6,7},{7,6},{8,9},{9,8},{10,11... | collective-permute-start | bytes 884744 | tf_op jit(solution)/shard_map/ppermute | solution.py:23
  35.9 20.8 %collective-permute-start.9 = (bf16[8,16,2304]{2,1,0:T(8,128)(2,1)S(1)}, bf16[8,16,2304]{2,1,0:T(8,128)(2,1)S(1)}, u32[]{:S(2)}, u32[]{:S(2)}) collective-permute-start(bf16[8,16,2304]{2,1,0:T(8,128)(2,1)S(1)} %pad_maximum_fusion.a_near), channel_id=1, source_target_pairs={{0,12},{4,8},{8,4},{12,0},{1,13},{5,9},{9,5},{13,1},{2,14},{6,10},... | collective-permute-start | bytes 1769480 | tf_op jit(solution)/shard_map/ppermute | solution.py:23
  39.9 19.2 %collective-permute-start.15 = (bf16[8,16,2304]{2,1,0:T(8,128)(2,1)S(1)}, bf16[8,16,2304]{2,1,0:T(8,128)(2,1)}, u32[]{:S(2)}, u32[]{:S(2)}) collective-permute-start(bf16[8,16,2304]{2,1,0:T(8,128)(2,1)S(1)} %pad_maximum_fusion.1.b_near), channel_id=1, source_target_pairs={{0,3},{1,2},{2,1},{3,0},{4,7},{5,6},{6,5},{7,4},{8,11},{9,10},{10,... | collective-permute-start | bytes 1769480 | tf_op jit(solution)/shard_map/ppermute | solution.py:23
  44.5 37.1 %collective-permute-start.10 = (bf16[8,16,2304]{2,1,0:T(8,128)(2,1)S(1)}, bf16[8,16,2304]{2,1,0:T(8,128)(2,1)}, u32[]{:S(2)}, u32[]{:S(2)}) collective-permute-start(bf16[8,16,2304]{2,1,0:T(8,128)(2,1)S(1)} %pad_maximum_fusion.a_near), channel_id=1, source_target_pairs={{0,16},{16,0},{32,48},{48,32},{64,80},{80,64},{96,112},{112,96},{1... | collective-permute-start | bytes 1769480 | tf_op jit(solution)/shard_map/ppermute | solution.py:23
  54.7 26.9 %collective-permute-start.16 = (bf16[8,16,2304]{2,1,0:T(8,128)(2,1)S(1)}, bf16[8,16,2304]{2,1,0:T(8,128)(2,1)}, u32[]{:S(2)}, u32[]{:S(2)}) collective-permute-start(bf16[8,16,2304]{2,1,0:T(8,128)(2,1)S(1)} %pad_maximum_fusion.1.b_near), channel_id=1, source_target_pairs={{0,16},{16,0},{32,48},{48,32},{64,80},{80,64},{96,112},{112,96},{1... | collective-permute-start | bytes 1769480 | tf_op jit(solution)/shard_map/ppermute | solution.py:23
  56.7 24.9 %collective-permute-start.11 = (bf16[8,16,2304]{2,1,0:T(8,128)(2,1)S(1)}, bf16[8,16,2304]{2,1,0:T(8,128)(2,1)}, u32[]{:S(2)}, u32[]{:S(2)}) collective-permute-start(bf16[8,16,2304]{2,1,0:T(8,128)(2,1)S(1)} %collective-permute-done.9.a_far), channel_id=1, source_target_pairs={{0,16},{16,0},{32,48},{48,32},{64,80},{80,64},{96,112},{112,96},{1... | collective-permute-start | bytes 1769480 | tf_op jit(solution)/shard_map/ppermute | solution.py:23
  59.1 22.5 %collective-permute-start.17 = (bf16[8,16,2304]{2,1,0:T(8,128)(2,1)}, bf16[8,16,2304]{2,1,0:T(8,128)(2,1)}, u32[]{:S(2)}, u32[]{:S(2)}) collective-permute-start(bf16[8,16,2304]{2,1,0:T(8,128)(2,1)} %collective-permute-done.15.b_far), channel_id=1, source_target_pairs={{0,16},{16,0},{32,48},{48,32},{64,80},{80,64},{96,112},{112,96},{1... | collective-permute-start | bytes 1769480 | tf_op jit(solution)/shard_map/ppermute | solution.py:23
  62.6 4.7 %collective-permute-start.3 = (f32[1,1024]{1,0:T(1,128)S(1)}, f32[1,1024]{1,0:T(1,128)S(1)}, u32[]{:S(2)}, u32[]{:S(2)}) collective-permute-start(f32[1,1024]{1,0:T(1,128)S(1)} %get-tuple-element.52), channel_id=1, source_target_pairs={{0,3},{1,0},{2,1},{3,2},{4,7},{5,4},{6,5},{7,6},{8,11},{9,8},{10,9... | collective-permute-start | bytes 12296 | tf_op jit(solution)/shard_map/ppermute | solution.py:28
  67.3 5.8 %collective-permute-start.5 = (f32[1,1024]{1,0:T(1,128)S(1)}, f32[1,1024]{1,0:T(1,128)S(1)}, u32[]{:S(2)}, u32[]{:S(2)}) collective-permute-start(f32[1,1024]{1,0:T(1,128)S(1)} %get-tuple-element.53), channel_id=1, source_target_pairs={{0,1},{1,2},{2,3},{3,0},{4,5},{5,6},{6,7},{7,4},{8,9},{9,10},{10,1... | collective-permute-start | bytes 12296 | tf_op jit(solution)/shard_map/ppermute | solution.py:28
  73.1 8.5 %collective-permute-start.4 = (f32[1,1024]{1,0:T(1,128)S(1)}, f32[1,1024]{1,0:T(1,128)S(1)}, u32[]{:S(2)}, u32[]{:S(2)}) collective-permute-start(f32[1,1024]{1,0:T(1,128)S(1)} %get-tuple-element.54), channel_id=1, source_target_pairs={{0,2},{1,3},{2,0},{3,1},{4,6},{5,7},{6,4},{7,5},{8,10},{9,11},{10,... | collective-permute-start | bytes 12296 | tf_op jit(solution)/shard_map/ppermute | solution.py:28
  104.4 8.2 %collective-permute-start.31 = (bf16[2,4096]{1,0:T(2,128)(2,1)S(1)}, bf16[2,4096]{1,0:T(2,128)(2,1)S(1)}, u32[]{:S(2)}, u32[]{:S(2)}) collective-permute-start(bf16[2,4096]{1,0:T(2,128)(2,1)S(1)} %pad_maximum_fusion.8), channel_id=1, source_target_pairs={{0,3},{1,2},{2,1},{3,0},{4,7},{5,6},{6,5},{7,4},{8,11},{9,10},{10,... | collective-permute-start | bytes 49160 | tf_op jit(solution)/shard_map/ppermute | solution.py:23
  107.2 24.5 %collective-permute-start.19 = (bf16[2,4,16,2304]{3,2,1,0:T(8,128)(2,1)}, bf16[2,4,16,2304]{3,2,1,0:T(8,128)(2,1)S(1)}, u32[]{:S(2)}, u32[]{:S(2)}) collective-permute-start(bf16[2,4,16,2304]{3,2,1,0:T(8,128)(2,1)} %get-tuple-element.28), channel_id=1, source_target_pairs={{0,16},{16,0},{32,48},{48,32},{64,80},{80,64},{96,112},{112,96},{1... | collective-permute-start | bytes 1769480 | tf_op jit(solution)/shard_map/ppermute | solution.py:23
  112.7 4.7 %collective-permute-start.32 = (bf16[4,4096]{1,0:T(4,128)(2,1)S(1)}, bf16[4,4096]{1,0:T(4,128)(2,1)S(1)}, u32[]{:S(2)}, u32[]{:S(2)}) collective-permute-start(bf16[4,4096]{1,0:T(4,128)(2,1)S(1)} %pad_maximum_fusion.7), channel_id=1, source_target_pairs={{0,4},{4,0},{8,12},{12,8},{1,5},{5,1},{9,13},{13,9},{2,6},{6,2},{1... | collective-permute-start | bytes 98312 | tf_op jit(solution)/shard_map/ppermute | solution.py:23
  117.4 12.2 %collective-permute-start.33 = (bf16[8,4096]{1,0:T(8,128)(2,1)S(1)}, bf16[8,4096]{1,0:T(8,128)(2,1)S(1)}, u32[]{:S(2)}, u32[]{:S(2)}) collective-permute-start(bf16[8,4096]{1,0:T(8,128)(2,1)S(1)} %pad_maximum_fusion.6), channel_id=1, source_target_pairs={{0,12},{4,8},{8,4},{12,0},{1,13},{5,9},{9,5},{13,1},{2,14},{6,10},... | collective-permute-start | bytes 196616 | tf_op jit(solution)/shard_map/ppermute | solution.py:23
  119.9 20.0 %collective-permute-start.18 = (bf16[2,4,16,2304]{3,2,1,0:T(8,128)(2,1)}, bf16[2,4,16,2304]{3,2,1,0:T(8,128)(2,1)}, u32[]{:S(2)}, u32[]{:S(2)}) collective-permute-start(bf16[2,4,16,2304]{3,2,1,0:T(8,128)(2,1)} %get-tuple-element.26), channel_id=1, source_target_pairs={{0,16},{16,0},{32,48},{48,32},{64,80},{80,64},{96,112},{112,96},{1... | collective-permute-start | bytes 1769480 | tf_op jit(solution)/shard_map/ppermute | solution.py:23
  125.3 28.7 %collective-permute-start.24 = (bf16[2,4,16,2304]{3,2,1,0:T(8,128)(2,1)}, bf16[2,4,16,2304]{3,2,1,0:T(8,128)(2,1)S(1)}, u32[]{:S(2)}, u32[]{:S(2)}) collective-permute-start(bf16[2,4,16,2304]{3,2,1,0:T(8,128)(2,1)} %get-tuple-element.30), channel_id=1, source_target_pairs={{0,16},{16,0},{32,48},{48,32},{64,80},{80,64},{96,112},{112,96},{1... | collective-permute-start | bytes 1769480 | tf_op jit(solution)/shard_map/ppermute | solution.py:23
  127.2 9.9 %collective-permute-start.25 = (bf16[2,4,16,2304]{3,2,1,0:T(8,128)(2,1)}, bf16[2,4,16,2304]{3,2,1,0:T(8,128)(2,1)S(1)}, u32[]{:S(2)}, u32[]{:S(2)}) collective-permute-start(bf16[2,4,16,2304]{3,2,1,0:T(8,128)(2,1)} %get-tuple-element.32), channel_id=1, source_target_pairs={{0,16},{16,0},{32,48},{48,32},{64,80},{80,64},{96,112},{112,96},{1... | collective-permute-start | bytes 1769480 | tf_op jit(solution)/shard_map/ppermute | solution.py:23
  129.8 44.0 %collective-permute-start.34 = (bf16[16,4096]{1,0:T(8,128)(2,1)S(1)}, bf16[16,4096]{1,0:T(8,128)(2,1)S(1)}, u32[]{:S(2)}, u32[]{:S(2)}) collective-permute-start(bf16[16,4096]{1,0:T(8,128)(2,1)S(1)} %concatenate.54.near), channel_id=1, source_target_pairs={{0,16},{16,0},{32,48},{48,32},{64,80},{80,64},{96,112},{112,96},{1... | collective-permute-start | bytes 393224 | tf_op jit(solution)/shard_map/ppermute | solution.py:23
  133.0 17.6 %collective-permute-start.20 = (bf16[2,4,16,2304]{3,2,1,0:T(8,128)(2,1)S(1)}, bf16[2,4,16,2304]{3,2,1,0:T(8,128)(2,1)S(1)}, u32[]{:S(2)}, u32[]{:S(2)}) collective-permute-start(bf16[2,4,16,2304]{3,2,1,0:T(8,128)(2,1)S(1)} %add_convert_fusion.4), channel_id=1, source_target_pairs={{0,12},{4,8},{8,4},{12,0},{1,13},{5,9},{9,5},{13,1},{2,14},{6,10},... | collective-permute-start | bytes 1769480 | tf_op jit(solution)/shard_map/ppermute | solution.py:23
  137.4 17.2 %collective-permute-start.26 = (bf16[2,4,16,2304]{3,2,1,0:T(8,128)(2,1)S(1)}, bf16[2,4,16,2304]{3,2,1,0:T(8,128)(2,1)S(1)}, u32[]{:S(2)}, u32[]{:S(2)}) collective-permute-start(bf16[2,4,16,2304]{3,2,1,0:T(8,128)(2,1)S(1)} %add_convert_fusion.1), channel_id=1, source_target_pairs={{0,3},{1,2},{2,1},{3,0},{4,7},{5,6},{6,5},{7,4},{8,11},{9,10},{10,... | collective-permute-start | bytes 1769480 | tf_op jit(solution)/shard_map/ppermute | solution.py:23
  152.1 9.0 %collective-permute-start.21 = (bf16[4,16,2304]{2,1,0:T(8,128)(2,1)S(1)}, bf16[4,16,2304]{2,1,0:T(8,128)(2,1)S(1)}, u32[]{:S(2)}, u32[]{:S(2)}) collective-permute-start(bf16[4,16,2304]{2,1,0:T(8,128)(2,1)S(1)} %slice_bitcast_fusion.2), channel_id=1, source_target_pairs={{0,4},{4,0},{8,12},{12,8},{1,5},{5,1},{9,13},{13,9},{2,6},{6,2},{1... | collective-permute-start | bytes 884744 | tf_op jit(solution)/shard_map/ppermute | solution.py:23
  154.8 8.9 %collective-permute-start.27 = (bf16[4,16,2304]{2,1,0:T(8,128)(2,1)S(1)}, bf16[4,16,2304]{2,1,0:T(8,128)(2,1)S(1)}, u32[]{:S(2)}, u32[]{:S(2)}) collective-permute-start(bf16[4,16,2304]{2,1,0:T(8,128)(2,1)S(1)} %slice_bitcast_fusion), channel_id=1, source_target_pairs={{0,1},{1,0},{2,3},{3,2},{4,5},{5,4},{6,7},{7,6},{8,9},{9,8},{10,11... | collective-permute-start | bytes 884744 | tf_op jit(solution)/shard_map/ppermute | solution.py:23
  161.2 7.1 %collective-permute-start.22 = (bf16[2,16,2304]{2,1,0:T(8,128)(2,1)S(1)}, bf16[2,16,2304]{2,1,0:T(8,128)(2,1)S(1)}, u32[]{:S(2)}, u32[]{:S(2)}) collective-permute-start(bf16[2,16,2304]{2,1,0:T(8,128)(2,1)S(1)} %slice.105), channel_id=1, source_target_pairs={{0,3},{1,2},{2,1},{3,0},{4,7},{5,6},{6,5},{7,4},{8,11},{9,10},{10,... | collective-permute-start | bytes 442376 | tf_op jit(solution)/shard_map/ppermute | solution.py:23
  163.8 7.4 %collective-permute-start.28 = (bf16[2,16,2304]{2,1,0:T(8,128)(2,1)S(1)}, bf16[2,16,2304]{2,1,0:T(8,128)(2,1)S(1)}, u32[]{:S(2)}, u32[]{:S(2)}) collective-permute-start(bf16[2,16,2304]{2,1,0:T(8,128)(2,1)S(1)} %slice.111), channel_id=1, source_target_pairs={{0,12},{4,8},{8,4},{12,0},{1,13},{5,9},{9,5},{13,1},{2,14},{6,10},... | collective-permute-start | bytes 442376 | tf_op jit(solution)/shard_map/ppermute | solution.py:23
  169.0 5.3 %collective-permute-start.23 = (bf16[16,2304]{1,0:T(8,128)(2,1)S(1)}, bf16[16,2304]{1,0:T(8,128)(2,1)S(1)}, u32[]{:S(2)}, u32[]{:S(2)}) collective-permute-start(bf16[16,2304]{1,0:T(8,128)(2,1)S(1)} %get-tuple-element.48), channel_id=1, source_target_pairs={{0,1},{1,0},{2,3},{3,2},{4,5},{5,4},{6,7},{7,6},{8,9},{9,8},{10,11... | collective-permute-start | bytes 221192 | tf_op jit(solution)/shard_map/ppermute | solution.py:23
  171.9 5.1 %collective-permute-start.29 = (bf16[16,2304]{1,0:T(8,128)(2,1)S(1)}, bf16[16,2304]{1,0:T(8,128)(2,1)S(1)}, u32[]{:S(2)}, u32[]{:S(2)}) collective-permute-start(bf16[16,2304]{1,0:T(8,128)(2,1)S(1)} %get-tuple-element.46), channel_id=1, source_target_pairs={{0,4},{4,0},{8,12},{12,8},{1,5},{5,1},{9,13},{13,9},{2,6},{6,2},{1... | collective-permute-start | bytes 221192 | tf_op jit(solution)/shard_map/ppermute | solution.py:23
  179.8 9.3 %collective-permute-start.35 = (bf16[32,1024]{1,0:T(8,128)(2,1)}, bf16[32,1024]{1,0:T(8,128)(2,1)S(1)}, u32[]{:S(2)}, u32[]{:S(2)}) collective-permute-start(bf16[32,1024]{1,0:T(8,128)(2,1)} %get-tuple-element.35), channel_id=1, source_target_pairs={{0,32},{16,48},{32,0},{48,16},{64,96},{80,112},{96,64},{112,80},{1... | collective-permute-start | bytes 196616 | tf_op jit(solution)/shard_map/ppermute | solution.py:23
  182.3 7.5 %collective-permute-start.36 = (bf16[32,1024]{1,0:T(8,128)(2,1)}, bf16[32,1024]{1,0:T(8,128)(2,1)S(1)}, u32[]{:S(2)}, u32[]{:S(2)}) collective-permute-start(bf16[32,1024]{1,0:T(8,128)(2,1)} %get-tuple-element.36), channel_id=1, source_target_pairs={{0,64},{16,80},{32,96},{48,112},{64,0},{80,16},{96,32},{112,48},{1... | collective-permute-start | bytes 196616 | tf_op jit(solution)/shard_map/ppermute | solution.py:23
  187.2 7.7 %collective-permute-start.37 = (bf16[32,1024]{1,0:T(8,128)(2,1)}, bf16[32,1024]{1,0:T(8,128)(2,1)S(1)}, u32[]{:S(2)}, u32[]{:S(2)}) collective-permute-start(bf16[32,1024]{1,0:T(8,128)(2,1)} %get-tuple-element.37), channel_id=1, source_target_pairs={{0,96},{16,112},{32,64},{48,80},{64,32},{80,48},{96,0},{112,16},{1... | collective-permute-start | bytes 196616 | tf_op jit(solution)/shard_map/ppermute | solution.py:23
  197.1 18.0 %collective-permute-start.38 = (bf16[16,512]{1,0:T(8,128)(2,1)}, bf16[16,512]{1,0:T(8,128)(2,1)S(1)}, u32[]{:S(2)}, u32[]{:S(2)}) collective-permute-start(bf16[16,512]{1,0:T(8,128)(2,1)} %get-tuple-element.39), channel_id=1, source_target_pairs={{0,128},{16,144},{32,160},{48,176},{64,192},{80,208},{96,224},{112... | collective-permute-start | bytes 49160 | tf_op jit(solution)/shard_map/ppermute | solution.py:23
  205.4 13.4 %collective-permute-start.39 = (bf16[16,512]{1,0:T(8,128)(2,1)}, bf16[16,512]{1,0:T(8,128)(2,1)S(1)}, u32[]{:S(2)}, u32[]{:S(2)}) collective-permute-start(bf16[16,512]{1,0:T(8,128)(2,1)} %get-tuple-element.40), channel_id=1, source_target_pairs={{0,256},{16,272},{32,288},{48,304},{64,320},{80,336},{96,352},{112... | collective-permute-start | bytes 49160 | tf_op jit(solution)/shard_map/ppermute | solution.py:23
  213.2 8.6 %collective-permute-start.40 = (bf16[16,512]{1,0:T(8,128)(2,1)}, bf16[16,512]{1,0:T(8,128)(2,1)S(1)}, u32[]{:S(2)}, u32[]{:S(2)}) collective-permute-start(bf16[16,512]{1,0:T(8,128)(2,1)} %get-tuple-element.41), channel_id=1, source_target_pairs={{0,384},{16,400},{32,416},{48,432},{64,448},{80,464},{96,480},{112... | collective-permute-start | bytes 49160 | tf_op jit(solution)/shard_map/ppermute | solution.py:23
  222.5 16.2 %collective-permute-start.43 = (bf16[16,512]{1,0:T(8,128)(2,1)S(1)}, bf16[16,512]{1,0:T(8,128)(2,1)S(1)}, u32[]{:S(2)}, u32[]{:S(2)}) collective-permute-start(bf16[16,512]{1,0:T(8,128)(2,1)S(1)} %add_convert_fusion.8.own), channel_id=1, source_target_pairs={{0,384},{16,400},{32,416},{48,432},{64,448},{80,464},{96,480},{112... | collective-permute-start | bytes 49160 | tf_op jit(solution)/shard_map/ppermute | solution.py:23
  225.5 13.2 %collective-permute-start.42 = (bf16[16,512]{1,0:T(8,128)(2,1)S(1)}, bf16[16,512]{1,0:T(8,128)(2,1)S(1)}, u32[]{:S(2)}, u32[]{:S(2)}) collective-permute-start(bf16[16,512]{1,0:T(8,128)(2,1)S(1)} %add_convert_fusion.8.own), channel_id=1, source_target_pairs={{0,256},{16,272},{32,288},{48,304},{64,320},{80,336},{96,352},{112... | collective-permute-start | bytes 49160 | tf_op jit(solution)/shard_map/ppermute | solution.py:23
  235.0 8.4 %collective-permute-start.41 = (bf16[16,512]{1,0:T(8,128)(2,1)S(1)}, bf16[16,512]{1,0:T(8,128)(2,1)S(1)}, u32[]{:S(2)}, u32[]{:S(2)}) collective-permute-start(bf16[16,512]{1,0:T(8,128)(2,1)S(1)} %add_convert_fusion.8.own), channel_id=1, source_target_pairs={{0,128},{16,144},{32,160},{48,176},{64,192},{80,208},{96,224},{112... | collective-permute-start | bytes 49160 | tf_op jit(solution)/shard_map/ppermute | solution.py:23
  245.5 21.5 %collective-permute-start.46 = (bf16[32,1024]{1,0:T(8,128)(2,1)}, bf16[32,1024]{1,0:T(8,128)(2,1)S(1)}, u32[]{:S(2)}, u32[]{:S(2)}) collective-permute-start(bf16[32,1024]{1,0:T(8,128)(2,1)} %join.1.rest_0_), channel_id=1, source_target_pairs={{0,96},{16,112},{32,64},{48,80},{64,32},{80,48},{96,0},{112,16},{1... | collective-permute-start | bytes 196616 | tf_op jit(solution)/shard_map/ppermute | solution.py:23
  248.7 20.3 %collective-permute-start.45 = (bf16[32,1024]{1,0:T(8,128)(2,1)}, bf16[32,1024]{1,0:T(8,128)(2,1)S(1)}, u32[]{:S(2)}, u32[]{:S(2)}) collective-permute-start(bf16[32,1024]{1,0:T(8,128)(2,1)} %join.1.rest_0_), channel_id=1, source_target_pairs={{0,64},{16,80},{32,96},{48,112},{64,0},{80,16},{96,32},{112,48},{1... | collective-permute-start | bytes 196616 | tf_op jit(solution)/shard_map/ppermute | solution.py:23
  250.6 20.8 %collective-permute-start.44 = (bf16[32,1024]{1,0:T(8,128)(2,1)}, bf16[32,1024]{1,0:T(8,128)(2,1)S(1)}, u32[]{:S(2)}, u32[]{:S(2)}) collective-permute-start(bf16[32,1024]{1,0:T(8,128)(2,1)} %join.1.rest_0_), channel_id=1, source_target_pairs={{0,32},{16,48},{32,0},{48,16},{64,96},{80,112},{96,64},{112,80},{1... | collective-permute-start | bytes 196616 | tf_op jit(solution)/shard_map/ppermute | solution.py:23
  254.8 18.6 %collective-permute-start.47 = (bf16[32,1024]{1,0:T(8,128)(2,1)}, bf16[32,1024]{1,0:T(8,128)(2,1)S(1)}, u32[]{:S(2)}, u32[]{:S(2)}) collective-permute-start(bf16[32,1024]{1,0:T(8,128)(2,1)} %join.1.rest_0_), channel_id=1, source_target_pairs={{0,16},{16,0},{32,48},{48,32},{64,80},{80,64},{96,112},{112,96},{1... | collective-permute-start | bytes 196616 | tf_op jit(solution)/shard_map/ppermute | solution.py:23
  267.0 6.3 %collective-permute-start.50 = (bf16[32,1024]{1,0:T(8,128)(2,1)S(1)}, bf16[32,1024]{1,0:T(8,128)(2,1)S(1)}, u32[]{:S(2)}, u32[]{:S(2)}) collective-permute-start(bf16[32,1024]{1,0:T(8,128)(2,1)S(1)} %collective-permute-done.46.rest_3_), channel_id=1, source_target_pairs={{0,16},{16,0},{32,48},{48,32},{64,80},{80,64},{96,112},{112,96},{1... | collective-permute-start | bytes 196616 | tf_op jit(solution)/shard_map/ppermute | solution.py:23
  (29 other events, 359.7 us)

commit v2 on v1

--- a/solution.py
+++ b/solution.py
@@ -1,5 +1,3 @@
-import functools
-
 import jax
 import jax.numpy as jnp
 from jax import lax
@@ -12,7 +10,6 @@
 ROWS = 384
 FRONT = 24
 NORM_EPS = 1e-05
-XOR = (0, 1, 3, 2)
 TAP_SHIFTS = [(a - 1) * PITCH + (b - 1) for a in range(3) for b in range(3)]
 VMEM_BYTES = 58 * 1024 * 1024
 F32 = jnp.float32
@@ -23,9 +20,8 @@
     return lax.ppermute(block, axis, [(i, i ^ bits) for i in range(lax.axis_size(axis))])
 
 
-def turned(block, axis, distance):
-    size = lax.axis_size(axis)
-    return lax.ppermute(block, axis, [(i, (i + distance) % size) for i in range(size)])
+def exchange(blocks, axis, groups=None):
+    return lax.all_to_all(blocks, axis, 0, 0, axis_index_groups=groups, tiled=True)
 
 
 def nn(left, right):
@@ -59,26 +55,18 @@
 
 
 def trunk_kernel(
-    where, context, w_first, w_second, embed, code_col, code_row, cotangent,
-    a_near, a_far, a_near2, a_far2, b_near, b_far, b_near2, b_far2,
-    own_a_hi, own_a_lo, own_b_hi, own_b_lo, oth_a_hi, oth_a_lo, oth_b_hi, oth_b_lo, vectors,
+    where, context, w_first, w_second, embed, code_col, code_row, cotangent, mine, theirs,
+    own, other, vectors,
     wt, patches, gt, normed, rscales, buf, grad,
 ):
-    s, h, c = where[0], where[1], where[2]
-
-    def rows_of(jx, core, part):
-        return pl.ds(pl.multiple_of((h ^ XOR[jx]) * 64 + core * 32 + part * 16, 16), 16)
-
-    for core, near, far in ((c, a_near, a_far), (1 - c, a_near2, a_far2)):
-        for jy in range(4):
-            for jx in range(4):
-                source = near if jy < 2 else far
-                wt[s ^ XOR[jy], rows_of(jx, core, 0), :] = source[(jy % 2) * 4 + jx]
-    for core, near, far in ((c, b_near, b_far), (1 - c, b_near2, b_far2)):
-        for jx in range(4):
-            for jy in range(4):
-                source = near if jx < 2 else far
-                wt[s ^ XOR[jy], rows_of(jx, core, 1), :] = source[(jx % 2) * 4 + jy]
+    c = where[2]
+
+    def rows_of(shard, core):
+        return pl.ds(pl.multiple_of(shard * 64 + core * 32, 32), 32)
+
+    for core, pieces in ((c, mine), (1 - c, theirs)):
+        for place in range(16):
+            wt[place // 4, rows_of(place % 4, core), :] = pieces[place]
 
     point = lax.broadcasted_iota(jnp.int32, (ROWS, 1), 0)
     column = point - ((point * 3277) >> 16) * PITCH
@@ -151,21 +139,23 @@
         first = 3072 + place * channels
         vectors[0:1, first : first + channels] = rounded.astype(F32)[row : row + 1]
 
-    for core, pieces in (
-        (c, (own_a_lo, own_a_hi, own_b_lo, own_b_hi)),
-        (1 - c, (oth_a_lo, oth_a_hi, oth_b_lo, oth_b_hi)),
-    ):
-        for jy in range(4):
-            for jx in range(4):
-                block = s ^ XOR[jy]
-                pieces[jy // 2][jy % 2, jx] = gt[block, rows_of(jx, core, 0), :]
-                pieces[2 + jx // 2][jx % 2, jy] = gt[block, rows_of(jx, core, 1), :]
-
-
-def pack_kernel(where, a_own, a_come, b_own, b_come, near, far, *rest):
-    outs, whole, product = rest[:4], rest[4], rest[5]
+    for core, pieces in ((c, own), (1 - c, other)):
+        for place in range(16):
+            pieces[place] = gt[place // 4, rows_of(place % 4, core), :]
+
+
+def chunk_rows(piece):
+    row = (piece % 4) // 2 * 16
+    return slice(row, row + 16)
+
+
+def chunk_lanes(piece):
+    lane = piece % 2 * 512
+    return slice(lane, lane + 512)
+
+
+def pack_kernel(where, pieces, near, far, out, whole, product):
     first = where[0] * 256 + where[1] * 64 + where[2] * 32
-    low = where[3]
     lanes = pl.multiple_of((first // 128) * 128, 128)
     rows = pl.ds(pl.multiple_of(first - lanes, 32), 32)
     whole[:, :, 896:1024] = jnp.zeros((4, 32, 128), F32)
@@ -179,9 +169,9 @@
             whole[group, :, inside : inside + take] = block[:, done : done + take]
             done += take
 
-    conv = jnp.concatenate(
-        [a_own[...].astype(F32) + a_come[...], b_own[...].astype(F32) + b_come[...]], axis=0
-    )
+    conv = pieces[0].astype(F32)
+    for piece in range(1, 16):
+        conv += pieces[piece].astype(F32)
     spread(0, conv)
     product[:, 0:1024] = tn(near[:, pl.ds(lanes, 128)], near[:, 2048:3072]) + tn(
         far[:, pl.ds(lanes, 128)], far[:, 2048:3072]
@@ -197,38 +187,16 @@
     for piece in range(6):
         row = piece // 4
         whole[piece % 4, row : row + 1, 896:1024] = stones[:, piece * 128 : (piece + 1) * 128]
-    for k in range(4):
-        outs[k][...] = whole[low ^ k].astype(BF16)
-
-
-def split_kernel(where, own, one, two, three, *rest):
-    outs, total = rest[:4], rest[4]
-    high = where[4]
-    total[...] = own[...].astype(F32) + one[...] + two[...] + three[...]
-    for k in range(4):
-        place = high ^ k
-        rows = pl.ds(pl.multiple_of((place // 2) * 16, 16), 16)
-        lanes = pl.ds(pl.multiple_of((place % 2) * 512, 512), 512)
-        outs[k][...] = total[rows, lanes].astype(BF16)
-
-
-def join_kernel(where, own, one, two, three, out):
-    high = where[4]
-    for k, piece in enumerate((own, one, two, three)):
-        place = high ^ k
-        rows = pl.ds(pl.multiple_of((place // 2) * 16, 16), 16)
-        lanes = pl.ds(pl.multiple_of((place % 2) * 512, 512), 512)
-        out[rows, lanes] = piece[...]
-
-
-def finish_kernel(where, *rest):
-    own, other = rest[0:4], rest[4:8]
-    conv, first, second, stones, whole, rows3 = rest[8:]
-    c, low = where[2], where[3]
-    for core, pieces in ((c, own), (1 - c, other)):
-        rows = pl.ds(pl.multiple_of(core * 32, 32), 32)
-        for k in range(4):
-            whole[low ^ k, rows, :] = pieces[k][...].astype(F32) * (1.0 / 512.0)
+    for piece in range(16):
+        out[piece] = whole[piece // 4, chunk_rows(piece), chunk_lanes(piece)].astype(BF16)
+
+
+def finish_kernel(where, mine, theirs, conv, first, second, stones, whole, rows3):
+    c = where[2]
+    for core, pieces in ((c, mine), (1 - c, theirs)):
+        for piece in range(16):
+            rows = pl.ds(pl.multiple_of(core * 32 + chunk_rows(piece).start, 16), 16)
+            whole[piece // 4, rows, chunk_lanes(piece)] = pieces[piece].astype(F32) * (1.0 / 512.0)
     for group in range(4):
         for out, start, width in ((conv, 0, 2304), (first, 2304, 1024), (second, 3328, 256)):
             begin = max(start, group * 896)
@@ -250,31 +218,20 @@
     h = lax.axis_index("shard")
     s = lax.axis_index("section")
     dp = lax.axis_index("dp")
-    c, z = dp % 2, dp // 2
-    where = jnp.stack([s, h, c, z % 4, z // 4]).astype(jnp.int32)
+    c = dp % 2
+    where = jnp.stack([s, h, c]).astype(jnp.int32)
     channels = embed.shape[1]
     taps = conv_weight.shape[1]
-
-    mine = lax.dynamic_slice_in_dim(conv_weight[0].T, c * 32, 32, 0).reshape(2, 16, taps)
-
-    def gather(unit, first, second):
-        block = unit[None]
-        block = jnp.concatenate([block, swap(block, first, 1)])
-        block = jnp.concatenate([block, swap(block, first, 3)])
-        block = jnp.concatenate([block, swap(block, second, 1)])
-        return block, swap(block, second, 3)
-
-    a_near, a_far = gather(mine[0], "shard", "section")
-    b_near, b_far = gather(mine[1], "section", "shard")
-    weights = (
-        a_near, a_far, swap(a_near, "dp", 1), swap(a_far, "dp", 1),
-        b_near, b_far, swap(b_near, "dp", 1), swap(b_far, "dp", 1),
-    )
+    plane = ("section", "shard")
+
+    unit = lax.dynamic_slice_in_dim(conv_weight[0].T, c * 32, 32, 0)[None]
+    mine = lax.all_gather(unit, plane, axis=0, tiled=True)
+    theirs = swap(mine, "dp", 1)
 
     ids = lax.dynamic_slice_in_dim(neighbours, s, 1, 0)
     count = lax.dynamic_slice_in_dim(counts, s, 1, 0)
     asked = jnp.concatenate([ids, count[:, None]], axis=1)
-    asked = jnp.concatenate([asked] + [turned(asked, "shard", d) for d in (1, 2, 3)])
+    asked = exchange(jnp.broadcast_to(asked, (4, asked.shape[1])), "shard")
     slots = ids.shape[1]
     live = lax.broadcasted_iota(jnp.int32, (4, slots), 1) < asked[:, slots:]
     stored = database.shape[0]
@@ -282,9 +239,7 @@
     hits = (asked[:, :slots, None] == positions) & live[:, :, None]
     picks = jnp.sum(hits.astype(F32), axis=1).astype(BF16)
     partial = jnp.dot(picks, database, preferred_element_type=F32)
-    summed = partial[0:1]
-    for d in (1, 2, 3):
-        summed = summed + turned(partial[d : d + 1], "shard", -d)
+    summed = jnp.sum(exchange(partial, "shard"), axis=0, keepdims=True)
     context = (summed / jnp.maximum(count, 1).astype(F32)[:, None]).astype(BF16)
     context = jnp.broadcast_to(context, (16, context.shape[1]))
 
@@ -295,10 +250,10 @@
     upper = jnp.pad(upper.reshape(BOARD, BOARD, channels), ((0, 0), (0, 1), (0, 0)))
     upper = jnp.pad(upper.reshape(-1, channels), ((0, ROWS - BOARD * PITCH), (0, 0)))
 
-    part = jax.ShapeDtypeStruct((2, 4, 16, taps), BF16)
-    own_a_hi, own_a_lo, own_b_hi, own_b_lo, oth_a_hi, oth_a_lo, oth_b_hi, oth_b_lo, vectors = vmem_call(
+    part = jax.ShapeDtypeStruct((16, 32, taps), BF16)
+    own, other, vectors = vmem_call(
         trunk_kernel,
-        (part,) * 8 + (jax.ShapeDtypeStruct((8, 4096), F32),),
+        (part, part, jax.ShapeDtypeStruct((8, 4096), F32)),
         [
             pltpu.VMEM((4, channels, taps), BF16),
             pltpu.VMEM((4, ROWS, taps), BF16),
@@ -311,51 +266,24 @@
         "trunk",
         12 * 2 * ROWS * taps * channels,
         16 << 20,
-    )(where, context, w_first, w_second, embed, code[:, None], code[None, :], upper, *weights)
-
-    def plus(kept, come):
-        return (kept.astype(F32) + come.astype(F32)).astype(BF16)
-
-    a_hi = plus(own_a_hi, swap(oth_a_hi, "dp", 1))
-    b_hi = plus(own_b_hi, swap(oth_b_hi, "dp", 1))
-    a_lo = plus(own_a_lo, swap(oth_a_lo, "dp", 1))
-    b_lo = plus(own_b_lo, swap(oth_b_lo, "dp", 1))
-
-    def scatter(low, high, first, second):
-        block = plus(low, swap(high, first, 3))
-        block = plus(block[0], swap(block[1], first, 1))
-        block = plus(block[0:2], swap(block[2:4], second, 3))
-        return block[0], swap(block[1], second, 1)
-
-    a_own, a_come = scatter(a_lo, a_hi, "section", "shard")
-    b_own, b_come = scatter(b_lo, b_hi, "shard", "section")
-
-    rows = vectors[0:1].astype(BF16)
-    rows = jnp.concatenate([rows, swap(rows, "shard", 1)])
-    rows = jnp.concatenate([rows, swap(rows, "shard", 3)])
-    rows = jnp.concatenate([rows, swap(rows, "section", 1)])
-    rows = jnp.concatenate([rows, swap(rows, "section", 3)])
-    group = jax.ShapeDtypeStruct((32, 1024), BF16)
-    groups = vmem_call(
+    )(where, context, w_first, w_second, embed, code[:, None], code[None, :], upper, mine, theirs)
+
+    pieces = (own.astype(F32) + swap(other, "dp", 1).astype(F32)).astype(BF16)
+    pieces = exchange(pieces, plane)
+
+    rows = lax.all_gather(vectors[0:1].astype(BF16), plane, axis=0, tiled=True)
+    (chunks,) = vmem_call(
         pack_kernel,
-        (group,) * 4,
+        (jax.ShapeDtypeStruct((16, 16, 512), BF16),),
         [pltpu.VMEM((4, 32, 1024), F32), pltpu.VMEM((128, 1280), F32)],
         "pack",
         4 * 32 * 128 * 1280,
-        1 << 20,
-    )(where, a_own, a_come, b_own, b_come, rows, swap(rows, "dp", 1))
-
-    come = [swap(groups[k], "dp", 2 * k) for k in (1, 2, 3)]
-    chunk = jax.ShapeDtypeStruct((16, 512), BF16)
-    chunks = vmem_call(
-        split_kernel, (chunk,) * 4, [pltpu.VMEM((32, 1024), F32)], "split", 1 << 17, 1 << 19
-    )(where, groups[0], *come)
-    come = [swap(chunks[k], "dp", 8 * k) for k in (1, 2, 3)]
-    total = plus(plus(chunks[0], come[0]).astype(F32), plus(come[1], come[2]).astype(F32))
-    come = [swap(total, "dp", 8 * k) for k in (1, 2, 3)]
-    (joined,) = vmem_call(join_kernel, (group,), [], "join", 1 << 10, 1 << 18)(where, total, *come)
-    own = [joined] + [swap(joined, "dp", 2 * k) for k in (1, 2, 3)]
-    other = [swap(piece, "dp", 1) for piece in own]
+        3 << 20,
+    )(where, pieces, rows, swap(rows, "dp", 1))
+
+    line = [[2 * i + core for i in range(lax.axis_size("dp") // 2)] for core in (0, 1)]
+    total = jnp.sum(exchange(chunks, "dp", line).astype(F32), axis=0, keepdims=True).astype(BF16)
+    mine = exchange(jnp.broadcast_to(total, chunks.shape), "dp", line)
     conv, w1_grad, w2_grad, embed_grad = vmem_call(
         finish_kernel,
         (
@@ -368,7 +296,7 @@
         "finish",
         1 << 18,
         1 << 20,
-    )(where, *own, *other)
+    )(where, mine, swap(mine, "dp", 1))
     return (w1_grad, w2_grad, embed_grad, conv.T[None])
 
 

time: 279 us -> 265 us (0.950)
  starting transfers between devices: 181 us -> 34.4 us
  blocking collectives: 0 us -> 94.7 us
  waiting for transfers between devices: 49.8 us -> 77.9 us
  between operations: 2.51 us -> 14.9 us
    ppermute x45 -> x4, starting transfers between devices: 163 us -> 22.4 us  [swap(): lax.ppermute(block, axis, [(i, i ^ bits) for i in range(lax.axis_size(axi...]
    all_gather x0 -> x1, waiting for transfers between devices: none -> 68.1 us  [body(): mine = lax.all_gather(unit, plane, axis=0, tiled=True)]
    all_to_all x0 -> x2, blocking collectives: none -> 49.5 us  [exchange(): lax.all_to_all(blocks, axis, 0, 0, axis_index_groups=groups, tiled=True)]
    all_gather x0 -> x1, blocking collectives: none -> 45.2 us  [body(): rows = lax.all_gather(vectors[0:1].astype(BF16), plane, axis=0, tiled=True)]
    ppermute x45 -> x4, waiting for transfers between devices: 45.2 us -> 6.46 us  [swap(): lax.ppermute(block, axis, [(i, i ^ bits) for i in range(lax.axis_size(axi...]
    ppermute x6 -> x0, starting transfers between devices: 17.7 us -> none  [turned(): lax.ppermute(block, axis, [(i, (i + distance) % size) for i in range(size)])]
    all_to_all x0 -> x3, starting transfers between devices: none -> 12 us  [exchange(): lax.all_to_all(blocks, axis, 0, 0, axis_index_groups=groups, tiled=True)]
    ppermute x6 -> x0, waiting for transfers between devices: 4.63 us -> none  [turned(): lax.ppermute(block, axis, [(i, (i + distance) % size) for i in range(size)])]
  transfers between devices with their start and end apart: 51 -> 8, of which waited for: 20 -> 5; matrix products, arithmetic and copies ran while one was open for 5% -> 4% of each run, Pallas kernels for 0% -> 0%
where the time goes in v2:
time: 265 us; the launch traced here: 264 us
  blocking collectives  94.7 us (36%)
  waiting for transfers between devices  77.9 us (29%)
  starting transfers between devices  34.4 us (13%)
  Pallas kernels  22 us (8%)
  between operations  14.9 us (6%)
  local copies, waits for them, and re-layouts  13.7 us (5%)
  other arithmetic  5.28 us (2%)
    all_gather x1, waiting for transfers between devices, body(): mine = lax.all_gather(unit, plane, axis=0, tiled=True)  68.1 us
    all_to_all x2, blocking collectives, exchange(): lax.all_to_all(blocks, axis, 0, 0, axis_index_groups=groups, tiled=True)  49.5 us
    all_gather x1, blocking collectives, body(): rows = lax.all_gather(vectors[0:1].astype(BF16), plane, axis=0, tiled=True)  45.2 us
    ppermute x4, starting transfers between devices, swap(): lax.ppermute(block, axis, [(i, i ^ bits) for i in range(lax.axis_size(axi...  22.4 us
    pallas_call x3, Pallas kernels, call(): pl.pallas_call(kernel, out_shape=outs, in_specs=[pl.BlockSpec(memory_spac...  22 us
    all_to_all x3, starting transfers between devices, exchange(): lax.all_to_all(blocks, axis, 0, 0, axis_index_groups=groups, tiled=True)  12 us
    ppermute x4, waiting for transfers between devices, swap(): lax.ppermute(block, axis, [(i, i ^ bits) for i in range(lax.axis_size(axi...  6.46 us
  transfers between devices with their start and end apart: 8, of which 5 were waited for; matrix products, arithmetic and copies ran while one was open for 4% of the time, Pallas kernels for 0%

profile of v2, /device:TPU:1, one launch (start us, length us, event | category | flops | bytes accessed | tf_op | source)
XLA Modules:
  0.0 264.2 jit_solution(8624961188102601582)
XLA Ops:
  7.2 0.0 copy-start
  7.2 0.0 all-gather.4.cloned.1.call-start
  7.2 1.6 dynamic-slice_bitcast_fusion
  8.9 0.0 all-gather.4.cloned.1.call-update
  8.9 68.1 %all-gather.4.cloned.1.call-done = bf16[512,2304]{1,0:T(8,128)(2,1)} async-done(((bf16[32,2304]{1,0:T(8,128)(2,1)}), bf16[512,2304]{1,0:T(8,128)(2,1)}) %all-gather.4.cloned.1.call-update) | async-done | bytes 2359312 | tf_op jit(solution)/shard_map/all_gather | solution.py:228
  77.0 3.6 %collective-permute-start = (bf16[16,32,2304]{2,1,0:T(8,128)(2,1)}, bf16[16,32,2304]{2,1,0:T(8,128)(2,1)}, u32[]{:S(2)}, u32[]{:S(2)}) collective-permute-start(bf16[16,32,2304]{2,1,0:T(8,128)(2,1)} %bitcast.30), channel_id=1, source_target_pairs={{0,16},{16,0},{32,48},{48,32},{64,80},{80,64},{96,112},{112,96},{1... | collective-permute-start | bytes 7077896 | tf_op jit(solution)/shard_map/ppermute | solution.py:20
  80.6 1.3 dynamic_slice.18
  81.9 0.7 constant_dynamic-slice_fusion
  82.6 0.7 add_bitcast_fusion
  83.3 0.6 broadcast_in_dim.17
  83.9 3.2 %all-to-all-start = ((s32[4,1,11]{2,1,0:T(1,128)}), s32[4,1,11]{2,1,0:T(1,128)S(1)}, u32[]{:S(2)}, u32[]{:S(2)}) async-start(s32[4,1,11]{2,1,0:T(1,128)} %broadcast_in_dim.17), calls=%async_computation | async-start | bytes 4096 | tf_op jit(solution)/shard_map/all_to_all | solution.py:24
  87.1 0.7 pad_add_fusion.where
  87.8 3.4 %all-to-all-done = s32[4,1,11]{2,1,0:T(1,128)S(1)} async-done(((s32[4,1,11]{2,1,0:T(1,128)}), s32[4,1,11]{2,1,0:T(1,128)S(1)}, u32[]{:S(2)}, u32[]{:S(2)}) %all-to-all-start) | async-done | bytes 208 | tf_op jit(solution)/shard_map/all_to_all | solution.py:24
  91.2 0.1 copy.18
  91.3 0.2 slice_reduce_fusion
  91.5 0.1 convert_reduce_fusion
  91.6 1.2 convolution_bitcast_fusion
  92.8 0.6 copy.19
  93.4 3.3 %all-to-all-start.1 = ((f32[4,1,1024]{2,1,0:T(1,128)}), f32[4,1,1024]{2,1,0:T(1,128)S(1)}, u32[]{:S(2)}, u32[]{:S(2)}) async-start(f32[4,1,1024]{2,1,0:T(1,128)} %copy.19), calls=%async_computation.1 | async-start | bytes 32768 | tf_op jit(solution)/shard_map/all_to_all | solution.py:24
  96.7 1.1 dynamic-slice_reduce_fusion
  97.8 0.7 dynamic-slice_reduce_fusion.1
  98.5 0.1 reshape.72
  98.6 0.1 reshape.73
  98.7 0.6 broadcast_in_dim.39.code_row
  99.3 0.8 broadcast_in_dim.43.code_col
  100.7 0.1 reshape.74
  100.9 0.7 pad.19.cotangent
  101.6 0.6 broadcast_in_dim.18.context
  102.2 16.9 %trunk.1 = (bf16[16,32,2304]{2,1,0:T(8,128)(2,1)}, bf16[16,32,2304]{2,1,0:T(8,128)(2,1)}, f32[8,4096]{1,0:T(8,128)}) custom-call(s32[3]{0:T(128)} %pad_add_fusion.where, bf16[16,1024]{1,0:T(8,128)(2,1)} %broadcast_in_dim.18.context, bf16[1024,1024]{1,0:T(8,128)(2,1)} %w_first.1, bf16[1024,256]{1,0:T(8,128)(2,1)} %w_second.1, bf16[3,256]{1,0:T(4,128)(2,1)} %embed.1, ...), custom_call_target="tpu_custom_call" | custom-call | flops 5435817984 | bytes 16777216 | tf_op jit(solution)/shard_map/trunk/pallas_call | solution.py:43
  119.1 3.8 %collective-permute-start.1 = (bf16[16,32,2304]{2,1,0:T(8,128)(2,1)}, bf16[16,32,2304]{2,1,0:T(8,128)(2,1)S(1)}, u32[]{:S(2)}, u32[]{:S(2)}) collective-permute-start(bf16[16,32,2304]{2,1,0:T(8,128)(2,1)} %get-tuple-element.12), channel_id=1, source_target_pairs={{0,16},{16,0},{32,48},{48,32},{64,80},{80,64},{96,112},{112,96},{1... | collective-permute-start | bytes 7077896 | tf_op jit(solution)/shard_map/ppermute | solution.py:20
  122.9 4.3 %collective-permute-done.1 = bf16[16,32,2304]{2,1,0:T(8,128)(2,1)S(1)} collective-permute-done((bf16[16,32,2304]{2,1,0:T(8,128)(2,1)}, bf16[16,32,2304]{2,1,0:T(8,128)(2,1)S(1)}, u32[]{:S(2)}, u32[]{:S(2)}) %collective-permute-start.1) | collective-permute-done | bytes 2359328 | tf_op jit(solution)/shard_map/ppermute | solution.py:20
  127.3 3.7 %add_convert_fusion = bf16[16,32,2304]{2,1,0:T(8,128)(2,1)} fusion(bf16[16,32,2304]{2,1,0:T(8,128)(2,1)S(1)} %collective-permute-done.1, bf16[16,32,2304]{2,1,0:T(8,128)(2,1)} %get-tuple-element.11), kind=kLoop, calls=%fused_computation | loop fusion | flops 4718592 | bytes 7077888 | tf_op jit(solution)/shard_map/convert_element_type | solution.py:271
  131.0 5.5 %all-to-all-start.2 = ((bf16[16,32,2304]{2,1,0:T(8,128)(2,1)}), bf16[16,32,2304]{2,1,0:T(8,128)(2,1)S(1)}, u32[]{:S(2)}, u32[]{:S(2)}) async-start(bf16[16,32,2304]{2,1,0:T(8,128)(2,1)} %add_convert_fusion), calls=%async_computation.2 | async-start | bytes 4718592 | tf_op jit(solution)/shard_map/all_to_all | solution.py:24
  136.5 0.9 fusion
  137.4 45.2 %all-gather.1 = bf16[16,1,4096]{2,1,0:T(2,128)(2,1)S(1)} all-gather(bf16[1,1,4096]{2,1,0:T(2,128)(2,1)S(1)} %fusion), channel_id=1, replica_groups=mesh['dp'=32,'section'=4,'shard'=4] {'section','shard'}, dimensions={0}, use_global_device_ids=true | all-gather | bytes 139264 | tf_op jit(solution)/shard_map/all_gather | solution.py:274
  182.6 0.1 copy.24
  182.8 0.0 copy-start.3
  182.8 7.4 %collective-permute-start.2 = (bf16[16,4096]{1,0:T(8,128)(2,1)S(1)}, bf16[16,4096]{1,0:T(8,128)(2,1)S(1)}, u32[]{:S(2)}, u32[]{:S(2)}) collective-permute-start(bf16[16,4096]{1,0:T(8,128)(2,1)S(1)} %bitcast.26), channel_id=1, source_target_pairs={{0,16},{16,0},{32,48},{48,32},{64,80},{80,64},{96,112},{112,96},{1... | collective-permute-start | bytes 393224 | tf_op jit(solution)/shard_map/ppermute | solution.py:20
  190.2 1.0 collective-permute-done.2.far
  191.1 0.6 copy-done.5
  191.8 1.4 copy-done.1
  193.2 3.2 %pack.1 = bf16[16,16,512]{2,1,0:T(8,128)(2,1)} custom-call(s32[3]{0:T(128)} %pad_add_fusion.where, bf16[16,32,2304]{2,1,0:T(8,128)(2,1)} %copy-done.1, bf16[16,4096]{1,0:T(8,128)(2,1)} %bitcast.27, bf16[16,4096]{1,0:T(8,128)(2,1)} %copy-done.5), custom_call_target="tpu_custom_call" | custom-call | flops 20971520 | bytes 3145728 | tf_op jit(solution)/shard_map/pack/pallas_call | solution.py:43
  196.4 26.0 %all_to_all.33 = bf16[16,16,512]{2,1,0:T(8,128)(2,1)S(1)} all-to-all(bf16[16,16,512]{2,1,0:T(8,128)(2,1)} %pack.1), channel_id=1, replica_groups={{0,32,64,96,128,160,192,224,256,288,320,352,384,416,448,480},{16,48,80,..., dimensions={0} | all-to-all | bytes 524288 | tf_op jit(solution)/shard_map/all_to_all | solution.py:24
  222.5 23.4 %all_to_all.34.mine = bf16[16,16,512]{2,1,0:T(8,128)(2,1)S(1)} all-to-all(bf16[16,16,512]{2,1,0:T(8,128)(2,1)S(1)} %broadcast_in_dim.41), channel_id=1, replica_groups={{0,32,64,96,128,160,192,224,256,288,320,352,384,416,448,480},{16,48,80,..., dimensions={0} | all-to-all | bytes 524288 | tf_op jit(solution)/shard_map/all_to_all | solution.py:24
  245.9 7.6 %collective-permute-start.3 = (bf16[16,16,512]{2,1,0:T(8,128)(2,1)S(1)}, bf16[16,16,512]{2,1,0:T(8,128)(2,1)S(1)}, u32[]{:S(2)}, u32[]{:S(2)}) collective-permute-start(bf16[16,16,512]{2,1,0:T(8,128)(2,1)S(1)} %all_to_all.34.mine), channel_id=1, source_target_pairs={{0,16},{16,0},{32,48},{48,32},{64,80},{80,64},{96,112},{112,96},{1... | collective-permute-start | bytes 786440 | tf_op jit(solution)/shard_map/ppermute | solution.py:20
  253.6 1.1 collective-permute-done.3.theirs
  254.7 0.7 copy-done.4
  255.4 1.9 finish.1
  (20 shorter events, 0.2 us)
Async XLA Ops:
  7.2 89.5 %copy-start = (bf16[4,361,256]{2,0,1:T(4,128)(2,1)S(1)}, bf16[4,361,256]{2,0,1:T(4,128)(2,1)}, u32[]{:S(2)}) copy-start(bf16[4,361,256]{2,0,1:T(4,128)(2,1)} %param.17) | copy-start | bytes 2217988
  7.2 69.8 %all-gather.4.cloned.1.call-start = ((), (), s32[]{:S(2)}) async-start(), calls=%async_computation.5 | async-start | bytes 2506752 | tf_op jit(solution)/shard_map/all_gather | solution.py:228
  77.0 24.6 %collective-permute-start = (bf16[16,32,2304]{2,1,0:T(8,128)(2,1)}, bf16[16,32,2304]{2,1,0:T(8,128)(2,1)}, u32[]{:S(2)}, u32[]{:S(2)}) collective-permute-start(bf16[16,32,2304]{2,1,0:T(8,128)(2,1)} %bitcast.30), channel_id=1, source_target_pairs={{0,16},{16,0},{32,48},{48,32},{64,80},{80,64},{96,112},{112,96},{1... | collective-permute-start | bytes 7077896 | tf_op jit(solution)/shard_map/ppermute | solution.py:20
  83.9 7.3 %all-to-all-start = ((s32[4,1,11]{2,1,0:T(1,128)}), s32[4,1,11]{2,1,0:T(1,128)S(1)}, u32[]{:S(2)}, u32[]{:S(2)}) async-start(s32[4,1,11]{2,1,0:T(1,128)} %broadcast_in_dim.17), calls=%async_computation | async-start | bytes 4096 | tf_op jit(solution)/shard_map/all_to_all | solution.py:24
  93.4 8.1 %all-to-all-start.1 = ((f32[4,1,1024]{2,1,0:T(1,128)}), f32[4,1,1024]{2,1,0:T(1,128)S(1)}, u32[]{:S(2)}, u32[]{:S(2)}) async-start(f32[4,1,1024]{2,1,0:T(1,128)} %copy.19), calls=%async_computation.1 | async-start | bytes 32768 | tf_op jit(solution)/shard_map/all_to_all | solution.py:24
  119.1 8.2 %collective-permute-start.1 = (bf16[16,32,2304]{2,1,0:T(8,128)(2,1)}, bf16[16,32,2304]{2,1,0:T(8,128)(2,1)S(1)}, u32[]{:S(2)}, u32[]{:S(2)}) collective-permute-start(bf16[16,32,2304]{2,1,0:T(8,128)(2,1)} %get-tuple-element.12), channel_id=1, source_target_pairs={{0,16},{16,0},{32,48},{48,32},{64,80},{80,64},{96,112},{112,96},{1... | collective-permute-start | bytes 7077896 | tf_op jit(solution)/shard_map/ppermute | solution.py:20
  131.0 60.1 %all-to-all-start.2 = ((bf16[16,32,2304]{2,1,0:T(8,128)(2,1)}), bf16[16,32,2304]{2,1,0:T(8,128)(2,1)S(1)}, u32[]{:S(2)}, u32[]{:S(2)}) async-start(bf16[16,32,2304]{2,1,0:T(8,128)(2,1)} %add_convert_fusion), calls=%async_computation.2 | async-start | bytes 4718592 | tf_op jit(solution)/shard_map/all_to_all | solution.py:24
  182.8 8.4 %copy-start.3 = (bf16[16,1,4096]{2,0,1:T(8,128)(2,1)}, bf16[16,1,4096]{2,0,1:T(8,128)(2,1)S(1)}, u32[]{:S(2)}) copy-start(bf16[16,1,4096]{2,0,1:T(8,128)(2,1)S(1)} %copy.24) | copy-start | bytes 393220
  182.8 8.3 %collective-permute-start.2 = (bf16[16,4096]{1,0:T(8,128)(2,1)S(1)}, bf16[16,4096]{1,0:T(8,128)(2,1)S(1)}, u32[]{:S(2)}, u32[]{:S(2)}) collective-permute-start(bf16[16,4096]{1,0:T(8,128)(2,1)S(1)} %bitcast.26), channel_id=1, source_target_pairs={{0,16},{16,0},{32,48},{48,32},{64,80},{80,64},{96,112},{112,96},{1... | collective-permute-start | bytes 393224 | tf_op jit(solution)/shard_map/ppermute | solution.py:20
  191.1 0.6 copy-start.5
  191.8 1.4 copy-start.1
  245.9 8.8 %copy-start.2 = (bf16[16,16,512]{2,1,0:T(8,128)(2,1)}, bf16[16,16,512]{2,1,0:T(8,128)(2,1)S(1)}, u32[]{:S(2)}) copy-start(bf16[16,16,512]{2,1,0:T(8,128)(2,1)S(1)} %all_to_all.34.mine) | copy-start | bytes 786436
  245.9 8.8 %collective-permute-start.3 = (bf16[16,16,512]{2,1,0:T(8,128)(2,1)S(1)}, bf16[16,16,512]{2,1,0:T(8,128)(2,1)S(1)}, u32[]{:S(2)}, u32[]{:S(2)}) collective-permute-start(bf16[16,16,512]{2,1,0:T(8,128)(2,1)S(1)} %all_to_all.34.mine), channel_id=1, source_target_pairs={{0,16},{16,0},{32,48},{48,32},{64,80},{80,64},{96,112},{112,96},{1... | collective-permute-start | bytes 786440 | tf_op jit(solution)/shard_map/ppermute | solution.py:20
  254.7 0.7 copy-start.4
Sparse Core Ops, SparseCore 0:
  11.6 65.3 all-gather.3

commit v3 on v2

--- a/solution.py
+++ b/solution.py
@@ -20,8 +20,8 @@
     return lax.ppermute(block, axis, [(i, i ^ bits) for i in range(lax.axis_size(axis))])
 
 
-def exchange(blocks, axis, groups=None):
-    return lax.all_to_all(blocks, axis, 0, 0, axis_index_groups=groups, tiled=True)
+def exchange(blocks, axis):
+    return lax.all_to_all(blocks, axis, 0, 0, tiled=True)
 
 
 def nn(left, right):
@@ -56,8 +56,8 @@
 
 def trunk_kernel(
     where, context, w_first, w_second, embed, code_col, code_row, cotangent, mine, theirs,
-    own, other, vectors,
-    wt, patches, gt, normed, rscales, buf, grad,
+    own, other,
+    wt, patches, gt, normed, rscales, buf, grad, vectors,
 ):
     c = where[2]
 
@@ -131,87 +131,102 @@
     rounded = sums.astype(BF16)
     density = jnp.exp(-0.5 * preact * preact) * 0.3989422804014327
     pre_grad = (nt(rounded, w_second[...]) * (cdf + preact * density)).astype(BF16)
-    vectors[...] = jnp.zeros(vectors.shape, F32)
-    vectors[0:1, 0:1024] = context[...].astype(F32)[0:1]
-    vectors[0:1, 1024:2048] = hidden.astype(F32)[0:1]
-    vectors[0:1, 2048:3072] = pre_grad.astype(F32)[3:4]
-    for place, row in enumerate((3, 0, 1, 2)):
-        first = 3072 + place * channels
-        vectors[0:1, first : first + channels] = rounded.astype(F32)[row : row + 1]
-
+    parts = ((context[...], 0, 8), (hidden, 0, 8), (pre_grad, 3, 8))
+    parts += tuple((rounded, row, 2) for row in (3, 0, 1, 2))
+    place = 0
+    for array, row, count in parts:
+        for piece in range(count):
+            vectors[place : place + 1, :] = array.astype(F32)[
+                row : row + 1, piece * 128 : (piece + 1) * 128
+            ]
+            place += 1
+    tail = vectors[...].astype(BF16)
+    taps = gt.shape[2]
     for core, pieces in ((c, own), (1 - c, other)):
         for place in range(16):
-            pieces[place] = gt[place // 4, rows_of(place % 4, core), :]
-
-
-def chunk_rows(piece):
-    row = (piece % 4) // 2 * 16
-    return slice(row, row + 16)
-
-
-def chunk_lanes(piece):
-    lane = piece % 2 * 512
-    return slice(lane, lane + 512)
-
-
-def pack_kernel(where, pieces, near, far, out, whole, product):
+            pieces[place, :, 0:taps] = gt[place // 4, rows_of(place % 4, core), :]
+            pieces[place, :, taps:] = tail
+
+
+def merge_kernel(own, come, out):
+    taps = own.shape[2] - 128
+    out[:, :, 0:taps] = (own[:, :, 0:taps].astype(F32) + come[:, :, 0:taps].astype(F32)).astype(BF16)
+    out[:, :, taps : taps + 128] = own[:, :, taps:]
+    out[:, :, taps + 128 :] = come[:, :, taps:]
+
+
+def merge(own, come):
+    count, rows, width = own.shape
+    spec = pl.BlockSpec((2, rows, width), lambda i: (i, 0, 0))
+    return pl.pallas_call(
+        merge_kernel,
+        grid=(count // 2,),
+        in_specs=[spec, spec],
+        out_specs=pl.BlockSpec((2, rows, width + 128), lambda i: (i, 0, 0)),
+        out_shape=jax.ShapeDtypeStruct((count, rows, width + 128), BF16),
+        compiler_params=pltpu.CompilerParams(vmem_limit_bytes=VMEM_BYTES),
+        cost_estimate=pl.CostEstimate(
+            flops=own.size, bytes_accessed=6 * own.size, transcendentals=0
+        ),
+        name="merge",
+    )(own, come)
+
+
+def pack_kernel(where, pieces, out, vectors, product, stones):
     first = where[0] * 256 + where[1] * 64 + where[2] * 32
-    lanes = pl.multiple_of((first // 128) * 128, 128)
-    rows = pl.ds(pl.multiple_of(first - lanes, 32), 32)
-    whole[:, :, 896:1024] = jnp.zeros((4, 32, 128), F32)
-
-    def spread(place, block):
-        width = block.shape[1]
-        done = 0
-        while done < width:
-            group, inside = divmod(place + done, 896)
-            take = min(width - done, 896 - inside)
-            whole[group, :, inside : inside + take] = block[:, done : done + take]
-            done += take
-
-    conv = pieces[0].astype(F32)
-    for piece in range(1, 16):
-        conv += pieces[piece].astype(F32)
-    spread(0, conv)
-    product[:, 0:1024] = tn(near[:, pl.ds(lanes, 128)], near[:, 2048:3072]) + tn(
-        far[:, pl.ds(lanes, 128)], far[:, 2048:3072]
-    )
-    lanes2 = pl.multiple_of(lanes + 1024, 128)
-    product[:, 1024:1280] = tn(near[:, pl.ds(lanes2, 128)], near[:, 3072:3328]) + tn(
-        far[:, pl.ds(lanes2, 128)], far[:, 3072:3328]
-    )
-    spread(2304, product[rows, :])
-    stones = jnp.sum(
-        near[:, 3328:4096].astype(F32) + far[:, 3328:4096].astype(F32), axis=0, keepdims=True
-    )
+    row = first // 128
+    rows = pl.ds(pl.multiple_of(first - row * 128, 32), 32)
+    taps = pieces.shape[2] - 256
+    for piece in range(16):
+        for core in (0, 1):
+            state = piece * 2 + core
+            lane = taps + core * 128
+            vectors[state * 32 : (state + 1) * 32, :] = pieces[piece, :, lane : lane + 128].astype(F32)
+
+    def of_states(place):
+        return vectors[pl.ds(place, 32, stride=32), :]
+
+    context = of_states(row).astype(BF16)
+    hidden = of_states(row + 8).astype(BF16)
+    for piece in range(8):
+        lanes = slice(piece * 128, (piece + 1) * 128)
+        product[:, lanes] = tn(context, of_states(16 + piece).astype(BF16))
+    for piece in range(2):
+        lanes = slice(1024 + piece * 128, 1024 + (piece + 1) * 128)
+        product[:, lanes] = tn(hidden, of_states(24 + piece).astype(BF16))
+    stones[...] = jnp.zeros(stones.shape, F32)
     for piece in range(6):
-        row = piece // 4
-        whole[piece % 4, row : row + 1, 896:1024] = stones[:, piece * 128 : (piece + 1) * 128]
-    for piece in range(16):
-        out[piece] = whole[piece // 4, chunk_rows(piece), chunk_lanes(piece)].astype(BF16)
-
-
-def finish_kernel(where, mine, theirs, conv, first, second, stones, whole, rows3):
-    c = where[2]
-    for core, pieces in ((c, mine), (1 - c, theirs)):
-        for piece in range(16):
-            rows = pl.ds(pl.multiple_of(core * 32 + chunk_rows(piece).start, 16), 16)
-            whole[piece // 4, rows, chunk_lanes(piece)] = pieces[piece].astype(F32) * (1.0 / 512.0)
-    for group in range(4):
-        for out, start, width in ((conv, 0, 2304), (first, 2304, 1024), (second, 3328, 256)):
-            begin = max(start, group * 896)
-            end = min(start + width, (group + 1) * 896)
-            if begin < end:
-                out[:, begin - start : end - start] = whole[
-                    group, :, begin - group * 896 : end - group * 896
-                ].astype(BF16)
-    for piece in range(6):
-        row = piece // 4
         v, half = divmod(piece, 2)
-        rows3[v : v + 1, half * 128 : (half + 1) * 128] = whole[
-            piece % 4, row : row + 1, 896:1024
-        ]
-    stones[...] = rows3[0:3, :].astype(BF16)
+        stones[v : v + 1, half * 128 : (half + 1) * 128] = jnp.sum(
+            of_states(26 + piece), axis=0, keepdims=True
+        )
+    for column in range(taps // 256):
+        lanes = slice(column * 256, (column + 1) * 256)
+        block = pieces[0, :, lanes].astype(F32)
+        for piece in range(1, 16):
+            block += pieces[piece, :, lanes].astype(F32)
+        out[2 * column] = block[0:16].astype(BF16)
+        out[2 * column + 1] = block[16:32].astype(BF16)
+    for column in range(5):
+        block = product[rows, column * 256 : (column + 1) * 256]
+        place = 2 * (taps // 256 + column)
+        out[place] = block[0:16].astype(BF16)
+        out[place + 1] = block[16:32].astype(BF16)
+    out[28] = stones[...].astype(BF16)
+    for place in (29, 30, 31):
+        out[place] = jnp.zeros(out.shape[1:], BF16)
+
+
+def finish_kernel(where, pieces, conv, first, second, stones):
+    for out, start in ((conv, 0), (first, conv.shape[1]), (second, conv.shape[1] + first.shape[1])):
+        for column in range(out.shape[1] // 256):
+            for half in range(2):
+                for core in range(2):
+                    row = core * 32 + half * 16
+                    out[row : row + 16, column * 256 : (column + 1) * 256] = (
+                        pieces[2 * (start // 256 + column) + half, core].astype(F32) * (1.0 / 512.0)
+                    ).astype(BF16)
+    stones[...] = (pieces[28, 0].astype(F32) * (1.0 / 512.0))[0:3].astype(BF16)
 
 
 def body(boards, neighbours, counts, database, w_first, w_second, embed, conv_weight, cotangent):
@@ -225,7 +240,7 @@
     plane = ("section", "shard")
 
     unit = lax.dynamic_slice_in_dim(conv_weight[0].T, c * 32, 32, 0)[None]
-    mine = lax.all_gather(unit, plane, axis=0, tiled=True)
+    mine = exchange(jnp.broadcast_to(unit, (16,) + unit.shape[1:]), plane)
     theirs = swap(mine, "dp", 1)
 
     ids = lax.dynamic_slice_in_dim(neighbours, s, 1, 0)
@@ -250,10 +265,10 @@
     upper = jnp.pad(upper.reshape(BOARD, BOARD, channels), ((0, 0), (0, 1), (0, 0)))
     upper = jnp.pad(upper.reshape(-1, channels), ((0, ROWS - BOARD * PITCH), (0, 0)))
 
-    part = jax.ShapeDtypeStruct((16, 32, taps), BF16)
-    own, other, vectors = vmem_call(
+    part = jax.ShapeDtypeStruct((16, 32, taps + 128), BF16)
+    own, other = vmem_call(
         trunk_kernel,
-        (part, part, jax.ShapeDtypeStruct((8, 4096), F32)),
+        (part, part),
         [
             pltpu.VMEM((4, channels, taps), BF16),
             pltpu.VMEM((4, ROWS, taps), BF16),
@@ -262,28 +277,30 @@
             pltpu.VMEM((4, ROWS, 1), F32),
             pltpu.VMEM((2 * FRONT + ROWS, channels), F32),
             pltpu.VMEM((ROWS, channels), F32),
+            pltpu.VMEM((32, 128), F32),
         ],
         "trunk",
         12 * 2 * ROWS * taps * channels,
         16 << 20,
     )(where, context, w_first, w_second, embed, code[:, None], code[None, :], upper, mine, theirs)
 
-    pieces = (own.astype(F32) + swap(other, "dp", 1).astype(F32)).astype(BF16)
-    pieces = exchange(pieces, plane)
-
-    rows = lax.all_gather(vectors[0:1].astype(BF16), plane, axis=0, tiled=True)
+    pieces = exchange(merge(own, swap(other, "dp", 1)), plane)
     (chunks,) = vmem_call(
         pack_kernel,
-        (jax.ShapeDtypeStruct((16, 16, 512), BF16),),
-        [pltpu.VMEM((4, 32, 1024), F32), pltpu.VMEM((128, 1280), F32)],
+        (jax.ShapeDtypeStruct((32, 16, 256), BF16),),
+        [
+            pltpu.VMEM((1024, 128), F32),
+            pltpu.VMEM((128, 1280), F32),
+            pltpu.VMEM((16, 256), F32),
+        ],
         "pack",
         4 * 32 * 128 * 1280,
         3 << 20,
-    )(where, pieces, rows, swap(rows, "dp", 1))
-
-    line = [[2 * i + core for i in range(lax.axis_size("dp") // 2)] for core in (0, 1)]
-    total = jnp.sum(exchange(chunks, "dp", line).astype(F32), axis=0, keepdims=True).astype(BF16)
-    mine = exchange(jnp.broadcast_to(total, chunks.shape), "dp", line)
+    )(where, pieces)
+
+    total = exchange(chunks, "dp").astype(F32).reshape(-1, 2, 16, 256)
+    total = jnp.sum(total, axis=0, keepdims=True).astype(BF16)
+    chunks = exchange(jnp.broadcast_to(total, (lax.axis_size("dp"),) + total.shape[1:]), "dp")
     conv, w1_grad, w2_grad, embed_grad = vmem_call(
         finish_kernel,
         (
@@ -292,11 +309,11 @@
             jax.ShapeDtypeStruct((64, channels), BF16),
             jax.ShapeDtypeStruct((3, channels), BF16),
         ),
-        [pltpu.VMEM((4, 64, 1024), F32), pltpu.VMEM((8, channels), F32)],
+        [],
         "finish",
         1 << 18,
         1 << 20,
-    )(where, mine, swap(mine, "dp", 1))
+    )(where, chunks)
     return (w1_grad, w2_grad, embed_grad, conv.T[None])
 
 

time: 265 us -> 219 us (0.83)
  waiting for transfers between devices: 77.9 us -> 7.85 us
  blocking collectives: 94.7 us -> 151 us
  starting transfers between devices: 34.4 us -> 14.7 us
  between operations: 14.9 us -> 1.47 us
  Pallas kernels: 22 us -> 28.3 us
  other arithmetic: 5.28 us -> 1.57 us
    all_to_all x2 -> x4, blocking collectives: 49.5 us -> 151 us  [exchange(): return lax.all_to_all(blocks, axis, 0, 0, tiled=True)]
    all_gather x1 -> x0, waiting for transfers between devices: 68.1 us -> none  [body(): mine = lax.all_gather(unit, plane, axis=0, tiled=True)]
    all_gather x1 -> x0, blocking collectives: 45.2 us -> none  [body(): rows = lax.all_gather(vectors[0:1].astype(BF16), plane, axis=0, tiled=True)]
    ppermute x4 -> x2, starting transfers between devices: 22.4 us -> 8.23 us  [swap(): lax.ppermute(block, axis, [(i, i ^ bits) for i in range(lax.axis_size(axi...]
    pallas_call x0 -> x1, Pallas kernels: none -> 6.49 us  [merge(): pl.pallas_call(merge_kernel, grid=(count // 2,), in_specs=[spec, spec], o...]
    all_to_all x3 -> x2, starting transfers between devices: 12 us -> 6.48 us  [exchange(): return lax.all_to_all(blocks, axis, 0, 0, tiled=True)]
    convert_element_type x1 -> x0, other arithmetic: 3.72 us -> none  [body(): pieces = (own.astype(F32) + swap(other, 'dp', 1).astype(F32)).astype(BF16)]
    ppermute x4 -> x2, waiting for transfers between devices: 6.46 us -> 4.54 us  [swap(): lax.ppermute(block, axis, [(i, i ^ bits) for i in range(lax.axis_size(axi...]
  transfers between devices with their start and end apart: 8 -> 4, of which waited for: 5 -> 2; matrix products, arithmetic and copies ran while one was open for 4% -> 5% of each run, Pallas kernels for 0% -> 0%
where the time goes in v3:
time: 219 us; the launch traced here: 218 us
  blocking collectives  151 us (69%)
  Pallas kernels  28.3 us (13%)
  starting transfers between devices  14.7 us (7%)
  local copies, waits for them, and re-layouts  12 us (5%)
  waiting for transfers between devices  7.85 us (4%)
    all_to_all x4, blocking collectives, exchange(): return lax.all_to_all(blocks, axis, 0, 0, tiled=True)  151 us
    pallas_call x3, Pallas kernels, call(): pl.pallas_call(kernel, out_shape=outs, in_specs=[pl.BlockSpec(memory_spac...  21.8 us
    ppermute x2, starting transfers between devices, swap(): lax.ppermute(block, axis, [(i, i ^ bits) for i in range(lax.axis_size(axi...  8.23 us
    pallas_call x1, Pallas kernels, merge(): pl.pallas_call(merge_kernel, grid=(count // 2,), in_specs=[spec, spec], o...  6.49 us
    all_to_all x2, starting transfers between devices, exchange(): return lax.all_to_all(blocks, axis, 0, 0, tiled=True)  6.48 us
    ppermute x2, waiting for transfers between devices, swap(): lax.ppermute(block, axis, [(i, i ^ bits) for i in range(lax.axis_size(axi...  4.54 us
  transfers between devices with their start and end apart: 4, of which 2 were waited for; matrix products, arithmetic and copies ran while one was open for 5% of the time, Pallas kernels for 0%

profile of v3, /device:TPU:1, one launch (start us, length us, event | category | flops | bytes accessed | tf_op | source)
XLA Modules:
  0.0 218.5 jit_solution(4715778824581822729)
XLA Ops:
  0.6 0.0 copy-start
  0.7 1.0 dynamic-slice_bitcast_fusion
  1.7 0.2 broadcast_in_dim.21
  1.9 0.0 copy-start.3
  1.9 37.0 %all_to_all.38.mine = bf16[16,32,2304]{2,1,0:T(8,128)(2,1)S(1)} all-to-all(bf16[16,32,2304]{2,1,0:T(8,128)(2,1)S(1)} %broadcast_in_dim.21), channel_id=1, replica_groups=mesh['dp'=32,'section'=4,'shard'=4] {'section','shard'}, dimensions={0} | all-to-all | bytes 4718592 | tf_op jit(solution)/shard_map/all_to_all | solution.py:24
  38.9 0.0 copy-start.2
  38.9 5.2 %collective-permute-start = (bf16[16,32,2304]{2,1,0:T(8,128)(2,1)S(1)}, bf16[16,32,2304]{2,1,0:T(8,128)(2,1)}, u32[]{:S(2)}, u32[]{:S(2)}) collective-permute-start(bf16[16,32,2304]{2,1,0:T(8,128)(2,1)S(1)} %all_to_all.38.mine), channel_id=1, source_target_pairs={{0,16},{16,0},{32,48},{48,32},{64,80},{80,64},{96,112},{112,96},{1... | collective-permute-start | bytes 7077896 | tf_op jit(solution)/shard_map/ppermute | solution.py:20
  44.1 0.0 copy-done.3
  44.1 0.7 dynamic_slice.18
  44.8 0.7 constant_dynamic-slice_fusion
  45.5 0.7 add_bitcast_fusion
  46.2 0.6 broadcast_in_dim.17
  46.8 3.2 %all-to-all-start = ((s32[4,1,11]{2,1,0:T(1,128)}), s32[4,1,11]{2,1,0:T(1,128)S(1)}, u32[]{:S(2)}, u32[]{:S(2)}) async-start(s32[4,1,11]{2,1,0:T(1,128)} %broadcast_in_dim.17), calls=%async_computation | async-start | bytes 4096 | tf_op jit(solution)/shard_map/all_to_all | solution.py:24
  50.0 0.7 pad_add_fusion.where
  50.7 3.3 %all-to-all-done = s32[4,1,11]{2,1,0:T(1,128)S(1)} async-done(((s32[4,1,11]{2,1,0:T(1,128)}), s32[4,1,11]{2,1,0:T(1,128)S(1)}, u32[]{:S(2)}, u32[]{:S(2)}) %all-to-all-start) | async-done | bytes 208 | tf_op jit(solution)/shard_map/all_to_all | solution.py:24
  54.0 0.1 copy.16
  54.1 0.2 slice_reduce_fusion
  54.3 0.1 convert_reduce_fusion
  54.4 1.2 convolution_bitcast_fusion
  55.6 0.6 copy.17
  56.2 3.3 %all-to-all-start.1 = ((f32[4,1,1024]{2,1,0:T(1,128)}), f32[4,1,1024]{2,1,0:T(1,128)S(1)}, u32[]{:S(2)}, u32[]{:S(2)}) async-start(f32[4,1,1024]{2,1,0:T(1,128)} %copy.17), calls=%async_computation.1 | async-start | bytes 32768 | tf_op jit(solution)/shard_map/all_to_all | solution.py:24
  59.5 0.0 copy-done
  59.5 1.1 dynamic-slice_reduce_fusion
  60.6 0.7 dynamic-slice_reduce_fusion.1
  61.3 0.1 reshape.79
  61.4 0.1 reshape.80
  61.5 0.6 broadcast_in_dim.20.code_row
  62.1 0.8 broadcast_in_dim.46.code_col
  63.5 0.1 reshape.81
  63.6 0.7 pad.18
  64.3 1.0 reshape.82
  65.3 0.7 pad.19.cotangent
  66.0 0.0 all-to-all-done.1
  66.0 0.0 collective-permute-done.theirs
  66.1 0.6 broadcast_in_dim.18.context
  66.7 0.0 copy-done.2
  66.7 16.9 %trunk.1 = (bf16[16,32,2432]{2,1,0:T(8,128)(2,1)}, bf16[16,32,2432]{2,1,0:T(8,128)(2,1)}) custom-call(s32[3]{0:T(128)} %pad_add_fusion.where, bf16[16,1024]{1,0:T(8,128)(2,1)} %broadcast_in_dim.18.context, bf16[1024,1024]{1,0:T(8,128)(2,1)} %w_first.1, bf16[1024,256]{1,0:T(8,128)(2,1)} %w_second.1, bf16[3,256]{1,0:T(4,128)(2,1)} %embed.1, ...), custom_call_target="tpu_custom_call" | custom-call | flops 5435817984 | bytes 16777216 | tf_op jit(solution)/shard_map/trunk/pallas_call | solution.py:43
  83.6 3.0 %collective-permute-start.1 = (bf16[16,32,2432]{2,1,0:T(8,128)(2,1)}, bf16[16,32,2432]{2,1,0:T(8,128)(2,1)S(1)}, u32[]{:S(2)}, u32[]{:S(2)}) collective-permute-start(bf16[16,32,2432]{2,1,0:T(8,128)(2,1)} %get-tuple-element.11), channel_id=1, source_target_pairs={{0,16},{16,0},{32,48},{48,32},{64,80},{80,64},{96,112},{112,96},{1... | collective-permute-start | bytes 7471112 | tf_op jit(solution)/shard_map/ppermute | solution.py:20
  86.7 4.5 %collective-permute-done.1.come = bf16[16,32,2432]{2,1,0:T(8,128)(2,1)S(1)} collective-permute-done((bf16[16,32,2432]{2,1,0:T(8,128)(2,1)}, bf16[16,32,2432]{2,1,0:T(8,128)(2,1)S(1)}, u32[]{:S(2)}, u32[]{:S(2)}) %collective-permute-start.1) | collective-permute-done | bytes 2490400 | tf_op jit(solution)/shard_map/ppermute | solution.py:20
  91.2 0.0 copy-start.1
  91.2 1.5 copy-done.1
  92.7 6.5 %merge.1 = bf16[16,32,2560]{2,1,0:T(8,128)(2,1)} custom-call(bf16[16,32,2432]{2,1,0:T(8,128)(2,1)} %get-tuple-element.10.own, bf16[16,32,2432]{2,1,0:T(8,128)(2,1)} %copy-done.1), custom_call_target="tpu_custom_call" | custom-call | flops 1245184 | bytes 7471104 | tf_op jit(solution)/shard_map/merge/pallas_call | solution.py:161
  99.2 38.3 %all_to_all.39.pieces = bf16[16,32,2560]{2,1,0:T(8,128)(2,1)} all-to-all(bf16[16,32,2560]{2,1,0:T(8,128)(2,1)} %merge.1), channel_id=1, replica_groups=mesh['dp'=32,'section'=4,'shard'=4] {'section','shard'}, dimensions={0} | all-to-all | bytes 5242880 | tf_op jit(solution)/shard_map/all_to_all | solution.py:24
  137.5 3.0 %pack.1 = bf16[32,16,256]{2,1,0:T(8,128)(2,1)} custom-call(s32[3]{0:T(128)} %pad_add_fusion.where, bf16[16,32,2560]{2,1,0:T(8,128)(2,1)} %all_to_all.39.pieces), custom_call_target="tpu_custom_call" | custom-call | flops 20971520 | bytes 3145728 | tf_op jit(solution)/shard_map/pack/pallas_call | solution.py:43
  140.5 38.1 %all_to_all.40 = bf16[32,16,256]{2,1,0:T(8,128)(2,1)S(1)} all-to-all(bf16[32,16,256]{2,1,0:T(8,128)(2,1)} %pack.1), channel_id=1, replica_groups=mesh['dp'=32,'section'=4,'shard'=4] {'dp'}, dimensions={0} | all-to-all | bytes 524288 | tf_op jit(solution)/shard_map/all_to_all | solution.py:24
  178.7 0.1 broadcast_in_dim.44
  178.7 37.9 %all_to_all.41.pieces = bf16[32,2,16,256]{3,2,1,0:T(8,128)(2,1)} all-to-all(bf16[32,2,16,256]{3,2,1,0:T(8,128)(2,1)S(1)} %broadcast_in_dim.44), channel_id=1, replica_groups=mesh['dp'=32,'section'=4,'shard'=4] {'dp'}, dimensions={0} | all-to-all | bytes 1048576 | tf_op jit(solution)/shard_map/all_to_all | solution.py:24
  216.6 1.8 finish.1
  (7 shorter events, 0.1 us)
Async XLA Ops:
  0.6 58.9 %copy-start = (bf16[4,361,256]{2,0,1:T(4,128)(2,1)S(1)}, bf16[4,361,256]{2,0,1:T(4,128)(2,1)}, u32[]{:S(2)}) copy-start(bf16[4,361,256]{2,0,1:T(4,128)(2,1)} %param.17) | copy-start | bytes 2217988
  1.9 42.2 %copy-start.3 = (s32[4]{0:T(128)S(1)}, s32[4]{0:T(128)}, u32[]{:S(2)}) copy-start(s32[4]{0:T(128)} %param.11) | copy-start | bytes 52
  38.9 27.7 %copy-start.2 = (bf16[16,32,2304]{2,1,0:T(8,128)(2,1)}, bf16[16,32,2304]{2,1,0:T(8,128)(2,1)S(1)}, u32[]{:S(2)}) copy-start(bf16[16,32,2304]{2,1,0:T(8,128)(2,1)S(1)} %all_to_all.38.mine) | copy-start | bytes 7077892
  38.9 27.1 %collective-permute-start = (bf16[16,32,2304]{2,1,0:T(8,128)(2,1)S(1)}, bf16[16,32,2304]{2,1,0:T(8,128)(2,1)}, u32[]{:S(2)}, u32[]{:S(2)}) collective-permute-start(bf16[16,32,2304]{2,1,0:T(8,128)(2,1)S(1)} %all_to_all.38.mine), channel_id=1, source_target_pairs={{0,16},{16,0},{32,48},{48,32},{64,80},{80,64},{96,112},{112,96},{1... | collective-permute-start | bytes 7077896 | tf_op jit(solution)/shard_map/ppermute | solution.py:20
  46.8 7.2 %all-to-all-start = ((s32[4,1,11]{2,1,0:T(1,128)}), s32[4,1,11]{2,1,0:T(1,128)S(1)}, u32[]{:S(2)}, u32[]{:S(2)}) async-start(s32[4,1,11]{2,1,0:T(1,128)} %broadcast_in_dim.17), calls=%async_computation | async-start | bytes 4096 | tf_op jit(solution)/shard_map/all_to_all | solution.py:24
  56.2 9.8 %all-to-all-start.1 = ((f32[4,1,1024]{2,1,0:T(1,128)}), f32[4,1,1024]{2,1,0:T(1,128)S(1)}, u32[]{:S(2)}, u32[]{:S(2)}) async-start(f32[4,1,1024]{2,1,0:T(1,128)} %copy.17), calls=%async_computation.1 | async-start | bytes 32768 | tf_op jit(solution)/shard_map/all_to_all | solution.py:24
  83.6 7.6 %collective-permute-start.1 = (bf16[16,32,2432]{2,1,0:T(8,128)(2,1)}, bf16[16,32,2432]{2,1,0:T(8,128)(2,1)S(1)}, u32[]{:S(2)}, u32[]{:S(2)}) collective-permute-start(bf16[16,32,2432]{2,1,0:T(8,128)(2,1)} %get-tuple-element.11), channel_id=1, source_target_pairs={{0,16},{16,0},{32,48},{48,32},{64,80},{80,64},{96,112},{112,96},{1... | collective-permute-start | bytes 7471112 | tf_op jit(solution)/shard_map/ppermute | solution.py:20
  91.2 1.5 copy-start.1

commit v4 on v3

--- a/solution.py
+++ b/solution.py
@@ -11,13 +11,18 @@
 FRONT = 24
 NORM_EPS = 1e-05
 TAP_SHIFTS = [(a - 1) * PITCH + (b - 1) for a in range(3) for b in range(3)]
-VMEM_BYTES = 58 * 1024 * 1024
+VMEM_BYTES = 40 * 1024 * 1024
 F32 = jnp.float32
 BF16 = jnp.bfloat16
 
 
 def swap(block, axis, bits):
     return lax.ppermute(block, axis, [(i, i ^ bits) for i in range(lax.axis_size(axis))])
+
+
+def turned(block, axis, distance):
+    size = lax.axis_size(axis)
+    return lax.ppermute(block, axis, [(i, (i + distance) % size) for i in range(size)])
 
 
 def exchange(blocks, axis):
@@ -56,7 +61,7 @@
 
 def trunk_kernel(
     where, context, w_first, w_second, embed, code_col, code_row, cotangent, mine, theirs,
-    own, other,
+    own, other, tail,
     wt, patches, gt, normed, rscales, buf, grad, vectors,
 ):
     c = where[2]
@@ -140,48 +145,20 @@
                 row : row + 1, piece * 128 : (piece + 1) * 128
             ]
             place += 1
-    tail = vectors[...].astype(BF16)
-    taps = gt.shape[2]
+    tail[...] = vectors[...].astype(BF16)
     for core, pieces in ((c, own), (1 - c, other)):
         for place in range(16):
-            pieces[place, :, 0:taps] = gt[place // 4, rows_of(place % 4, core), :]
-            pieces[place, :, taps:] = tail
-
-
-def merge_kernel(own, come, out):
-    taps = own.shape[2] - 128
-    out[:, :, 0:taps] = (own[:, :, 0:taps].astype(F32) + come[:, :, 0:taps].astype(F32)).astype(BF16)
-    out[:, :, taps : taps + 128] = own[:, :, taps:]
-    out[:, :, taps + 128 :] = come[:, :, taps:]
-
-
-def merge(own, come):
-    count, rows, width = own.shape
-    spec = pl.BlockSpec((2, rows, width), lambda i: (i, 0, 0))
-    return pl.pallas_call(
-        merge_kernel,
-        grid=(count // 2,),
-        in_specs=[spec, spec],
-        out_specs=pl.BlockSpec((2, rows, width + 128), lambda i: (i, 0, 0)),
-        out_shape=jax.ShapeDtypeStruct((count, rows, width + 128), BF16),
-        compiler_params=pltpu.CompilerParams(vmem_limit_bytes=VMEM_BYTES),
-        cost_estimate=pl.CostEstimate(
-            flops=own.size, bytes_accessed=6 * own.size, transcendentals=0
-        ),
-        name="merge",
-    )(own, come)
-
-
-def pack_kernel(where, pieces, out, vectors, product, stones):
+            pieces[place] = gt[place // 4, rows_of(place % 4, core), :]
+
+
+def pack_kernel(where, pieces, near, far, out, vectors, product, stones):
     first = where[0] * 256 + where[1] * 64 + where[2] * 32
     row = first // 128
     rows = pl.ds(pl.multiple_of(first - row * 128, 32), 32)
-    taps = pieces.shape[2] - 256
+    taps = pieces.shape[2]
     for piece in range(16):
-        for core in (0, 1):
-            state = piece * 2 + core
-            lane = taps + core * 128
-            vectors[state * 32 : (state + 1) * 32, :] = pieces[piece, :, lane : lane + 128].astype(F32)
+        vectors[piece * 32 : (piece + 1) * 32, :] = near[piece].astype(F32)
+        vectors[(16 + piece) * 32 : (17 + piece) * 32, :] = far[piece].astype(F32)
 
     def of_states(place):
         return vectors[pl.ds(place, 32, stride=32), :]
@@ -217,16 +194,17 @@
         out[place] = jnp.zeros(out.shape[1:], BF16)
 
 
-def finish_kernel(where, pieces, conv, first, second, stones):
+def finish_kernel(where, mine, theirs, conv, first, second, stones):
+    c = where[2]
     for out, start in ((conv, 0), (first, conv.shape[1]), (second, conv.shape[1] + first.shape[1])):
         for column in range(out.shape[1] // 256):
             for half in range(2):
-                for core in range(2):
-                    row = core * 32 + half * 16
-                    out[row : row + 16, column * 256 : (column + 1) * 256] = (
-                        pieces[2 * (start // 256 + column) + half, core].astype(F32) * (1.0 / 512.0)
+                for core, pieces in ((c, mine), (1 - c, theirs)):
+                    rows = pl.ds(pl.multiple_of(core * 32 + half * 16, 16), 16)
+                    out[rows, column * 256 : (column + 1) * 256] = (
+                        pieces[2 * (start // 256 + column) + half].astype(F32) * (1.0 / 512.0)
                     ).astype(BF16)
-    stones[...] = (pieces[28, 0].astype(F32) * (1.0 / 512.0))[0:3].astype(BF16)
+    stones[...] = (mine[28].astype(F32) * (1.0 / 512.0))[0:3].astype(BF16)
 
 
 def body(boards, neighbours, counts, database, w_first, w_second, embed, conv_weight, cotangent):
@@ -246,7 +224,7 @@
     ids = lax.dynamic_slice_in_dim(neighbours, s, 1, 0)
     count = lax.dynamic_slice_in_dim(counts, s, 1, 0)
     asked = jnp.concatenate([ids, count[:, None]], axis=1)
-    asked = exchange(jnp.broadcast_to(asked, (4, asked.shape[1])), "shard")
+    asked = jnp.concatenate([asked] + [turned(asked, "shard", d) for d in (1, 2, 3)])
     slots = ids.shape[1]
     live = lax.broadcasted_iota(jnp.int32, (4, slots), 1) < asked[:, slots:]
     stored = database.shape[0]
@@ -254,7 +232,9 @@
     hits = (asked[:, :slots, None] == positions) & live[:, :, None]
     picks = jnp.sum(hits.astype(F32), axis=1).astype(BF16)
     partial = jnp.dot(picks, database, preferred_element_type=F32)
-    summed = jnp.sum(exchange(partial, "shard"), axis=0, keepdims=True)
+    summed = partial[0:1]
+    for d in (1, 2, 3):
+        summed = summed + turned(partial[d : d + 1], "shard", -d)
     context = (summed / jnp.maximum(count, 1).astype(F32)[:, None]).astype(BF16)
     context = jnp.broadcast_to(context, (16, context.shape[1]))
 
@@ -265,10 +245,10 @@
     upper = jnp.pad(upper.reshape(BOARD, BOARD, channels), ((0, 0), (0, 1), (0, 0)))
     upper = jnp.pad(upper.reshape(-1, channels), ((0, ROWS - BOARD * PITCH), (0, 0)))
 
-    part = jax.ShapeDtypeStruct((16, 32, taps + 128), BF16)
-    own, other = vmem_call(
+    part = jax.ShapeDtypeStruct((16, 32, taps), BF16)
+    own, other, rows = vmem_call(
         trunk_kernel,
-        (part, part),
+        (part, part, jax.ShapeDtypeStruct((32, 128), BF16)),
         [
             pltpu.VMEM((4, channels, taps), BF16),
             pltpu.VMEM((4, ROWS, taps), BF16),
@@ -284,7 +264,11 @@
         16 << 20,
     )(where, context, w_first, w_second, embed, code[:, None], code[None, :], upper, mine, theirs)
 
-    pieces = exchange(merge(own, swap(other, "dp", 1)), plane)
+    pieces = exchange((own.astype(F32) + swap(other, "dp", 1).astype(F32)).astype(BF16), plane)
+
+    rows = rows[None]
+    for axis, bits in (("shard", 1), ("shard", 3), ("section", 1), ("section", 3)):
+        rows = jnp.concatenate([rows, swap(rows, axis, bits)])
     (chunks,) = vmem_call(
         pack_kernel,
         (jax.ShapeDtypeStruct((32, 16, 256), BF16),),
@@ -296,11 +280,23 @@
         "pack",
         4 * 32 * 128 * 1280,
         3 << 20,
-    )(where, pieces)
-
-    total = exchange(chunks, "dp").astype(F32).reshape(-1, 2, 16, 256)
-    total = jnp.sum(total, axis=0, keepdims=True).astype(BF16)
-    chunks = exchange(jnp.broadcast_to(total, (lax.axis_size("dp"),) + total.shape[1:]), "dp")
+    )(where, pieces, rows, swap(rows, "dp", 1))
+
+    def along_z(blocks, groups, step):
+        return lax.all_to_all(
+            blocks.reshape((4, step) + blocks.shape[-2:]), "dp", 0, 0,
+            axis_index_groups=groups, tiled=True,
+        )
+
+    fours = range(lax.axis_size("dp") // 8)
+    low = [[8 * i + 2 * j + core for j in range(4)] for i in fours for core in (0, 1)]
+    high = [[8 * i + 2 * j + core for i in fours] for j in range(4) for core in (0, 1)]
+    chunks = jnp.sum(along_z(chunks, low, 8).astype(F32), axis=0).astype(BF16)
+    chunks = jnp.sum(along_z(chunks, high, 2).astype(F32), axis=0).astype(BF16)
+    chunks = along_z(jnp.broadcast_to(chunks, (4,) + chunks.shape), high, 2)
+    chunks = chunks.reshape((8,) + chunks.shape[-2:])
+    chunks = along_z(jnp.broadcast_to(chunks, (4,) + chunks.shape), low, 8)
+    chunks = chunks.reshape((32,) + chunks.shape[-2:])
     conv, w1_grad, w2_grad, embed_grad = vmem_call(
         finish_kernel,
         (
@@ -313,7 +309,7 @@
         "finish",
         1 << 18,
         1 << 20,
-    )(where, chunks)
+    )(where, chunks, swap(chunks, "dp", 1))
     return (w1_grad, w2_grad, embed_grad, conv.T[None])
 
 

time: 219 us -> 236 us (1.078)
  blocking collectives: 151 us -> 95.9 us
  waiting for transfers between devices: 7.85 us -> 50.3 us
  starting transfers between devices: 14.7 us -> 53.7 us
  Pallas kernels: 28.3 us -> 15.6 us
  other arithmetic: 1.57 us -> 4.65 us
    all_to_all x4 -> x1, blocking collectives: 151 us -> 37 us  [exchange(): return lax.all_to_all(blocks, axis, 0, 0, tiled=True)]
    all_to_all x0 -> x4, blocking collectives: none -> 58.8 us  [along_z(): lax.all_to_all(blocks.reshape((4, step) + blocks.shape[-2:]), 'dp', 0, 0,...]
    ppermute x2 -> x8, waiting for transfers between devices: 4.54 us -> 46.9 us  [swap(): lax.ppermute(block, axis, [(i, i ^ bits) for i in range(lax.axis_size(axi...]
    ppermute x2 -> x8, starting transfers between devices: 8.23 us -> 34.2 us  [swap(): lax.ppermute(block, axis, [(i, i ^ bits) for i in range(lax.axis_size(axi...]
    ppermute x0 -> x6, starting transfers between devices: none -> 15.3 us  [turned(): lax.ppermute(block, axis, [(i, (i + distance) % size) for i in range(size)])]
    pallas_call x1 -> x0, Pallas kernels: 6.49 us -> none  [merge(): pl.pallas_call(merge_kernel, grid=(count // 2,), in_specs=[spec, spec], o...]
    pallas_call x3, Pallas kernels: 21.8 us -> 15.6 us  [call(): pl.pallas_call(kernel, out_shape=outs, in_specs=[pl.BlockSpec(memory_spac...]
    ppermute x0 -> x6, waiting for transfers between devices: none -> 3.49 us  [turned(): lax.ppermute(block, axis, [(i, (i + distance) % size) for i in range(size)])]
  transfers between devices with their start and end apart: 4 -> 15, of which waited for: 2 -> 9; matrix products, arithmetic and copies ran while one was open for 5% -> 5% of each run, Pallas kernels for 0% -> 0%
where the time goes in v4:
time: 236 us; the launch traced here: 235 us
  blocking collectives  95.9 us (41%)
  starting transfers between devices  53.7 us (23%)
  waiting for transfers between devices  50.3 us (21%)
  Pallas kernels  15.6 us (7%)
  local copies, waits for them, and re-layouts  12.2 us (5%)
  other arithmetic  4.65 us (2%)
    all_to_all x4, blocking collectives, along_z(): lax.all_to_all(blocks.reshape((4, step) + blocks.shape[-2:]), 'dp', 0, 0,...  58.8 us
    ppermute x8, waiting for transfers between devices, swap(): lax.ppermute(block, axis, [(i, i ^ bits) for i in range(lax.axis_size(axi...  46.9 us
    all_to_all x1, blocking collectives, exchange(): return lax.all_to_all(blocks, axis, 0, 0, tiled=True)  37 us
    ppermute x8, starting transfers between devices, swap(): lax.ppermute(block, axis, [(i, i ^ bits) for i in range(lax.axis_size(axi...  34.2 us
    pallas_call x3, Pallas kernels, call(): pl.pallas_call(kernel, out_shape=outs, in_specs=[pl.BlockSpec(memory_spac...  15.6 us
    ppermute x6, starting transfers between devices, turned(): lax.ppermute(block, axis, [(i, (i + distance) % size) for i in range(size)])  15.3 us
  transfers between devices with their start and end apart: 15, of which 9 were waited for; matrix products, arithmetic and copies ran while one was open for 5% of the time, Pallas kernels for 0%

profile of v4, /device:TPU:1, one launch (start us, length us, event | category | flops | bytes accessed | tf_op | source)
XLA Modules:
  0.0 235.4 jit_solution(8022140894155819163)
XLA Ops:
  0.7 1.0 dynamic-slice_bitcast_fusion
  1.9 37.0 %all_to_all.30.mine = bf16[16,32,2304]{2,1,0:T(8,128)(2,1)S(1)} all-to-all(bf16[16,32,2304]{2,1,0:T(8,128)(2,1)S(1)} %broadcast_in_dim.42), channel_id=1, replica_groups=mesh['dp'=32,'section'=4,'shard'=4] {'section','shard'}, dimensions={0} | all-to-all | bytes 4718592 | tf_op jit(solution)/shard_map/all_to_all | solution.py:29
  38.9 5.3 %collective-permute-start.6 = (bf16[16,32,2304]{2,1,0:T(8,128)(2,1)S(1)}, bf16[16,32,2304]{2,1,0:T(8,128)(2,1)}, u32[]{:S(2)}, u32[]{:S(2)}) collective-permute-start(bf16[16,32,2304]{2,1,0:T(8,128)(2,1)S(1)} %all_to_all.30.mine), channel_id=1, source_target_pairs={{0,16},{16,0},{32,48},{48,32},{64,80},{80,64},{96,112},{112,96},{1... | collective-permute-start | bytes 7077896 | tf_op jit(solution)/shard_map/ppermute | solution.py:20
  44.3 0.7 dynamic_slice.18
  44.9 0.7 constant_dynamic-slice_fusion
  45.6 0.8 pad_add_fusion.2
  46.4 2.0 collective-permute-start.2
  48.4 3.7 %collective-permute-start.1 = (s32[1,11]{1,0:T(1,128)S(1)}, s32[1,11]{1,0:T(1,128)S(1)}, u32[]{:S(2)}, u32[]{:S(2)}) collective-permute-start(s32[1,11]{1,0:T(1,128)S(1)} %pad_add_fusion.2), channel_id=1, source_target_pairs={{0,2},{1,3},{2,0},{3,1},{4,6},{5,7},{6,4},{7,5},{8,10},{9,11},{10,... | collective-permute-start | bytes 140 | tf_op jit(solution)/shard_map/ppermute | solution.py:25
  52.0 1.9 collective-permute-start
  54.2 3.4 %collective-permute-done = s32[1,11]{1,0:T(1,128)S(1)} collective-permute-done((s32[1,11]{1,0:T(1,128)S(1)}, s32[1,11]{1,0:T(1,128)S(1)}, u32[]{:S(2)}, u32[]{:S(2)}) %collective-permute-start) | collective-permute-done | bytes 76 | tf_op jit(solution)/shard_map/ppermute | solution.py:25
  57.5 0.8 pad_add_fusion
  58.7 1.2 fusion.5
  59.9 0.6 copy-done.4
  60.5 0.6 fusion.4
  61.1 2.7 %collective-permute-start.3 = (f32[1,1024]{1,0:T(1,128)}, f32[1,1024]{1,0:T(1,128)S(1)}, u32[]{:S(2)}, u32[]{:S(2)}) collective-permute-start(f32[1,1024]{1,0:T(1,128)} %get-tuple-element.18), channel_id=1, source_target_pairs={{0,3},{1,0},{2,1},{3,2},{4,7},{5,4},{6,5},{7,6},{8,11},{9,8},{10,9... | collective-permute-start | bytes 12296 | tf_op jit(solution)/shard_map/ppermute | solution.py:25
  63.9 2.6 %collective-permute-start.5 = (f32[1,1024]{1,0:T(1,128)}, f32[1,1024]{1,0:T(1,128)}, u32[]{:S(2)}, u32[]{:S(2)}) collective-permute-start(f32[1,1024]{1,0:T(1,128)} %get-tuple-element.19), channel_id=1, source_target_pairs={{0,1},{1,2},{2,3},{3,0},{4,5},{5,6},{6,7},{7,4},{8,9},{9,10},{10,1... | collective-permute-start | bytes 12296 | tf_op jit(solution)/shard_map/ppermute | solution.py:25
  66.4 2.4 %collective-permute-start.4 = (f32[1,1024]{1,0:T(1,128)}, f32[1,1024]{1,0:T(1,128)}, u32[]{:S(2)}, u32[]{:S(2)}) collective-permute-start(f32[1,1024]{1,0:T(1,128)} %get-tuple-element.20), channel_id=1, source_target_pairs={{0,2},{1,3},{2,0},{3,1},{4,6},{5,7},{6,4},{7,5},{8,10},{9,11},{10,... | collective-permute-start | bytes 12296 | tf_op jit(solution)/shard_map/ppermute | solution.py:25
  68.9 1.7 dynamic-slice_reduce_fusion
  70.6 0.7 dynamic-slice_reduce_fusion.1
  72.4 1.0 reshape.69
  73.4 0.7 pad.18
  74.1 1.0 reshape.70
  75.1 0.8 convert_reduce_fusion.1
  75.9 1.6 copy-done.1
  77.5 1.0 copy-done.2
  78.6 13.1 %trunk.1 = (bf16[16,32,2304]{2,1,0:T(8,128)(2,1)S(1)}, bf16[16,32,2304]{2,1,0:T(8,128)(2,1)S(1)}, bf16[32,128]{1,0:T(8,128)(2,1)S(1)}) custom-call(s32[3]{0:T(128)S(1)} %pad_add_fusion.1.where, bf16[16,1024]{1,0:T(8,128)(2,1)S(1)} %broadcast_in_dim.39.context, bf16[1024,1024]{1,0:T(8,128)(2,1)S(1)} %copy-done.1, bf16[1024,256]{1,0:T(8,128)(2,1)S(1)} %copy-done.2, ...), custom_call_target="tpu_custom_call" | custom-call | flops 5435817984 | bytes 16777216 | tf_op jit(solution)/shard_map/trunk/pallas_call | solution.py:48
  91.7 4.2 %collective-permute-start.7 = (bf16[16,32,2304]{2,1,0:T(8,128)(2,1)S(1)}, bf16[16,32,2304]{2,1,0:T(8,128)(2,1)S(1)}, u32[]{:S(2)}, u32[]{:S(2)}) collective-permute-start(bf16[16,32,2304]{2,1,0:T(8,128)(2,1)S(1)} %get-tuple-element.12), channel_id=1, source_target_pairs={{0,16},{16,0},{32,48},{48,32},{64,80},{80,64},{96,112},{112,96},{1... | collective-permute-start | bytes 7077896 | tf_op jit(solution)/shard_map/ppermute | solution.py:20
  95.9 4.1 %collective-permute-done.7 = bf16[16,32,2304]{2,1,0:T(8,128)(2,1)S(1)} collective-permute-done((bf16[16,32,2304]{2,1,0:T(8,128)(2,1)S(1)}, bf16[16,32,2304]{2,1,0:T(8,128)(2,1)S(1)}, u32[]{:S(2)}, u32[]{:S(2)}) %collective-permute-start.7) | collective-permute-done | bytes 2359328 | tf_op jit(solution)/shard_map/ppermute | solution.py:20
  100.0 2.1 add_convert_fusion
  102.1 4.2 %all-to-all-start.1 = ((bf16[16,32,2304]{2,1,0:T(8,128)(2,1)}), bf16[16,32,2304]{2,1,0:T(8,128)(2,1)S(1)}, u32[]{:S(2)}, u32[]{:S(2)}) async-start(bf16[16,32,2304]{2,1,0:T(8,128)(2,1)} %add_convert_fusion), calls=%async_computation.1 | async-start | bytes 4718592 | tf_op jit(solution)/shard_map/all_to_all | solution.py:29
  106.4 3.6 %collective-permute-start.8 = (bf16[1,32,128]{2,1,0:T(8,128)(2,1)S(1)}, bf16[1,32,128]{2,1,0:T(8,128)(2,1)S(1)}, u32[]{:S(2)}, u32[]{:S(2)}) collective-permute-start(bf16[1,32,128]{2,1,0:T(8,128)(2,1)S(1)} %bitcast.24), channel_id=1, source_target_pairs={{0,1},{1,0},{2,3},{3,2},{4,5},{5,4},{6,7},{7,6},{8,9},{9,8},{10,11... | collective-permute-start | bytes 24584 | tf_op jit(solution)/shard_map/ppermute | solution.py:20
  110.0 30.8 %collective-permute-done.8 = bf16[1,32,128]{2,1,0:T(8,128)(2,1)S(1)} collective-permute-done((bf16[1,32,128]{2,1,0:T(8,128)(2,1)S(1)}, bf16[1,32,128]{2,1,0:T(8,128)(2,1)S(1)}, u32[]{:S(2)}, u32[]{:S(2)}) %collective-permute-start.8) | collective-permute-done | bytes 8224 | tf_op jit(solution)/shard_map/ppermute | solution.py:20
  140.8 2.3 collective-permute-start.9
  143.2 3.3 %collective-permute-done.9 = bf16[2,32,128]{2,1,0:T(8,128)(2,1)S(1)} collective-permute-done((bf16[2,32,128]{2,1,0:T(8,128)(2,1)S(1)}, bf16[2,32,128]{2,1,0:T(8,128)(2,1)S(1)}, u32[]{:S(2)}, u32[]{:S(2)}) %collective-permute-start.9) | collective-permute-done | bytes 16416 | tf_op jit(solution)/shard_map/ppermute | solution.py:20
  146.5 1.9 collective-permute-start.10
  148.4 2.7 %collective-permute-done.10 = bf16[4,32,128]{2,1,0:T(8,128)(2,1)S(1)} collective-permute-done((bf16[4,32,128]{2,1,0:T(8,128)(2,1)S(1)}, bf16[4,32,128]{2,1,0:T(8,128)(2,1)S(1)}, u32[]{:S(2)}, u32[]{:S(2)}) %collective-permute-start.10) | collective-permute-done | bytes 32800 | tf_op jit(solution)/shard_map/ppermute | solution.py:20
  151.2 2.4 %collective-permute-start.11 = (bf16[8,32,128]{2,1,0:T(8,128)(2,1)S(1)}, bf16[8,32,128]{2,1,0:T(8,128)(2,1)S(1)}, u32[]{:S(2)}, u32[]{:S(2)}) collective-permute-start(bf16[8,32,128]{2,1,0:T(8,128)(2,1)S(1)} %pad_maximum_fusion), channel_id=1, source_target_pairs={{0,12},{4,8},{8,4},{12,0},{1,13},{5,9},{9,5},{13,1},{2,14},{6,10},... | collective-permute-start | bytes 196616 | tf_op jit(solution)/shard_map/ppermute | solution.py:20
  153.6 3.8 %collective-permute-done.11 = bf16[8,32,128]{2,1,0:T(8,128)(2,1)S(1)} collective-permute-done((bf16[8,32,128]{2,1,0:T(8,128)(2,1)S(1)}, bf16[8,32,128]{2,1,0:T(8,128)(2,1)S(1)}, u32[]{:S(2)}, u32[]{:S(2)}) %collective-permute-start.11) | collective-permute-done | bytes 65568 | tf_op jit(solution)/shard_map/ppermute | solution.py:20
  157.4 6.9 %collective-permute-start.12 = (bf16[16,32,128]{2,1,0:T(8,128)(2,1)S(1)}, bf16[16,32,128]{2,1,0:T(8,128)(2,1)S(1)}, u32[]{:S(2)}, u32[]{:S(2)}) collective-permute-start(bf16[16,32,128]{2,1,0:T(8,128)(2,1)S(1)} %constant_dynamic-update-slice_fusion.near), channel_id=1, source_target_pairs={{0,16},{16,0},{32,48},{48,32},{64,80},{80,64},{96,112},{112,96},{1... | collective-permute-start | bytes 393224 | tf_op jit(solution)/shard_map/ppermute | solution.py:20
  164.3 1.0 collective-permute-done.12.far
  165.3 1.1 pack.1
  166.4 11.2 %all_to_all.31 = bf16[4,8,16,256]{3,2,1,0:T(8,128)(2,1)S(1)} all-to-all(bf16[4,8,16,256]{3,2,1,0:T(8,128)(2,1)S(1)} %bitcast.21), channel_id=1, replica_groups={{0,32,64,96},{16,48,80,112},{128,160,192,224},{144,176,208,240},{256,28..., dimensions={0} | all-to-all | bytes 524288 | tf_op jit(solution)/shard_map/all_to_all | solution.py:286
  177.7 23.9 %all_to_all.32 = bf16[4,2,16,256]{3,2,1,0:T(8,128)(2,1)S(1)} all-to-all(bf16[4,2,16,256]{3,2,1,0:T(8,128)(2,1)S(1)} %bitcast.28), channel_id=1, replica_groups={{0,128,256,384},{16,144,272,400},{32,160,288,416},{48,176,304,432},{64,..., dimensions={0} | all-to-all | bytes 131072 | tf_op jit(solution)/shard_map/all_to_all | solution.py:286
  201.7 14.4 %all_to_all.33 = bf16[4,2,16,256]{3,2,1,0:T(8,128)(2,1)S(1)} all-to-all(bf16[4,2,16,256]{3,2,1,0:T(8,128)(2,1)S(1)} %broadcast_in_dim.44), channel_id=1, replica_groups={{0,128,256,384},{16,144,272,400},{32,160,288,416},{48,176,304,432},{64,..., dimensions={0} | all-to-all | bytes 131072 | tf_op jit(solution)/shard_map/all_to_all | solution.py:286
  216.1 9.3 %all_to_all.34 = bf16[4,8,16,256]{3,2,1,0:T(8,128)(2,1)S(1)} all-to-all(bf16[4,8,16,256]{3,2,1,0:T(8,128)(2,1)S(1)} %broadcast_in_dim.45), channel_id=1, replica_groups={{0,32,64,96},{16,48,80,112},{128,160,192,224},{144,176,208,240},{256,28..., dimensions={0} | all-to-all | bytes 524288 | tf_op jit(solution)/shard_map/all_to_all | solution.py:286
  225.4 7.5 %collective-permute-start.13 = (bf16[32,16,256]{2,1,0:T(8,128)(2,1)S(1)}, bf16[32,16,256]{2,1,0:T(8,128)(2,1)S(1)}, u32[]{:S(2)}, u32[]{:S(2)}) collective-permute-start(bf16[32,16,256]{2,1,0:T(8,128)(2,1)S(1)} %bitcast.22), channel_id=1, source_target_pairs={{0,16},{16,0},{32,48},{48,32},{64,80},{80,64},{96,112},{112,96},{1... | collective-permute-start | bytes 786440 | tf_op jit(solution)/shard_map/ppermute | solution.py:20
  232.9 1.1 collective-permute-done.13.theirs
  234.0 1.4 finish.1
  (43 shorter events, 1.3 us)
Async XLA Ops:
  0.6 68.3 %copy-start = (bf16[4,361,256]{2,0,1:T(4,128)(2,1)S(1)}, bf16[4,361,256]{2,0,1:T(4,128)(2,1)}, u32[]{:S(2)}) copy-start(bf16[4,361,256]{2,0,1:T(4,128)(2,1)} %param.17) | copy-start | bytes 2217988
  1.9 42.4 %copy-start.5 = (s32[4]{0:T(128)S(1)}, s32[4]{0:T(128)}, u32[]{:S(2)}) copy-start(s32[4]{0:T(128)} %param.11) | copy-start | bytes 52
  38.9 37.0 %copy-start.3 = (bf16[3,256]{1,0:T(4,128)(2,1)S(1)}, bf16[3,256]{1,0:T(4,128)(2,1)}, u32[]{:S(2)}) copy-start(bf16[3,256]{1,0:T(4,128)(2,1)} %embed.1) | copy-start | bytes 4612
  38.9 37.0 %collective-permute-start.6 = (bf16[16,32,2304]{2,1,0:T(8,128)(2,1)S(1)}, bf16[16,32,2304]{2,1,0:T(8,128)(2,1)}, u32[]{:S(2)}, u32[]{:S(2)}) collective-permute-start(bf16[16,32,2304]{2,1,0:T(8,128)(2,1)S(1)} %all_to_all.30.mine), channel_id=1, source_target_pairs={{0,16},{16,0},{32,48},{48,32},{64,80},{80,64},{96,112},{112,96},{1... | collective-permute-start | bytes 7077896 | tf_op jit(solution)/shard_map/ppermute | solution.py:20
  46.4 7.7 %collective-permute-start.2 = (s32[1,11]{1,0:T(1,128)S(1)}, s32[1,11]{1,0:T(1,128)S(1)}, u32[]{:S(2)}, u32[]{:S(2)}) collective-permute-start(s32[1,11]{1,0:T(1,128)S(1)} %pad_add_fusion.2), channel_id=1, source_target_pairs={{0,3},{1,0},{2,1},{3,2},{4,7},{5,4},{6,5},{7,6},{8,11},{9,8},{10,9... | collective-permute-start | bytes 140 | tf_op jit(solution)/shard_map/ppermute | solution.py:25
  48.4 5.8 %collective-permute-start.1 = (s32[1,11]{1,0:T(1,128)S(1)}, s32[1,11]{1,0:T(1,128)S(1)}, u32[]{:S(2)}, u32[]{:S(2)}) collective-permute-start(s32[1,11]{1,0:T(1,128)S(1)} %pad_add_fusion.2), channel_id=1, source_target_pairs={{0,2},{1,3},{2,0},{3,1},{4,6},{5,7},{6,4},{7,5},{8,10},{9,11},{10,... | collective-permute-start | bytes 140 | tf_op jit(solution)/shard_map/ppermute | solution.py:25
  52.0 5.5 %collective-permute-start = (s32[1,11]{1,0:T(1,128)S(1)}, s32[1,11]{1,0:T(1,128)S(1)}, u32[]{:S(2)}, u32[]{:S(2)}) collective-permute-start(s32[1,11]{1,0:T(1,128)S(1)} %pad_add_fusion.2), channel_id=1, source_target_pairs={{0,1},{1,2},{2,3},{3,0},{4,5},{5,6},{6,7},{7,4},{8,9},{9,10},{10,1... | collective-permute-start | bytes 140 | tf_op jit(solution)/shard_map/ppermute | solution.py:25
  59.9 0.6 copy-start.4
  61.1 14.0 %collective-permute-start.3 = (f32[1,1024]{1,0:T(1,128)}, f32[1,1024]{1,0:T(1,128)S(1)}, u32[]{:S(2)}, u32[]{:S(2)}) collective-permute-start(f32[1,1024]{1,0:T(1,128)} %get-tuple-element.18), channel_id=1, source_target_pairs={{0,3},{1,0},{2,1},{3,2},{4,7},{5,4},{6,5},{7,6},{8,11},{9,8},{10,9... | collective-permute-start | bytes 12296 | tf_op jit(solution)/shard_map/ppermute | solution.py:25
  63.9 11.3 %collective-permute-start.5 = (f32[1,1024]{1,0:T(1,128)}, f32[1,1024]{1,0:T(1,128)}, u32[]{:S(2)}, u32[]{:S(2)}) collective-permute-start(f32[1,1024]{1,0:T(1,128)} %get-tuple-element.19), channel_id=1, source_target_pairs={{0,1},{1,2},{2,3},{3,0},{4,5},{5,6},{6,7},{7,4},{8,9},{9,10},{10,1... | collective-permute-start | bytes 12296 | tf_op jit(solution)/shard_map/ppermute | solution.py:25
  66.4 8.7 %collective-permute-start.4 = (f32[1,1024]{1,0:T(1,128)}, f32[1,1024]{1,0:T(1,128)}, u32[]{:S(2)}, u32[]{:S(2)}) collective-permute-start(f32[1,1024]{1,0:T(1,128)} %get-tuple-element.20), channel_id=1, source_target_pairs={{0,2},{1,3},{2,0},{3,1},{4,6},{5,7},{6,4},{7,5},{8,10},{9,11},{10,... | collective-permute-start | bytes 12296 | tf_op jit(solution)/shard_map/ppermute | solution.py:25
  75.9 1.6 copy-start.1
  77.5 1.0 copy-start.2
  91.7 8.3 %collective-permute-start.7 = (bf16[16,32,2304]{2,1,0:T(8,128)(2,1)S(1)}, bf16[16,32,2304]{2,1,0:T(8,128)(2,1)S(1)}, u32[]{:S(2)}, u32[]{:S(2)}) collective-permute-start(bf16[16,32,2304]{2,1,0:T(8,128)(2,1)S(1)} %get-tuple-element.12), channel_id=1, source_target_pairs={{0,16},{16,0},{32,48},{48,32},{64,80},{80,64},{96,112},{112,96},{1... | collective-permute-start | bytes 7077896 | tf_op jit(solution)/shard_map/ppermute | solution.py:20
  102.1 63.1 %all-to-all-start.1 = ((bf16[16,32,2304]{2,1,0:T(8,128)(2,1)}), bf16[16,32,2304]{2,1,0:T(8,128)(2,1)S(1)}, u32[]{:S(2)}, u32[]{:S(2)}) async-start(bf16[16,32,2304]{2,1,0:T(8,128)(2,1)} %add_convert_fusion), calls=%async_computation.1 | async-start | bytes 4718592 | tf_op jit(solution)/shard_map/all_to_all | solution.py:29
  106.4 34.4 %collective-permute-start.8 = (bf16[1,32,128]{2,1,0:T(8,128)(2,1)S(1)}, bf16[1,32,128]{2,1,0:T(8,128)(2,1)S(1)}, u32[]{:S(2)}, u32[]{:S(2)}) collective-permute-start(bf16[1,32,128]{2,1,0:T(8,128)(2,1)S(1)} %bitcast.24), channel_id=1, source_target_pairs={{0,1},{1,0},{2,3},{3,2},{4,5},{5,4},{6,7},{7,6},{8,9},{9,8},{10,11... | collective-permute-start | bytes 24584 | tf_op jit(solution)/shard_map/ppermute | solution.py:20
  140.8 5.7 %collective-permute-start.9 = (bf16[2,32,128]{2,1,0:T(8,128)(2,1)S(1)}, bf16[2,32,128]{2,1,0:T(8,128)(2,1)S(1)}, u32[]{:S(2)}, u32[]{:S(2)}) collective-permute-start(bf16[2,32,128]{2,1,0:T(8,128)(2,1)S(1)} %pad_maximum_fusion.2), channel_id=1, source_target_pairs={{0,3},{1,2},{2,1},{3,0},{4,7},{5,6},{6,5},{7,4},{8,11},{9,10},{10,... | collective-permute-start | bytes 49160 | tf_op jit(solution)/shard_map/ppermute | solution.py:20
  146.5 4.6 %collective-permute-start.10 = (bf16[4,32,128]{2,1,0:T(8,128)(2,1)S(1)}, bf16[4,32,128]{2,1,0:T(8,128)(2,1)S(1)}, u32[]{:S(2)}, u32[]{:S(2)}) collective-permute-start(bf16[4,32,128]{2,1,0:T(8,128)(2,1)S(1)} %pad_maximum_fusion.1), channel_id=1, source_target_pairs={{0,4},{4,0},{8,12},{12,8},{1,5},{5,1},{9,13},{13,9},{2,6},{6,2},{1... | collective-permute-start | bytes 98312 | tf_op jit(solution)/shard_map/ppermute | solution.py:20
  151.2 6.2 %collective-permute-start.11 = (bf16[8,32,128]{2,1,0:T(8,128)(2,1)S(1)}, bf16[8,32,128]{2,1,0:T(8,128)(2,1)S(1)}, u32[]{:S(2)}, u32[]{:S(2)}) collective-permute-start(bf16[8,32,128]{2,1,0:T(8,128)(2,1)S(1)} %pad_maximum_fusion), channel_id=1, source_target_pairs={{0,12},{4,8},{8,4},{12,0},{1,13},{5,9},{9,5},{13,1},{2,14},{6,10},... | collective-permute-start | bytes 196616 | tf_op jit(solution)/shard_map/ppermute | solution.py:20
  157.4 7.9 %collective-permute-start.12 = (bf16[16,32,128]{2,1,0:T(8,128)(2,1)S(1)}, bf16[16,32,128]{2,1,0:T(8,128)(2,1)S(1)}, u32[]{:S(2)}, u32[]{:S(2)}) collective-permute-start(bf16[16,32,128]{2,1,0:T(8,128)(2,1)S(1)} %constant_dynamic-update-slice_fusion.near), channel_id=1, source_target_pairs={{0,16},{16,0},{32,48},{48,32},{64,80},{80,64},{96,112},{112,96},{1... | collective-permute-start | bytes 393224 | tf_op jit(solution)/shard_map/ppermute | solution.py:20
  225.4 8.7 %collective-permute-start.13 = (bf16[32,16,256]{2,1,0:T(8,128)(2,1)S(1)}, bf16[32,16,256]{2,1,0:T(8,128)(2,1)S(1)}, u32[]{:S(2)}, u32[]{:S(2)}) collective-permute-start(bf16[32,16,256]{2,1,0:T(8,128)(2,1)S(1)} %bitcast.22), channel_id=1, source_target_pairs={{0,16},{16,0},{32,48},{48,32},{64,80},{80,64},{96,112},{112,96},{1... | collective-permute-start | bytes 786440 | tf_op jit(solution)/shard_map/ppermute | solution.py:20

commit v5 on v4

--- a/solution.py
+++ b/solution.py
@@ -59,9 +59,18 @@
     return call
 
 
+def encoder_kernel(where, context, w_first, w_second, preact, hidden, encoded):
+    value = nn(context[...], w_first[...])
+    preact[...] = value
+    rounded = (value * (0.5 * (1.0 + lax.erf(value * 0.7071067811865476)))).astype(BF16)
+    hidden[...] = rounded
+    encoded[...] = nn(rounded, w_second[...])
+
+
 def trunk_kernel(
-    where, context, w_first, w_second, embed, code_col, code_row, cotangent, mine, theirs,
-    own, other, tail,
+    where, context, preact_in, hidden_in, encoded_in, w_second, embed, code_col, code_row, cotangent,
+    mine, theirs,
+    own, other,
     wt, patches, gt, normed, rscales, buf, grad, vectors,
 ):
     c = where[2]
@@ -77,10 +86,7 @@
     column = point - ((point * 3277) >> 16) * PITCH
     mask = jnp.where((column < BOARD) & (point < BOARD * PITCH), 1.0, 0.0).astype(F32)
 
-    preact = nn(context[...], w_first[...])
-    cdf = 0.5 * (1.0 + lax.erf(preact * 0.7071067811865476))
-    hidden = (preact * cdf).astype(BF16)
-    encoded = nn(hidden, w_second[...])
+    preact, hidden, encoded = preact_in[...], hidden_in[...], encoded_in[...]
     code = code_col[...]
     stone = embed[...].astype(F32)
     stones = jnp.where(code == 0, stone[0:1], jnp.where(code == 1, stone[1:2], stone[2:3]))
@@ -134,6 +140,7 @@
     picked = ((kind < 3) & (codes == kind)) | ((kind == 3) & (codes < 3))
     sums = nn(jnp.where(picked, 1.0, 0.0).astype(BF16), grad[...].astype(BF16))
     rounded = sums.astype(BF16)
+    cdf = 0.5 * (1.0 + lax.erf(preact * 0.7071067811865476))
     density = jnp.exp(-0.5 * preact * preact) * 0.3989422804014327
     pre_grad = (nt(rounded, w_second[...]) * (cdf + preact * density)).astype(BF16)
     parts = ((context[...], 0, 8), (hidden, 0, 8), (pre_grad, 3, 8))
@@ -145,20 +152,26 @@
                 row : row + 1, piece * 128 : (piece + 1) * 128
             ]
             place += 1
-    tail[...] = vectors[...].astype(BF16)
-    for core, pieces in ((c, own), (1 - c, other)):
+    tail = vectors[...].astype(BF16)
+    empty = jnp.zeros(tail.shape, BF16)
+    taps = gt.shape[2]
+    for core, pieces, first, second in ((c, own, tail, empty), (1 - c, other, empty, tail)):
         for place in range(16):
-            pieces[place] = gt[place // 4, rows_of(place % 4, core), :]
-
-
-def pack_kernel(where, pieces, near, far, out, vectors, product, stones):
+            pieces[place, :, 0:taps] = gt[place // 4, rows_of(place % 4, core), :]
+            pieces[place, :, taps : taps + 128] = first
+            pieces[place, :, taps + 128 :] = second
+
+
+def pack_kernel(where, pieces, out, vectors, product, stones):
     first = where[0] * 256 + where[1] * 64 + where[2] * 32
     row = first // 128
     rows = pl.ds(pl.multiple_of(first - row * 128, 32), 32)
-    taps = pieces.shape[2]
+    taps = pieces.shape[2] - 256
     for piece in range(16):
-        vectors[piece * 32 : (piece + 1) * 32, :] = near[piece].astype(F32)
-        vectors[(16 + piece) * 32 : (17 + piece) * 32, :] = far[piece].astype(F32)
+        for core in (0, 1):
+            state = piece * 2 + core
+            lane = taps + core * 128
+            vectors[state * 32 : (state + 1) * 32, :] = pieces[piece, :, lane : lane + 128].astype(F32)
 
     def of_states(place):
         return vectors[pl.ds(place, 32, stride=32), :]
@@ -217,14 +230,15 @@
     taps = conv_weight.shape[1]
     plane = ("section", "shard")
 
-    unit = lax.dynamic_slice_in_dim(conv_weight[0].T, c * 32, 32, 0)[None]
-    mine = exchange(jnp.broadcast_to(unit, (16,) + unit.shape[1:]), plane)
-    theirs = swap(mine, "dp", 1)
-
     ids = lax.dynamic_slice_in_dim(neighbours, s, 1, 0)
     count = lax.dynamic_slice_in_dim(counts, s, 1, 0)
     asked = jnp.concatenate([ids, count[:, None]], axis=1)
-    asked = jnp.concatenate([asked] + [turned(asked, "shard", d) for d in (1, 2, 3)])
+    asked = exchange(jnp.broadcast_to(asked, (4, asked.shape[1])), "shard")
+
+    unit = lax.dynamic_slice_in_dim(conv_weight[0].T, c * 32, 32, 0)[None]
+    asked, unit = lax.optimization_barrier((asked, unit))
+    mine = exchange(jnp.broadcast_to(unit, (16,) + unit.shape[1:]), plane)
+
     slots = ids.shape[1]
     live = lax.broadcasted_iota(jnp.int32, (4, slots), 1) < asked[:, slots:]
     stored = database.shape[0]
@@ -232,9 +246,10 @@
     hits = (asked[:, :slots, None] == positions) & live[:, :, None]
     picks = jnp.sum(hits.astype(F32), axis=1).astype(BF16)
     partial = jnp.dot(picks, database, preferred_element_type=F32)
-    summed = partial[0:1]
+    summed = lax.dynamic_slice_in_dim(partial, h, 1, 0)
     for d in (1, 2, 3):
-        summed = summed + turned(partial[d : d + 1], "shard", -d)
+        piece = lax.dynamic_slice_in_dim(partial, (h + 4 - d) % 4, 1, 0)
+        summed = summed + turned(piece, "shard", -d)
     context = (summed / jnp.maximum(count, 1).astype(F32)[:, None]).astype(BF16)
     context = jnp.broadcast_to(context, (16, context.shape[1]))
 
@@ -245,10 +260,25 @@
     upper = jnp.pad(upper.reshape(BOARD, BOARD, channels), ((0, 0), (0, 1), (0, 0)))
     upper = jnp.pad(upper.reshape(-1, channels), ((0, ROWS - BOARD * PITCH), (0, 0)))
 
-    part = jax.ShapeDtypeStruct((16, 32, taps), BF16)
-    own, other, rows = vmem_call(
+    mine, context, upper = lax.optimization_barrier((mine, context, upper))
+    theirs = swap(mine, "dp", 1)
+    width = context.shape[1]
+    preact, hidden, encoded = vmem_call(
+        encoder_kernel,
+        (
+            jax.ShapeDtypeStruct((16, width), F32),
+            jax.ShapeDtypeStruct((16, width), BF16),
+            jax.ShapeDtypeStruct((16, channels), F32),
+        ),
+        [],
+        "encoder",
+        2 * 16 * width * (width + channels),
+        3 << 20,
+    )(where, context, w_first, w_second)
+    part = jax.ShapeDtypeStruct((16, 32, taps + 256), BF16)
+    own, other = vmem_call(
         trunk_kernel,
-        (part, part, jax.ShapeDtypeStruct((32, 128), BF16)),
+        (part, part),
         [
             pltpu.VMEM((4, channels, taps), BF16),
             pltpu.VMEM((4, ROWS, taps), BF16),
@@ -262,13 +292,13 @@
         "trunk",
         12 * 2 * ROWS * taps * channels,
         16 << 20,
-    )(where, context, w_first, w_second, embed, code[:, None], code[None, :], upper, mine, theirs)
+    )(
+        where, context, preact, hidden, encoded, w_second, embed,
+        code[:, None], code[None, :], upper, mine, theirs,
+    )
 
     pieces = exchange((own.astype(F32) + swap(other, "dp", 1).astype(F32)).astype(BF16), plane)
 
-    rows = rows[None]
-    for axis, bits in (("shard", 1), ("shard", 3), ("section", 1), ("section", 3)):
-        rows = jnp.concatenate([rows, swap(rows, axis, bits)])
     (chunks,) = vmem_call(
         pack_kernel,
         (jax.ShapeDtypeStruct((32, 16, 256), BF16),),
@@ -280,23 +310,16 @@
         "pack",
         4 * 32 * 128 * 1280,
         3 << 20,
-    )(where, pieces, rows, swap(rows, "dp", 1))
-
-    def along_z(blocks, groups, step):
-        return lax.all_to_all(
-            blocks.reshape((4, step) + blocks.shape[-2:]), "dp", 0, 0,
-            axis_index_groups=groups, tiled=True,
-        )
-
-    fours = range(lax.axis_size("dp") // 8)
-    low = [[8 * i + 2 * j + core for j in range(4)] for i in fours for core in (0, 1)]
-    high = [[8 * i + 2 * j + core for i in fours] for j in range(4) for core in (0, 1)]
-    chunks = jnp.sum(along_z(chunks, low, 8).astype(F32), axis=0).astype(BF16)
-    chunks = jnp.sum(along_z(chunks, high, 2).astype(F32), axis=0).astype(BF16)
-    chunks = along_z(jnp.broadcast_to(chunks, (4,) + chunks.shape), high, 2)
-    chunks = chunks.reshape((8,) + chunks.shape[-2:])
-    chunks = along_z(jnp.broadcast_to(chunks, (4,) + chunks.shape), low, 8)
-    chunks = chunks.reshape((32,) + chunks.shape[-2:])
+    )(where, pieces)
+
+    line = [[2 * i + core for i in range(lax.axis_size("dp") // 2)] for core in (0, 1)]
+
+    def along_z(blocks):
+        return lax.all_to_all(blocks, "dp", 0, 0, axis_index_groups=line, tiled=True)
+
+    total = along_z(chunks.reshape(16, 2, 16, 256))
+    total = jnp.sum(total.astype(F32), axis=0, keepdims=True).astype(BF16)
+    chunks = along_z(jnp.broadcast_to(total, (16,) + total.shape[1:])).reshape(32, 16, 256)
     conv, w1_grad, w2_grad, embed_grad = vmem_call(
         finish_kernel,
         (

time: 236 us -> 182 us (0.77)
  waiting for transfers between devices: 50.3 us -> 20.8 us
  starting transfers between devices: 53.7 us -> 39 us
  blocking collectives: 95.9 us -> 87.1 us
    ppermute x8 -> x3, waiting for transfers between devices: 46.9 us -> 6.02 us  [swap(): lax.ppermute(block, axis, [(i, i ^ bits) for i in range(lax.axis_size(axi...]
    ppermute x8 -> x3, starting transfers between devices: 34.2 us -> 19.2 us  [swap(): lax.ppermute(block, axis, [(i, i ^ bits) for i in range(lax.axis_size(axi...]
    ppermute x6 -> x3, waiting for transfers between devices: 3.49 us -> 11.7 us  [turned(): lax.ppermute(block, axis, [(i, (i + distance) % size) for i in range(size)])]
    all_to_all x4 -> x2, blocking collectives: 58.8 us -> 50.8 us  [along_z(): lax.all_to_all(blocks, 'dp', 0, 0, axis_index_groups=line, tiled=True)]
    all_to_all x1 -> x2, starting transfers between devices: 4.24 us -> 9.74 us  [exchange(): return lax.all_to_all(blocks, axis, 0, 0, tiled=True)]
    ppermute x6 -> x3, starting transfers between devices: 15.3 us -> 10 us  [turned(): lax.ppermute(block, axis, [(i, (i + distance) % size) for i in range(size)])]
    all_to_all x1 -> x2, waiting for transfers between devices: 0.01 us -> 3.11 us  [exchange(): return lax.all_to_all(blocks, axis, 0, 0, tiled=True)]
    pallas_call x3 -> x4, Pallas kernels: 15.6 us -> 16.4 us  [call(): pl.pallas_call(kernel, out_shape=outs, in_specs=[pl.BlockSpec(memory_spac...]
  transfers between devices with their start and end apart: 15 -> 8, of which waited for: 9 -> 5; matrix products, arithmetic and copies ran while one was open for 5% -> 4% of each run, Pallas kernels for 0% -> 1%
where the time goes in v5:
time: 182 us; the launch traced here: 181 us
  blocking collectives  87.1 us (48%)
  starting transfers between devices  39 us (21%)
  waiting for transfers between devices  20.8 us (11%)
  Pallas kernels  16.4 us (9%)
  local copies, waits for them, and re-layouts  12.6 us (7%)
  other arithmetic  2.41 us (1%)
    all_to_all x2, blocking collectives, along_z(): lax.all_to_all(blocks, 'dp', 0, 0, axis_index_groups=line, tiled=True)  50.8 us
    all_to_all x1, blocking collectives, exchange(): return lax.all_to_all(blocks, axis, 0, 0, tiled=True)  36.3 us
    ppermute x3, starting transfers between devices, swap(): lax.ppermute(block, axis, [(i, i ^ bits) for i in range(lax.axis_size(axi...  19.2 us
    pallas_call x4, Pallas kernels, call(): pl.pallas_call(kernel, out_shape=outs, in_specs=[pl.BlockSpec(memory_spac...  16.4 us
    ppermute x3, waiting for transfers between devices, turned(): lax.ppermute(block, axis, [(i, (i + distance) % size) for i in range(size)])  11.7 us
    ppermute x3, starting transfers between devices, turned(): lax.ppermute(block, axis, [(i, (i + distance) % size) for i in range(size)])  10 us
    all_to_all x2, starting transfers between devices, exchange(): return lax.all_to_all(blocks, axis, 0, 0, tiled=True)  9.74 us
    ppermute x3, waiting for transfers between devices, swap(): lax.ppermute(block, axis, [(i, i ^ bits) for i in range(lax.axis_size(axi...  6.02 us
  transfers between devices with their start and end apart: 8, of which 5 were waited for; matrix products, arithmetic and copies ran while one was open for 4% of the time, Pallas kernels for 1%

profile of v5, /device:TPU:1, one launch (start us, length us, event | category | flops | bytes accessed | tf_op | source)
XLA Modules:
  0.0 181.0 jit_solution(14305305790689614811)
XLA Ops:
  0.6 0.0 copy-start
  0.7 1.3 dynamic_slice.30
  2.0 0.7 constant_dynamic-slice_fusion.4
  2.6 0.7 add_bitcast_fusion
  3.4 0.6 broadcast_in_dim.44
  3.9 4.8 %all-to-all-start = ((s32[4,1,11]{2,1,0:T(1,128)}), s32[4,1,11]{2,1,0:T(1,128)S(1)}, u32[]{:S(2)}, u32[]{:S(2)}) async-start(s32[4,1,11]{2,1,0:T(1,128)} %broadcast_in_dim.44), calls=%async_computation | async-start | bytes 4096 | tf_op jit(solution)/shard_map/all_to_all | solution.py:29
  8.8 0.9 dynamic-slice_bitcast_fusion
  9.7 3.1 %all-to-all-done = s32[4,1,11]{2,1,0:T(1,128)S(1)} async-done(((s32[4,1,11]{2,1,0:T(1,128)}), s32[4,1,11]{2,1,0:T(1,128)S(1)}, u32[]{:S(2)}, u32[]{:S(2)}) %all-to-all-start) | async-done | bytes 208 | tf_op jit(solution)/shard_map/all_to_all | solution.py:29
  12.8 1.6 broadcast_in_dim.47
  14.5 4.9 %all-to-all-start.1 = ((bf16[16,32,2304]{2,1,0:T(8,128)(2,1)}), bf16[16,32,2304]{2,1,0:T(8,128)(2,1)S(1)}, u32[]{:S(2)}, u32[]{:S(2)}) async-start(bf16[16,32,2304]{2,1,0:T(8,128)(2,1)} %broadcast_in_dim.47), calls=%async_computation.1 | async-start | bytes 4718592 | tf_op jit(solution)/shard_map/all_to_all | solution.py:29
  19.4 0.1 copy.15
  19.5 0.2 slice_reduce_fusion
  19.7 0.1 convert_reduce_fusion
  19.8 1.2 fusion.3
  21.0 0.6 constant_dynamic-slice_fusion.3
  21.6 4.4 %collective-permute-start = (f32[1,1024]{1,0:T(1,128)}, f32[1,1024]{1,0:T(1,128)S(1)}, u32[]{:S(2)}, u32[]{:S(2)}) collective-permute-start(f32[1,1024]{1,0:T(1,128)} %get-tuple-element.32), channel_id=1, source_target_pairs={{0,3},{1,0},{2,1},{3,2},{4,7},{5,4},{6,5},{7,6},{8,11},{9,8},{10,9... | collective-permute-start | bytes 12296 | tf_op jit(solution)/shard_map/ppermute | solution.py:25
  26.1 1.9 %collective-permute-start.2 = (f32[1,1024]{1,0:T(1,128)S(1)}, f32[1,1024]{1,0:T(1,128)}, u32[]{:S(2)}, u32[]{:S(2)}) collective-permute-start(f32[1,1024]{1,0:T(1,128)S(1)} %get-tuple-element.33), channel_id=1, source_target_pairs={{0,1},{1,2},{2,3},{3,0},{4,5},{5,6},{6,7},{7,4},{8,9},{9,10},{10,1... | collective-permute-start | bytes 12296 | tf_op jit(solution)/shard_map/ppermute | solution.py:25
  28.0 0.0 copy-start.3
  28.0 3.7 %collective-permute-start.1 = (f32[1,1024]{1,0:T(1,128)S(1)}, f32[1,1024]{1,0:T(1,128)}, u32[]{:S(2)}, u32[]{:S(2)}) collective-permute-start(f32[1,1024]{1,0:T(1,128)S(1)} %get-tuple-element.34), channel_id=1, source_target_pairs={{0,2},{1,3},{2,0},{3,1},{4,6},{5,7},{6,4},{7,5},{8,10},{9,11},{10,... | collective-permute-start | bytes 12296 | tf_op jit(solution)/shard_map/ppermute | solution.py:25
  31.7 1.1 dynamic-slice_reduce_fusion
  33.4 0.1 reshape.71
  33.5 0.7 pad.16
  34.2 1.0 reshape.72
  35.2 8.0 %collective-permute-done = f32[1,1024]{1,0:T(1,128)S(1)} collective-permute-done((f32[1,1024]{1,0:T(1,128)}, f32[1,1024]{1,0:T(1,128)S(1)}, u32[]{:S(2)}, u32[]{:S(2)}) %collective-permute-start) | collective-permute-done | bytes 4128 | tf_op jit(solution)/shard_map/ppermute | solution.py:25
  43.2 3.7 %collective-permute-done.2 = f32[1,1024]{1,0:T(1,128)} collective-permute-done((f32[1,1024]{1,0:T(1,128)S(1)}, f32[1,1024]{1,0:T(1,128)}, u32[]{:S(2)}, u32[]{:S(2)}) %collective-permute-start.2) | collective-permute-done | bytes 4128 | tf_op jit(solution)/shard_map/ppermute | solution.py:25
  46.9 0.0 collective-permute-done.1
  46.9 0.7 convert_reduce_fusion.1
  47.6 0.0 all-to-all-done.1.mine
  47.6 8.6 %collective-permute-start.3 = (bf16[16,32,2304]{2,1,0:T(8,128)(2,1)S(1)}, bf16[16,32,2304]{2,1,0:T(8,128)(2,1)}, u32[]{:S(2)}, u32[]{:S(2)}) collective-permute-start(bf16[16,32,2304]{2,1,0:T(8,128)(2,1)S(1)} %all-to-all-done.1.mine), channel_id=1, source_target_pairs={{0,16},{16,0},{32,48},{48,32},{64,80},{80,64},{96,112},{112,96},{1... | collective-permute-start | bytes 7077896 | tf_op jit(solution)/shard_map/ppermute | solution.py:20
  56.2 0.7 fusion.2
  57.0 0.1 reshape.73
  57.1 0.1 reshape.74
  57.2 0.1 broadcast_in_dim.54.code_col
  57.3 0.1 pad_add_fusion.where
  57.4 1.6 copy-done.1
  59.0 1.0 copy-done.2
  60.0 1.1 encoder.1
  61.1 12.8 %trunk.1 = (bf16[16,32,2560]{2,1,0:T(8,128)(2,1)S(1)}, bf16[16,32,2560]{2,1,0:T(8,128)(2,1)S(1)}) custom-call(s32[3]{0:T(128)S(1)} %pad_add_fusion.where, bf16[16,1024]{1,0:T(8,128)(2,1)S(1)} %broadcast_in_dim.49.context, f32[16,1024]{1,0:T(8,128)S(1)} %get-tuple-element.21.preact_in, bf16[16,1024]{1,0:T(8,128)(2,1)S(1)} %get-tuple-element.22.hidden_in, ...), custom_call_target="tpu_custom_call" | custom-call | flops 5435817984 | bytes 16777216 | tf_op jit(solution)/shard_map/trunk/pallas_call | solution.py:48
  73.9 1.9 %collective-permute-start.4 = (bf16[16,32,2560]{2,1,0:T(8,128)(2,1)S(1)}, bf16[16,32,2560]{2,1,0:T(8,128)(2,1)S(1)}, u32[]{:S(2)}, u32[]{:S(2)}) collective-permute-start(bf16[16,32,2560]{2,1,0:T(8,128)(2,1)S(1)} %get-tuple-element.27), channel_id=1, source_target_pairs={{0,16},{16,0},{32,48},{48,32},{64,80},{80,64},{96,112},{112,96},{1... | collective-permute-start | bytes 7864328 | tf_op jit(solution)/shard_map/ppermute | solution.py:20
  75.8 4.9 %collective-permute-done.4 = bf16[16,32,2560]{2,1,0:T(8,128)(2,1)S(1)} collective-permute-done((bf16[16,32,2560]{2,1,0:T(8,128)(2,1)S(1)}, bf16[16,32,2560]{2,1,0:T(8,128)(2,1)S(1)}, u32[]{:S(2)}, u32[]{:S(2)}) %collective-permute-start.4) | collective-permute-done | bytes 2621472 | tf_op jit(solution)/shard_map/ppermute | solution.py:20
  80.7 0.7 add_convert_fusion
  81.5 36.3 %all_to_all.29.pieces = bf16[16,32,2560]{2,1,0:T(8,128)(2,1)S(1)} all-to-all(bf16[16,32,2560]{2,1,0:T(8,128)(2,1)S(1)} %add_convert_fusion), channel_id=1, replica_groups=mesh['dp'=32,'section'=4,'shard'=4] {'section','shard'}, dimensions={0} | all-to-all | bytes 5242880 | tf_op jit(solution)/shard_map/all_to_all | solution.py:29
  117.8 1.1 pack.1
  118.9 28.0 %all_to_all.30 = bf16[16,2,16,256]{3,2,1,0:T(8,128)(2,1)S(1)} all-to-all(bf16[16,2,16,256]{3,2,1,0:T(8,128)(2,1)S(1)} %bitcast.23), channel_id=1, replica_groups={{0,32,64,96,128,160,192,224,256,288,320,352,384,416,448,480},{16,48,80,..., dimensions={0} | all-to-all | bytes 524288 | tf_op jit(solution)/shard_map/all_to_all | solution.py:318
  147.0 22.8 %all_to_all.31 = bf16[16,2,16,256]{3,2,1,0:T(8,128)(2,1)S(1)} all-to-all(bf16[16,2,16,256]{3,2,1,0:T(8,128)(2,1)S(1)} %broadcast_in_dim.52), channel_id=1, replica_groups={{0,32,64,96,128,160,192,224,256,288,320,352,384,416,448,480},{16,48,80,..., dimensions={0} | all-to-all | bytes 524288 | tf_op jit(solution)/shard_map/all_to_all | solution.py:318
  169.8 8.7 %collective-permute-start.5 = (bf16[32,16,256]{2,1,0:T(8,128)(2,1)S(1)}, bf16[32,16,256]{2,1,0:T(8,128)(2,1)S(1)}, u32[]{:S(2)}, u32[]{:S(2)}) collective-permute-start(bf16[32,16,256]{2,1,0:T(8,128)(2,1)S(1)} %bitcast.24), channel_id=1, source_target_pairs={{0,16},{16,0},{32,48},{48,32},{64,80},{80,64},{96,112},{112,96},{1... | collective-permute-start | bytes 786440 | tf_op jit(solution)/shard_map/ppermute | solution.py:20
  178.5 1.1 collective-permute-done.5.theirs
  179.6 1.4 finish.1
  (14 shorter events, 0.1 us)
Async XLA Ops:
  0.6 31.1 %copy-start = (bf16[4,361,256]{2,0,1:T(4,128)(2,1)S(1)}, bf16[4,361,256]{2,0,1:T(4,128)(2,1)}, u32[]{:S(2)}) copy-start(bf16[4,361,256]{2,0,1:T(4,128)(2,1)} %param.17) | copy-start | bytes 2217988
  3.9 8.9 %all-to-all-start = ((s32[4,1,11]{2,1,0:T(1,128)}), s32[4,1,11]{2,1,0:T(1,128)S(1)}, u32[]{:S(2)}, u32[]{:S(2)}) async-start(s32[4,1,11]{2,1,0:T(1,128)} %broadcast_in_dim.44), calls=%async_computation | async-start | bytes 4096 | tf_op jit(solution)/shard_map/all_to_all | solution.py:29
  14.5 33.2 %all-to-all-start.1 = ((bf16[16,32,2304]{2,1,0:T(8,128)(2,1)}), bf16[16,32,2304]{2,1,0:T(8,128)(2,1)S(1)}, u32[]{:S(2)}, u32[]{:S(2)}) async-start(bf16[16,32,2304]{2,1,0:T(8,128)(2,1)} %broadcast_in_dim.47), calls=%async_computation.1 | async-start | bytes 4718592 | tf_op jit(solution)/shard_map/all_to_all | solution.py:29
  21.6 21.5 %collective-permute-start = (f32[1,1024]{1,0:T(1,128)}, f32[1,1024]{1,0:T(1,128)S(1)}, u32[]{:S(2)}, u32[]{:S(2)}) collective-permute-start(f32[1,1024]{1,0:T(1,128)} %get-tuple-element.32), channel_id=1, source_target_pairs={{0,3},{1,0},{2,1},{3,2},{4,7},{5,4},{6,5},{7,6},{8,11},{9,8},{10,9... | collective-permute-start | bytes 12296 | tf_op jit(solution)/shard_map/ppermute | solution.py:25
  26.1 20.8 %collective-permute-start.2 = (f32[1,1024]{1,0:T(1,128)S(1)}, f32[1,1024]{1,0:T(1,128)}, u32[]{:S(2)}, u32[]{:S(2)}) collective-permute-start(f32[1,1024]{1,0:T(1,128)S(1)} %get-tuple-element.33), channel_id=1, source_target_pairs={{0,1},{1,2},{2,3},{3,0},{4,5},{5,6},{6,7},{7,4},{8,9},{9,10},{10,1... | collective-permute-start | bytes 12296 | tf_op jit(solution)/shard_map/ppermute | solution.py:25
  28.0 33.1 %copy-start.3 = (bf16[3,256]{1,0:T(4,128)(2,1)S(1)}, bf16[3,256]{1,0:T(4,128)(2,1)}, u32[]{:S(2)}) copy-start(bf16[3,256]{1,0:T(4,128)(2,1)} %embed.1) | copy-start | bytes 4612
  28.0 18.9 %collective-permute-start.1 = (f32[1,1024]{1,0:T(1,128)S(1)}, f32[1,1024]{1,0:T(1,128)}, u32[]{:S(2)}, u32[]{:S(2)}) collective-permute-start(f32[1,1024]{1,0:T(1,128)S(1)} %get-tuple-element.34), channel_id=1, source_target_pairs={{0,2},{1,3},{2,0},{3,1},{4,6},{5,7},{6,4},{7,5},{8,10},{9,11},{10,... | collective-permute-start | bytes 12296 | tf_op jit(solution)/shard_map/ppermute | solution.py:25
  47.6 13.5 %collective-permute-start.3 = (bf16[16,32,2304]{2,1,0:T(8,128)(2,1)S(1)}, bf16[16,32,2304]{2,1,0:T(8,128)(2,1)}, u32[]{:S(2)}, u32[]{:S(2)}) collective-permute-start(bf16[16,32,2304]{2,1,0:T(8,128)(2,1)S(1)} %all-to-all-done.1.mine), channel_id=1, source_target_pairs={{0,16},{16,0},{32,48},{48,32},{64,80},{80,64},{96,112},{112,96},{1... | collective-permute-start | bytes 7077896 | tf_op jit(solution)/shard_map/ppermute | solution.py:20
  57.4 1.6 copy-start.1
  59.0 1.0 copy-start.2
  73.9 6.8 %collective-permute-start.4 = (bf16[16,32,2560]{2,1,0:T(8,128)(2,1)S(1)}, bf16[16,32,2560]{2,1,0:T(8,128)(2,1)S(1)}, u32[]{:S(2)}, u32[]{:S(2)}) collective-permute-start(bf16[16,32,2560]{2,1,0:T(8,128)(2,1)S(1)} %get-tuple-element.27), channel_id=1, source_target_pairs={{0,16},{16,0},{32,48},{48,32},{64,80},{80,64},{96,112},{112,96},{1... | collective-permute-start | bytes 7864328 | tf_op jit(solution)/shard_map/ppermute | solution.py:20
  169.8 9.8 %collective-permute-start.5 = (bf16[32,16,256]{2,1,0:T(8,128)(2,1)S(1)}, bf16[32,16,256]{2,1,0:T(8,128)(2,1)S(1)}, u32[]{:S(2)}, u32[]{:S(2)}) collective-permute-start(bf16[32,16,256]{2,1,0:T(8,128)(2,1)S(1)} %bitcast.24), channel_id=1, source_target_pairs={{0,16},{16,0},{32,48},{48,32},{64,80},{80,64},{96,112},{112,96},{1... | collective-permute-start | bytes 786440 | tf_op jit(solution)/shard_map/ppermute | solution.py:20

commit v6 on v5

--- a/solution.py
+++ b/solution.py
@@ -75,12 +75,16 @@
 ):
     c = where[2]
 
-    def rows_of(shard, core):
-        return pl.ds(pl.multiple_of(shard * 64 + core * 32, 32), 32)
+    def block_rows(outer, inner, core):
+        block = jnp.where(core == 0, inner, outer)
+        shard = jnp.where(core == 0, outer, inner)
+        return block, pl.ds(pl.multiple_of(shard * 64 + core * 32, 32), 32)
 
     for core, pieces in ((c, mine), (1 - c, theirs)):
-        for place in range(16):
-            wt[place // 4, rows_of(place % 4, core), :] = pieces[place]
+        for outer in range(4):
+            for inner in range(4):
+                block, rows = block_rows(inner, outer, core)
+                wt[block, rows, :] = pieces[outer, inner]
 
     point = lax.broadcasted_iota(jnp.int32, (ROWS, 1), 0)
     column = point - ((point * 3277) >> 16) * PITCH
@@ -156,22 +160,34 @@
     empty = jnp.zeros(tail.shape, BF16)
     taps = gt.shape[2]
     for core, pieces, first, second in ((c, own, tail, empty), (1 - c, other, empty, tail)):
-        for place in range(16):
-            pieces[place, :, 0:taps] = gt[place // 4, rows_of(place % 4, core), :]
-            pieces[place, :, taps : taps + 128] = first
-            pieces[place, :, taps + 128 :] = second
+        for outer in range(4):
+            for inner in range(4):
+                block, rows = block_rows(outer, inner, core)
+                pieces[outer, inner, :, 0:taps] = gt[block, rows, :]
+                pieces[outer, inner, :, taps : taps + 128] = first
+                pieces[outer, inner, :, taps + 128 :] = second
+
+
+def fold_kernel(where, pieces, out):
+    taps = pieces.shape[3] - 256
+    for inner in range(4):
+        total = pieces[0, inner, :, 0:taps].astype(F32)
+        for source in range(1, 4):
+            total += pieces[source, inner, :, 0:taps].astype(F32)
+        out[inner, :, 0:taps] = total.astype(BF16)
+        for source in range(4):
+            lane = taps + source * 256
+            out[inner, :, lane : lane + 256] = pieces[source, inner, :, taps:]
 
 
 def pack_kernel(where, pieces, out, vectors, product, stones):
     first = where[0] * 256 + where[1] * 64 + where[2] * 32
     row = first // 128
     rows = pl.ds(pl.multiple_of(first - row * 128, 32), 32)
-    taps = pieces.shape[2] - 256
-    for piece in range(16):
-        for core in (0, 1):
-            state = piece * 2 + core
-            lane = taps + core * 128
-            vectors[state * 32 : (state + 1) * 32, :] = pieces[piece, :, lane : lane + 128].astype(F32)
+    taps = pieces.shape[2] - 1024
+    for state in range(32):
+        lane = taps + state % 8 * 128
+        vectors[state * 32 : (state + 1) * 32, :] = pieces[state // 8, :, lane : lane + 128].astype(F32)
 
     def of_states(place):
         return vectors[pl.ds(place, 32, stride=32), :]
@@ -193,7 +209,7 @@
     for column in range(taps // 256):
         lanes = slice(column * 256, (column + 1) * 256)
         block = pieces[0, :, lanes].astype(F32)
-        for piece in range(1, 16):
+        for piece in range(1, 4):
             block += pieces[piece, :, lanes].astype(F32)
         out[2 * column] = block[0:16].astype(BF16)
         out[2 * column + 1] = block[16:32].astype(BF16)
@@ -228,18 +244,32 @@
     where = jnp.stack([s, h, c]).astype(jnp.int32)
     channels = embed.shape[1]
     taps = conv_weight.shape[1]
-    plane = ("section", "shard")
-
-    ids = lax.dynamic_slice_in_dim(neighbours, s, 1, 0)
-    count = lax.dynamic_slice_in_dim(counts, s, 1, 0)
-    asked = jnp.concatenate([ids, count[:, None]], axis=1)
-    asked = exchange(jnp.broadcast_to(asked, (4, asked.shape[1])), "shard")
-
-    unit = lax.dynamic_slice_in_dim(conv_weight[0].T, c * 32, 32, 0)[None]
+
+    along_x, along_y = [], []
+    for place in range(lax.axis_size("dp")):
+        lines = ([[place * 16 + i * 4 + j for j in range(4)] for i in range(4)],
+                 [[place * 16 + i * 4 + j for i in range(4)] for j in range(4)])
+        along_x += lines[place % 2]
+        along_y += lines[1 - place % 2]
+
+    def ring(blocks, groups):
+        return lax.all_to_all(
+            blocks, ("dp", "section", "shard"), 0, 0, axis_index_groups=groups, tiled=True
+        )
+
+    slots = neighbours.shape[1]
+    asked = jnp.concatenate([neighbours, counts[:, None]], axis=1)
+    state = lax.broadcasted_iota(jnp.int32, asked.shape, 0)
+    asked = jnp.sum(jnp.where(state == s, asked, 0), axis=0, keepdims=True)
+    count = asked[:, slots]
+    asked = exchange(jnp.broadcast_to(asked, (4, slots + 1)), "shard")
+
+    unit = lax.dynamic_slice_in_dim(conv_weight[0].T, c * 32, 32, 0)
+    unit = jnp.broadcast_to(unit[None], (4,) + unit.shape)
     asked, unit = lax.optimization_barrier((asked, unit))
-    mine = exchange(jnp.broadcast_to(unit, (16,) + unit.shape[1:]), plane)
-
-    slots = ids.shape[1]
+    mine = ring(unit, along_x)
+    mine = ring(jnp.broadcast_to(mine[None], (4,) + mine.shape), along_y)
+
     live = lax.broadcasted_iota(jnp.int32, (4, slots), 1) < asked[:, slots:]
     stored = database.shape[0]
     positions = lax.broadcasted_iota(jnp.int32, (1, 1, stored), 2) + h * stored
@@ -275,7 +305,7 @@
         2 * 16 * width * (width + channels),
         3 << 20,
     )(where, context, w_first, w_second)
-    part = jax.ShapeDtypeStruct((16, 32, taps + 256), BF16)
+    part = jax.ShapeDtypeStruct((4, 4, 32, taps + 256), BF16)
     own, other = vmem_call(
         trunk_kernel,
         (part, part),
@@ -297,8 +327,16 @@
         code[:, None], code[None, :], upper, mine, theirs,
     )
 
-    pieces = exchange((own.astype(F32) + swap(other, "dp", 1).astype(F32)).astype(BF16), plane)
-
+    pieces = ring((own.astype(F32) + swap(other, "dp", 1).astype(F32)).astype(BF16), along_x)
+    (pieces,) = vmem_call(
+        fold_kernel,
+        (jax.ShapeDtypeStruct((4, 32, taps + 1024), BF16),),
+        [],
+        "fold",
+        pieces.size,
+        3 << 20,
+    )(where, pieces)
+    pieces = ring(pieces, along_y)
     (chunks,) = vmem_call(
         pack_kernel,
         (jax.ShapeDtypeStruct((32, 16, 256), BF16),),

time: 182 us -> 172 us (0.945)
  waiting for transfers between devices: 20.8 us -> 9.77 us
  blocking collectives: 87.1 us -> 90 us
  starting transfers between devices: 39 us -> 36.9 us
    ppermute x3, waiting for transfers between devices: 11.7 us -> 0.64 us  [turned(): lax.ppermute(block, axis, [(i, (i + distance) % size) for i in range(size)])]
    all_to_all x1 -> x3, blocking collectives: 36.3 us -> 43.9 us  [ring(): lax.all_to_all(blocks, ('dp', 'section', 'shard'), 0, 0, axis_index_group...]
    all_to_all x2 -> x1, starting transfers between devices: 9.74 us -> 4.84 us  [exchange(): return lax.all_to_all(blocks, axis, 0, 0, tiled=True)]
    all_to_all x2, blocking collectives: 50.8 us -> 46.1 us  [along_z(): lax.all_to_all(blocks, 'dp', 0, 0, axis_index_groups=line, tiled=True)]
    all_to_all x0 -> x1, starting transfers between devices: none -> 3.63 us  [ring(): lax.all_to_all(blocks, ('dp', 'section', 'shard'), 0, 0, axis_index_group...]
    pallas_call x4 -> x5, Pallas kernels: 16.4 us -> 17 us  [call(): pl.pallas_call(kernel, out_shape=outs, in_specs=[pl.BlockSpec(memory_spac...]
  transfers between devices with their start and end apart: 8 -> 8, of which waited for: 5 -> 4; matrix products, arithmetic and copies ran while one was open for 4% -> 5% of each run, Pallas kernels for 1% -> 1%
where the time goes in v6:
time: 172 us; the launch traced here: 171 us
  blocking collectives  90 us (52%)
  starting transfers between devices  36.9 us (21%)
  Pallas kernels  17 us (10%)
  local copies, waits for them, and re-layouts  12 us (7%)
  waiting for transfers between devices  9.77 us (6%)
  other arithmetic  2.47 us (1%)
    all_to_all x2, blocking collectives, along_z(): lax.all_to_all(blocks, 'dp', 0, 0, axis_index_groups=line, tiled=True)  46.1 us
    all_to_all x3, blocking collectives, ring(): lax.all_to_all(blocks, ('dp', 'section', 'shard'), 0, 0, axis_index_group...  43.9 us
    ppermute x3, starting transfers between devices, swap(): lax.ppermute(block, axis, [(i, i ^ bits) for i in range(lax.axis_size(axi...  18.4 us
    pallas_call x5, Pallas kernels, call(): pl.pallas_call(kernel, out_shape=outs, in_specs=[pl.BlockSpec(memory_spac...  17 us
    ppermute x3, starting transfers between devices, turned(): lax.ppermute(block, axis, [(i, (i + distance) % size) for i in range(size)])  10.1 us
    ppermute x3, waiting for transfers between devices, swap(): lax.ppermute(block, axis, [(i, i ^ bits) for i in range(lax.axis_size(axi...  6.01 us
    all_to_all x1, starting transfers between devices, exchange(): return lax.all_to_all(blocks, axis, 0, 0, tiled=True)  4.84 us
    all_to_all x1, starting transfers between devices, ring(): lax.all_to_all(blocks, ('dp', 'section', 'shard'), 0, 0, axis_index_group...  3.63 us
  transfers between devices with their start and end apart: 8, of which 4 were waited for; matrix products, arithmetic and copies ran while one was open for 5% of the time, Pallas kernels for 1%

profile of v6, /device:TPU:1, one launch (start us, length us, event | category | flops | bytes accessed | tf_op | source)
XLA Modules:
  0.0 170.9 jit_solution(743318587378369692)
XLA Ops:
  0.6 0.0 copy-start
  0.7 0.8 copy.18
  1.5 0.8 fusion
  2.2 0.6 broadcast_in_dim.54
  2.8 4.8 %all-to-all-start = ((s32[4,1,11]{2,1,0:T(1,128)}), s32[4,1,11]{2,1,0:T(1,128)S(1)}, u32[]{:S(2)}, u32[]{:S(2)}) async-start(s32[4,1,11]{2,1,0:T(1,128)} %broadcast_in_dim.54), calls=%async_computation | async-start | bytes 4096 | tf_op jit(solution)/shard_map/all_to_all | solution.py:29
  7.7 0.9 dynamic-slice_bitcast_fusion
  8.6 3.1 %all-to-all-done = s32[4,1,11]{2,1,0:T(1,128)S(1)} async-done(((s32[4,1,11]{2,1,0:T(1,128)}), s32[4,1,11]{2,1,0:T(1,128)S(1)}, u32[]{:S(2)}, u32[]{:S(2)}) %all-to-all-start) | async-done | bytes 208 | tf_op jit(solution)/shard_map/all_to_all | solution.py:29
  11.7 11.3 %all_to_all.39 = bf16[4,32,2304]{2,1,0:T(8,128)(2,1)S(1)} all-to-all(bf16[4,32,2304]{2,1,0:T(8,128)(2,1)S(1)} %broadcast_in_dim.55), channel_id=1, replica_groups={{0,1,2,3},{4,5,6,7},{8,9,10,11},{12,13,14,15},{16,20,24,28},{17,21,25,2..., dimensions={0} | all-to-all | bytes 1179648 | tf_op jit(solution)/shard_map/all_to_all | solution.py:256
  23.0 1.6 broadcast_in_dim.56
  24.7 3.6 %all-to-all-start.2 = ((bf16[4,4,32,2304]{3,2,1,0:T(8,128)(2,1)}), bf16[4,4,32,2304]{3,2,1,0:T(8,128)(2,1)S(1)}, u32[]{:S(2)}, u32[]{:S(2)}) async-start(bf16[4,4,32,2304]{3,2,1,0:T(8,128)(2,1)} %broadcast_in_dim.56), calls=%async_computation.2 | async-start | bytes 4718592 | tf_op jit(solution)/shard_map/all_to_all | solution.py:256
  28.4 0.1 copy.19
  28.5 0.2 slice_reduce_fusion
  28.6 0.1 convert_reduce_fusion
  28.8 1.2 fusion.4
  30.0 0.6 constant_dynamic-slice_fusion.3
  30.6 4.5 %collective-permute-start = (f32[1,1024]{1,0:T(1,128)}, f32[1,1024]{1,0:T(1,128)S(1)}, u32[]{:S(2)}, u32[]{:S(2)}) collective-permute-start(f32[1,1024]{1,0:T(1,128)} %get-tuple-element.32), channel_id=1, source_target_pairs={{0,3},{1,0},{2,1},{3,2},{4,7},{5,4},{6,5},{7,6},{8,11},{9,8},{10,9... | collective-permute-start | bytes 12296 | tf_op jit(solution)/shard_map/ppermute | solution.py:25
  35.1 1.9 %collective-permute-start.2 = (f32[1,1024]{1,0:T(1,128)S(1)}, f32[1,1024]{1,0:T(1,128)}, u32[]{:S(2)}, u32[]{:S(2)}) collective-permute-start(f32[1,1024]{1,0:T(1,128)S(1)} %get-tuple-element.33), channel_id=1, source_target_pairs={{0,1},{1,2},{2,3},{3,0},{4,5},{5,6},{6,7},{7,4},{8,9},{9,10},{10,1... | collective-permute-start | bytes 12296 | tf_op jit(solution)/shard_map/ppermute | solution.py:25
  37.0 0.0 copy-start.3
  37.0 3.7 %collective-permute-start.1 = (f32[1,1024]{1,0:T(1,128)S(1)}, f32[1,1024]{1,0:T(1,128)}, u32[]{:S(2)}, u32[]{:S(2)}) collective-permute-start(f32[1,1024]{1,0:T(1,128)S(1)} %get-tuple-element.34), channel_id=1, source_target_pairs={{0,2},{1,3},{2,0},{3,1},{4,6},{5,7},{6,4},{7,5},{8,10},{9,11},{10,... | collective-permute-start | bytes 12296 | tf_op jit(solution)/shard_map/ppermute | solution.py:25
  40.7 1.1 dynamic-slice_reduce_fusion
  41.8 0.6 slice.14
  43.0 0.1 reshape.77
  43.1 0.7 pad.16
  43.8 1.0 reshape.78
  44.8 0.6 collective-permute-done.1
  45.5 0.7 convert_reduce_fusion.1
  46.2 7.8 %collective-permute-start.3 = (bf16[4,4,32,2304]{3,2,1,0:T(8,128)(2,1)S(1)}, bf16[4,4,32,2304]{3,2,1,0:T(8,128)(2,1)}, u32[]{:S(2)}, u32[]{:S(2)}) collective-permute-start(bf16[4,4,32,2304]{3,2,1,0:T(8,128)(2,1)S(1)} %all-to-all-done.2.mine), channel_id=1, source_target_pairs={{0,16},{16,0},{32,48},{48,32},{64,80},{80,64},{96,112},{112,96},{1... | collective-permute-start | bytes 7077896 | tf_op jit(solution)/shard_map/ppermute | solution.py:20
  54.0 0.7 fusion.3
  54.7 0.1 reshape.79
  54.8 0.1 reshape.80
  55.0 0.1 broadcast_in_dim.64.code_col
  55.1 0.1 pad_add_fusion.where
  55.2 1.6 copy-done.1
  56.8 1.0 copy-done.2
  57.8 1.1 encoder.1
  58.9 12.7 %trunk.1 = (bf16[4,4,32,2560]{3,2,1,0:T(8,128)(2,1)S(1)}, bf16[4,4,32,2560]{3,2,1,0:T(8,128)(2,1)S(1)}) custom-call(s32[3]{0:T(128)S(1)} %pad_add_fusion.where, bf16[16,1024]{1,0:T(8,128)(2,1)S(1)} %broadcast_in_dim.59.context, f32[16,1024]{1,0:T(8,128)S(1)} %get-tuple-element.21.preact_in, bf16[16,1024]{1,0:T(8,128)(2,1)S(1)} %get-tuple-element.22.hidden_in, ...), custom_call_target="tpu_custom_call" | custom-call | flops 5435817984 | bytes 16777216 | tf_op jit(solution)/shard_map/trunk/pallas_call | solution.py:48
  71.7 1.9 %collective-permute-start.4 = (bf16[4,4,32,2560]{3,2,1,0:T(8,128)(2,1)S(1)}, bf16[4,4,32,2560]{3,2,1,0:T(8,128)(2,1)S(1)}, u32[]{:S(2)}, u32[]{:S(2)}) collective-permute-start(bf16[4,4,32,2560]{3,2,1,0:T(8,128)(2,1)S(1)} %get-tuple-element.27), channel_id=1, source_target_pairs={{0,16},{16,0},{32,48},{48,32},{64,80},{80,64},{96,112},{112,96},{1... | collective-permute-start | bytes 7864328 | tf_op jit(solution)/shard_map/ppermute | solution.py:20
  73.6 4.9 %collective-permute-done.4 = bf16[4,4,32,2560]{3,2,1,0:T(8,128)(2,1)S(1)} collective-permute-done((bf16[4,4,32,2560]{3,2,1,0:T(8,128)(2,1)S(1)}, bf16[4,4,32,2560]{3,2,1,0:T(8,128)(2,1)S(1)}, u32[]{:S(2)}, u32[]{:S(2)}) %collective-permute-start.4) | collective-permute-done | bytes 2621472 | tf_op jit(solution)/shard_map/ppermute | solution.py:20
  78.5 0.7 add_convert_fusion
  79.2 20.8 %all_to_all.40.pieces = bf16[4,4,32,2560]{3,2,1,0:T(8,128)(2,1)S(1)} all-to-all(bf16[4,4,32,2560]{3,2,1,0:T(8,128)(2,1)S(1)} %add_convert_fusion), channel_id=1, replica_groups={{0,1,2,3},{4,5,6,7},{8,9,10,11},{12,13,14,15},{16,20,24,28},{17,21,25,2..., dimensions={0} | all-to-all | bytes 5242880 | tf_op jit(solution)/shard_map/all_to_all | solution.py:256
  100.1 0.8 fold.1
  100.9 11.8 %all_to_all.41.pieces = bf16[4,32,3328]{2,1,0:T(8,128)(2,1)S(1)} all-to-all(bf16[4,32,3328]{2,1,0:T(8,128)(2,1)S(1)} %fold.1), channel_id=1, replica_groups={{0,4,8,12},{1,5,9,13},{2,6,10,14},{3,7,11,15},{16,17,18,19},{20,21,22,2..., dimensions={0} | all-to-all | bytes 1703936 | tf_op jit(solution)/shard_map/all_to_all | solution.py:256
  112.7 0.9 pack.1
  113.6 24.1 %all_to_all.42 = bf16[16,2,16,256]{3,2,1,0:T(8,128)(2,1)S(1)} all-to-all(bf16[16,2,16,256]{3,2,1,0:T(8,128)(2,1)S(1)} %bitcast.21), channel_id=1, replica_groups={{0,32,64,96,128,160,192,224,256,288,320,352,384,416,448,480},{16,48,80,..., dimensions={0} | all-to-all | bytes 524288 | tf_op jit(solution)/shard_map/all_to_all | solution.py:356
  137.8 22.0 %all_to_all.43 = bf16[16,2,16,256]{3,2,1,0:T(8,128)(2,1)S(1)} all-to-all(bf16[16,2,16,256]{3,2,1,0:T(8,128)(2,1)S(1)} %broadcast_in_dim.62), channel_id=1, replica_groups={{0,32,64,96,128,160,192,224,256,288,320,352,384,416,448,480},{16,48,80,..., dimensions={0} | all-to-all | bytes 524288 | tf_op jit(solution)/shard_map/all_to_all | solution.py:356
  159.8 8.6 %collective-permute-start.5 = (bf16[32,16,256]{2,1,0:T(8,128)(2,1)S(1)}, bf16[32,16,256]{2,1,0:T(8,128)(2,1)S(1)}, u32[]{:S(2)}, u32[]{:S(2)}) collective-permute-start(bf16[32,16,256]{2,1,0:T(8,128)(2,1)S(1)} %bitcast.19), channel_id=1, source_target_pairs={{0,16},{16,0},{32,48},{48,32},{64,80},{80,64},{96,112},{112,96},{1... | collective-permute-start | bytes 786440 | tf_op jit(solution)/shard_map/ppermute | solution.py:20
  168.4 1.1 collective-permute-done.5.theirs
  169.6 1.4 finish.1
  (19 shorter events, 0.2 us)
Async XLA Ops:
  0.6 40.0 %copy-start = (bf16[4,361,256]{2,0,1:T(4,128)(2,1)S(1)}, bf16[4,361,256]{2,0,1:T(4,128)(2,1)}, u32[]{:S(2)}) copy-start(bf16[4,361,256]{2,0,1:T(4,128)(2,1)} %param.17) | copy-start | bytes 2217988
  2.8 8.9 %all-to-all-start = ((s32[4,1,11]{2,1,0:T(1,128)}), s32[4,1,11]{2,1,0:T(1,128)S(1)}, u32[]{:S(2)}, u32[]{:S(2)}) async-start(s32[4,1,11]{2,1,0:T(1,128)} %broadcast_in_dim.54), calls=%async_computation | async-start | bytes 4096 | tf_op jit(solution)/shard_map/all_to_all | solution.py:29
  24.7 21.5 %all-to-all-start.2 = ((bf16[4,4,32,2304]{3,2,1,0:T(8,128)(2,1)}), bf16[4,4,32,2304]{3,2,1,0:T(8,128)(2,1)S(1)}, u32[]{:S(2)}, u32[]{:S(2)}) async-start(bf16[4,4,32,2304]{3,2,1,0:T(8,128)(2,1)} %broadcast_in_dim.56), calls=%async_computation.2 | async-start | bytes 4718592 | tf_op jit(solution)/shard_map/all_to_all | solution.py:256
  30.6 14.2 %collective-permute-start = (f32[1,1024]{1,0:T(1,128)}, f32[1,1024]{1,0:T(1,128)S(1)}, u32[]{:S(2)}, u32[]{:S(2)}) collective-permute-start(f32[1,1024]{1,0:T(1,128)} %get-tuple-element.32), channel_id=1, source_target_pairs={{0,3},{1,0},{2,1},{3,2},{4,7},{5,4},{6,5},{7,6},{8,11},{9,8},{10,9... | collective-permute-start | bytes 12296 | tf_op jit(solution)/shard_map/ppermute | solution.py:25
  35.1 9.7 %collective-permute-start.2 = (f32[1,1024]{1,0:T(1,128)S(1)}, f32[1,1024]{1,0:T(1,128)}, u32[]{:S(2)}, u32[]{:S(2)}) collective-permute-start(f32[1,1024]{1,0:T(1,128)S(1)} %get-tuple-element.33), channel_id=1, source_target_pairs={{0,1},{1,2},{2,3},{3,0},{4,5},{5,6},{6,7},{7,4},{8,9},{9,10},{10,1... | collective-permute-start | bytes 12296 | tf_op jit(solution)/shard_map/ppermute | solution.py:25
  37.0 21.9 %copy-start.3 = (bf16[3,256]{1,0:T(4,128)(2,1)S(1)}, bf16[3,256]{1,0:T(4,128)(2,1)}, u32[]{:S(2)}) copy-start(bf16[3,256]{1,0:T(4,128)(2,1)} %embed.1) | copy-start | bytes 4612
  37.0 8.4 %collective-permute-start.1 = (f32[1,1024]{1,0:T(1,128)S(1)}, f32[1,1024]{1,0:T(1,128)}, u32[]{:S(2)}, u32[]{:S(2)}) collective-permute-start(f32[1,1024]{1,0:T(1,128)S(1)} %get-tuple-element.34), channel_id=1, source_target_pairs={{0,2},{1,3},{2,0},{3,1},{4,6},{5,7},{6,4},{7,5},{8,10},{9,11},{10,... | collective-permute-start | bytes 12296 | tf_op jit(solution)/shard_map/ppermute | solution.py:25
  46.2 12.7 %collective-permute-start.3 = (bf16[4,4,32,2304]{3,2,1,0:T(8,128)(2,1)S(1)}, bf16[4,4,32,2304]{3,2,1,0:T(8,128)(2,1)}, u32[]{:S(2)}, u32[]{:S(2)}) collective-permute-start(bf16[4,4,32,2304]{3,2,1,0:T(8,128)(2,1)S(1)} %all-to-all-done.2.mine), channel_id=1, source_target_pairs={{0,16},{16,0},{32,48},{48,32},{64,80},{80,64},{96,112},{112,96},{1... | collective-permute-start | bytes 7077896 | tf_op jit(solution)/shard_map/ppermute | solution.py:20
  55.2 1.6 copy-start.1
  56.7 1.0 copy-start.2
  71.7 6.8 %collective-permute-start.4 = (bf16[4,4,32,2560]{3,2,1,0:T(8,128)(2,1)S(1)}, bf16[4,4,32,2560]{3,2,1,0:T(8,128)(2,1)S(1)}, u32[]{:S(2)}, u32[]{:S(2)}) collective-permute-start(bf16[4,4,32,2560]{3,2,1,0:T(8,128)(2,1)S(1)} %get-tuple-element.27), channel_id=1, source_target_pairs={{0,16},{16,0},{32,48},{48,32},{64,80},{80,64},{96,112},{112,96},{1... | collective-permute-start | bytes 7864328 | tf_op jit(solution)/shard_map/ppermute | solution.py:20
  159.8 9.8 %collective-permute-start.5 = (bf16[32,16,256]{2,1,0:T(8,128)(2,1)S(1)}, bf16[32,16,256]{2,1,0:T(8,128)(2,1)S(1)}, u32[]{:S(2)}, u32[]{:S(2)}) collective-permute-start(bf16[32,16,256]{2,1,0:T(8,128)(2,1)S(1)} %bitcast.19), channel_id=1, source_target_pairs={{0,16},{16,0},{32,48},{48,32},{64,80},{80,64},{96,112},{112,96},{1... | collective-permute-start | bytes 786440 | tf_op jit(solution)/shard_map/ppermute | solution.py:20

commit v7 on v6

--- a/solution.py
+++ b/solution.py
@@ -25,6 +25,11 @@
     return lax.ppermute(block, axis, [(i, (i + distance) % size) for i in range(size)])
 
 
+def turned(block, axis, distance):
+    size = lax.axis_size(axis)
+    return lax.ppermute(block, axis, [(i, (i + distance) % size) for i in range(size)])
+
+
 def exchange(blocks, axis):
     return lax.all_to_all(blocks, axis, 0, 0, tiled=True)
 
@@ -41,14 +46,16 @@
     return lax.dot_general(left, right, (((0,), (0,)), ((), ())), preferred_element_type=F32)
 
 
-def vmem_call(kernel, outs, scratch, name, flops, moved):
+def vmem_call(kernel, outs, scratch, name, flops, moved, far=0):
     spec = pl.BlockSpec(memory_space=pltpu.VMEM)
 
     def call(scalars, *arrays):
         return pl.pallas_call(
             kernel,
             out_shape=outs,
-            in_specs=[pl.BlockSpec(memory_space=pltpu.SMEM)] + [spec] * len(arrays),
+            in_specs=[pl.BlockSpec(memory_space=pltpu.SMEM)]
+            + [spec] * (len(arrays) - far)
+            + [pl.BlockSpec(memory_space=pltpu.HBM)] * far,
             out_specs=tuple(spec for _ in outs),
             scratch_shapes=scratch,
             compiler_params=pltpu.CompilerParams(vmem_limit_bytes=VMEM_BYTES),
@@ -71,7 +78,7 @@
     where, context, preact_in, hidden_in, encoded_in, w_second, embed, code_col, code_row, cotangent,
     mine, theirs,
     own, other,
-    wt, patches, gt, normed, rscales, buf, grad, vectors,
+    wt, patches, normed, rscales, buf, grad, vectors, arrived,
 ):
     c = where[2]
 
@@ -80,11 +87,20 @@
         shard = jnp.where(core == 0, outer, inner)
         return block, pl.ds(pl.multiple_of(shard * 64 + core * 32, 32), 32)
 
-    for core, pieces in ((c, mine), (1 - c, theirs)):
-        for outer in range(4):
-            for inner in range(4):
-                block, rows = block_rows(inner, outer, core)
-                wt[block, rows, :] = pieces[outer, inner]
+    copies = []
+    for place in range(16):
+        outer, inner = divmod(place, 4)
+        block, rows = block_rows(inner, outer, 1 - c)
+        copies.append(
+            pltpu.make_async_copy(
+                theirs.at[outer, inner], wt.at[block, rows, :], arrived.at[place]
+            )
+        )
+        copies[-1].start()
+    for place in range(16):
+        outer, inner = divmod(place, 4)
+        block, rows = block_rows(inner, outer, c)
+        wt[block, rows, :] = mine[outer, inner]
 
     point = lax.broadcasted_iota(jnp.int32, (ROWS, 1), 0)
     column = point - ((point * 3277) >> 16) * PITCH
@@ -100,6 +116,7 @@
     buf[FRONT + ROWS :, :] = jnp.zeros((FRONT, buf.shape[1]), F32)
     buf[FRONT : FRONT + ROWS, :] = start
     channels = start.shape[1]
+    taps = wt.shape[2]
 
     def forward(block, carry):
         for tap, shift in enumerate(TAP_SHIFTS):
@@ -115,6 +132,8 @@
         buf[FRONT : FRONT + ROWS, :] = stream.astype(BF16).astype(F32) * mask
         return carry
 
+    for copy in copies:
+        copy.wait()
     lax.fori_loop(0, 4, forward, 0)
     grad[...] = cotangent[...].astype(F32)
 
@@ -126,7 +145,18 @@
         dnorm = upper * (sigma * (1.0 + value * (1.0 - sigma)))
         inner = jnp.mean(dnorm * value, axis=-1, keepdims=True)
         dconv = rscales[block] * (dnorm - value * inner)
-        gt[block] = nn(dconv.T.astype(BF16), patches[block]).astype(BF16)
+        product = nn(dconv.T.astype(BF16), patches[block]).astype(BF16)
+        for half in range(2):
+            for pieces, core in ((own, half), (other, 1 - half)):
+
+                @pl.when(c == core)
+                def _():
+                    for shard in range(4):
+                        outer = shard if half == 0 else block
+                        inner = block if half == 0 else shard
+                        first = shard * 64 + half * 32
+                        pieces[outer, inner, :, 0:taps] = product[first : first + 32]
+
         buf[FRONT : FRONT + ROWS, :] = dconv.astype(BF16).astype(F32)
         total = upper
         for tap, shift in enumerate(TAP_SHIFTS):
@@ -158,12 +188,9 @@
             place += 1
     tail = vectors[...].astype(BF16)
     empty = jnp.zeros(tail.shape, BF16)
-    taps = gt.shape[2]
-    for core, pieces, first, second in ((c, own, tail, empty), (1 - c, other, empty, tail)):
+    for pieces, first, second in ((own, tail, empty), (other, empty, tail)):
         for outer in range(4):
             for inner in range(4):
-                block, rows = block_rows(outer, inner, core)
-                pieces[outer, inner, :, 0:taps] = gt[block, rows, :]
                 pieces[outer, inner, :, taps : taps + 128] = first
                 pieces[outer, inner, :, taps + 128 :] = second
 
@@ -262,12 +289,12 @@
     state = lax.broadcasted_iota(jnp.int32, asked.shape, 0)
     asked = jnp.sum(jnp.where(state == s, asked, 0), axis=0, keepdims=True)
     count = asked[:, slots]
-    asked = exchange(jnp.broadcast_to(asked, (4, slots + 1)), "shard")
+    asked = jnp.concatenate([asked] + [turned(asked, "shard", d) for d in (1, 2, 3)])
 
     unit = lax.dynamic_slice_in_dim(conv_weight[0].T, c * 32, 32, 0)
     unit = jnp.broadcast_to(unit[None], (4,) + unit.shape)
-    asked, unit = lax.optimization_barrier((asked, unit))
     mine = ring(unit, along_x)
+    asked, mine = lax.optimization_barrier((asked, mine))
     mine = ring(jnp.broadcast_to(mine[None], (4,) + mine.shape), along_y)
 
     live = lax.broadcasted_iota(jnp.int32, (4, slots), 1) < asked[:, slots:]
@@ -276,10 +303,9 @@
     hits = (asked[:, :slots, None] == positions) & live[:, :, None]
     picks = jnp.sum(hits.astype(F32), axis=1).astype(BF16)
     partial = jnp.dot(picks, database, preferred_element_type=F32)
-    summed = lax.dynamic_slice_in_dim(partial, h, 1, 0)
+    summed = partial[0:1]
     for d in (1, 2, 3):
-        piece = lax.dynamic_slice_in_dim(partial, (h + 4 - d) % 4, 1, 0)
-        summed = summed + turned(piece, "shard", -d)
+        summed = summed + turned(partial[d : d + 1], "shard", -d)
     context = (summed / jnp.maximum(count, 1).astype(F32)[:, None]).astype(BF16)
     context = jnp.broadcast_to(context, (16, context.shape[1]))
 
@@ -312,16 +338,17 @@
         [
             pltpu.VMEM((4, channels, taps), BF16),
             pltpu.VMEM((4, ROWS, taps), BF16),
-            pltpu.VMEM((4, channels, taps), BF16),
             pltpu.VMEM((4, ROWS, channels), F32),
             pltpu.VMEM((4, ROWS, 1), F32),
             pltpu.VMEM((2 * FRONT + ROWS, channels), F32),
             pltpu.VMEM((ROWS, channels), F32),
             pltpu.VMEM((32, 128), F32),
+            pltpu.SemaphoreType.DMA((16,)),
         ],
         "trunk",
         12 * 2 * ROWS * taps * channels,
         16 << 20,
+        far=1,
     )(
         where, context, preact, hidden, encoded, w_second, embed,
         code[:, None], code[None, :], upper, mine, theirs,

time: 172 us -> 173 us (level)
  blocking collectives: 90 us -> 77.8 us
  starting transfers between devices: 36.9 us -> 49.1 us
  Pallas kernels: 17 us -> 19.3 us
    all_to_all x3 -> x2, blocking collectives: 43.9 us -> 32 us  [ring(): lax.all_to_all(blocks, ('dp', 'section', 'shard'), 0, 0, axis_index_group...]
    ppermute x3 -> x6, starting transfers between devices: 10.1 us -> 19.4 us  [turned(): lax.ppermute(block, axis, [(i, (i + distance) % size) for i in range(size)])]
    all_to_all x1 -> x2, starting transfers between devices: 3.63 us -> 8.64 us  [ring(): lax.all_to_all(blocks, ('dp', 'section', 'shard'), 0, 0, axis_index_group...]
    all_to_all x1 -> x0, starting transfers between devices: 4.84 us -> none  [exchange(): return lax.all_to_all(blocks, axis, 0, 0, tiled=True)]
    all_to_all x1 -> x0, waiting for transfers between devices: 3.11 us -> none  [exchange(): return lax.all_to_all(blocks, axis, 0, 0, tiled=True)]
    ppermute x3, starting transfers between devices: 18.4 us -> 21 us  [swap(): lax.ppermute(block, axis, [(i, i ^ bits) for i in range(lax.axis_size(axi...]
    ppermute x3 -> x6, waiting for transfers between devices: 0.64 us -> 3.27 us  [turned(): lax.ppermute(block, axis, [(i, (i + distance) % size) for i in range(size)])]
    pallas_call x5, Pallas kernels: 17 us -> 19.3 us  [call(): pl.pallas_call(kernel, out_shape=outs, in_specs=[pl.BlockSpec(memory_spac...]
  transfers between devices with their start and end apart: 8 -> 11, of which waited for: 4 -> 5; matrix products, arithmetic and copies ran while one was open for 5% -> 5% of each run, Pallas kernels for 1% -> 1%
where the time goes in v7:
time: 173 us; the launch traced here: 172 us
  blocking collectives  77.8 us (45%)
  starting transfers between devices  49.1 us (28%)
  Pallas kernels  19.3 us (11%)
  local copies, waits for them, and re-layouts  12.2 us (7%)
  waiting for transfers between devices  9.29 us (5%)
  other arithmetic  1.8 us (1%)
    all_to_all x2, blocking collectives, along_z(): lax.all_to_all(blocks, 'dp', 0, 0, axis_index_groups=line, tiled=True)  45.8 us
    all_to_all x2, blocking collectives, ring(): lax.all_to_all(blocks, ('dp', 'section', 'shard'), 0, 0, axis_index_group...  32 us
    ppermute x3, starting transfers between devices, swap(): lax.ppermute(block, axis, [(i, i ^ bits) for i in range(lax.axis_size(axi...  21 us
    ppermute x6, starting transfers between devices, turned(): lax.ppermute(block, axis, [(i, (i + distance) % size) for i in range(size)])  19.4 us
    pallas_call x5, Pallas kernels, call(): pl.pallas_call(kernel, out_shape=outs, in_specs=[pl.BlockSpec(memory_spac...  19.3 us
    all_to_all x2, starting transfers between devices, ring(): lax.all_to_all(blocks, ('dp', 'section', 'shard'), 0, 0, axis_index_group...  8.64 us
    ppermute x3, waiting for transfers between devices, swap(): lax.ppermute(block, axis, [(i, i ^ bits) for i in range(lax.axis_size(axi...  6.01 us
  transfers between devices with their start and end apart: 11, of which 5 were waited for; matrix products, arithmetic and copies ran while one was open for 5% of the time, Pallas kernels for 1%

profile of v7, /device:TPU:1, one launch (start us, length us, event | category | flops | bytes accessed | tf_op | source)
XLA Modules:
  0.0 172.3 jit_solution(12388267094978596825)
XLA Ops:
  0.7 1.0 dynamic-slice_bitcast_fusion
  1.7 0.9 broadcast_in_dim.50
  2.5 5.0 %all-to-all-start = ((bf16[4,32,2304]{2,1,0:T(8,128)(2,1)}), bf16[4,32,2304]{2,1,0:T(8,128)(2,1)S(1)}, u32[]{:S(2)}, u32[]{:S(2)}) async-start(bf16[4,32,2304]{2,1,0:T(8,128)(2,1)} %broadcast_in_dim.50), calls=%async_computation | async-start | bytes 1179648 | tf_op jit(solution)/shard_map/all_to_all | solution.py:283
  7.5 0.7 copy.16
  8.3 0.8 fusion.2
  9.0 4.4 %collective-permute-start.2 = (s32[1,11]{1,0:T(1,128)S(1)}, s32[1,11]{1,0:T(1,128)S(1)}, u32[]{:S(2)}, u32[]{:S(2)}) collective-permute-start(s32[1,11]{1,0:T(1,128)S(1)} %bitcast.22), channel_id=1, source_target_pairs={{0,3},{1,0},{2,1},{3,2},{4,7},{5,4},{6,5},{7,6},{8,11},{9,8},{10,9... | collective-permute-start | bytes 140 | tf_op jit(solution)/shard_map/ppermute | solution.py:30
  13.4 2.4 %collective-permute-start.1 = (s32[1,11]{1,0:T(1,128)S(1)}, s32[1,11]{1,0:T(1,128)S(1)}, u32[]{:S(2)}, u32[]{:S(2)}) collective-permute-start(s32[1,11]{1,0:T(1,128)S(1)} %bitcast.23), channel_id=1, source_target_pairs={{0,2},{1,3},{2,0},{3,1},{4,6},{5,7},{6,4},{7,5},{8,10},{9,11},{10,... | collective-permute-start | bytes 140 | tf_op jit(solution)/shard_map/ppermute | solution.py:30
  15.9 2.5 %collective-permute-start = (s32[1,11]{1,0:T(1,128)S(1)}, s32[1,11]{1,0:T(1,128)S(1)}, u32[]{:S(2)}, u32[]{:S(2)}) collective-permute-start(s32[1,11]{1,0:T(1,128)S(1)} %bitcast.24), channel_id=1, source_target_pairs={{0,1},{1,2},{2,3},{3,0},{4,5},{5,6},{6,7},{7,4},{8,9},{9,10},{10,1... | collective-permute-start | bytes 140 | tf_op jit(solution)/shard_map/ppermute | solution.py:30
  18.4 1.2 collective-permute-done.1
  19.6 1.8 %collective-permute-done = s32[1,11]{1,0:T(1,128)S(1)} collective-permute-done((s32[1,11]{1,0:T(1,128)S(1)}, s32[1,11]{1,0:T(1,128)S(1)}, u32[]{:S(2)}, u32[]{:S(2)}) %collective-permute-start) | collective-permute-done | bytes 76 | tf_op jit(solution)/shard_map/ppermute | solution.py:30
  21.4 1.6 broadcast_in_dim.51
  23.0 3.6 %all-to-all-start.1 = ((bf16[4,4,32,2304]{3,2,1,0:T(8,128)(2,1)}), bf16[4,4,32,2304]{3,2,1,0:T(8,128)(2,1)S(1)}, u32[]{:S(2)}, u32[]{:S(2)}) async-start(bf16[4,4,32,2304]{3,2,1,0:T(8,128)(2,1)} %broadcast_in_dim.51), calls=%async_computation.1 | async-start | bytes 4718592 | tf_op jit(solution)/shard_map/all_to_all | solution.py:283
  26.7 0.1 copy.17
  26.8 0.2 slice_reduce_fusion
  27.0 0.1 convert_reduce_fusion
  27.1 1.2 fusion.6
  28.3 0.6 fusion.5
  28.9 4.5 %collective-permute-start.3 = (f32[1,1024]{1,0:T(1,128)}, f32[1,1024]{1,0:T(1,128)S(1)}, u32[]{:S(2)}, u32[]{:S(2)}) collective-permute-start(f32[1,1024]{1,0:T(1,128)} %get-tuple-element.32), channel_id=1, source_target_pairs={{0,3},{1,0},{2,1},{3,2},{4,7},{5,4},{6,5},{7,6},{8,11},{9,8},{10,9... | collective-permute-start | bytes 12296 | tf_op jit(solution)/shard_map/ppermute | solution.py:30
  33.4 1.9 %collective-permute-start.5 = (f32[1,1024]{1,0:T(1,128)}, f32[1,1024]{1,0:T(1,128)S(1)}, u32[]{:S(2)}, u32[]{:S(2)}) collective-permute-start(f32[1,1024]{1,0:T(1,128)} %get-tuple-element.33), channel_id=1, source_target_pairs={{0,1},{1,2},{2,3},{3,0},{4,5},{5,6},{6,7},{7,4},{8,9},{9,10},{10,1... | collective-permute-start | bytes 12296 | tf_op jit(solution)/shard_map/ppermute | solution.py:30
  35.4 3.7 %collective-permute-start.4 = (f32[1,1024]{1,0:T(1,128)}, f32[1,1024]{1,0:T(1,128)S(1)}, u32[]{:S(2)}, u32[]{:S(2)}) collective-permute-start(f32[1,1024]{1,0:T(1,128)} %get-tuple-element.34), channel_id=1, source_target_pairs={{0,2},{1,3},{2,0},{3,1},{4,6},{5,7},{6,4},{7,5},{8,10},{9,11},{10,... | collective-permute-start | bytes 12296 | tf_op jit(solution)/shard_map/ppermute | solution.py:30
  39.0 1.1 dynamic-slice_reduce_fusion
  40.1 0.6 slice.30
  41.4 0.1 reshape.71
  41.4 0.7 pad.16
  42.2 1.0 reshape.72
  43.2 0.3 collective-permute-done.4
  43.5 10.5 %collective-permute-start.6 = (bf16[4,4,32,2304]{3,2,1,0:T(8,128)(2,1)S(1)}, bf16[4,4,32,2304]{3,2,1,0:T(8,128)(2,1)}, u32[]{:S(2)}, u32[]{:S(2)}) collective-permute-start(bf16[4,4,32,2304]{3,2,1,0:T(8,128)(2,1)S(1)} %all-to-all-done.1.mine), channel_id=1, source_target_pairs={{0,16},{16,0},{32,48},{48,32},{64,80},{80,64},{96,112},{112,96},{1... | collective-permute-start | bytes 7077896 | tf_op jit(solution)/shard_map/ppermute | solution.py:20
  54.0 0.7 dynamic-slice_reduce_fusion.1
  54.7 0.1 reshape.73
  54.8 0.1 reshape.74
  54.9 0.1 broadcast_in_dim.58.code_col
  55.1 0.1 pad_add_fusion.1.where
  55.1 1.6 copy-done.1
  56.7 1.0 copy-done.2
  57.8 1.1 encoder.1
  58.9 15.1 %trunk.1 = (bf16[4,4,32,2560]{3,2,1,0:T(8,128)(2,1)S(1)}, bf16[4,4,32,2560]{3,2,1,0:T(8,128)(2,1)S(1)}) custom-call(s32[3]{0:T(128)S(1)} %pad_add_fusion.1.where, bf16[16,1024]{1,0:T(8,128)(2,1)S(1)} %broadcast_in_dim.53.context, f32[16,1024]{1,0:T(8,128)S(1)} %get-tuple-element.21.preact_in, bf16[16,1024]{1,0:T(8,128)(2,1)S(1)} %get-tuple-element.22.hidden_in, ...), custom_call_target="tpu_custom_call" | custom-call | flops 5435817984 | bytes 16777216 | tf_op jit(solution)/shard_map/trunk/pallas_call | solution.py:53
  74.0 1.9 %collective-permute-start.7 = (bf16[4,4,32,2560]{3,2,1,0:T(8,128)(2,1)S(1)}, bf16[4,4,32,2560]{3,2,1,0:T(8,128)(2,1)S(1)}, u32[]{:S(2)}, u32[]{:S(2)}) collective-permute-start(bf16[4,4,32,2560]{3,2,1,0:T(8,128)(2,1)S(1)} %get-tuple-element.27), channel_id=1, source_target_pairs={{0,16},{16,0},{32,48},{48,32},{64,80},{80,64},{96,112},{112,96},{1... | collective-permute-start | bytes 7864328 | tf_op jit(solution)/shard_map/ppermute | solution.py:20
  75.9 4.9 %collective-permute-done.7 = bf16[4,4,32,2560]{3,2,1,0:T(8,128)(2,1)S(1)} collective-permute-done((bf16[4,4,32,2560]{3,2,1,0:T(8,128)(2,1)S(1)}, bf16[4,4,32,2560]{3,2,1,0:T(8,128)(2,1)S(1)}, u32[]{:S(2)}, u32[]{:S(2)}) %collective-permute-start.7) | collective-permute-done | bytes 2621472 | tf_op jit(solution)/shard_map/ppermute | solution.py:20
  80.8 0.7 add_convert_fusion
  81.5 20.9 %all_to_all.30.pieces = bf16[4,4,32,2560]{3,2,1,0:T(8,128)(2,1)S(1)} all-to-all(bf16[4,4,32,2560]{3,2,1,0:T(8,128)(2,1)S(1)} %add_convert_fusion), channel_id=1, replica_groups={{0,1,2,3},{4,5,6,7},{8,9,10,11},{12,13,14,15},{16,20,24,28},{17,21,25,2..., dimensions={0} | all-to-all | bytes 5242880 | tf_op jit(solution)/shard_map/all_to_all | solution.py:283
  102.4 0.8 fold.1
  103.3 11.1 %all_to_all.31.pieces = bf16[4,32,3328]{2,1,0:T(8,128)(2,1)S(1)} all-to-all(bf16[4,32,3328]{2,1,0:T(8,128)(2,1)S(1)} %fold.1), channel_id=1, replica_groups={{0,4,8,12},{1,5,9,13},{2,6,10,14},{3,7,11,15},{16,17,18,19},{20,21,22,2..., dimensions={0} | all-to-all | bytes 1703936 | tf_op jit(solution)/shard_map/all_to_all | solution.py:283
  114.3 0.9 pack.1
  115.3 23.8 %all_to_all.32 = bf16[16,2,16,256]{3,2,1,0:T(8,128)(2,1)S(1)} all-to-all(bf16[16,2,16,256]{3,2,1,0:T(8,128)(2,1)S(1)} %bitcast.20), channel_id=1, replica_groups={{0,32,64,96,128,160,192,224,256,288,320,352,384,416,448,480},{16,48,80,..., dimensions={0} | all-to-all | bytes 524288 | tf_op jit(solution)/shard_map/all_to_all | solution.py:383
  139.2 22.0 %all_to_all.33 = bf16[16,2,16,256]{3,2,1,0:T(8,128)(2,1)S(1)} all-to-all(bf16[16,2,16,256]{3,2,1,0:T(8,128)(2,1)S(1)} %broadcast_in_dim.56), channel_id=1, replica_groups={{0,32,64,96,128,160,192,224,256,288,320,352,384,416,448,480},{16,48,80,..., dimensions={0} | all-to-all | bytes 524288 | tf_op jit(solution)/shard_map/all_to_all | solution.py:383
  161.1 8.6 %collective-permute-start.8 = (bf16[32,16,256]{2,1,0:T(8,128)(2,1)S(1)}, bf16[32,16,256]{2,1,0:T(8,128)(2,1)S(1)}, u32[]{:S(2)}, u32[]{:S(2)}) collective-permute-start(bf16[32,16,256]{2,1,0:T(8,128)(2,1)S(1)} %bitcast.18), channel_id=1, source_target_pairs={{0,16},{16,0},{32,48},{48,32},{64,80},{80,64},{96,112},{112,96},{1... | collective-permute-start | bytes 786440 | tf_op jit(solution)/shard_map/ppermute | solution.py:20
  169.8 1.1 collective-permute-done.8.theirs
  170.9 1.4 finish.1
  (24 shorter events, 0.2 us)
Async XLA Ops:
  0.6 38.4 %copy-start = (bf16[4,361,256]{2,0,1:T(4,128)(2,1)S(1)}, bf16[4,361,256]{2,0,1:T(4,128)(2,1)}, u32[]{:S(2)}) copy-start(bf16[4,361,256]{2,0,1:T(4,128)(2,1)} %param.17) | copy-start | bytes 2217988
  2.5 18.9 %all-to-all-start = ((bf16[4,32,2304]{2,1,0:T(8,128)(2,1)}), bf16[4,32,2304]{2,1,0:T(8,128)(2,1)S(1)}, u32[]{:S(2)}, u32[]{:S(2)}) async-start(bf16[4,32,2304]{2,1,0:T(8,128)(2,1)} %broadcast_in_dim.50), calls=%async_computation | async-start | bytes 1179648 | tf_op jit(solution)/shard_map/all_to_all | solution.py:283
  9.0 9.3 %collective-permute-start.2 = (s32[1,11]{1,0:T(1,128)S(1)}, s32[1,11]{1,0:T(1,128)S(1)}, u32[]{:S(2)}, u32[]{:S(2)}) collective-permute-start(s32[1,11]{1,0:T(1,128)S(1)} %bitcast.22), channel_id=1, source_target_pairs={{0,3},{1,0},{2,1},{3,2},{4,7},{5,4},{6,5},{7,6},{8,11},{9,8},{10,9... | collective-permute-start | bytes 140 | tf_op jit(solution)/shard_map/ppermute | solution.py:30
  13.4 6.2 %collective-permute-start.1 = (s32[1,11]{1,0:T(1,128)S(1)}, s32[1,11]{1,0:T(1,128)S(1)}, u32[]{:S(2)}, u32[]{:S(2)}) collective-permute-start(s32[1,11]{1,0:T(1,128)S(1)} %bitcast.23), channel_id=1, source_target_pairs={{0,2},{1,3},{2,0},{3,1},{4,6},{5,7},{6,4},{7,5},{8,10},{9,11},{10,... | collective-permute-start | bytes 140 | tf_op jit(solution)/shard_map/ppermute | solution.py:30
  15.9 5.5 %collective-permute-start = (s32[1,11]{1,0:T(1,128)S(1)}, s32[1,11]{1,0:T(1,128)S(1)}, u32[]{:S(2)}, u32[]{:S(2)}) collective-permute-start(s32[1,11]{1,0:T(1,128)S(1)} %bitcast.24), channel_id=1, source_target_pairs={{0,1},{1,2},{2,3},{3,0},{4,5},{5,6},{6,7},{7,4},{8,9},{9,10},{10,1... | collective-permute-start | bytes 140 | tf_op jit(solution)/shard_map/ppermute | solution.py:30
  23.0 20.5 %all-to-all-start.1 = ((bf16[4,4,32,2304]{3,2,1,0:T(8,128)(2,1)}), bf16[4,4,32,2304]{3,2,1,0:T(8,128)(2,1)S(1)}, u32[]{:S(2)}, u32[]{:S(2)}) async-start(bf16[4,4,32,2304]{3,2,1,0:T(8,128)(2,1)} %broadcast_in_dim.51), calls=%async_computation.1 | async-start | bytes 4718592 | tf_op jit(solution)/shard_map/all_to_all | solution.py:283
  28.9 14.3 %collective-permute-start.3 = (f32[1,1024]{1,0:T(1,128)}, f32[1,1024]{1,0:T(1,128)S(1)}, u32[]{:S(2)}, u32[]{:S(2)}) collective-permute-start(f32[1,1024]{1,0:T(1,128)} %get-tuple-element.32), channel_id=1, source_target_pairs={{0,3},{1,0},{2,1},{3,2},{4,7},{5,4},{6,5},{7,6},{8,11},{9,8},{10,9... | collective-permute-start | bytes 12296 | tf_op jit(solution)/shard_map/ppermute | solution.py:30
  33.4 9.7 %collective-permute-start.5 = (f32[1,1024]{1,0:T(1,128)}, f32[1,1024]{1,0:T(1,128)S(1)}, u32[]{:S(2)}, u32[]{:S(2)}) collective-permute-start(f32[1,1024]{1,0:T(1,128)} %get-tuple-element.33), channel_id=1, source_target_pairs={{0,1},{1,2},{2,3},{3,0},{4,5},{5,6},{6,7},{7,4},{8,9},{9,10},{10,1... | collective-permute-start | bytes 12296 | tf_op jit(solution)/shard_map/ppermute | solution.py:30
  35.4 23.5 %copy-start.3 = (bf16[3,256]{1,0:T(4,128)(2,1)S(1)}, bf16[3,256]{1,0:T(4,128)(2,1)}, u32[]{:S(2)}) copy-start(bf16[3,256]{1,0:T(4,128)(2,1)} %embed.1) | copy-start | bytes 4612
  35.4 8.1 %collective-permute-start.4 = (f32[1,1024]{1,0:T(1,128)}, f32[1,1024]{1,0:T(1,128)S(1)}, u32[]{:S(2)}, u32[]{:S(2)}) collective-permute-start(f32[1,1024]{1,0:T(1,128)} %get-tuple-element.34), channel_id=1, source_target_pairs={{0,2},{1,3},{2,0},{3,1},{4,6},{5,7},{6,4},{7,5},{8,10},{9,11},{10,... | collective-permute-start | bytes 12296 | tf_op jit(solution)/shard_map/ppermute | solution.py:30
  43.5 15.4 %collective-permute-start.6 = (bf16[4,4,32,2304]{3,2,1,0:T(8,128)(2,1)S(1)}, bf16[4,4,32,2304]{3,2,1,0:T(8,128)(2,1)}, u32[]{:S(2)}, u32[]{:S(2)}) collective-permute-start(bf16[4,4,32,2304]{3,2,1,0:T(8,128)(2,1)S(1)} %all-to-all-done.1.mine), channel_id=1, source_target_pairs={{0,16},{16,0},{32,48},{48,32},{64,80},{80,64},{96,112},{112,96},{1... | collective-permute-start | bytes 7077896 | tf_op jit(solution)/shard_map/ppermute | solution.py:20
  55.1 1.6 copy-start.1
  56.7 1.0 copy-start.2
  74.0 6.8 %collective-permute-start.7 = (bf16[4,4,32,2560]{3,2,1,0:T(8,128)(2,1)S(1)}, bf16[4,4,32,2560]{3,2,1,0:T(8,128)(2,1)S(1)}, u32[]{:S(2)}, u32[]{:S(2)}) collective-permute-start(bf16[4,4,32,2560]{3,2,1,0:T(8,128)(2,1)S(1)} %get-tuple-element.27), channel_id=1, source_target_pairs={{0,16},{16,0},{32,48},{48,32},{64,80},{80,64},{96,112},{112,96},{1... | collective-permute-start | bytes 7864328 | tf_op jit(solution)/shard_map/ppermute | solution.py:20
  161.1 9.8 %collective-permute-start.8 = (bf16[32,16,256]{2,1,0:T(8,128)(2,1)S(1)}, bf16[32,16,256]{2,1,0:T(8,128)(2,1)S(1)}, u32[]{:S(2)}, u32[]{:S(2)}) collective-permute-start(bf16[32,16,256]{2,1,0:T(8,128)(2,1)S(1)} %bitcast.18), channel_id=1, source_target_pairs={{0,16},{16,0},{32,48},{48,32},{64,80},{80,64},{96,112},{112,96},{1... | collective-permute-start | bytes 786440 | tf_op jit(solution)/shard_map/ppermute | solution.py:20

commit v8 on v7

--- a/solution.py
+++ b/solution.py
@@ -18,6 +18,10 @@
 
 def swap(block, axis, bits):
     return lax.ppermute(block, axis, [(i, i ^ bits) for i in range(lax.axis_size(axis))])
+
+
+def exchange(blocks, axis):
+    return lax.all_to_all(blocks, axis, 0, 0, tiled=True)
 
 
 def turned(block, axis, distance):
@@ -78,7 +82,7 @@
     where, context, preact_in, hidden_in, encoded_in, w_second, embed, code_col, code_row, cotangent,
     mine, theirs,
     own, other,
-    wt, patches, normed, rscales, buf, grad, vectors, arrived,
+    wt, patches, gt, normed, rscales, buf, grad, vectors, arrived,
 ):
     c = where[2]
 
@@ -145,25 +149,13 @@
         dnorm = upper * (sigma * (1.0 + value * (1.0 - sigma)))
         inner = jnp.mean(dnorm * value, axis=-1, keepdims=True)
         dconv = rscales[block] * (dnorm - value * inner)
-        product = nn(dconv.T.astype(BF16), patches[block]).astype(BF16)
-        for half in range(2):
-            for pieces, core in ((own, half), (other, 1 - half)):
-
-                @pl.when(c == core)
-                def _():
-                    for shard in range(4):
-                        outer = shard if half == 0 else block
-                        inner = block if half == 0 else shard
-                        first = shard * 64 + half * 32
-                        pieces[outer, inner, :, 0:taps] = product[first : first + 32]
-
+        gt[block] = nn(dconv.T.astype(BF16), patches[block]).astype(BF16)
         buf[FRONT : FRONT + ROWS, :] = dconv.astype(BF16).astype(F32)
-        total = upper
-        for tap, shift in enumerate(TAP_SHIFTS):
-            total += nn(
-                buf[FRONT - shift : FRONT - shift + ROWS, :].astype(BF16),
-                wt[block, :, tap * channels : (tap + 1) * channels],
-            )
+        moved = [
+            buf[FRONT - shift : FRONT - shift + ROWS, :].astype(BF16) for shift in TAP_SHIFTS
+        ]
+        weights = [wt[block, :, tap * channels : (tap + 1) * channels] for tap in range(9)]
+        total = upper + nn(jnp.concatenate(moved, axis=1), jnp.concatenate(weights, axis=0))
         grad[...] = total.astype(BF16).astype(F32) * mask
         return carry
 
@@ -188,9 +180,11 @@
             place += 1
     tail = vectors[...].astype(BF16)
     empty = jnp.zeros(tail.shape, BF16)
-    for pieces, first, second in ((own, tail, empty), (other, empty, tail)):
+    for core, pieces, first, second in ((c, own, tail, empty), (1 - c, other, empty, tail)):
         for outer in range(4):
             for inner in range(4):
+                block, rows = block_rows(outer, inner, core)
+                pieces[outer, inner, :, 0:taps] = gt[block, rows, :]
                 pieces[outer, inner, :, taps : taps + 128] = first
                 pieces[outer, inner, :, taps + 128 :] = second
 
@@ -289,7 +283,7 @@
     state = lax.broadcasted_iota(jnp.int32, asked.shape, 0)
     asked = jnp.sum(jnp.where(state == s, asked, 0), axis=0, keepdims=True)
     count = asked[:, slots]
-    asked = jnp.concatenate([asked] + [turned(asked, "shard", d) for d in (1, 2, 3)])
+    asked = exchange(jnp.broadcast_to(asked, (4, slots + 1)), "shard")
 
     unit = lax.dynamic_slice_in_dim(conv_weight[0].T, c * 32, 32, 0)
     unit = jnp.broadcast_to(unit[None], (4,) + unit.shape)
@@ -303,9 +297,10 @@
     hits = (asked[:, :slots, None] == positions) & live[:, :, None]
     picks = jnp.sum(hits.astype(F32), axis=1).astype(BF16)
     partial = jnp.dot(picks, database, preferred_element_type=F32)
-    summed = partial[0:1]
+    summed = lax.dynamic_slice_in_dim(partial, h, 1, 0)
     for d in (1, 2, 3):
-        summed = summed + turned(partial[d : d + 1], "shard", -d)
+        piece = lax.dynamic_slice_in_dim(partial, (h + 4 - d) % 4, 1, 0)
+        summed = summed + turned(piece, "shard", -d)
     context = (summed / jnp.maximum(count, 1).astype(F32)[:, None]).astype(BF16)
     context = jnp.broadcast_to(context, (16, context.shape[1]))
 
@@ -338,6 +333,7 @@
         [
             pltpu.VMEM((4, channels, taps), BF16),
             pltpu.VMEM((4, ROWS, taps), BF16),
+            pltpu.VMEM((4, channels, taps), BF16),
             pltpu.VMEM((4, ROWS, channels), F32),
             pltpu.VMEM((4, ROWS, 1), F32),
             pltpu.VMEM((2 * FRONT + ROWS, channels), F32),

time: 173 us -> 172 us (level)
  blocking collectives: 77.8 us -> 90 us
  starting transfers between devices: 49.1 us -> 36.9 us
  Pallas kernels: 19.3 us -> 17.3 us
    all_to_all x2 -> x3, blocking collectives: 32 us -> 43.9 us  [ring(): lax.all_to_all(blocks, ('dp', 'section', 'shard'), 0, 0, axis_index_group...]
    ppermute x6 -> x3, starting transfers between devices: 19.4 us -> 10.1 us  [turned(): lax.ppermute(block, axis, [(i, (i + distance) % size) for i in range(size)])]
    all_to_all x2 -> x1, starting transfers between devices: 8.64 us -> 3.63 us  [ring(): lax.all_to_all(blocks, ('dp', 'section', 'shard'), 0, 0, axis_index_group...]
    all_to_all x0 -> x1, starting transfers between devices: none -> 4.84 us  [exchange(): return lax.all_to_all(blocks, axis, 0, 0, tiled=True)]
    all_to_all x0 -> x1, waiting for transfers between devices: none -> 3.11 us  [exchange(): return lax.all_to_all(blocks, axis, 0, 0, tiled=True)]
    ppermute x3, starting transfers between devices: 21 us -> 18.4 us  [swap(): lax.ppermute(block, axis, [(i, i ^ bits) for i in range(lax.axis_size(axi...]
    ppermute x6 -> x3, waiting for transfers between devices: 3.27 us -> 0.64 us  [turned(): lax.ppermute(block, axis, [(i, (i + distance) % size) for i in range(size)])]
    pallas_call x5, Pallas kernels: 19.3 us -> 17.3 us  [call(): pl.pallas_call(kernel, out_shape=outs, in_specs=[pl.BlockSpec(memory_spac...]
  transfers between devices with their start and end apart: 11 -> 8, of which waited for: 5 -> 4; matrix products, arithmetic and copies ran while one was open for 5% -> 5% of each run, Pallas kernels for 1% -> 1%
where the time goes in v8:
time: 172 us; the launch traced here: 171 us
  blocking collectives  90 us (52%)
  starting transfers between devices  36.9 us (21%)
  Pallas kernels  17.3 us (10%)
  local copies, waits for them, and re-layouts  12 us (7%)
  waiting for transfers between devices  9.77 us (6%)
  other arithmetic  2.47 us (1%)
    all_to_all x2, blocking collectives, along_z(): lax.all_to_all(blocks, 'dp', 0, 0, axis_index_groups=line, tiled=True)  46.1 us
    all_to_all x3, blocking collectives, ring(): lax.all_to_all(blocks, ('dp', 'section', 'shard'), 0, 0, axis_index_group...  43.9 us
    ppermute x3, starting transfers between devices, swap(): lax.ppermute(block, axis, [(i, i ^ bits) for i in range(lax.axis_size(axi...  18.4 us
    pallas_call x5, Pallas kernels, call(): pl.pallas_call(kernel, out_shape=outs, in_specs=[pl.BlockSpec(memory_spac...  17.3 us
    ppermute x3, starting transfers between devices, turned(): lax.ppermute(block, axis, [(i, (i + distance) % size) for i in range(size)])  10.1 us
    ppermute x3, waiting for transfers between devices, swap(): lax.ppermute(block, axis, [(i, i ^ bits) for i in range(lax.axis_size(axi...  6.01 us
    all_to_all x1, starting transfers between devices, exchange(): return lax.all_to_all(blocks, axis, 0, 0, tiled=True)  4.84 us
    all_to_all x1, starting transfers between devices, ring(): lax.all_to_all(blocks, ('dp', 'section', 'shard'), 0, 0, axis_index_group...  3.63 us
  transfers between devices with their start and end apart: 8, of which 4 were waited for; matrix products, arithmetic and copies ran while one was open for 5% of the time, Pallas kernels for 1%

profile of v8, /device:TPU:1, one launch (start us, length us, event | category | flops | bytes accessed | tf_op | source)
XLA Modules:
  0.0 171.2 jit_solution(18298845709643363460)
XLA Ops:
  0.6 0.0 copy-start
  0.7 0.8 copy.18
  1.5 0.8 fusion
  2.2 0.6 broadcast_in_dim.54
  2.8 4.8 %all-to-all-start = ((s32[4,1,11]{2,1,0:T(1,128)}), s32[4,1,11]{2,1,0:T(1,128)S(1)}, u32[]{:S(2)}, u32[]{:S(2)}) async-start(s32[4,1,11]{2,1,0:T(1,128)} %broadcast_in_dim.54), calls=%async_computation | async-start | bytes 4096 | tf_op jit(solution)/shard_map/all_to_all | solution.py:38
  7.7 0.9 dynamic-slice_bitcast_fusion
  8.6 3.1 %all-to-all-done = s32[4,1,11]{2,1,0:T(1,128)S(1)} async-done(((s32[4,1,11]{2,1,0:T(1,128)}), s32[4,1,11]{2,1,0:T(1,128)S(1)}, u32[]{:S(2)}, u32[]{:S(2)}) %all-to-all-start) | async-done | bytes 208 | tf_op jit(solution)/shard_map/all_to_all | solution.py:38
  11.7 11.3 %all_to_all.39 = bf16[4,32,2304]{2,1,0:T(8,128)(2,1)S(1)} all-to-all(bf16[4,32,2304]{2,1,0:T(8,128)(2,1)S(1)} %broadcast_in_dim.55), channel_id=1, replica_groups={{0,1,2,3},{4,5,6,7},{8,9,10,11},{12,13,14,15},{16,20,24,28},{17,21,25,2..., dimensions={0} | all-to-all | bytes 1179648 | tf_op jit(solution)/shard_map/all_to_all | solution.py:277
  23.0 1.6 broadcast_in_dim.56
  24.7 3.6 %all-to-all-start.2 = ((bf16[4,4,32,2304]{3,2,1,0:T(8,128)(2,1)}), bf16[4,4,32,2304]{3,2,1,0:T(8,128)(2,1)S(1)}, u32[]{:S(2)}, u32[]{:S(2)}) async-start(bf16[4,4,32,2304]{3,2,1,0:T(8,128)(2,1)} %broadcast_in_dim.56), calls=%async_computation.2 | async-start | bytes 4718592 | tf_op jit(solution)/shard_map/all_to_all | solution.py:277
  28.4 0.1 copy.19
  28.4 0.2 slice_reduce_fusion
  28.6 0.1 convert_reduce_fusion
  28.7 1.2 fusion.4
  30.0 0.6 constant_dynamic-slice_fusion.3
  30.6 4.5 %collective-permute-start = (f32[1,1024]{1,0:T(1,128)}, f32[1,1024]{1,0:T(1,128)S(1)}, u32[]{:S(2)}, u32[]{:S(2)}) collective-permute-start(f32[1,1024]{1,0:T(1,128)} %get-tuple-element.32), channel_id=1, source_target_pairs={{0,3},{1,0},{2,1},{3,2},{4,7},{5,4},{6,5},{7,6},{8,11},{9,8},{10,9... | collective-permute-start | bytes 12296 | tf_op jit(solution)/shard_map/ppermute | solution.py:34
  35.1 1.9 %collective-permute-start.2 = (f32[1,1024]{1,0:T(1,128)S(1)}, f32[1,1024]{1,0:T(1,128)}, u32[]{:S(2)}, u32[]{:S(2)}) collective-permute-start(f32[1,1024]{1,0:T(1,128)S(1)} %get-tuple-element.33), channel_id=1, source_target_pairs={{0,1},{1,2},{2,3},{3,0},{4,5},{5,6},{6,7},{7,4},{8,9},{9,10},{10,1... | collective-permute-start | bytes 12296 | tf_op jit(solution)/shard_map/ppermute | solution.py:34
  37.0 0.0 copy-start.3
  37.0 3.7 %collective-permute-start.1 = (f32[1,1024]{1,0:T(1,128)S(1)}, f32[1,1024]{1,0:T(1,128)}, u32[]{:S(2)}, u32[]{:S(2)}) collective-permute-start(f32[1,1024]{1,0:T(1,128)S(1)} %get-tuple-element.34), channel_id=1, source_target_pairs={{0,2},{1,3},{2,0},{3,1},{4,6},{5,7},{6,4},{7,5},{8,10},{9,11},{10,... | collective-permute-start | bytes 12296 | tf_op jit(solution)/shard_map/ppermute | solution.py:34
  40.7 1.1 dynamic-slice_reduce_fusion
  41.8 0.6 slice.14
  43.0 0.1 reshape.77
  43.1 0.7 pad.16
  43.8 1.0 reshape.78
  44.8 0.6 collective-permute-done.1
  45.5 0.7 convert_reduce_fusion.1
  46.2 7.8 %collective-permute-start.3 = (bf16[4,4,32,2304]{3,2,1,0:T(8,128)(2,1)S(1)}, bf16[4,4,32,2304]{3,2,1,0:T(8,128)(2,1)}, u32[]{:S(2)}, u32[]{:S(2)}) collective-permute-start(bf16[4,4,32,2304]{3,2,1,0:T(8,128)(2,1)S(1)} %all-to-all-done.2.mine), channel_id=1, source_target_pairs={{0,16},{16,0},{32,48},{48,32},{64,80},{80,64},{96,112},{112,96},{1... | collective-permute-start | bytes 7077896 | tf_op jit(solution)/shard_map/ppermute | solution.py:20
  54.0 0.7 fusion.3
  54.7 0.1 reshape.79
  54.8 0.1 reshape.80
  55.0 0.1 broadcast_in_dim.64.code_col
  55.1 0.1 pad_add_fusion.where
  55.1 1.6 copy-done.1
  56.7 1.0 copy-done.2
  57.8 1.1 encoder.1
  58.9 13.1 %trunk.1 = (bf16[4,4,32,2560]{3,2,1,0:T(8,128)(2,1)S(1)}, bf16[4,4,32,2560]{3,2,1,0:T(8,128)(2,1)S(1)}) custom-call(s32[3]{0:T(128)S(1)} %pad_add_fusion.where, bf16[16,1024]{1,0:T(8,128)(2,1)S(1)} %broadcast_in_dim.59.context, f32[16,1024]{1,0:T(8,128)S(1)} %get-tuple-element.21.preact_in, bf16[16,1024]{1,0:T(8,128)(2,1)S(1)} %get-tuple-element.22.hidden_in, ...), custom_call_target="tpu_custom_call" | custom-call | flops 5435817984 | bytes 16777216 | tf_op jit(solution)/shard_map/trunk/pallas_call | solution.py:57
  72.0 1.9 %collective-permute-start.4 = (bf16[4,4,32,2560]{3,2,1,0:T(8,128)(2,1)S(1)}, bf16[4,4,32,2560]{3,2,1,0:T(8,128)(2,1)S(1)}, u32[]{:S(2)}, u32[]{:S(2)}) collective-permute-start(bf16[4,4,32,2560]{3,2,1,0:T(8,128)(2,1)S(1)} %get-tuple-element.27), channel_id=1, source_target_pairs={{0,16},{16,0},{32,48},{48,32},{64,80},{80,64},{96,112},{112,96},{1... | collective-permute-start | bytes 7864328 | tf_op jit(solution)/shard_map/ppermute | solution.py:20
  73.9 4.9 %collective-permute-done.4 = bf16[4,4,32,2560]{3,2,1,0:T(8,128)(2,1)S(1)} collective-permute-done((bf16[4,4,32,2560]{3,2,1,0:T(8,128)(2,1)S(1)}, bf16[4,4,32,2560]{3,2,1,0:T(8,128)(2,1)S(1)}, u32[]{:S(2)}, u32[]{:S(2)}) %collective-permute-start.4) | collective-permute-done | bytes 2621472 | tf_op jit(solution)/shard_map/ppermute | solution.py:20
  78.8 0.7 add_convert_fusion
  79.5 20.8 %all_to_all.40.pieces = bf16[4,4,32,2560]{3,2,1,0:T(8,128)(2,1)S(1)} all-to-all(bf16[4,4,32,2560]{3,2,1,0:T(8,128)(2,1)S(1)} %add_convert_fusion), channel_id=1, replica_groups={{0,1,2,3},{4,5,6,7},{8,9,10,11},{12,13,14,15},{16,20,24,28},{17,21,25,2..., dimensions={0} | all-to-all | bytes 5242880 | tf_op jit(solution)/shard_map/all_to_all | solution.py:277
  100.4 0.8 fold.1
  101.2 11.8 %all_to_all.41.pieces = bf16[4,32,3328]{2,1,0:T(8,128)(2,1)S(1)} all-to-all(bf16[4,32,3328]{2,1,0:T(8,128)(2,1)S(1)} %fold.1), channel_id=1, replica_groups={{0,4,8,12},{1,5,9,13},{2,6,10,14},{3,7,11,15},{16,17,18,19},{20,21,22,2..., dimensions={0} | all-to-all | bytes 1703936 | tf_op jit(solution)/shard_map/all_to_all | solution.py:277
  113.0 0.9 pack.1
  113.9 24.1 %all_to_all.42 = bf16[16,2,16,256]{3,2,1,0:T(8,128)(2,1)S(1)} all-to-all(bf16[16,2,16,256]{3,2,1,0:T(8,128)(2,1)S(1)} %bitcast.21), channel_id=1, replica_groups={{0,32,64,96,128,160,192,224,256,288,320,352,384,416,448,480},{16,48,80,..., dimensions={0} | all-to-all | bytes 524288 | tf_op jit(solution)/shard_map/all_to_all | solution.py:379
  138.1 22.0 %all_to_all.43 = bf16[16,2,16,256]{3,2,1,0:T(8,128)(2,1)S(1)} all-to-all(bf16[16,2,16,256]{3,2,1,0:T(8,128)(2,1)S(1)} %broadcast_in_dim.62), channel_id=1, replica_groups={{0,32,64,96,128,160,192,224,256,288,320,352,384,416,448,480},{16,48,80,..., dimensions={0} | all-to-all | bytes 524288 | tf_op jit(solution)/shard_map/all_to_all | solution.py:379
  160.1 8.6 %collective-permute-start.5 = (bf16[32,16,256]{2,1,0:T(8,128)(2,1)S(1)}, bf16[32,16,256]{2,1,0:T(8,128)(2,1)S(1)}, u32[]{:S(2)}, u32[]{:S(2)}) collective-permute-start(bf16[32,16,256]{2,1,0:T(8,128)(2,1)S(1)} %bitcast.19), channel_id=1, source_target_pairs={{0,16},{16,0},{32,48},{48,32},{64,80},{80,64},{96,112},{112,96},{1... | collective-permute-start | bytes 786440 | tf_op jit(solution)/shard_map/ppermute | solution.py:20
  168.7 1.1 collective-permute-done.5.theirs
  169.9 1.4 finish.1
  (19 shorter events, 0.2 us)
Async XLA Ops:
  0.6 40.0 %copy-start = (bf16[4,361,256]{2,0,1:T(4,128)(2,1)S(1)}, bf16[4,361,256]{2,0,1:T(4,128)(2,1)}, u32[]{:S(2)}) copy-start(bf16[4,361,256]{2,0,1:T(4,128)(2,1)} %param.17) | copy-start | bytes 2217988
  2.8 8.9 %all-to-all-start = ((s32[4,1,11]{2,1,0:T(1,128)}), s32[4,1,11]{2,1,0:T(1,128)S(1)}, u32[]{:S(2)}, u32[]{:S(2)}) async-start(s32[4,1,11]{2,1,0:T(1,128)} %broadcast_in_dim.54), calls=%async_computation | async-start | bytes 4096 | tf_op jit(solution)/shard_map/all_to_all | solution.py:38
  24.7 21.5 %all-to-all-start.2 = ((bf16[4,4,32,2304]{3,2,1,0:T(8,128)(2,1)}), bf16[4,4,32,2304]{3,2,1,0:T(8,128)(2,1)S(1)}, u32[]{:S(2)}, u32[]{:S(2)}) async-start(bf16[4,4,32,2304]{3,2,1,0:T(8,128)(2,1)} %broadcast_in_dim.56), calls=%async_computation.2 | async-start | bytes 4718592 | tf_op jit(solution)/shard_map/all_to_all | solution.py:277
  30.6 14.2 %collective-permute-start = (f32[1,1024]{1,0:T(1,128)}, f32[1,1024]{1,0:T(1,128)S(1)}, u32[]{:S(2)}, u32[]{:S(2)}) collective-permute-start(f32[1,1024]{1,0:T(1,128)} %get-tuple-element.32), channel_id=1, source_target_pairs={{0,3},{1,0},{2,1},{3,2},{4,7},{5,4},{6,5},{7,6},{8,11},{9,8},{10,9... | collective-permute-start | bytes 12296 | tf_op jit(solution)/shard_map/ppermute | solution.py:34
  35.1 9.7 %collective-permute-start.2 = (f32[1,1024]{1,0:T(1,128)S(1)}, f32[1,1024]{1,0:T(1,128)}, u32[]{:S(2)}, u32[]{:S(2)}) collective-permute-start(f32[1,1024]{1,0:T(1,128)S(1)} %get-tuple-element.33), channel_id=1, source_target_pairs={{0,1},{1,2},{2,3},{3,0},{4,5},{5,6},{6,7},{7,4},{8,9},{9,10},{10,1... | collective-permute-start | bytes 12296 | tf_op jit(solution)/shard_map/ppermute | solution.py:34
  37.0 21.9 %copy-start.3 = (bf16[3,256]{1,0:T(4,128)(2,1)S(1)}, bf16[3,256]{1,0:T(4,128)(2,1)}, u32[]{:S(2)}) copy-start(bf16[3,256]{1,0:T(4,128)(2,1)} %embed.1) | copy-start | bytes 4612
  37.0 8.4 %collective-permute-start.1 = (f32[1,1024]{1,0:T(1,128)S(1)}, f32[1,1024]{1,0:T(1,128)}, u32[]{:S(2)}, u32[]{:S(2)}) collective-permute-start(f32[1,1024]{1,0:T(1,128)S(1)} %get-tuple-element.34), channel_id=1, source_target_pairs={{0,2},{1,3},{2,0},{3,1},{4,6},{5,7},{6,4},{7,5},{8,10},{9,11},{10,... | collective-permute-start | bytes 12296 | tf_op jit(solution)/shard_map/ppermute | solution.py:34
  46.2 12.7 %collective-permute-start.3 = (bf16[4,4,32,2304]{3,2,1,0:T(8,128)(2,1)S(1)}, bf16[4,4,32,2304]{3,2,1,0:T(8,128)(2,1)}, u32[]{:S(2)}, u32[]{:S(2)}) collective-permute-start(bf16[4,4,32,2304]{3,2,1,0:T(8,128)(2,1)S(1)} %all-to-all-done.2.mine), channel_id=1, source_target_pairs={{0,16},{16,0},{32,48},{48,32},{64,80},{80,64},{96,112},{112,96},{1... | collective-permute-start | bytes 7077896 | tf_op jit(solution)/shard_map/ppermute | solution.py:20
  55.1 1.6 copy-start.1
  56.7 1.0 copy-start.2
  72.0 6.8 %collective-permute-start.4 = (bf16[4,4,32,2560]{3,2,1,0:T(8,128)(2,1)S(1)}, bf16[4,4,32,2560]{3,2,1,0:T(8,128)(2,1)S(1)}, u32[]{:S(2)}, u32[]{:S(2)}) collective-permute-start(bf16[4,4,32,2560]{3,2,1,0:T(8,128)(2,1)S(1)} %get-tuple-element.27), channel_id=1, source_target_pairs={{0,16},{16,0},{32,48},{48,32},{64,80},{80,64},{96,112},{112,96},{1... | collective-permute-start | bytes 7864328 | tf_op jit(solution)/shard_map/ppermute | solution.py:20
  160.1 9.8 %collective-permute-start.5 = (bf16[32,16,256]{2,1,0:T(8,128)(2,1)S(1)}, bf16[32,16,256]{2,1,0:T(8,128)(2,1)S(1)}, u32[]{:S(2)}, u32[]{:S(2)}) collective-permute-start(bf16[32,16,256]{2,1,0:T(8,128)(2,1)S(1)} %bitcast.19), channel_id=1, source_target_pairs={{0,16},{16,0},{32,48},{48,32},{64,80},{80,64},{96,112},{112,96},{1... | collective-permute-start | bytes 786440 | tf_op jit(solution)/shard_map/ppermute | solution.py:20

commit v9 on v8

--- a/solution.py
+++ b/solution.py
@@ -18,10 +18,6 @@
 
 def swap(block, axis, bits):
     return lax.ppermute(block, axis, [(i, i ^ bits) for i in range(lax.axis_size(axis))])
-
-
-def exchange(blocks, axis):
-    return lax.all_to_all(blocks, axis, 0, 0, tiled=True)
 
 
 def turned(block, axis, distance):
@@ -151,11 +147,12 @@
         dconv = rscales[block] * (dnorm - value * inner)
         gt[block] = nn(dconv.T.astype(BF16), patches[block]).astype(BF16)
         buf[FRONT : FRONT + ROWS, :] = dconv.astype(BF16).astype(F32)
-        moved = [
-            buf[FRONT - shift : FRONT - shift + ROWS, :].astype(BF16) for shift in TAP_SHIFTS
-        ]
-        weights = [wt[block, :, tap * channels : (tap + 1) * channels] for tap in range(9)]
-        total = upper + nn(jnp.concatenate(moved, axis=1), jnp.concatenate(weights, axis=0))
+        total = upper
+        for tap, shift in enumerate(TAP_SHIFTS):
+            total += nn(
+                buf[FRONT - shift : FRONT - shift + ROWS, :].astype(BF16),
+                wt[block, :, tap * channels : (tap + 1) * channels],
+            )
         grad[...] = total.astype(BF16).astype(F32) * mask
         return carry
 
@@ -283,7 +280,8 @@
     state = lax.broadcasted_iota(jnp.int32, asked.shape, 0)
     asked = jnp.sum(jnp.where(state == s, asked, 0), axis=0, keepdims=True)
     count = asked[:, slots]
-    asked = exchange(jnp.broadcast_to(asked, (4, slots + 1)), "shard")
+    asked = jnp.broadcast_to(jnp.pad(asked, ((0, 0), (0, 127 - slots))), (8, 128))
+    asked = lax.all_gather(asked[None], "shard", axis=0, tiled=True)[:, 0, : slots + 1]
 
     unit = lax.dynamic_slice_in_dim(conv_weight[0].T, c * 32, 32, 0)
     unit = jnp.broadcast_to(unit[None], (4,) + unit.shape)

time: 172 us -> 167 us (0.971)
  blocking collectives: 90 us -> 86.1 us
  waiting for transfers between devices: 9.77 us -> 6.43 us
  starting transfers between devices: 36.9 us -> 39.2 us
    all_to_all x3 -> x2, blocking collectives: 43.9 us -> 32.6 us  [ring(): lax.all_to_all(blocks, ('dp', 'section', 'shard'), 0, 0, axis_index_group...]
    all_gather x0 -> x1, blocking collectives: none -> 7.64 us  [body(): lax.all_gather(asked[None], 'shard', axis=0, tiled=True)[:, 0, :slots + 1]]
    all_to_all x1 -> x2, starting transfers between devices: 3.63 us -> 8.64 us  [ring(): lax.all_to_all(blocks, ('dp', 'section', 'shard'), 0, 0, axis_index_group...]
    all_to_all x1 -> x0, starting transfers between devices: 4.84 us -> none  [exchange(): return lax.all_to_all(blocks, axis, 0, 0, tiled=True)]
    all_to_all x1 -> x0, waiting for transfers between devices: 3.11 us -> none  [exchange(): return lax.all_to_all(blocks, axis, 0, 0, tiled=True)]
    ppermute x3, starting transfers between devices: 18.4 us -> 20.5 us  [swap(): lax.ppermute(block, axis, [(i, i ^ bits) for i in range(lax.axis_size(axi...]
  transfers between devices with their start and end apart: 8 -> 8, of which waited for: 4 -> 3; matrix products, arithmetic and copies ran while one was open for 5% -> 5% of each run, Pallas kernels for 1% -> 1%
where the time goes in v9:
time: 167 us; the launch traced here: 166 us
  blocking collectives  86.1 us (52%)
  starting transfers between devices  39.2 us (23%)
  Pallas kernels  17.3 us (10%)
  local copies, waits for them, and re-layouts  12.2 us (7%)
  waiting for transfers between devices  6.43 us (4%)
  other arithmetic  2.47 us (1%)
    all_to_all x2, blocking collectives, along_z(): lax.all_to_all(blocks, 'dp', 0, 0, axis_index_groups=line, tiled=True)  45.8 us
    all_to_all x2, blocking collectives, ring(): lax.all_to_all(blocks, ('dp', 'section', 'shard'), 0, 0, axis_index_group...  32.6 us
    ppermute x3, starting transfers between devices, swap(): lax.ppermute(block, axis, [(i, i ^ bits) for i in range(lax.axis_size(axi...  20.5 us
    pallas_call x5, Pallas kernels, call(): pl.pallas_call(kernel, out_shape=outs, in_specs=[pl.BlockSpec(memory_spac...  17.3 us
    ppermute x3, starting transfers between devices, turned(): lax.ppermute(block, axis, [(i, (i + distance) % size) for i in range(size)])  10.1 us
    all_to_all x2, starting transfers between devices, ring(): lax.all_to_all(blocks, ('dp', 'section', 'shard'), 0, 0, axis_index_group...  8.64 us
    all_gather x1, blocking collectives, body(): lax.all_gather(asked[None], 'shard', axis=0, tiled=True)[:, 0, :slots + 1]  7.64 us
    ppermute x3, waiting for transfers between devices, swap(): lax.ppermute(block, axis, [(i, i ^ bits) for i in range(lax.axis_size(axi...  6.02 us
  transfers between devices with their start and end apart: 8, of which 3 were waited for; matrix products, arithmetic and copies ran while one was open for 5% of the time, Pallas kernels for 1%

profile of v9, /device:TPU:1, one launch (start us, length us, event | category | flops | bytes accessed | tf_op | source)
XLA Modules:
  0.0 166.5 jit_solution(10055710393227676006)
XLA Ops:
  0.6 0.0 copy-start
  0.7 1.0 dynamic-slice_bitcast_fusion
  1.7 0.8 broadcast_in_dim.50
  2.5 5.0 %all-to-all-start = ((bf16[4,32,2304]{2,1,0:T(8,128)(2,1)}), bf16[4,32,2304]{2,1,0:T(8,128)(2,1)S(1)}, u32[]{:S(2)}, u32[]{:S(2)}) async-start(bf16[4,32,2304]{2,1,0:T(8,128)(2,1)} %broadcast_in_dim.50), calls=%async_computation | async-start | bytes 1179648 | tf_op jit(solution)/shard_map/all_to_all | solution.py:274
  7.5 0.7 copy.18
  8.3 0.8 fusion
  9.0 7.6 %all-gather.1 = s32[4,1,128]{2,1,0:T(1,128)S(1)} all-gather(s32[1,1,128]{2,1,0:T(1,128)S(1)} %pad_bitcast_fusion), channel_id=3, replica_groups=mesh['dp'=32,'section'=4,'shard'=4] {'shard'}, dimensions={0}, use_global_device_ids=true | all-gather | bytes 2560 | tf_op jit(solution)/shard_map/all_gather | solution.py:284
  16.7 1.6 broadcast_in_dim.51
  18.3 3.6 %all-to-all-start.1 = ((bf16[4,4,32,2304]{3,2,1,0:T(8,128)(2,1)}), bf16[4,4,32,2304]{3,2,1,0:T(8,128)(2,1)S(1)}, u32[]{:S(2)}, u32[]{:S(2)}) async-start(bf16[4,4,32,2304]{3,2,1,0:T(8,128)(2,1)} %broadcast_in_dim.51), calls=%async_computation.1 | async-start | bytes 4718592 | tf_op jit(solution)/shard_map/all_to_all | solution.py:274
  22.0 0.1 copy.19
  22.1 0.2 slice_reduce_fusion
  22.3 0.1 convert_reduce_fusion
  22.4 1.2 fusion.4
  23.6 0.6 constant_dynamic-slice_fusion.3
  24.2 4.5 %collective-permute-start = (f32[1,1024]{1,0:T(1,128)}, f32[1,1024]{1,0:T(1,128)S(1)}, u32[]{:S(2)}, u32[]{:S(2)}) collective-permute-start(f32[1,1024]{1,0:T(1,128)} %get-tuple-element.32), channel_id=1, source_target_pairs={{0,3},{1,0},{2,1},{3,2},{4,7},{5,4},{6,5},{7,6},{8,11},{9,8},{10,9... | collective-permute-start | bytes 12296 | tf_op jit(solution)/shard_map/ppermute | solution.py:30
  28.7 1.9 %collective-permute-start.2 = (f32[1,1024]{1,0:T(1,128)S(1)}, f32[1,1024]{1,0:T(1,128)}, u32[]{:S(2)}, u32[]{:S(2)}) collective-permute-start(f32[1,1024]{1,0:T(1,128)S(1)} %get-tuple-element.33), channel_id=1, source_target_pairs={{0,1},{1,2},{2,3},{3,0},{4,5},{5,6},{6,7},{7,4},{8,9},{9,10},{10,1... | collective-permute-start | bytes 12296 | tf_op jit(solution)/shard_map/ppermute | solution.py:30
  30.7 0.0 copy-start.3
  30.7 3.7 %collective-permute-start.1 = (f32[1,1024]{1,0:T(1,128)S(1)}, f32[1,1024]{1,0:T(1,128)}, u32[]{:S(2)}, u32[]{:S(2)}) collective-permute-start(f32[1,1024]{1,0:T(1,128)S(1)} %get-tuple-element.34), channel_id=1, source_target_pairs={{0,2},{1,3},{2,0},{3,1},{4,6},{5,7},{6,4},{7,5},{8,10},{9,11},{10,... | collective-permute-start | bytes 12296 | tf_op jit(solution)/shard_map/ppermute | solution.py:30
  34.4 1.1 dynamic-slice_reduce_fusion
  35.4 0.6 slice.18
  36.7 0.1 reshape.74
  36.7 0.7 pad.24
  37.5 1.0 reshape.75
  38.5 0.0 collective-permute-done
  38.5 0.4 collective-permute-done.1
  38.9 0.7 convert_reduce_fusion.1
  39.6 9.9 %collective-permute-start.3 = (bf16[4,4,32,2304]{3,2,1,0:T(8,128)(2,1)S(1)}, bf16[4,4,32,2304]{3,2,1,0:T(8,128)(2,1)}, u32[]{:S(2)}, u32[]{:S(2)}) collective-permute-start(bf16[4,4,32,2304]{3,2,1,0:T(8,128)(2,1)S(1)} %all-to-all-done.1.mine), channel_id=1, source_target_pairs={{0,16},{16,0},{32,48},{48,32},{64,80},{80,64},{96,112},{112,96},{1... | collective-permute-start | bytes 7077896 | tf_op jit(solution)/shard_map/ppermute | solution.py:20
  49.6 0.7 fusion.3
  50.3 0.1 reshape.76
  50.4 0.1 reshape.77
  50.5 0.1 broadcast_in_dim.58.code_col
  50.6 0.1 pad_add_fusion.where
  50.7 1.6 copy-done.1
  52.3 1.0 copy-done.2
  53.3 1.1 encoder.1
  54.5 13.0 %trunk.1 = (bf16[4,4,32,2560]{3,2,1,0:T(8,128)(2,1)S(1)}, bf16[4,4,32,2560]{3,2,1,0:T(8,128)(2,1)S(1)}) custom-call(s32[3]{0:T(128)S(1)} %pad_add_fusion.where, bf16[16,1024]{1,0:T(8,128)(2,1)S(1)} %broadcast_in_dim.53.context, f32[16,1024]{1,0:T(8,128)S(1)} %get-tuple-element.21.preact_in, bf16[16,1024]{1,0:T(8,128)(2,1)S(1)} %get-tuple-element.22.hidden_in, ...), custom_call_target="tpu_custom_call" | custom-call | flops 5435817984 | bytes 16777216 | tf_op jit(solution)/shard_map/trunk/pallas_call | solution.py:53
  67.5 1.9 %collective-permute-start.4 = (bf16[4,4,32,2560]{3,2,1,0:T(8,128)(2,1)S(1)}, bf16[4,4,32,2560]{3,2,1,0:T(8,128)(2,1)S(1)}, u32[]{:S(2)}, u32[]{:S(2)}) collective-permute-start(bf16[4,4,32,2560]{3,2,1,0:T(8,128)(2,1)S(1)} %get-tuple-element.27), channel_id=1, source_target_pairs={{0,16},{16,0},{32,48},{48,32},{64,80},{80,64},{96,112},{112,96},{1... | collective-permute-start | bytes 7864328 | tf_op jit(solution)/shard_map/ppermute | solution.py:20
  69.4 4.9 %collective-permute-done.4 = bf16[4,4,32,2560]{3,2,1,0:T(8,128)(2,1)S(1)} collective-permute-done((bf16[4,4,32,2560]{3,2,1,0:T(8,128)(2,1)S(1)}, bf16[4,4,32,2560]{3,2,1,0:T(8,128)(2,1)S(1)}, u32[]{:S(2)}, u32[]{:S(2)}) %collective-permute-start.4) | collective-permute-done | bytes 2621472 | tf_op jit(solution)/shard_map/ppermute | solution.py:20
  74.3 0.7 add_convert_fusion
  75.1 20.8 %all_to_all.30.pieces = bf16[4,4,32,2560]{3,2,1,0:T(8,128)(2,1)S(1)} all-to-all(bf16[4,4,32,2560]{3,2,1,0:T(8,128)(2,1)S(1)} %add_convert_fusion), channel_id=1, replica_groups={{0,1,2,3},{4,5,6,7},{8,9,10,11},{12,13,14,15},{16,20,24,28},{17,21,25,2..., dimensions={0} | all-to-all | bytes 5242880 | tf_op jit(solution)/shard_map/all_to_all | solution.py:274
  95.9 0.8 fold.1
  96.7 11.8 %all_to_all.31.pieces = bf16[4,32,3328]{2,1,0:T(8,128)(2,1)S(1)} all-to-all(bf16[4,32,3328]{2,1,0:T(8,128)(2,1)S(1)} %fold.1), channel_id=1, replica_groups={{0,4,8,12},{1,5,9,13},{2,6,10,14},{3,7,11,15},{16,17,18,19},{20,21,22,2..., dimensions={0} | all-to-all | bytes 1703936 | tf_op jit(solution)/shard_map/all_to_all | solution.py:274
  108.5 0.9 pack.1
  109.5 23.8 %all_to_all.32 = bf16[16,2,16,256]{3,2,1,0:T(8,128)(2,1)S(1)} all-to-all(bf16[16,2,16,256]{3,2,1,0:T(8,128)(2,1)S(1)} %bitcast.24), channel_id=1, replica_groups={{0,32,64,96,128,160,192,224,256,288,320,352,384,416,448,480},{16,48,80,..., dimensions={0} | all-to-all | bytes 524288 | tf_op jit(solution)/shard_map/all_to_all | solution.py:377
  133.4 22.0 %all_to_all.33 = bf16[16,2,16,256]{3,2,1,0:T(8,128)(2,1)S(1)} all-to-all(bf16[16,2,16,256]{3,2,1,0:T(8,128)(2,1)S(1)} %broadcast_in_dim.56), channel_id=1, replica_groups={{0,32,64,96,128,160,192,224,256,288,320,352,384,416,448,480},{16,48,80,..., dimensions={0} | all-to-all | bytes 524288 | tf_op jit(solution)/shard_map/all_to_all | solution.py:377
  155.3 8.6 %collective-permute-start.5 = (bf16[32,16,256]{2,1,0:T(8,128)(2,1)S(1)}, bf16[32,16,256]{2,1,0:T(8,128)(2,1)S(1)}, u32[]{:S(2)}, u32[]{:S(2)}) collective-permute-start(bf16[32,16,256]{2,1,0:T(8,128)(2,1)S(1)} %bitcast.22), channel_id=1, source_target_pairs={{0,16},{16,0},{32,48},{48,32},{64,80},{80,64},{96,112},{112,96},{1... | collective-permute-start | bytes 786440 | tf_op jit(solution)/shard_map/ppermute | solution.py:20
  164.0 1.1 collective-permute-done.5.theirs
  165.1 1.4 finish.1
  (19 shorter events, 0.1 us)
Async XLA Ops:
  0.6 33.7 %copy-start = (bf16[4,361,256]{2,0,1:T(4,128)(2,1)S(1)}, bf16[4,361,256]{2,0,1:T(4,128)(2,1)}, u32[]{:S(2)}) copy-start(bf16[4,361,256]{2,0,1:T(4,128)(2,1)} %param.17) | copy-start | bytes 2217988
  2.5 14.2 %all-to-all-start = ((bf16[4,32,2304]{2,1,0:T(8,128)(2,1)}), bf16[4,32,2304]{2,1,0:T(8,128)(2,1)S(1)}, u32[]{:S(2)}, u32[]{:S(2)}) async-start(bf16[4,32,2304]{2,1,0:T(8,128)(2,1)} %broadcast_in_dim.50), calls=%async_computation | async-start | bytes 1179648 | tf_op jit(solution)/shard_map/all_to_all | solution.py:274
  18.3 21.3 %all-to-all-start.1 = ((bf16[4,4,32,2304]{3,2,1,0:T(8,128)(2,1)}), bf16[4,4,32,2304]{3,2,1,0:T(8,128)(2,1)S(1)}, u32[]{:S(2)}, u32[]{:S(2)}) async-start(bf16[4,4,32,2304]{3,2,1,0:T(8,128)(2,1)} %broadcast_in_dim.51), calls=%async_computation.1 | async-start | bytes 4718592 | tf_op jit(solution)/shard_map/all_to_all | solution.py:274
  24.2 14.2 %collective-permute-start = (f32[1,1024]{1,0:T(1,128)}, f32[1,1024]{1,0:T(1,128)S(1)}, u32[]{:S(2)}, u32[]{:S(2)}) collective-permute-start(f32[1,1024]{1,0:T(1,128)} %get-tuple-element.32), channel_id=1, source_target_pairs={{0,3},{1,0},{2,1},{3,2},{4,7},{5,4},{6,5},{7,6},{8,11},{9,8},{10,9... | collective-permute-start | bytes 12296 | tf_op jit(solution)/shard_map/ppermute | solution.py:30
  28.7 9.7 %collective-permute-start.2 = (f32[1,1024]{1,0:T(1,128)S(1)}, f32[1,1024]{1,0:T(1,128)}, u32[]{:S(2)}, u32[]{:S(2)}) collective-permute-start(f32[1,1024]{1,0:T(1,128)S(1)} %get-tuple-element.33), channel_id=1, source_target_pairs={{0,1},{1,2},{2,3},{3,0},{4,5},{5,6},{6,7},{7,4},{8,9},{9,10},{10,1... | collective-permute-start | bytes 12296 | tf_op jit(solution)/shard_map/ppermute | solution.py:30
  30.7 23.8 %copy-start.3 = (bf16[3,256]{1,0:T(4,128)(2,1)S(1)}, bf16[3,256]{1,0:T(4,128)(2,1)}, u32[]{:S(2)}) copy-start(bf16[3,256]{1,0:T(4,128)(2,1)} %embed.1) | copy-start | bytes 4612
  30.7 8.2 %collective-permute-start.1 = (f32[1,1024]{1,0:T(1,128)S(1)}, f32[1,1024]{1,0:T(1,128)}, u32[]{:S(2)}, u32[]{:S(2)}) collective-permute-start(f32[1,1024]{1,0:T(1,128)S(1)} %get-tuple-element.34), channel_id=1, source_target_pairs={{0,2},{1,3},{2,0},{3,1},{4,6},{5,7},{6,4},{7,5},{8,10},{9,11},{10,... | collective-permute-start | bytes 12296 | tf_op jit(solution)/shard_map/ppermute | solution.py:30
  39.6 14.8 %collective-permute-start.3 = (bf16[4,4,32,2304]{3,2,1,0:T(8,128)(2,1)S(1)}, bf16[4,4,32,2304]{3,2,1,0:T(8,128)(2,1)}, u32[]{:S(2)}, u32[]{:S(2)}) collective-permute-start(bf16[4,4,32,2304]{3,2,1,0:T(8,128)(2,1)S(1)} %all-to-all-done.1.mine), channel_id=1, source_target_pairs={{0,16},{16,0},{32,48},{48,32},{64,80},{80,64},{96,112},{112,96},{1... | collective-permute-start | bytes 7077896 | tf_op jit(solution)/shard_map/ppermute | solution.py:20
  50.7 1.6 copy-start.1
  52.3 1.0 copy-start.2
  67.5 6.8 %collective-permute-start.4 = (bf16[4,4,32,2560]{3,2,1,0:T(8,128)(2,1)S(1)}, bf16[4,4,32,2560]{3,2,1,0:T(8,128)(2,1)S(1)}, u32[]{:S(2)}, u32[]{:S(2)}) collective-permute-start(bf16[4,4,32,2560]{3,2,1,0:T(8,128)(2,1)S(1)} %get-tuple-element.27), channel_id=1, source_target_pairs={{0,16},{16,0},{32,48},{48,32},{64,80},{80,64},{96,112},{112,96},{1... | collective-permute-start | bytes 7864328 | tf_op jit(solution)/shard_map/ppermute | solution.py:20
  155.3 9.8 %collective-permute-start.5 = (bf16[32,16,256]{2,1,0:T(8,128)(2,1)S(1)}, bf16[32,16,256]{2,1,0:T(8,128)(2,1)S(1)}, u32[]{:S(2)}, u32[]{:S(2)}) collective-permute-start(bf16[32,16,256]{2,1,0:T(8,128)(2,1)S(1)} %bitcast.22), channel_id=1, source_target_pairs={{0,16},{16,0},{32,48},{48,32},{64,80},{80,64},{96,112},{112,96},{1... | collective-permute-start | bytes 786440 | tf_op jit(solution)/shard_map/ppermute | solution.py:20

commit v10 on v6

--- a/solution.py
+++ b/solution.py
@@ -11,13 +11,18 @@
 FRONT = 24
 NORM_EPS = 1e-05
 TAP_SHIFTS = [(a - 1) * PITCH + (b - 1) for a in range(3) for b in range(3)]
-VMEM_BYTES = 40 * 1024 * 1024
+VMEM_BYTES = 34 * 1024 * 1024
 F32 = jnp.float32
 BF16 = jnp.bfloat16
 
 
 def swap(block, axis, bits):
     return lax.ppermute(block, axis, [(i, i ^ bits) for i in range(lax.axis_size(axis))])
+
+
+def turned(block, axis, distance):
+    size = lax.axis_size(axis)
+    return lax.ppermute(block, axis, [(i, (i + distance) % size) for i in range(size)])
 
 
 def turned(block, axis, distance):
@@ -48,7 +53,8 @@
         return pl.pallas_call(
             kernel,
             out_shape=outs,
-            in_specs=[pl.BlockSpec(memory_space=pltpu.SMEM)] + [spec] * len(arrays),
+            in_specs=[pl.BlockSpec(memory_space=pltpu.SMEM)]
+            + [spec] * len(arrays),
             out_specs=tuple(spec for _ in outs),
             scratch_shapes=scratch,
             compiler_params=pltpu.CompilerParams(vmem_limit_bytes=VMEM_BYTES),
@@ -100,6 +106,7 @@
     buf[FRONT + ROWS :, :] = jnp.zeros((FRONT, buf.shape[1]), F32)
     buf[FRONT : FRONT + ROWS, :] = start
     channels = start.shape[1]
+    taps = wt.shape[2]
 
     def forward(block, carry):
         for tap, shift in enumerate(TAP_SHIFTS):
@@ -115,7 +122,7 @@
         buf[FRONT : FRONT + ROWS, :] = stream.astype(BF16).astype(F32) * mask
         return carry
 
-    lax.fori_loop(0, 4, forward, 0)
+    lax.fori_loop(0, 4, forward, 0, unroll=True)
     grad[...] = cotangent[...].astype(F32)
 
     def backward(step, carry):
@@ -137,7 +144,7 @@
         grad[...] = total.astype(BF16).astype(F32) * mask
         return carry
 
-    lax.fori_loop(0, 4, backward, 0)
+    lax.fori_loop(0, 4, backward, 0, unroll=True)
 
     kind = lax.broadcasted_iota(jnp.int32, (16, ROWS), 0)
     codes = code_row[...]
@@ -158,7 +165,6 @@
             place += 1
     tail = vectors[...].astype(BF16)
     empty = jnp.zeros(tail.shape, BF16)
-    taps = gt.shape[2]
     for core, pieces, first, second in ((c, own, tail, empty), (1 - c, other, empty, tail)):
         for outer in range(4):
             for inner in range(4):
@@ -262,12 +268,13 @@
     state = lax.broadcasted_iota(jnp.int32, asked.shape, 0)
     asked = jnp.sum(jnp.where(state == s, asked, 0), axis=0, keepdims=True)
     count = asked[:, slots]
-    asked = exchange(jnp.broadcast_to(asked, (4, slots + 1)), "shard")
+    asked = jnp.broadcast_to(jnp.pad(asked, ((0, 0), (0, 127 - slots))), (8, 128))
+    asked = lax.all_gather(asked[None], "shard", axis=0, tiled=True)[:, 0, : slots + 1]
 
     unit = lax.dynamic_slice_in_dim(conv_weight[0].T, c * 32, 32, 0)
     unit = jnp.broadcast_to(unit[None], (4,) + unit.shape)
-    asked, unit = lax.optimization_barrier((asked, unit))
     mine = ring(unit, along_x)
+    asked, mine = lax.optimization_barrier((asked, mine))
     mine = ring(jnp.broadcast_to(mine[None], (4,) + mine.shape), along_y)
 
     live = lax.broadcasted_iota(jnp.int32, (4, slots), 1) < asked[:, slots:]

time: 172 us -> 170 us (0.988)
  blocking collectives: 90 us -> 86.1 us
  waiting for transfers between devices: 9.77 us -> 6.21 us
  Pallas kernels: 17 us -> 19.9 us
  starting transfers between devices: 36.9 us -> 39.6 us
    all_to_all x3 -> x2, blocking collectives: 43.9 us -> 32.6 us  [ring(): lax.all_to_all(blocks, ('dp', 'section', 'shard'), 0, 0, axis_index_group...]
    all_gather x0 -> x1, blocking collectives: none -> 7.64 us  [body(): lax.all_gather(asked[None], 'shard', axis=0, tiled=True)[:, 0, :slots + 1]]
    all_to_all x1 -> x2, starting transfers between devices: 3.63 us -> 8.64 us  [ring(): lax.all_to_all(blocks, ('dp', 'section', 'shard'), 0, 0, axis_index_group...]
    all_to_all x1 -> x0, starting transfers between devices: 4.84 us -> none  [exchange(): return lax.all_to_all(blocks, axis, 0, 0, tiled=True)]
    all_to_all x1 -> x0, waiting for transfers between devices: 3.11 us -> none  [exchange(): return lax.all_to_all(blocks, axis, 0, 0, tiled=True)]
    pallas_call x5, Pallas kernels: 17 us -> 19.9 us  [call(): pl.pallas_call(kernel, out_shape=outs, in_specs=[pl.BlockSpec(memory_spac...]
    ppermute x3, starting transfers between devices: 18.4 us -> 20.9 us  [swap(): lax.ppermute(block, axis, [(i, i ^ bits) for i in range(lax.axis_size(axi...]
  transfers between devices with their start and end apart: 8 -> 8, of which waited for: 4 -> 3; matrix products, arithmetic and copies ran while one was open for 5% -> 5% of each run, Pallas kernels for 1% -> 1%
where the time goes in v10:
time: 170 us; the launch traced here: 169 us
  blocking collectives  86.1 us (51%)
  starting transfers between devices  39.6 us (23%)
  Pallas kernels  19.9 us (12%)
  local copies, waits for them, and re-layouts  12.2 us (7%)
  waiting for transfers between devices  6.21 us (4%)
  other arithmetic  2.5 us (1%)
    all_to_all x2, blocking collectives, along_z(): lax.all_to_all(blocks, 'dp', 0, 0, axis_index_groups=line, tiled=True)  45.8 us
    all_to_all x2, blocking collectives, ring(): lax.all_to_all(blocks, ('dp', 'section', 'shard'), 0, 0, axis_index_group...  32.6 us
    ppermute x3, starting transfers between devices, swap(): lax.ppermute(block, axis, [(i, i ^ bits) for i in range(lax.axis_size(axi...  20.9 us
    pallas_call x5, Pallas kernels, call(): pl.pallas_call(kernel, out_shape=outs, in_specs=[pl.BlockSpec(memory_spac...  19.9 us
    ppermute x3, starting transfers between devices, turned(): lax.ppermute(block, axis, [(i, (i + distance) % size) for i in range(size)])  10.1 us
    all_to_all x2, starting transfers between devices, ring(): lax.all_to_all(blocks, ('dp', 'section', 'shard'), 0, 0, axis_index_group...  8.64 us
    all_gather x1, blocking collectives, body(): lax.all_gather(asked[None], 'shard', axis=0, tiled=True)[:, 0, :slots + 1]  7.64 us
    ppermute x3, waiting for transfers between devices, swap(): lax.ppermute(block, axis, [(i, i ^ bits) for i in range(lax.axis_size(axi...  5.8 us
  transfers between devices with their start and end apart: 8, of which 3 were waited for; matrix products, arithmetic and copies ran while one was open for 5% of the time, Pallas kernels for 1%

profile of v10, /device:TPU:1, one launch (start us, length us, event | category | flops | bytes accessed | tf_op | source)
XLA Modules:
  0.0 169.4 jit_solution(9208436872390604260)
XLA Ops:
  0.6 0.0 copy-start
  0.7 1.0 dynamic-slice_bitcast_fusion
  1.7 0.8 broadcast_in_dim.50
  2.5 5.0 %all-to-all-start = ((bf16[4,32,2304]{2,1,0:T(8,128)(2,1)}), bf16[4,32,2304]{2,1,0:T(8,128)(2,1)S(1)}, u32[]{:S(2)}, u32[]{:S(2)}) async-start(bf16[4,32,2304]{2,1,0:T(8,128)(2,1)} %broadcast_in_dim.50), calls=%async_computation | async-start | bytes 1179648 | tf_op jit(solution)/shard_map/all_to_all | solution.py:262
  7.5 0.7 copy.18
  8.3 0.8 fusion
  9.0 7.6 %all-gather.1 = s32[4,1,128]{2,1,0:T(1,128)S(1)} all-gather(s32[1,1,128]{2,1,0:T(1,128)S(1)} %pad_bitcast_fusion), channel_id=3, replica_groups=mesh['dp'=32,'section'=4,'shard'=4] {'shard'}, dimensions={0}, use_global_device_ids=true | all-gather | bytes 2560 | tf_op jit(solution)/shard_map/all_gather | solution.py:272
  16.7 1.6 broadcast_in_dim.51
  18.3 3.6 %all-to-all-start.1 = ((bf16[4,4,32,2304]{3,2,1,0:T(8,128)(2,1)}), bf16[4,4,32,2304]{3,2,1,0:T(8,128)(2,1)S(1)}, u32[]{:S(2)}, u32[]{:S(2)}) async-start(bf16[4,4,32,2304]{3,2,1,0:T(8,128)(2,1)} %broadcast_in_dim.51), calls=%async_computation.1 | async-start | bytes 4718592 | tf_op jit(solution)/shard_map/all_to_all | solution.py:262
  22.0 0.1 copy.19
  22.1 0.2 slice_reduce_fusion
  22.3 0.1 convert_reduce_fusion
  22.4 1.2 fusion.4
  23.6 0.6 constant_dynamic-slice_fusion.3
  24.2 4.5 %collective-permute-start = (f32[1,1024]{1,0:T(1,128)}, f32[1,1024]{1,0:T(1,128)S(1)}, u32[]{:S(2)}, u32[]{:S(2)}) collective-permute-start(f32[1,1024]{1,0:T(1,128)} %get-tuple-element.32), channel_id=1, source_target_pairs={{0,3},{1,0},{2,1},{3,2},{4,7},{5,4},{6,5},{7,6},{8,11},{9,8},{10,9... | collective-permute-start | bytes 12296 | tf_op jit(solution)/shard_map/ppermute | solution.py:30
  28.7 1.9 %collective-permute-start.2 = (f32[1,1024]{1,0:T(1,128)S(1)}, f32[1,1024]{1,0:T(1,128)}, u32[]{:S(2)}, u32[]{:S(2)}) collective-permute-start(f32[1,1024]{1,0:T(1,128)S(1)} %get-tuple-element.33), channel_id=1, source_target_pairs={{0,1},{1,2},{2,3},{3,0},{4,5},{5,6},{6,7},{7,4},{8,9},{9,10},{10,1... | collective-permute-start | bytes 12296 | tf_op jit(solution)/shard_map/ppermute | solution.py:30
  30.7 0.0 copy-start.3
  30.7 3.7 %collective-permute-start.1 = (f32[1,1024]{1,0:T(1,128)S(1)}, f32[1,1024]{1,0:T(1,128)}, u32[]{:S(2)}, u32[]{:S(2)}) collective-permute-start(f32[1,1024]{1,0:T(1,128)S(1)} %get-tuple-element.34), channel_id=1, source_target_pairs={{0,2},{1,3},{2,0},{3,1},{4,6},{5,7},{6,4},{7,5},{8,10},{9,11},{10,... | collective-permute-start | bytes 12296 | tf_op jit(solution)/shard_map/ppermute | solution.py:30
  34.4 1.1 dynamic-slice_reduce_fusion
  35.4 0.6 slice.18
  36.7 0.1 reshape.74
  36.7 0.7 pad.24
  37.5 1.0 reshape.75
  38.5 0.0 collective-permute-done
  38.5 0.4 collective-permute-done.1
  38.9 0.7 convert_reduce_fusion.1
  39.6 10.1 %collective-permute-start.3 = (bf16[4,4,32,2304]{3,2,1,0:T(8,128)(2,1)S(1)}, bf16[4,4,32,2304]{3,2,1,0:T(8,128)(2,1)}, u32[]{:S(2)}, u32[]{:S(2)}) collective-permute-start(bf16[4,4,32,2304]{3,2,1,0:T(8,128)(2,1)S(1)} %all-to-all-done.1.mine), channel_id=1, source_target_pairs={{0,16},{16,0},{32,48},{48,32},{64,80},{80,64},{96,112},{112,96},{1... | collective-permute-start | bytes 7077896 | tf_op jit(solution)/shard_map/ppermute | solution.py:20
  49.7 0.7 fusion.3
  50.5 0.1 reshape.76
  50.6 0.1 reshape.77
  50.7 0.1 broadcast_in_dim.58.code_col
  50.8 0.1 pad_add_fusion.where
  50.9 1.6 copy-done.1
  52.5 1.0 copy-done.2
  53.5 1.1 encoder.1
  54.6 15.7 %trunk.1 = (bf16[4,4,32,2560]{3,2,1,0:T(8,128)(2,1)S(1)}, bf16[4,4,32,2560]{3,2,1,0:T(8,128)(2,1)S(1)}) custom-call(s32[3]{0:T(128)S(1)} %pad_add_fusion.where, bf16[16,1024]{1,0:T(8,128)(2,1)S(1)} %broadcast_in_dim.53.context, f32[16,1024]{1,0:T(8,128)S(1)} %get-tuple-element.21.preact_in, bf16[16,1024]{1,0:T(8,128)(2,1)S(1)} %get-tuple-element.22.hidden_in, ...), custom_call_target="tpu_custom_call" | custom-call | flops 5435817984 | bytes 16777216 | tf_op jit(solution)/shard_map/trunk/pallas_call | solution.py:53
  70.3 2.1 %collective-permute-start.4 = (bf16[4,4,32,2560]{3,2,1,0:T(8,128)(2,1)S(1)}, bf16[4,4,32,2560]{3,2,1,0:T(8,128)(2,1)S(1)}, u32[]{:S(2)}, u32[]{:S(2)}) collective-permute-start(bf16[4,4,32,2560]{3,2,1,0:T(8,128)(2,1)S(1)} %get-tuple-element.27), channel_id=1, source_target_pairs={{0,16},{16,0},{32,48},{48,32},{64,80},{80,64},{96,112},{112,96},{1... | collective-permute-start | bytes 7864328 | tf_op jit(solution)/shard_map/ppermute | solution.py:20
  72.5 4.7 %collective-permute-done.4 = bf16[4,4,32,2560]{3,2,1,0:T(8,128)(2,1)S(1)} collective-permute-done((bf16[4,4,32,2560]{3,2,1,0:T(8,128)(2,1)S(1)}, bf16[4,4,32,2560]{3,2,1,0:T(8,128)(2,1)S(1)}, u32[]{:S(2)}, u32[]{:S(2)}) %collective-permute-start.4) | collective-permute-done | bytes 2621472 | tf_op jit(solution)/shard_map/ppermute | solution.py:20
  77.2 0.8 add_convert_fusion
  77.9 20.8 %all_to_all.30.pieces = bf16[4,4,32,2560]{3,2,1,0:T(8,128)(2,1)S(1)} all-to-all(bf16[4,4,32,2560]{3,2,1,0:T(8,128)(2,1)S(1)} %add_convert_fusion), channel_id=1, replica_groups={{0,1,2,3},{4,5,6,7},{8,9,10,11},{12,13,14,15},{16,20,24,28},{17,21,25,2..., dimensions={0} | all-to-all | bytes 5242880 | tf_op jit(solution)/shard_map/all_to_all | solution.py:262
  98.8 0.8 fold.1
  99.6 11.8 %all_to_all.31.pieces = bf16[4,32,3328]{2,1,0:T(8,128)(2,1)S(1)} all-to-all(bf16[4,32,3328]{2,1,0:T(8,128)(2,1)S(1)} %fold.1), channel_id=1, replica_groups={{0,4,8,12},{1,5,9,13},{2,6,10,14},{3,7,11,15},{16,17,18,19},{20,21,22,2..., dimensions={0} | all-to-all | bytes 1703936 | tf_op jit(solution)/shard_map/all_to_all | solution.py:262
  111.4 0.9 pack.1
  112.3 23.8 %all_to_all.32 = bf16[16,2,16,256]{3,2,1,0:T(8,128)(2,1)S(1)} all-to-all(bf16[16,2,16,256]{3,2,1,0:T(8,128)(2,1)S(1)} %bitcast.24), channel_id=1, replica_groups={{0,32,64,96,128,160,192,224,256,288,320,352,384,416,448,480},{16,48,80,..., dimensions={0} | all-to-all | bytes 524288 | tf_op jit(solution)/shard_map/all_to_all | solution.py:363
  136.2 22.0 %all_to_all.33 = bf16[16,2,16,256]{3,2,1,0:T(8,128)(2,1)S(1)} all-to-all(bf16[16,2,16,256]{3,2,1,0:T(8,128)(2,1)S(1)} %broadcast_in_dim.56), channel_id=1, replica_groups={{0,32,64,96,128,160,192,224,256,288,320,352,384,416,448,480},{16,48,80,..., dimensions={0} | all-to-all | bytes 524288 | tf_op jit(solution)/shard_map/all_to_all | solution.py:363
  158.2 8.6 %collective-permute-start.5 = (bf16[32,16,256]{2,1,0:T(8,128)(2,1)S(1)}, bf16[32,16,256]{2,1,0:T(8,128)(2,1)S(1)}, u32[]{:S(2)}, u32[]{:S(2)}) collective-permute-start(bf16[32,16,256]{2,1,0:T(8,128)(2,1)S(1)} %bitcast.22), channel_id=1, source_target_pairs={{0,16},{16,0},{32,48},{48,32},{64,80},{80,64},{96,112},{112,96},{1... | collective-permute-start | bytes 786440 | tf_op jit(solution)/shard_map/ppermute | solution.py:20
  166.9 1.1 collective-permute-done.5.theirs
  168.0 1.4 finish.1
  (19 shorter events, 0.1 us)
Async XLA Ops:
  0.6 33.7 %copy-start = (bf16[4,361,256]{2,0,1:T(4,128)(2,1)S(1)}, bf16[4,361,256]{2,0,1:T(4,128)(2,1)}, u32[]{:S(2)}) copy-start(bf16[4,361,256]{2,0,1:T(4,128)(2,1)} %param.17) | copy-start | bytes 2217988
  2.5 14.2 %all-to-all-start = ((bf16[4,32,2304]{2,1,0:T(8,128)(2,1)}), bf16[4,32,2304]{2,1,0:T(8,128)(2,1)S(1)}, u32[]{:S(2)}, u32[]{:S(2)}) async-start(bf16[4,32,2304]{2,1,0:T(8,128)(2,1)} %broadcast_in_dim.50), calls=%async_computation | async-start | bytes 1179648 | tf_op jit(solution)/shard_map/all_to_all | solution.py:262
  18.3 21.3 %all-to-all-start.1 = ((bf16[4,4,32,2304]{3,2,1,0:T(8,128)(2,1)}), bf16[4,4,32,2304]{3,2,1,0:T(8,128)(2,1)S(1)}, u32[]{:S(2)}, u32[]{:S(2)}) async-start(bf16[4,4,32,2304]{3,2,1,0:T(8,128)(2,1)} %broadcast_in_dim.51), calls=%async_computation.1 | async-start | bytes 4718592 | tf_op jit(solution)/shard_map/all_to_all | solution.py:262
  24.2 14.2 %collective-permute-start = (f32[1,1024]{1,0:T(1,128)}, f32[1,1024]{1,0:T(1,128)S(1)}, u32[]{:S(2)}, u32[]{:S(2)}) collective-permute-start(f32[1,1024]{1,0:T(1,128)} %get-tuple-element.32), channel_id=1, source_target_pairs={{0,3},{1,0},{2,1},{3,2},{4,7},{5,4},{6,5},{7,6},{8,11},{9,8},{10,9... | collective-permute-start | bytes 12296 | tf_op jit(solution)/shard_map/ppermute | solution.py:30
  28.7 9.7 %collective-permute-start.2 = (f32[1,1024]{1,0:T(1,128)S(1)}, f32[1,1024]{1,0:T(1,128)}, u32[]{:S(2)}, u32[]{:S(2)}) collective-permute-start(f32[1,1024]{1,0:T(1,128)S(1)} %get-tuple-element.33), channel_id=1, source_target_pairs={{0,1},{1,2},{2,3},{3,0},{4,5},{5,6},{6,7},{7,4},{8,9},{9,10},{10,1... | collective-permute-start | bytes 12296 | tf_op jit(solution)/shard_map/ppermute | solution.py:30
  30.7 24.0 %copy-start.3 = (bf16[3,256]{1,0:T(4,128)(2,1)S(1)}, bf16[3,256]{1,0:T(4,128)(2,1)}, u32[]{:S(2)}) copy-start(bf16[3,256]{1,0:T(4,128)(2,1)} %embed.1) | copy-start | bytes 4612
  30.7 8.2 %collective-permute-start.1 = (f32[1,1024]{1,0:T(1,128)S(1)}, f32[1,1024]{1,0:T(1,128)}, u32[]{:S(2)}, u32[]{:S(2)}) collective-permute-start(f32[1,1024]{1,0:T(1,128)S(1)} %get-tuple-element.34), channel_id=1, source_target_pairs={{0,2},{1,3},{2,0},{3,1},{4,6},{5,7},{6,4},{7,5},{8,10},{9,11},{10,... | collective-permute-start | bytes 12296 | tf_op jit(solution)/shard_map/ppermute | solution.py:30
  39.6 15.0 %collective-permute-start.3 = (bf16[4,4,32,2304]{3,2,1,0:T(8,128)(2,1)S(1)}, bf16[4,4,32,2304]{3,2,1,0:T(8,128)(2,1)}, u32[]{:S(2)}, u32[]{:S(2)}) collective-permute-start(bf16[4,4,32,2304]{3,2,1,0:T(8,128)(2,1)S(1)} %all-to-all-done.1.mine), channel_id=1, source_target_pairs={{0,16},{16,0},{32,48},{48,32},{64,80},{80,64},{96,112},{112,96},{1... | collective-permute-start | bytes 7077896 | tf_op jit(solution)/shard_map/ppermute | solution.py:20
  50.9 1.6 copy-start.1
  52.5 1.0 copy-start.2
  70.3 6.8 %collective-permute-start.4 = (bf16[4,4,32,2560]{3,2,1,0:T(8,128)(2,1)S(1)}, bf16[4,4,32,2560]{3,2,1,0:T(8,128)(2,1)S(1)}, u32[]{:S(2)}, u32[]{:S(2)}) collective-permute-start(bf16[4,4,32,2560]{3,2,1,0:T(8,128)(2,1)S(1)} %get-tuple-element.27), channel_id=1, source_target_pairs={{0,16},{16,0},{32,48},{48,32},{64,80},{80,64},{96,112},{112,96},{1... | collective-permute-start | bytes 7864328 | tf_op jit(solution)/shard_map/ppermute | solution.py:20
  158.2 9.8 %collective-permute-start.5 = (bf16[32,16,256]{2,1,0:T(8,128)(2,1)S(1)}, bf16[32,16,256]{2,1,0:T(8,128)(2,1)S(1)}, u32[]{:S(2)}, u32[]{:S(2)}) collective-permute-start(bf16[32,16,256]{2,1,0:T(8,128)(2,1)S(1)} %bitcast.22), channel_id=1, source_target_pairs={{0,16},{16,0},{32,48},{48,32},{64,80},{80,64},{96,112},{112,96},{1... | collective-permute-start | bytes 786440 | tf_op jit(solution)/shard_map/ppermute | solution.py:20

commit v11 on v10

--- a/solution.py
+++ b/solution.py
@@ -86,11 +86,14 @@
         shard = jnp.where(core == 0, outer, inner)
         return block, pl.ds(pl.multiple_of(shard * 64 + core * 32, 32), 32)
 
-    for core, pieces in ((c, mine), (1 - c, theirs)):
-        for outer in range(4):
-            for inner in range(4):
-                block, rows = block_rows(inner, outer, core)
-                wt[block, rows, :] = pieces[outer, inner]
+    def assemble(place, carry):
+        outer, inner = place >> 2, place & 3
+        for core, pieces in ((c, mine), (1 - c, theirs)):
+            block, rows = block_rows(inner, outer, core)
+            wt[block, rows, :] = pieces[outer, inner]
+        return carry
+
+    lax.fori_loop(0, 16, assemble, 0)
 
     point = lax.broadcasted_iota(jnp.int32, (ROWS, 1), 0)
     column = point - ((point * 3277) >> 16) * PITCH
@@ -122,7 +125,7 @@
         buf[FRONT : FRONT + ROWS, :] = stream.astype(BF16).astype(F32) * mask
         return carry
 
-    lax.fori_loop(0, 4, forward, 0, unroll=True)
+    lax.fori_loop(0, 4, forward, 0)
     grad[...] = cotangent[...].astype(F32)
 
     def backward(step, carry):
@@ -144,7 +147,7 @@
         grad[...] = total.astype(BF16).astype(F32) * mask
         return carry
 
-    lax.fori_loop(0, 4, backward, 0, unroll=True)
+    lax.fori_loop(0, 4, backward, 0)
 
     kind = lax.broadcasted_iota(jnp.int32, (16, ROWS), 0)
     codes = code_row[...]
@@ -165,13 +168,17 @@
             place += 1
     tail = vectors[...].astype(BF16)
     empty = jnp.zeros(tail.shape, BF16)
-    for core, pieces, first, second in ((c, own, tail, empty), (1 - c, other, empty, tail)):
-        for outer in range(4):
-            for inner in range(4):
-                block, rows = block_rows(outer, inner, core)
-                pieces[outer, inner, :, 0:taps] = gt[block, rows, :]
-                pieces[outer, inner, :, taps : taps + 128] = first
-                pieces[outer, inner, :, taps + 128 :] = second
+
+    def hand_out(place, carry):
+        outer, inner = place >> 2, place & 3
+        for core, pieces, first, second in ((c, own, tail, empty), (1 - c, other, empty, tail)):
+            block, rows = block_rows(outer, inner, core)
+            pieces[outer, inner, :, 0:taps] = gt[block, rows, :]
+            pieces[outer, inner, :, taps : taps + 128] = first
+            pieces[outer, inner, :, taps + 128 :] = second
+        return carry
+
+    lax.fori_loop(0, 16, hand_out, 0)
 
 
 def fold_kernel(where, pieces, out):

time: 170 us -> 167 us (0.982)
  Pallas kernels: 19.9 us -> 17.3 us
    pallas_call x5, Pallas kernels: 19.9 us -> 17.3 us  [call(): pl.pallas_call(kernel, out_shape=outs, in_specs=[pl.BlockSpec(memory_spac...]
where the time goes in v11:
time: 167 us
  blocking collectives  86.1 us (52%)
  starting transfers between devices  39.2 us (23%)
  Pallas kernels  17.3 us (10%)
  local copies, waits for them, and re-layouts  12.2 us (7%)
  waiting for transfers between devices  6.43 us (4%)
  other arithmetic  2.5 us (1%)
    all_to_all x2, blocking collectives, along_z(): lax.all_to_all(blocks, 'dp', 0, 0, axis_index_groups=line, tiled=True)  45.8 us
    all_to_all x2, blocking collectives, ring(): lax.all_to_all(blocks, ('dp', 'section', 'shard'), 0, 0, axis_index_group...  32.6 us
    ppermute x3, starting transfers between devices, swap(): lax.ppermute(block, axis, [(i, i ^ bits) for i in range(lax.axis_size(axi...  20.5 us
    pallas_call x5, Pallas kernels, call(): pl.pallas_call(kernel, out_shape=outs, in_specs=[pl.BlockSpec(memory_spac...  17.3 us
    ppermute x3, starting transfers between devices, turned(): lax.ppermute(block, axis, [(i, (i + distance) % size) for i in range(size)])  10.1 us
    all_to_all x2, starting transfers between devices, ring(): lax.all_to_all(blocks, ('dp', 'section', 'shard'), 0, 0, axis_index_group...  8.64 us
    all_gather x1, blocking collectives, body(): lax.all_gather(asked[None], 'shard', axis=0, tiled=True)[:, 0, :slots + 1]  7.64 us
    ppermute x3, waiting for transfers between devices, swap(): lax.ppermute(block, axis, [(i, i ^ bits) for i in range(lax.axis_size(axi...  6.01 us
  transfers between devices with their start and end apart: 8, of which 3 were waited for; matrix products, arithmetic and copies ran while one was open for 5% of the time, Pallas kernels for 1%

profile of v11, /device:TPU:1, one launch (start us, length us, event | category | flops | bytes accessed | tf_op | source)
XLA Modules:
  0.0 166.6 jit_solution(3293719303173246750)
XLA Ops:
  0.6 0.0 copy-start
  0.7 1.0 dynamic-slice_bitcast_fusion
  1.7 0.8 broadcast_in_dim.50
  2.5 5.0 %all-to-all-start = ((bf16[4,32,2304]{2,1,0:T(8,128)(2,1)}), bf16[4,32,2304]{2,1,0:T(8,128)(2,1)S(1)}, u32[]{:S(2)}, u32[]{:S(2)}) async-start(bf16[4,32,2304]{2,1,0:T(8,128)(2,1)} %broadcast_in_dim.50), calls=%async_computation | async-start | bytes 1179648 | tf_op jit(solution)/shard_map/all_to_all | solution.py:269
  7.5 0.7 copy.18
  8.3 0.8 fusion
  9.0 7.6 %all-gather.1 = s32[4,1,128]{2,1,0:T(1,128)S(1)} all-gather(s32[1,1,128]{2,1,0:T(1,128)S(1)} %pad_bitcast_fusion), channel_id=3, replica_groups=mesh['dp'=32,'section'=4,'shard'=4] {'shard'}, dimensions={0}, use_global_device_ids=true | all-gather | bytes 2560 | tf_op jit(solution)/shard_map/all_gather | solution.py:279
  16.7 0.0 all-to-all-done
  16.7 1.6 broadcast_in_dim.51
  18.3 3.6 %all-to-all-start.1 = ((bf16[4,4,32,2304]{3,2,1,0:T(8,128)(2,1)}), bf16[4,4,32,2304]{3,2,1,0:T(8,128)(2,1)S(1)}, u32[]{:S(2)}, u32[]{:S(2)}) async-start(bf16[4,4,32,2304]{3,2,1,0:T(8,128)(2,1)} %broadcast_in_dim.51), calls=%async_computation.1 | async-start | bytes 4718592 | tf_op jit(solution)/shard_map/all_to_all | solution.py:269
  22.0 0.1 copy.19
  22.1 0.2 slice_reduce_fusion
  22.3 0.1 convert_reduce_fusion
  22.4 1.2 fusion.4
  23.6 0.6 constant_dynamic-slice_fusion.3
  24.2 4.5 %collective-permute-start = (f32[1,1024]{1,0:T(1,128)}, f32[1,1024]{1,0:T(1,128)S(1)}, u32[]{:S(2)}, u32[]{:S(2)}) collective-permute-start(f32[1,1024]{1,0:T(1,128)} %get-tuple-element.32), channel_id=1, source_target_pairs={{0,3},{1,0},{2,1},{3,2},{4,7},{5,4},{6,5},{7,6},{8,11},{9,8},{10,9... | collective-permute-start | bytes 12296 | tf_op jit(solution)/shard_map/ppermute | solution.py:30
  28.7 1.9 %collective-permute-start.2 = (f32[1,1024]{1,0:T(1,128)S(1)}, f32[1,1024]{1,0:T(1,128)}, u32[]{:S(2)}, u32[]{:S(2)}) collective-permute-start(f32[1,1024]{1,0:T(1,128)S(1)} %get-tuple-element.33), channel_id=1, source_target_pairs={{0,1},{1,2},{2,3},{3,0},{4,5},{5,6},{6,7},{7,4},{8,9},{9,10},{10,1... | collective-permute-start | bytes 12296 | tf_op jit(solution)/shard_map/ppermute | solution.py:30
  30.7 0.0 copy-start.3
  30.7 3.7 %collective-permute-start.1 = (f32[1,1024]{1,0:T(1,128)S(1)}, f32[1,1024]{1,0:T(1,128)}, u32[]{:S(2)}, u32[]{:S(2)}) collective-permute-start(f32[1,1024]{1,0:T(1,128)S(1)} %get-tuple-element.34), channel_id=1, source_target_pairs={{0,2},{1,3},{2,0},{3,1},{4,6},{5,7},{6,4},{7,5},{8,10},{9,11},{10,... | collective-permute-start | bytes 12296 | tf_op jit(solution)/shard_map/ppermute | solution.py:30
  34.4 1.1 dynamic-slice_reduce_fusion
  35.4 0.6 slice.18
  36.7 0.1 reshape.74
  36.7 0.7 pad.24
  37.5 1.0 reshape.75
  38.5 0.4 collective-permute-done.1
  38.9 0.7 convert_reduce_fusion.1
  39.6 9.9 %collective-permute-start.3 = (bf16[4,4,32,2304]{3,2,1,0:T(8,128)(2,1)S(1)}, bf16[4,4,32,2304]{3,2,1,0:T(8,128)(2,1)}, u32[]{:S(2)}, u32[]{:S(2)}) collective-permute-start(bf16[4,4,32,2304]{3,2,1,0:T(8,128)(2,1)S(1)} %all-to-all-done.1.mine), channel_id=1, source_target_pairs={{0,16},{16,0},{32,48},{48,32},{64,80},{80,64},{96,112},{112,96},{1... | collective-permute-start | bytes 7077896 | tf_op jit(solution)/shard_map/ppermute | solution.py:20
  49.6 0.7 fusion.3
  50.3 0.1 reshape.76
  50.4 0.1 reshape.77
  50.5 0.1 broadcast_in_dim.58.code_col
  50.6 0.1 pad_add_fusion.where
  50.7 1.6 copy-done.1
  52.3 1.0 copy-done.2
  53.3 1.1 encoder.1
  54.5 13.1 %trunk.1 = (bf16[4,4,32,2560]{3,2,1,0:T(8,128)(2,1)S(1)}, bf16[4,4,32,2560]{3,2,1,0:T(8,128)(2,1)S(1)}) custom-call(s32[3]{0:T(128)S(1)} %pad_add_fusion.where, bf16[16,1024]{1,0:T(8,128)(2,1)S(1)} %broadcast_in_dim.53.context, f32[16,1024]{1,0:T(8,128)S(1)} %get-tuple-element.21.preact_in, bf16[16,1024]{1,0:T(8,128)(2,1)S(1)} %get-tuple-element.22.hidden_in, ...), custom_call_target="tpu_custom_call" | custom-call | flops 5435817984 | bytes 16777216 | tf_op jit(solution)/shard_map/trunk/pallas_call | solution.py:53
  67.6 1.9 %collective-permute-start.4 = (bf16[4,4,32,2560]{3,2,1,0:T(8,128)(2,1)S(1)}, bf16[4,4,32,2560]{3,2,1,0:T(8,128)(2,1)S(1)}, u32[]{:S(2)}, u32[]{:S(2)}) collective-permute-start(bf16[4,4,32,2560]{3,2,1,0:T(8,128)(2,1)S(1)} %get-tuple-element.27), channel_id=1, source_target_pairs={{0,16},{16,0},{32,48},{48,32},{64,80},{80,64},{96,112},{112,96},{1... | collective-permute-start | bytes 7864328 | tf_op jit(solution)/shard_map/ppermute | solution.py:20
  69.5 4.9 %collective-permute-done.4 = bf16[4,4,32,2560]{3,2,1,0:T(8,128)(2,1)S(1)} collective-permute-done((bf16[4,4,32,2560]{3,2,1,0:T(8,128)(2,1)S(1)}, bf16[4,4,32,2560]{3,2,1,0:T(8,128)(2,1)S(1)}, u32[]{:S(2)}, u32[]{:S(2)}) %collective-permute-start.4) | collective-permute-done | bytes 2621472 | tf_op jit(solution)/shard_map/ppermute | solution.py:20
  74.4 0.8 add_convert_fusion
  75.1 20.8 %all_to_all.30.pieces = bf16[4,4,32,2560]{3,2,1,0:T(8,128)(2,1)S(1)} all-to-all(bf16[4,4,32,2560]{3,2,1,0:T(8,128)(2,1)S(1)} %add_convert_fusion), channel_id=1, replica_groups={{0,1,2,3},{4,5,6,7},{8,9,10,11},{12,13,14,15},{16,20,24,28},{17,21,25,2..., dimensions={0} | all-to-all | bytes 5242880 | tf_op jit(solution)/shard_map/all_to_all | solution.py:269
  96.0 0.8 fold.1
  96.8 11.8 %all_to_all.31.pieces = bf16[4,32,3328]{2,1,0:T(8,128)(2,1)S(1)} all-to-all(bf16[4,32,3328]{2,1,0:T(8,128)(2,1)S(1)} %fold.1), channel_id=1, replica_groups={{0,4,8,12},{1,5,9,13},{2,6,10,14},{3,7,11,15},{16,17,18,19},{20,21,22,2..., dimensions={0} | all-to-all | bytes 1703936 | tf_op jit(solution)/shard_map/all_to_all | solution.py:269
  108.6 0.9 pack.1
  109.5 23.8 %all_to_all.32 = bf16[16,2,16,256]{3,2,1,0:T(8,128)(2,1)S(1)} all-to-all(bf16[16,2,16,256]{3,2,1,0:T(8,128)(2,1)S(1)} %bitcast.24), channel_id=1, replica_groups={{0,32,64,96,128,160,192,224,256,288,320,352,384,416,448,480},{16,48,80,..., dimensions={0} | all-to-all | bytes 524288 | tf_op jit(solution)/shard_map/all_to_all | solution.py:370
  133.4 22.0 %all_to_all.33 = bf16[16,2,16,256]{3,2,1,0:T(8,128)(2,1)S(1)} all-to-all(bf16[16,2,16,256]{3,2,1,0:T(8,128)(2,1)S(1)} %broadcast_in_dim.56), channel_id=1, replica_groups={{0,32,64,96,128,160,192,224,256,288,320,352,384,416,448,480},{16,48,80,..., dimensions={0} | all-to-all | bytes 524288 | tf_op jit(solution)/shard_map/all_to_all | solution.py:370
  155.4 8.6 %collective-permute-start.5 = (bf16[32,16,256]{2,1,0:T(8,128)(2,1)S(1)}, bf16[32,16,256]{2,1,0:T(8,128)(2,1)S(1)}, u32[]{:S(2)}, u32[]{:S(2)}) collective-permute-start(bf16[32,16,256]{2,1,0:T(8,128)(2,1)S(1)} %bitcast.22), channel_id=1, source_target_pairs={{0,16},{16,0},{32,48},{48,32},{64,80},{80,64},{96,112},{112,96},{1... | collective-permute-start | bytes 786440 | tf_op jit(solution)/shard_map/ppermute | solution.py:20
  164.1 1.1 collective-permute-done.5.theirs
  165.2 1.4 finish.1
  (19 shorter events, 0.1 us)
Async XLA Ops:
  0.6 33.7 %copy-start = (bf16[4,361,256]{2,0,1:T(4,128)(2,1)S(1)}, bf16[4,361,256]{2,0,1:T(4,128)(2,1)}, u32[]{:S(2)}) copy-start(bf16[4,361,256]{2,0,1:T(4,128)(2,1)} %param.17) | copy-start | bytes 2217988
  2.5 14.2 %all-to-all-start = ((bf16[4,32,2304]{2,1,0:T(8,128)(2,1)}), bf16[4,32,2304]{2,1,0:T(8,128)(2,1)S(1)}, u32[]{:S(2)}, u32[]{:S(2)}) async-start(bf16[4,32,2304]{2,1,0:T(8,128)(2,1)} %broadcast_in_dim.50), calls=%async_computation | async-start | bytes 1179648 | tf_op jit(solution)/shard_map/all_to_all | solution.py:269
  18.3 21.3 %all-to-all-start.1 = ((bf16[4,4,32,2304]{3,2,1,0:T(8,128)(2,1)}), bf16[4,4,32,2304]{3,2,1,0:T(8,128)(2,1)S(1)}, u32[]{:S(2)}, u32[]{:S(2)}) async-start(bf16[4,4,32,2304]{3,2,1,0:T(8,128)(2,1)} %broadcast_in_dim.51), calls=%async_computation.1 | async-start | bytes 4718592 | tf_op jit(solution)/shard_map/all_to_all | solution.py:269
  24.2 14.2 %collective-permute-start = (f32[1,1024]{1,0:T(1,128)}, f32[1,1024]{1,0:T(1,128)S(1)}, u32[]{:S(2)}, u32[]{:S(2)}) collective-permute-start(f32[1,1024]{1,0:T(1,128)} %get-tuple-element.32), channel_id=1, source_target_pairs={{0,3},{1,0},{2,1},{3,2},{4,7},{5,4},{6,5},{7,6},{8,11},{9,8},{10,9... | collective-permute-start | bytes 12296 | tf_op jit(solution)/shard_map/ppermute | solution.py:30
  28.7 9.7 %collective-permute-start.2 = (f32[1,1024]{1,0:T(1,128)S(1)}, f32[1,1024]{1,0:T(1,128)}, u32[]{:S(2)}, u32[]{:S(2)}) collective-permute-start(f32[1,1024]{1,0:T(1,128)S(1)} %get-tuple-element.33), channel_id=1, source_target_pairs={{0,1},{1,2},{2,3},{3,0},{4,5},{5,6},{6,7},{7,4},{8,9},{9,10},{10,1... | collective-permute-start | bytes 12296 | tf_op jit(solution)/shard_map/ppermute | solution.py:30
  30.7 23.8 %copy-start.3 = (bf16[3,256]{1,0:T(4,128)(2,1)S(1)}, bf16[3,256]{1,0:T(4,128)(2,1)}, u32[]{:S(2)}) copy-start(bf16[3,256]{1,0:T(4,128)(2,1)} %embed.1) | copy-start | bytes 4612
  30.7 8.2 %collective-permute-start.1 = (f32[1,1024]{1,0:T(1,128)S(1)}, f32[1,1024]{1,0:T(1,128)}, u32[]{:S(2)}, u32[]{:S(2)}) collective-permute-start(f32[1,1024]{1,0:T(1,128)S(1)} %get-tuple-element.34), channel_id=1, source_target_pairs={{0,2},{1,3},{2,0},{3,1},{4,6},{5,7},{6,4},{7,5},{8,10},{9,11},{10,... | collective-permute-start | bytes 12296 | tf_op jit(solution)/shard_map/ppermute | solution.py:30
  39.6 14.8 %collective-permute-start.3 = (bf16[4,4,32,2304]{3,2,1,0:T(8,128)(2,1)S(1)}, bf16[4,4,32,2304]{3,2,1,0:T(8,128)(2,1)}, u32[]{:S(2)}, u32[]{:S(2)}) collective-permute-start(bf16[4,4,32,2304]{3,2,1,0:T(8,128)(2,1)S(1)} %all-to-all-done.1.mine), channel_id=1, source_target_pairs={{0,16},{16,0},{32,48},{48,32},{64,80},{80,64},{96,112},{112,96},{1... | collective-permute-start | bytes 7077896 | tf_op jit(solution)/shard_map/ppermute | solution.py:20
  50.7 1.6 copy-start.1
  52.3 1.0 copy-start.2
  67.6 6.8 %collective-permute-start.4 = (bf16[4,4,32,2560]{3,2,1,0:T(8,128)(2,1)S(1)}, bf16[4,4,32,2560]{3,2,1,0:T(8,128)(2,1)S(1)}, u32[]{:S(2)}, u32[]{:S(2)}) collective-permute-start(bf16[4,4,32,2560]{3,2,1,0:T(8,128)(2,1)S(1)} %get-tuple-element.27), channel_id=1, source_target_pairs={{0,16},{16,0},{32,48},{48,32},{64,80},{80,64},{96,112},{112,96},{1... | collective-permute-start | bytes 7864328 | tf_op jit(solution)/shard_map/ppermute | solution.py:20
  155.4 9.8 %collective-permute-start.5 = (bf16[32,16,256]{2,1,0:T(8,128)(2,1)S(1)}, bf16[32,16,256]{2,1,0:T(8,128)(2,1)S(1)}, u32[]{:S(2)}, u32[]{:S(2)}) collective-permute-start(bf16[32,16,256]{2,1,0:T(8,128)(2,1)S(1)} %bitcast.22), channel_id=1, source_target_pairs={{0,16},{16,0},{32,48},{48,32},{64,80},{80,64},{96,112},{112,96},{1... | collective-permute-start | bytes 786440 | tf_op jit(solution)/shard_map/ppermute | solution.py:20

commit v12 on v11

--- a/solution.py
+++ b/solution.py
@@ -11,7 +11,8 @@
 FRONT = 24
 NORM_EPS = 1e-05
 TAP_SHIFTS = [(a - 1) * PITCH + (b - 1) for a in range(3) for b in range(3)]
-VMEM_BYTES = 34 * 1024 * 1024
+SMALL_VMEM = 8 * 1024 * 1024
+TRUNK_VMEM = 24 * 1024 * 1024
 F32 = jnp.float32
 BF16 = jnp.bfloat16
 
@@ -46,7 +47,7 @@
     return lax.dot_general(left, right, (((0,), (0,)), ((), ())), preferred_element_type=F32)
 
 
-def vmem_call(kernel, outs, scratch, name, flops, moved):
+def vmem_call(kernel, outs, scratch, name, flops, moved, vmem=SMALL_VMEM):
     spec = pl.BlockSpec(memory_space=pltpu.VMEM)
 
     def call(scalars, *arrays):
@@ -57,7 +58,7 @@
             + [spec] * len(arrays),
             out_specs=tuple(spec for _ in outs),
             scratch_shapes=scratch,
-            compiler_params=pltpu.CompilerParams(vmem_limit_bytes=VMEM_BYTES),
+            compiler_params=pltpu.CompilerParams(vmem_limit_bytes=vmem),
             cost_estimate=pl.CostEstimate(flops=flops, bytes_accessed=moved, transcendentals=0),
             name=name,
         )(scalars, *arrays)
@@ -336,6 +337,7 @@
         "trunk",
         12 * 2 * ROWS * taps * channels,
         16 << 20,
+        vmem=TRUNK_VMEM,
     )(
         where, context, preact, hidden, encoded, w_second, embed,
         code[:, None], code[None, :], upper, mine, theirs,

time: 167 us -> 167 us (level)
  no operation moved by 1% of the time
where the time goes in v12:
time: 167 us
  blocking collectives  86.1 us (52%)
  starting transfers between devices  39.2 us (23%)
  Pallas kernels  17.3 us (10%)
  local copies, waits for them, and re-layouts  12.2 us (7%)
  waiting for transfers between devices  6.43 us (4%)
  other arithmetic  2.5 us (1%)
    all_to_all x2, blocking collectives, along_z(): lax.all_to_all(blocks, 'dp', 0, 0, axis_index_groups=line, tiled=True)  45.8 us
    all_to_all x2, blocking collectives, ring(): lax.all_to_all(blocks, ('dp', 'section', 'shard'), 0, 0, axis_index_group...  32.6 us
    ppermute x3, starting transfers between devices, swap(): lax.ppermute(block, axis, [(i, i ^ bits) for i in range(lax.axis_size(axi...  20.5 us
    pallas_call x5, Pallas kernels, call(): pl.pallas_call(kernel, out_shape=outs, in_specs=[pl.BlockSpec(memory_spac...  17.3 us
    ppermute x3, starting transfers between devices, turned(): lax.ppermute(block, axis, [(i, (i + distance) % size) for i in range(size)])  10.1 us
    all_to_all x2, starting transfers between devices, ring(): lax.all_to_all(blocks, ('dp', 'section', 'shard'), 0, 0, axis_index_group...  8.64 us
    all_gather x1, blocking collectives, body(): lax.all_gather(asked[None], 'shard', axis=0, tiled=True)[:, 0, :slots + 1]  7.64 us
    ppermute x3, waiting for transfers between devices, swap(): lax.ppermute(block, axis, [(i, i ^ bits) for i in range(lax.axis_size(axi...  6.02 us
  transfers between devices with their start and end apart: 8, of which 3 were waited for; matrix products, arithmetic and copies ran while one was open for 5% of the time, Pallas kernels for 1%

profile of v12, /device:TPU:1, one launch (start us, length us, event | category | flops | bytes accessed | tf_op | source)
XLA Modules:
  0.0 166.6 jit_solution(530399105058562817)
XLA Ops:
  0.6 0.0 copy-start
  0.7 1.0 dynamic-slice_bitcast_fusion
  1.7 0.8 broadcast_in_dim.50
  2.5 5.0 %all-to-all-start = ((bf16[4,32,2304]{2,1,0:T(8,128)(2,1)}), bf16[4,32,2304]{2,1,0:T(8,128)(2,1)S(1)}, u32[]{:S(2)}, u32[]{:S(2)}) async-start(bf16[4,32,2304]{2,1,0:T(8,128)(2,1)} %broadcast_in_dim.50), calls=%async_computation | async-start | bytes 1179648 | tf_op jit(solution)/shard_map/all_to_all | solution.py:270
  7.5 0.7 copy.18
  8.3 0.8 fusion
  9.0 7.6 %all-gather.1 = s32[4,1,128]{2,1,0:T(1,128)S(1)} all-gather(s32[1,1,128]{2,1,0:T(1,128)S(1)} %pad_bitcast_fusion), channel_id=3, replica_groups=mesh['dp'=32,'section'=4,'shard'=4] {'shard'}, dimensions={0}, use_global_device_ids=true | all-gather | bytes 2560 | tf_op jit(solution)/shard_map/all_gather | solution.py:280
  16.7 1.6 broadcast_in_dim.51
  18.3 3.6 %all-to-all-start.1 = ((bf16[4,4,32,2304]{3,2,1,0:T(8,128)(2,1)}), bf16[4,4,32,2304]{3,2,1,0:T(8,128)(2,1)S(1)}, u32[]{:S(2)}, u32[]{:S(2)}) async-start(bf16[4,4,32,2304]{3,2,1,0:T(8,128)(2,1)} %broadcast_in_dim.51), calls=%async_computation.1 | async-start | bytes 4718592 | tf_op jit(solution)/shard_map/all_to_all | solution.py:270
  22.0 0.1 copy.19
  22.1 0.2 slice_reduce_fusion
  22.3 0.1 convert_reduce_fusion
  22.4 1.2 fusion.4
  23.6 0.6 constant_dynamic-slice_fusion.3
  24.2 4.5 %collective-permute-start = (f32[1,1024]{1,0:T(1,128)}, f32[1,1024]{1,0:T(1,128)S(1)}, u32[]{:S(2)}, u32[]{:S(2)}) collective-permute-start(f32[1,1024]{1,0:T(1,128)} %get-tuple-element.32), channel_id=1, source_target_pairs={{0,3},{1,0},{2,1},{3,2},{4,7},{5,4},{6,5},{7,6},{8,11},{9,8},{10,9... | collective-permute-start | bytes 12296 | tf_op jit(solution)/shard_map/ppermute | solution.py:31
  28.7 1.9 %collective-permute-start.2 = (f32[1,1024]{1,0:T(1,128)S(1)}, f32[1,1024]{1,0:T(1,128)}, u32[]{:S(2)}, u32[]{:S(2)}) collective-permute-start(f32[1,1024]{1,0:T(1,128)S(1)} %get-tuple-element.33), channel_id=1, source_target_pairs={{0,1},{1,2},{2,3},{3,0},{4,5},{5,6},{6,7},{7,4},{8,9},{9,10},{10,1... | collective-permute-start | bytes 12296 | tf_op jit(solution)/shard_map/ppermute | solution.py:31
  30.7 0.0 copy-start.4
  30.7 3.7 %collective-permute-start.1 = (f32[1,1024]{1,0:T(1,128)S(1)}, f32[1,1024]{1,0:T(1,128)}, u32[]{:S(2)}, u32[]{:S(2)}) collective-permute-start(f32[1,1024]{1,0:T(1,128)S(1)} %get-tuple-element.34), channel_id=1, source_target_pairs={{0,2},{1,3},{2,0},{3,1},{4,6},{5,7},{6,4},{7,5},{8,10},{9,11},{10,... | collective-permute-start | bytes 12296 | tf_op jit(solution)/shard_map/ppermute | solution.py:31
  34.4 1.1 dynamic-slice_reduce_fusion
  35.4 0.6 slice.18
  36.7 0.1 reshape.74
  36.7 0.7 pad.24
  37.5 1.0 reshape.75
  38.5 0.4 collective-permute-done.1
  38.9 0.7 convert_reduce_fusion.1
  39.6 9.9 %collective-permute-start.3 = (bf16[4,4,32,2304]{3,2,1,0:T(8,128)(2,1)S(1)}, bf16[4,4,32,2304]{3,2,1,0:T(8,128)(2,1)}, u32[]{:S(2)}, u32[]{:S(2)}) collective-permute-start(bf16[4,4,32,2304]{3,2,1,0:T(8,128)(2,1)S(1)} %all-to-all-done.1.mine), channel_id=1, source_target_pairs={{0,16},{16,0},{32,48},{48,32},{64,80},{80,64},{96,112},{112,96},{1... | collective-permute-start | bytes 7077896 | tf_op jit(solution)/shard_map/ppermute | solution.py:21
  49.6 0.7 fusion.3
  50.3 0.1 reshape.76
  50.4 0.1 reshape.77
  50.5 0.1 broadcast_in_dim.58.code_col
  50.6 0.1 pad_add_fusion.where
  50.7 1.6 copy-done.1
  52.3 1.0 copy-done.2
  53.3 1.1 encoder.1
  54.5 0.0 copy-done.3
  54.5 13.1 %trunk.1 = (bf16[4,4,32,2560]{3,2,1,0:T(8,128)(2,1)S(1)}, bf16[4,4,32,2560]{3,2,1,0:T(8,128)(2,1)S(1)}) custom-call(s32[3]{0:T(128)S(1)} %pad_add_fusion.where, bf16[16,1024]{1,0:T(8,128)(2,1)S(1)} %broadcast_in_dim.53.context, f32[16,1024]{1,0:T(8,128)S(1)} %get-tuple-element.21.preact_in, bf16[16,1024]{1,0:T(8,128)(2,1)S(1)} %get-tuple-element.22.hidden_in, ...), custom_call_target="tpu_custom_call" | custom-call | flops 5435817984 | bytes 16777216 | tf_op jit(solution)/shard_map/trunk/pallas_call | solution.py:54
  67.6 1.9 %collective-permute-start.4 = (bf16[4,4,32,2560]{3,2,1,0:T(8,128)(2,1)S(1)}, bf16[4,4,32,2560]{3,2,1,0:T(8,128)(2,1)S(1)}, u32[]{:S(2)}, u32[]{:S(2)}) collective-permute-start(bf16[4,4,32,2560]{3,2,1,0:T(8,128)(2,1)S(1)} %get-tuple-element.27), channel_id=1, source_target_pairs={{0,16},{16,0},{32,48},{48,32},{64,80},{80,64},{96,112},{112,96},{1... | collective-permute-start | bytes 7864328 | tf_op jit(solution)/shard_map/ppermute | solution.py:21
  69.5 4.9 %collective-permute-done.4 = bf16[4,4,32,2560]{3,2,1,0:T(8,128)(2,1)S(1)} collective-permute-done((bf16[4,4,32,2560]{3,2,1,0:T(8,128)(2,1)S(1)}, bf16[4,4,32,2560]{3,2,1,0:T(8,128)(2,1)S(1)}, u32[]{:S(2)}, u32[]{:S(2)}) %collective-permute-start.4) | collective-permute-done | bytes 2621472 | tf_op jit(solution)/shard_map/ppermute | solution.py:21
  74.4 0.8 add_convert_fusion
  75.2 20.8 %all_to_all.30.pieces = bf16[4,4,32,2560]{3,2,1,0:T(8,128)(2,1)S(1)} all-to-all(bf16[4,4,32,2560]{3,2,1,0:T(8,128)(2,1)S(1)} %add_convert_fusion), channel_id=1, replica_groups={{0,1,2,3},{4,5,6,7},{8,9,10,11},{12,13,14,15},{16,20,24,28},{17,21,25,2..., dimensions={0} | all-to-all | bytes 5242880 | tf_op jit(solution)/shard_map/all_to_all | solution.py:270
  96.0 0.8 fold.1
  96.8 11.8 %all_to_all.31.pieces = bf16[4,32,3328]{2,1,0:T(8,128)(2,1)S(1)} all-to-all(bf16[4,32,3328]{2,1,0:T(8,128)(2,1)S(1)} %fold.1), channel_id=1, replica_groups={{0,4,8,12},{1,5,9,13},{2,6,10,14},{3,7,11,15},{16,17,18,19},{20,21,22,2..., dimensions={0} | all-to-all | bytes 1703936 | tf_op jit(solution)/shard_map/all_to_all | solution.py:270
  108.6 0.9 pack.1
  109.5 23.8 %all_to_all.32 = bf16[16,2,16,256]{3,2,1,0:T(8,128)(2,1)S(1)} all-to-all(bf16[16,2,16,256]{3,2,1,0:T(8,128)(2,1)S(1)} %bitcast.24), channel_id=1, replica_groups={{0,32,64,96,128,160,192,224,256,288,320,352,384,416,448,480},{16,48,80,..., dimensions={0} | all-to-all | bytes 524288 | tf_op jit(solution)/shard_map/all_to_all | solution.py:372
  133.5 22.0 %all_to_all.33 = bf16[16,2,16,256]{3,2,1,0:T(8,128)(2,1)S(1)} all-to-all(bf16[16,2,16,256]{3,2,1,0:T(8,128)(2,1)S(1)} %broadcast_in_dim.56), channel_id=1, replica_groups={{0,32,64,96,128,160,192,224,256,288,320,352,384,416,448,480},{16,48,80,..., dimensions={0} | all-to-all | bytes 524288 | tf_op jit(solution)/shard_map/all_to_all | solution.py:372
  155.4 8.6 %collective-permute-start.5 = (bf16[32,16,256]{2,1,0:T(8,128)(2,1)S(1)}, bf16[32,16,256]{2,1,0:T(8,128)(2,1)S(1)}, u32[]{:S(2)}, u32[]{:S(2)}) collective-permute-start(bf16[32,16,256]{2,1,0:T(8,128)(2,1)S(1)} %bitcast.22), channel_id=1, source_target_pairs={{0,16},{16,0},{32,48},{48,32},{64,80},{80,64},{96,112},{112,96},{1... | collective-permute-start | bytes 786440 | tf_op jit(solution)/shard_map/ppermute | solution.py:21
  164.1 1.1 collective-permute-done.5.theirs
  165.2 1.4 finish.1
  (21 shorter events, 0.1 us)
Async XLA Ops:
  0.6 33.7 %copy-start = (bf16[4,361,256]{2,0,1:T(4,128)(2,1)S(1)}, bf16[4,361,256]{2,0,1:T(4,128)(2,1)}, u32[]{:S(2)}) copy-start(bf16[4,361,256]{2,0,1:T(4,128)(2,1)} %param.17) | copy-start | bytes 2217988
  2.5 14.2 %all-to-all-start = ((bf16[4,32,2304]{2,1,0:T(8,128)(2,1)}), bf16[4,32,2304]{2,1,0:T(8,128)(2,1)S(1)}, u32[]{:S(2)}, u32[]{:S(2)}) async-start(bf16[4,32,2304]{2,1,0:T(8,128)(2,1)} %broadcast_in_dim.50), calls=%async_computation | async-start | bytes 1179648 | tf_op jit(solution)/shard_map/all_to_all | solution.py:270
  18.3 21.3 %all-to-all-start.1 = ((bf16[4,4,32,2304]{3,2,1,0:T(8,128)(2,1)}), bf16[4,4,32,2304]{3,2,1,0:T(8,128)(2,1)S(1)}, u32[]{:S(2)}, u32[]{:S(2)}) async-start(bf16[4,4,32,2304]{3,2,1,0:T(8,128)(2,1)} %broadcast_in_dim.51), calls=%async_computation.1 | async-start | bytes 4718592 | tf_op jit(solution)/shard_map/all_to_all | solution.py:270
  24.2 14.2 %collective-permute-start = (f32[1,1024]{1,0:T(1,128)}, f32[1,1024]{1,0:T(1,128)S(1)}, u32[]{:S(2)}, u32[]{:S(2)}) collective-permute-start(f32[1,1024]{1,0:T(1,128)} %get-tuple-element.32), channel_id=1, source_target_pairs={{0,3},{1,0},{2,1},{3,2},{4,7},{5,4},{6,5},{7,6},{8,11},{9,8},{10,9... | collective-permute-start | bytes 12296 | tf_op jit(solution)/shard_map/ppermute | solution.py:31
  28.7 9.7 %collective-permute-start.2 = (f32[1,1024]{1,0:T(1,128)S(1)}, f32[1,1024]{1,0:T(1,128)}, u32[]{:S(2)}, u32[]{:S(2)}) collective-permute-start(f32[1,1024]{1,0:T(1,128)S(1)} %get-tuple-element.33), channel_id=1, source_target_pairs={{0,1},{1,2},{2,3},{3,0},{4,5},{5,6},{6,7},{7,4},{8,9},{9,10},{10,1... | collective-permute-start | bytes 12296 | tf_op jit(solution)/shard_map/ppermute | solution.py:31
  30.7 23.8 %copy-start.4 = (bf16[3,256]{1,0:T(4,128)(2,1)S(1)}, bf16[3,256]{1,0:T(4,128)(2,1)}, u32[]{:S(2)}) copy-start(bf16[3,256]{1,0:T(4,128)(2,1)} %embed.1) | copy-start | bytes 4612
  30.7 8.2 %collective-permute-start.1 = (f32[1,1024]{1,0:T(1,128)S(1)}, f32[1,1024]{1,0:T(1,128)}, u32[]{:S(2)}, u32[]{:S(2)}) collective-permute-start(f32[1,1024]{1,0:T(1,128)S(1)} %get-tuple-element.34), channel_id=1, source_target_pairs={{0,2},{1,3},{2,0},{3,1},{4,6},{5,7},{6,4},{7,5},{8,10},{9,11},{10,... | collective-permute-start | bytes 12296 | tf_op jit(solution)/shard_map/ppermute | solution.py:31
  39.6 14.8 %collective-permute-start.3 = (bf16[4,4,32,2304]{3,2,1,0:T(8,128)(2,1)S(1)}, bf16[4,4,32,2304]{3,2,1,0:T(8,128)(2,1)}, u32[]{:S(2)}, u32[]{:S(2)}) collective-permute-start(bf16[4,4,32,2304]{3,2,1,0:T(8,128)(2,1)S(1)} %all-to-all-done.1.mine), channel_id=1, source_target_pairs={{0,16},{16,0},{32,48},{48,32},{64,80},{80,64},{96,112},{112,96},{1... | collective-permute-start | bytes 7077896 | tf_op jit(solution)/shard_map/ppermute | solution.py:21
  50.7 1.6 copy-start.1
  52.3 1.0 copy-start.2
  53.3 1.1 copy-start.3
  67.6 6.8 %collective-permute-start.4 = (bf16[4,4,32,2560]{3,2,1,0:T(8,128)(2,1)S(1)}, bf16[4,4,32,2560]{3,2,1,0:T(8,128)(2,1)S(1)}, u32[]{:S(2)}, u32[]{:S(2)}) collective-permute-start(bf16[4,4,32,2560]{3,2,1,0:T(8,128)(2,1)S(1)} %get-tuple-element.27), channel_id=1, source_target_pairs={{0,16},{16,0},{32,48},{48,32},{64,80},{80,64},{96,112},{112,96},{1... | collective-permute-start | bytes 7864328 | tf_op jit(solution)/shard_map/ppermute | solution.py:21
  155.4 9.8 %collective-permute-start.5 = (bf16[32,16,256]{2,1,0:T(8,128)(2,1)S(1)}, bf16[32,16,256]{2,1,0:T(8,128)(2,1)S(1)}, u32[]{:S(2)}, u32[]{:S(2)}) collective-permute-start(bf16[32,16,256]{2,1,0:T(8,128)(2,1)S(1)} %bitcast.22), channel_id=1, source_target_pairs={{0,16},{16,0},{32,48},{48,32},{64,80},{80,64},{96,112},{112,96},{1... | collective-permute-start | bytes 786440 | tf_op jit(solution)/shard_map/ppermute | solution.py:21

commit v13 on v11

--- a/solution.py
+++ b/solution.py
@@ -18,20 +18,6 @@
 
 def swap(block, axis, bits):
     return lax.ppermute(block, axis, [(i, i ^ bits) for i in range(lax.axis_size(axis))])
-
-
-def turned(block, axis, distance):
-    size = lax.axis_size(axis)
-    return lax.ppermute(block, axis, [(i, (i + distance) % size) for i in range(size)])
-
-
-def turned(block, axis, distance):
-    size = lax.axis_size(axis)
-    return lax.ppermute(block, axis, [(i, (i + distance) % size) for i in range(size)])
-
-
-def exchange(blocks, axis):
-    return lax.all_to_all(blocks, axis, 0, 0, tiled=True)
 
 
 def nn(left, right):
@@ -275,8 +261,8 @@
     state = lax.broadcasted_iota(jnp.int32, asked.shape, 0)
     asked = jnp.sum(jnp.where(state == s, asked, 0), axis=0, keepdims=True)
     count = asked[:, slots]
-    asked = jnp.broadcast_to(jnp.pad(asked, ((0, 0), (0, 127 - slots))), (8, 128))
-    asked = lax.all_gather(asked[None], "shard", axis=0, tiled=True)[:, 0, : slots + 1]
+    asked = jnp.concatenate([asked, swap(asked, "shard", 1)])
+    asked = jnp.concatenate([asked, swap(asked, "shard", 3)])
 
     unit = lax.dynamic_slice_in_dim(conv_weight[0].T, c * 32, 32, 0)
     unit = jnp.broadcast_to(unit[None], (4,) + unit.shape)
@@ -290,10 +276,9 @@
     hits = (asked[:, :slots, None] == positions) & live[:, :, None]
     picks = jnp.sum(hits.astype(F32), axis=1).astype(BF16)
     partial = jnp.dot(picks, database, preferred_element_type=F32)
-    summed = lax.dynamic_slice_in_dim(partial, h, 1, 0)
-    for d in (1, 2, 3):
-        piece = lax.dynamic_slice_in_dim(partial, (h + 4 - d) % 4, 1, 0)
-        summed = summed + turned(piece, "shard", -d)
+    summed = partial[0:1]
+    for place, bits in ((1, 1), (2, 3), (3, 2)):
+        summed = summed + swap(partial[place : place + 1], "shard", bits)
     context = (summed / jnp.maximum(count, 1).astype(F32)[:, None]).astype(BF16)
     context = jnp.broadcast_to(context, (16, context.shape[1]))
 

time: 167 us -> 171 us (1.024)
  starting transfers between devices: 39.2 us -> 46.7 us
  blocking collectives: 86.1 us -> 80.1 us
  waiting for transfers between devices: 6.43 us -> 9.34 us
    ppermute x3 -> x8, starting transfers between devices: 20.5 us -> 37.7 us  [swap(): lax.ppermute(block, axis, [(i, i ^ bits) for i in range(lax.axis_size(axi...]
    ppermute x3 -> x0, starting transfers between devices: 10.1 us -> none  [turned(): lax.ppermute(block, axis, [(i, (i + distance) % size) for i in range(size)])]
    all_gather x1 -> x0, blocking collectives: 7.64 us -> none  [body(): lax.all_gather(asked[None], 'shard', axis=0, tiled=True)[:, 0, :slots + 1]]
    ppermute x3 -> x8, waiting for transfers between devices: 6.01 us -> 9.34 us  [swap(): lax.ppermute(block, axis, [(i, i ^ bits) for i in range(lax.axis_size(axi...]
  transfers between devices with their start and end apart: 8 -> 10, of which waited for: 3 -> 5; matrix products, arithmetic and copies ran while one was open for 5% -> 5% of each run, Pallas kernels for 1% -> 1%
where the time goes in v13:
time: 171 us; the launch traced here: 170 us
  blocking collectives  80.1 us (47%)
  starting transfers between devices  46.7 us (27%)
  Pallas kernels  17.3 us (10%)
  local copies, waits for them, and re-layouts  12.2 us (7%)
  waiting for transfers between devices  9.34 us (5%)
  other arithmetic  1.83 us (1%)
    all_to_all x2, blocking collectives, along_z(): lax.all_to_all(blocks, 'dp', 0, 0, axis_index_groups=line, tiled=True)  45.8 us
    ppermute x8, starting transfers between devices, swap(): lax.ppermute(block, axis, [(i, i ^ bits) for i in range(lax.axis_size(axi...  37.7 us
    all_to_all x2, blocking collectives, ring(): lax.all_to_all(blocks, ('dp', 'section', 'shard'), 0, 0, axis_index_group...  34.3 us
    pallas_call x5, Pallas kernels, call(): pl.pallas_call(kernel, out_shape=outs, in_specs=[pl.BlockSpec(memory_spac...  17.3 us
    ppermute x8, waiting for transfers between devices, swap(): lax.ppermute(block, axis, [(i, i ^ bits) for i in range(lax.axis_size(axi...  9.34 us
    all_to_all x2, starting transfers between devices, ring(): lax.all_to_all(blocks, ('dp', 'section', 'shard'), 0, 0, axis_index_group...  9 us
  transfers between devices with their start and end apart: 10, of which 5 were waited for; matrix products, arithmetic and copies ran while one was open for 5% of the time, Pallas kernels for 1%

profile of v13, /device:TPU:1, one launch (start us, length us, event | category | flops | bytes accessed | tf_op | source)
XLA Modules:
  0.0 170.3 jit_solution(5702720799067683669)
XLA Ops:
  0.6 0.0 copy-start
  0.7 1.0 dynamic-slice_bitcast_fusion
  1.7 0.8 broadcast_in_dim.50
  2.5 5.0 %all-to-all-start = ((bf16[4,32,2304]{2,1,0:T(8,128)(2,1)}), bf16[4,32,2304]{2,1,0:T(8,128)(2,1)S(1)}, u32[]{:S(2)}, u32[]{:S(2)}) async-start(bf16[4,32,2304]{2,1,0:T(8,128)(2,1)} %broadcast_in_dim.50), calls=%async_computation | async-start | bytes 1179648 | tf_op jit(solution)/shard_map/all_to_all | solution.py:255
  7.5 0.7 copy.16
  8.3 0.8 fusion.2
  9.0 3.1 %collective-permute-start = (s32[1,11]{1,0:T(1,128)S(1)}, s32[1,11]{1,0:T(1,128)S(1)}, u32[]{:S(2)}, u32[]{:S(2)}) collective-permute-start(s32[1,11]{1,0:T(1,128)S(1)} %bitcast.22), channel_id=1, source_target_pairs={{0,1},{1,0},{2,3},{3,2},{4,5},{5,4},{6,7},{7,6},{8,9},{9,8},{10,11... | collective-permute-start | bytes 140 | tf_op jit(solution)/shard_map/ppermute | solution.py:20
  12.2 1.2 collective-permute-done
  13.3 4.4 %collective-permute-start.1 = (s32[2,11]{1,0:T(2,128)S(1)}, s32[2,11]{1,0:T(2,128)S(1)}, u32[]{:S(2)}, u32[]{:S(2)}) collective-permute-start(s32[2,11]{1,0:T(2,128)S(1)} %pad_add_fusion.1), channel_id=1, source_target_pairs={{0,3},{1,2},{2,1},{3,0},{4,7},{5,6},{6,5},{7,4},{8,11},{9,10},{10,... | collective-permute-start | bytes 272 | tf_op jit(solution)/shard_map/ppermute | solution.py:20
  17.7 1.3 collective-permute-done.1
  19.0 1.7 broadcast_in_dim.51
  20.7 4.0 %all-to-all-start.1 = ((bf16[4,4,32,2304]{3,2,1,0:T(8,128)(2,1)}), bf16[4,4,32,2304]{3,2,1,0:T(8,128)(2,1)S(1)}, u32[]{:S(2)}, u32[]{:S(2)}) async-start(bf16[4,4,32,2304]{3,2,1,0:T(8,128)(2,1)} %broadcast_in_dim.51), calls=%async_computation.1 | async-start | bytes 4718592 | tf_op jit(solution)/shard_map/all_to_all | solution.py:255
  24.7 0.1 copy.17
  24.8 0.2 slice_reduce_fusion
  25.0 0.1 convert_reduce_fusion
  25.1 1.2 fusion.6
  26.3 0.6 fusion.5
  26.9 3.4 %collective-permute-start.2 = (f32[1,1024]{1,0:T(1,128)}, f32[1,1024]{1,0:T(1,128)S(1)}, u32[]{:S(2)}, u32[]{:S(2)}) collective-permute-start(f32[1,1024]{1,0:T(1,128)} %get-tuple-element.32), channel_id=1, source_target_pairs={{0,1},{1,0},{2,3},{3,2},{4,5},{5,4},{6,7},{7,6},{8,9},{9,8},{10,11... | collective-permute-start | bytes 12296 | tf_op jit(solution)/shard_map/ppermute | solution.py:20
  30.3 4.3 %collective-permute-start.4 = (f32[1,1024]{1,0:T(1,128)}, f32[1,1024]{1,0:T(1,128)S(1)}, u32[]{:S(2)}, u32[]{:S(2)}) collective-permute-start(f32[1,1024]{1,0:T(1,128)} %get-tuple-element.33), channel_id=1, source_target_pairs={{0,2},{1,3},{2,0},{3,1},{4,6},{5,7},{6,4},{7,5},{8,10},{9,11},{10,... | collective-permute-start | bytes 12296 | tf_op jit(solution)/shard_map/ppermute | solution.py:20
  34.6 1.9 %collective-permute-start.3 = (f32[1,1024]{1,0:T(1,128)}, f32[1,1024]{1,0:T(1,128)S(1)}, u32[]{:S(2)}, u32[]{:S(2)}) collective-permute-start(f32[1,1024]{1,0:T(1,128)} %get-tuple-element.34), channel_id=1, source_target_pairs={{0,3},{1,2},{2,1},{3,0},{4,7},{5,6},{6,5},{7,4},{8,11},{9,10},{10,... | collective-permute-start | bytes 12296 | tf_op jit(solution)/shard_map/ppermute | solution.py:20
  36.5 1.1 dynamic-slice_reduce_fusion
  37.6 0.6 slice.30
  38.8 0.1 reshape.71
  38.9 0.7 pad.16
  39.6 1.0 reshape.72
  40.6 0.9 collective-permute-done.4
  41.6 10.0 %collective-permute-start.5 = (bf16[4,4,32,2304]{3,2,1,0:T(8,128)(2,1)S(1)}, bf16[4,4,32,2304]{3,2,1,0:T(8,128)(2,1)}, u32[]{:S(2)}, u32[]{:S(2)}) collective-permute-start(bf16[4,4,32,2304]{3,2,1,0:T(8,128)(2,1)S(1)} %all-to-all-done.1.mine), channel_id=1, source_target_pairs={{0,16},{16,0},{32,48},{48,32},{64,80},{80,64},{96,112},{112,96},{1... | collective-permute-start | bytes 7077896 | tf_op jit(solution)/shard_map/ppermute | solution.py:20
  51.6 0.7 dynamic-slice_reduce_fusion.1
  52.3 0.1 reshape.73
  52.4 0.1 reshape.74
  52.5 0.1 broadcast_in_dim.58.code_col
  52.6 0.1 pad_add_fusion.2.where
  52.7 1.6 copy-done.1
  54.3 1.0 copy-done.2
  55.4 1.1 encoder.1
  56.5 13.1 %trunk.1 = (bf16[4,4,32,2560]{3,2,1,0:T(8,128)(2,1)S(1)}, bf16[4,4,32,2560]{3,2,1,0:T(8,128)(2,1)S(1)}) custom-call(s32[3]{0:T(128)S(1)} %pad_add_fusion.2.where, bf16[16,1024]{1,0:T(8,128)(2,1)S(1)} %broadcast_in_dim.53.context, f32[16,1024]{1,0:T(8,128)S(1)} %get-tuple-element.21.preact_in, bf16[16,1024]{1,0:T(8,128)(2,1)S(1)} %get-tuple-element.22.hidden_in, ...), custom_call_target="tpu_custom_call" | custom-call | flops 5435817984 | bytes 16777216 | tf_op jit(solution)/shard_map/trunk/pallas_call | solution.py:39
  69.6 1.9 %collective-permute-start.6 = (bf16[4,4,32,2560]{3,2,1,0:T(8,128)(2,1)S(1)}, bf16[4,4,32,2560]{3,2,1,0:T(8,128)(2,1)S(1)}, u32[]{:S(2)}, u32[]{:S(2)}) collective-permute-start(bf16[4,4,32,2560]{3,2,1,0:T(8,128)(2,1)S(1)} %get-tuple-element.27), channel_id=1, source_target_pairs={{0,16},{16,0},{32,48},{48,32},{64,80},{80,64},{96,112},{112,96},{1... | collective-permute-start | bytes 7864328 | tf_op jit(solution)/shard_map/ppermute | solution.py:20
  71.5 4.9 %collective-permute-done.6 = bf16[4,4,32,2560]{3,2,1,0:T(8,128)(2,1)S(1)} collective-permute-done((bf16[4,4,32,2560]{3,2,1,0:T(8,128)(2,1)S(1)}, bf16[4,4,32,2560]{3,2,1,0:T(8,128)(2,1)S(1)}, u32[]{:S(2)}, u32[]{:S(2)}) %collective-permute-start.6) | collective-permute-done | bytes 2621472 | tf_op jit(solution)/shard_map/ppermute | solution.py:20
  76.4 0.8 add_convert_fusion
  77.2 22.6 %all_to_all.30.pieces = bf16[4,4,32,2560]{3,2,1,0:T(8,128)(2,1)S(1)} all-to-all(bf16[4,4,32,2560]{3,2,1,0:T(8,128)(2,1)S(1)} %add_convert_fusion), channel_id=1, replica_groups={{0,1,2,3},{4,5,6,7},{8,9,10,11},{12,13,14,15},{16,20,24,28},{17,21,25,2..., dimensions={0} | all-to-all | bytes 5242880 | tf_op jit(solution)/shard_map/all_to_all | solution.py:255
  99.7 0.8 fold.1
  100.6 11.7 %all_to_all.31.pieces = bf16[4,32,3328]{2,1,0:T(8,128)(2,1)S(1)} all-to-all(bf16[4,32,3328]{2,1,0:T(8,128)(2,1)S(1)} %fold.1), channel_id=1, replica_groups={{0,4,8,12},{1,5,9,13},{2,6,10,14},{3,7,11,15},{16,17,18,19},{20,21,22,2..., dimensions={0} | all-to-all | bytes 1703936 | tf_op jit(solution)/shard_map/all_to_all | solution.py:255
  112.3 0.9 pack.1
  113.2 23.8 %all_to_all.32 = bf16[16,2,16,256]{3,2,1,0:T(8,128)(2,1)S(1)} all-to-all(bf16[16,2,16,256]{3,2,1,0:T(8,128)(2,1)S(1)} %bitcast.20), channel_id=1, replica_groups={{0,32,64,96,128,160,192,224,256,288,320,352,384,416,448,480},{16,48,80,..., dimensions={0} | all-to-all | bytes 524288 | tf_op jit(solution)/shard_map/all_to_all | solution.py:355
  137.1 22.0 %all_to_all.33 = bf16[16,2,16,256]{3,2,1,0:T(8,128)(2,1)S(1)} all-to-all(bf16[16,2,16,256]{3,2,1,0:T(8,128)(2,1)S(1)} %broadcast_in_dim.56), channel_id=1, replica_groups={{0,32,64,96,128,160,192,224,256,288,320,352,384,416,448,480},{16,48,80,..., dimensions={0} | all-to-all | bytes 524288 | tf_op jit(solution)/shard_map/all_to_all | solution.py:355
  159.1 8.6 %collective-permute-start.7 = (bf16[32,16,256]{2,1,0:T(8,128)(2,1)S(1)}, bf16[32,16,256]{2,1,0:T(8,128)(2,1)S(1)}, u32[]{:S(2)}, u32[]{:S(2)}) collective-permute-start(bf16[32,16,256]{2,1,0:T(8,128)(2,1)S(1)} %bitcast.18), channel_id=1, source_target_pairs={{0,16},{16,0},{32,48},{48,32},{64,80},{80,64},{96,112},{112,96},{1... | collective-permute-start | bytes 786440 | tf_op jit(solution)/shard_map/ppermute | solution.py:20
  167.7 1.1 collective-permute-done.7.theirs
  168.9 1.4 finish.1
  (23 shorter events, 0.2 us)
Async XLA Ops:
  0.6 35.9 %copy-start = (bf16[4,361,256]{2,0,1:T(4,128)(2,1)S(1)}, bf16[4,361,256]{2,0,1:T(4,128)(2,1)}, u32[]{:S(2)}) copy-start(bf16[4,361,256]{2,0,1:T(4,128)(2,1)} %param.17) | copy-start | bytes 2217988
  2.5 16.5 %all-to-all-start = ((bf16[4,32,2304]{2,1,0:T(8,128)(2,1)}), bf16[4,32,2304]{2,1,0:T(8,128)(2,1)S(1)}, u32[]{:S(2)}, u32[]{:S(2)}) async-start(bf16[4,32,2304]{2,1,0:T(8,128)(2,1)} %broadcast_in_dim.50), calls=%async_computation | async-start | bytes 1179648 | tf_op jit(solution)/shard_map/all_to_all | solution.py:255
  9.0 4.3 %collective-permute-start = (s32[1,11]{1,0:T(1,128)S(1)}, s32[1,11]{1,0:T(1,128)S(1)}, u32[]{:S(2)}, u32[]{:S(2)}) collective-permute-start(s32[1,11]{1,0:T(1,128)S(1)} %bitcast.22), channel_id=1, source_target_pairs={{0,1},{1,0},{2,3},{3,2},{4,5},{5,4},{6,7},{7,6},{8,9},{9,8},{10,11... | collective-permute-start | bytes 140 | tf_op jit(solution)/shard_map/ppermute | solution.py:20
  13.3 5.7 %collective-permute-start.1 = (s32[2,11]{1,0:T(2,128)S(1)}, s32[2,11]{1,0:T(2,128)S(1)}, u32[]{:S(2)}, u32[]{:S(2)}) collective-permute-start(s32[2,11]{1,0:T(2,128)S(1)} %pad_add_fusion.1), channel_id=1, source_target_pairs={{0,3},{1,2},{2,1},{3,0},{4,7},{5,6},{6,5},{7,4},{8,11},{9,10},{10,... | collective-permute-start | bytes 272 | tf_op jit(solution)/shard_map/ppermute | solution.py:20
  20.7 20.9 %all-to-all-start.1 = ((bf16[4,4,32,2304]{3,2,1,0:T(8,128)(2,1)}), bf16[4,4,32,2304]{3,2,1,0:T(8,128)(2,1)S(1)}, u32[]{:S(2)}, u32[]{:S(2)}) async-start(bf16[4,4,32,2304]{3,2,1,0:T(8,128)(2,1)} %broadcast_in_dim.51), calls=%async_computation.1 | async-start | bytes 4718592 | tf_op jit(solution)/shard_map/all_to_all | solution.py:255
  26.9 13.7 %collective-permute-start.2 = (f32[1,1024]{1,0:T(1,128)}, f32[1,1024]{1,0:T(1,128)S(1)}, u32[]{:S(2)}, u32[]{:S(2)}) collective-permute-start(f32[1,1024]{1,0:T(1,128)} %get-tuple-element.32), channel_id=1, source_target_pairs={{0,1},{1,0},{2,3},{3,2},{4,5},{5,4},{6,7},{7,6},{8,9},{9,8},{10,11... | collective-permute-start | bytes 12296 | tf_op jit(solution)/shard_map/ppermute | solution.py:20
  30.3 11.3 %collective-permute-start.4 = (f32[1,1024]{1,0:T(1,128)}, f32[1,1024]{1,0:T(1,128)S(1)}, u32[]{:S(2)}, u32[]{:S(2)}) collective-permute-start(f32[1,1024]{1,0:T(1,128)} %get-tuple-element.33), channel_id=1, source_target_pairs={{0,2},{1,3},{2,0},{3,1},{4,6},{5,7},{6,4},{7,5},{8,10},{9,11},{10,... | collective-permute-start | bytes 12296 | tf_op jit(solution)/shard_map/ppermute | solution.py:20
  34.6 21.9 %copy-start.3 = (bf16[3,256]{1,0:T(4,128)(2,1)S(1)}, bf16[3,256]{1,0:T(4,128)(2,1)}, u32[]{:S(2)}) copy-start(bf16[3,256]{1,0:T(4,128)(2,1)} %embed.1) | copy-start | bytes 4612
  34.6 6.9 %collective-permute-start.3 = (f32[1,1024]{1,0:T(1,128)}, f32[1,1024]{1,0:T(1,128)S(1)}, u32[]{:S(2)}, u32[]{:S(2)}) collective-permute-start(f32[1,1024]{1,0:T(1,128)} %get-tuple-element.34), channel_id=1, source_target_pairs={{0,3},{1,2},{2,1},{3,0},{4,7},{5,6},{6,5},{7,4},{8,11},{9,10},{10,... | collective-permute-start | bytes 12296 | tf_op jit(solution)/shard_map/ppermute | solution.py:20
  41.6 14.9 %collective-permute-start.5 = (bf16[4,4,32,2304]{3,2,1,0:T(8,128)(2,1)S(1)}, bf16[4,4,32,2304]{3,2,1,0:T(8,128)(2,1)}, u32[]{:S(2)}, u32[]{:S(2)}) collective-permute-start(bf16[4,4,32,2304]{3,2,1,0:T(8,128)(2,1)S(1)} %all-to-all-done.1.mine), channel_id=1, source_target_pairs={{0,16},{16,0},{32,48},{48,32},{64,80},{80,64},{96,112},{112,96},{1... | collective-permute-start | bytes 7077896 | tf_op jit(solution)/shard_map/ppermute | solution.py:20
  52.7 1.6 copy-start.1
  54.3 1.0 copy-start.2
  69.6 6.8 %collective-permute-start.6 = (bf16[4,4,32,2560]{3,2,1,0:T(8,128)(2,1)S(1)}, bf16[4,4,32,2560]{3,2,1,0:T(8,128)(2,1)S(1)}, u32[]{:S(2)}, u32[]{:S(2)}) collective-permute-start(bf16[4,4,32,2560]{3,2,1,0:T(8,128)(2,1)S(1)} %get-tuple-element.27), channel_id=1, source_target_pairs={{0,16},{16,0},{32,48},{48,32},{64,80},{80,64},{96,112},{112,96},{1... | collective-permute-start | bytes 7864328 | tf_op jit(solution)/shard_map/ppermute | solution.py:20
  159.1 9.8 %collective-permute-start.7 = (bf16[32,16,256]{2,1,0:T(8,128)(2,1)S(1)}, bf16[32,16,256]{2,1,0:T(8,128)(2,1)S(1)}, u32[]{:S(2)}, u32[]{:S(2)}) collective-permute-start(bf16[32,16,256]{2,1,0:T(8,128)(2,1)S(1)} %bitcast.18), channel_id=1, source_target_pairs={{0,16},{16,0},{32,48},{48,32},{64,80},{80,64},{96,112},{112,96},{1... | collective-permute-start | bytes 786440 | tf_op jit(solution)/shard_map/ppermute | solution.py:20
